TPU v7x, 32 devices: a whole 2x2x4 slice. The times are simulated.
32 devices in a mesh: section: 2 (over core), ctx: 4 (over y, x), wt: 4 (over z).
Axes of the slice: x: 2, y: 2, z: 4, core: 2. Of those that a mesh axis runs over, the one named last changes fastest.
Arguments:
- tokens: bfloat16 [2, 1024, 1536], P(None, ('ctx', 'wt')), may hold values from -6 to 6
- cotangent: bfloat16 [2, 1024, 1536], P(None, ('ctx', 'wt')), may hold values from -6 to 6
- blocks: int32 [2, 8], replicated, may hold values from 0 to 7, each once within a row
- routes: int32 [2, 2, 1024, 8], P('section', None, 'ctx'), may hold values from 0 to 15, all different within a row; in each aligned block of 256 rows (0 to 255, 256 to 511, ..., all dimensions but the last counted through in order) at most 160 rows name the same one
- norm_gain: float32 [2, 2, 1536], P('section'), may hold values from 0.5 to 1.5
- w_query: bfloat16 [2, 1536, 1536], P('section', 'ctx', 'wt'), may hold values from -1.25 to 1.25
- key_value_weight: bfloat16 [2, 1536, 8, 128], P('section', 'ctx', 'wt'), may hold values from -0.15625 to 0.15625
- w_attn_out: bfloat16 [2, 1536, 1536], P('section', 'wt', 'ctx'), may hold values from -2.5 to 2.5
- router: bfloat16 [2, 1536, 16], P('section'), may hold values from -0.078125 to 0.078125
- w_in: bfloat16 [2, 16, 1536, 1024], P('section', 'wt', 'ctx'), may hold values from -0.15625 to 0.15625
- w_down: bfloat16 [2, 16, 512, 1536], P('section', 'wt', 'ctx'), may hold values from -1 to 1
Outputs:
- layer_out: bfloat16 [2, 2, 1024, 1536], P('section', None, ('ctx', 'wt'))
- input_grads: bfloat16 [2, 2, 1024, 1536], P('section', None, ('ctx', 'wt'))
- grad_gain: float32 [2, 2, 1536], P('section', None, ('ctx', 'wt'))
- grad_query: float32 [2, 1536, 1536], P('section', 'ctx', 'wt')
- grad_kv: float32 [2, 1536, 8, 128], P('section', 'ctx', 'wt')
- grad_attn_out: float32 [2, 1536, 1536], P('section', 'wt', 'ctx')
- grad_router: float32 [2, 1536, 16], P('section', ('ctx', 'wt'))
- grad_in: float32 [2, 16, 1536, 1024], P('section', 'wt', 'ctx')
- grad_down: float32 [2, 16, 512, 1536], P('section', 'wt', 'ctx')
Inputs may be any that keep to these rules, and one draw needn't show every extreme that they name: `blocks`: each row names every stored block of a micro-batch once. `routes`: each token names 8 different experts; among the 256 rows of one index of ctx in one micro-batch no expert is named by more than 160 rows, and in every draw some expert is named by exactly 160.
All inputs are finite; a program needn't handle non-finite values.
Results may differ from a plain program's by a relative error of at most 0.034.
Values may be sent and summed in bfloat16 or wider, within the bound.
A program may use at most 256 MiB of HBM per device.

v0:
```python
import jax
import jax.numpy as jnp
from jax import lax
from jax.sharding import PartitionSpec as P

MODEL_WIDTH = 1536
HEAD_SIZE = 64
FF = 512
TOPK = 8
CONT_LEN = 1024


EPSILON = 1e-06
ROPE_BASE = 10000.0
MASKED = -1e30


def passed_along(shard, axis, by):
    devices = lax.axis_size(axis)
    pairs = [(i, i + by) for i in range(devices) if 0 <= i + by < devices]
    return lax.ppermute(shard, axis, pairs)


def inverse_freq(head_width):
    return jnp.power(ROPE_BASE, -jnp.arange(head_width // 2, dtype=jnp.float32) * 2.0 / head_width)


def rotate(values, angles):
    half_width = values.shape[-1] // 2
    cosine = jnp.cos(angles)[:, None, :]
    sine_part = jnp.sin(angles)[:, None, :]
    leading = values[..., :half_width]
    trailing = values[..., half_width:]
    return jnp.concatenate(
        [leading * cosine - trailing * sine_part, trailing * cosine + leading * sine_part], -1
    )


def unrotate(gradient, angles):
    half_width = gradient.shape[-1] // 2
    cosine = jnp.cos(angles)[:, None, :]
    sine_part = jnp.sin(angles)[:, None, :]
    leading = gradient[..., :half_width]
    trailing = gradient[..., half_width:]
    return jnp.concatenate(
        [leading * cosine + trailing * sine_part, trailing * cosine - leading * sine_part], -1
    )


def layout(blocks, micro_index, seq_len):
    chosen = lax.dynamic_index_in_dim(blocks, micro_index, 0, False)
    block_len = seq_len // blocks.shape[1]
    placed = (
        chosen[:, None] * block_len + jnp.arange(block_len, dtype=jnp.int32)[None, :]
    ).reshape(-1)
    is_later = micro_index > 0
    rpos = jnp.where(is_later, seq_len + placed % CONT_LEN, placed)
    seg = jnp.where(is_later, 1 + placed // CONT_LEN, 0)
    return (rpos, seg)


def norm_scale(stream):
    return lax.rsqrt(jnp.mean(stream * stream, -1, keepdims=True) + EPSILON)


def norm_back(stream, gain_vec, d_normed):
    scale_rows = norm_scale(stream)
    weighted = gain_vec * d_normed
    gain_grad = jnp.sum(d_normed * stream * scale_rows, 0)
    d_stream = scale_rows * weighted - stream * scale_rows * scale_rows * scale_rows * jnp.mean(
        weighted * stream, -1, keepdims=True
    )
    return (d_stream, gain_grad)


def gather_rows(values):
    return lax.all_gather(values, "wt", axis=0, tiled=True)


def sum_rows(values):
    return lax.psum_scatter(
        values.astype(jnp.bfloat16), "wt", scatter_dimension=0, tiled=True
    ).astype(jnp.float32)


def gather_grads(values):
    return lax.all_gather(values, "wt", axis=0, tiled=True)


def scores(query_rows, key_part, q_pos, q_seg, k_pos, k_seg):
    logit_block = jnp.einsum(
        "qhgd,khd->hgqk", query_rows, key_part, preferred_element_type=jnp.float32
    ) * (1.0 / HEAD_SIZE)
    allowed = ((k_seg[None, :] == 0) | (k_seg[None, :] == q_seg[:, None])) & (
        k_pos[None, :] <= q_pos[:, None]
    )
    return (logit_block, allowed)


def key_slice(keyset, k_pos, k_seg, block_index, block_span_width):
    offset = block_index * block_span_width
    return (
        lax.dynamic_slice_in_dim(keyset, offset, block_span_width, 0),
        lax.dynamic_slice_in_dim(k_pos, offset, block_span_width, 0),
        lax.dynamic_slice_in_dim(k_seg, offset, block_span_width, 0),
    )


def stat_sweep(row_stats, query_rows, q_pos, q_seg, keyset, k_pos, k_seg):
    block_span_width = min(512, keyset.shape[0])

    def stat_sweep_step(current, block_index):
        running, summed = current
        key_block, pos_block, seg_block = key_slice(
            keyset, k_pos, k_seg, block_index, block_span_width
        )
        logit_block, allowed = scores(
            query_rows, key_block[..., :HEAD_SIZE], q_pos, q_seg, pos_block, seg_block
        )
        logit_block = jnp.where(allowed, logit_block, MASKED)
        new_max = jnp.maximum(running, jnp.max(logit_block, -1))
        summed = summed * jnp.exp(running - new_max) + jnp.sum(
            jnp.where(allowed, jnp.exp(logit_block - new_max[..., None]), 0.0), -1
        )
        return ((new_max, summed), None)

    row_stats, unused = lax.scan(
        stat_sweep_step, row_stats, jnp.arange(keyset.shape[0] // block_span_width)
    )
    return row_stats


def value_sweep(accumulated, query_rows, q_pos, q_seg, keyset, k_pos, k_seg, log_total):
    block_span_width = min(512, keyset.shape[0])

    def value_sweep_step(current, block_index):
        key_block, pos_block, seg_block = key_slice(
            keyset, k_pos, k_seg, block_index, block_span_width
        )
        logit_block, allowed = scores(
            query_rows, key_block[..., :HEAD_SIZE], q_pos, q_seg, pos_block, seg_block
        )
        attn_probs = jnp.where(allowed, jnp.exp(logit_block - log_total[..., None]), 0.0).astype(
            jnp.bfloat16
        )
        return (
            current
            + jnp.einsum(
                "hgqk,khd->qhgd",
                attn_probs,
                key_block[..., HEAD_SIZE:],
                preferred_element_type=jnp.float32,
            ),
            None,
        )

    accumulated, unused = lax.scan(
        value_sweep_step, accumulated, jnp.arange(keyset.shape[0] // block_span_width)
    )
    return accumulated


def grad_sweep(
    d_query, query_rows, q_pos, q_seg, keyset, k_pos, k_seg, log_total, d_out, delta_row
):
    block_span_width = min(512, keyset.shape[0])

    def grad_sweep_step(current, block_index):
        key_block, pos_block, seg_block = key_slice(
            keyset, k_pos, k_seg, block_index, block_span_width
        )
        key_part = key_block[..., :HEAD_SIZE]
        value_part = key_block[..., HEAD_SIZE:]
        logit_block, allowed = scores(query_rows, key_part, q_pos, q_seg, pos_block, seg_block)
        attn_probs = jnp.where(allowed, jnp.exp(logit_block - log_total[..., None]), 0.0)
        d_probs = jnp.einsum(
            "qhgd,khd->hgqk", d_out, value_part, preferred_element_type=jnp.float32
        )
        d_score = (attn_probs * (d_probs - delta_row[..., None])).astype(jnp.bfloat16)
        current = current + jnp.einsum(
            "hgqk,khd->qhgd", d_score, key_part, preferred_element_type=jnp.float32
        ) * (1.0 / HEAD_SIZE)
        d_keys = jnp.einsum(
            "hgqk,qhgd->khd", d_score, query_rows, preferred_element_type=jnp.float32
        ) * (1.0 / HEAD_SIZE)
        d_values = jnp.einsum(
            "hgqk,qhgd->khd",
            attn_probs.astype(jnp.bfloat16),
            d_out,
            preferred_element_type=jnp.float32,
        )
        return (current, jnp.concatenate([d_keys, d_values], -1))

    d_query, d_pairs = lax.scan(
        grad_sweep_step, d_query, jnp.arange(keyset.shape[0] // block_span_width)
    )
    return (d_query, d_pairs.reshape(keyset.shape[0], keyset.shape[1], 2 * HEAD_SIZE))


def route_gates(normed_mid, router_table, route_rows):
    logits = jnp.dot(normed_mid, router_table, preferred_element_type=jnp.float32)
    onehot = (
        route_rows[:, :, None] == jnp.arange(router_table.shape[1], dtype=jnp.int32)[None, None, :]
    )
    chosen = jnp.sum(jnp.where(onehot, logits[:, None, :], 0.0), -1)
    chosen = chosen - jnp.max(chosen, 1, keepdims=True)
    expos = jnp.exp(chosen)
    return expos / jnp.sum(expos, 1, keepdims=True)


def dispatch(route_rows, gates, first_expert, expert_count, capacity):
    count_of_rows = route_rows.shape[0]
    local_ids = first_expert + jnp.arange(expert_count, dtype=jnp.int32)
    route_hits = route_rows[:, :, None] == local_ids[None, None, :]
    any_hit = jnp.any(route_hits, 1)
    slot_rank = jnp.cumsum(any_hit.astype(jnp.int32), 0) - 1
    target = jnp.where(any_hit, slot_rank, capacity)
    owner = jnp.broadcast_to(
        jnp.arange(expert_count, dtype=jnp.int32)[None, :], (count_of_rows, expert_count)
    )
    source = jnp.broadcast_to(
        jnp.arange(count_of_rows, dtype=jnp.int32)[:, None], (count_of_rows, expert_count)
    )
    slot_rows = (
        jnp.zeros((expert_count, capacity + 1), jnp.int32)
        .at[owner, target]
        .set(source)[:, :capacity]
    )
    filled = jnp.sum(any_hit.astype(jnp.int32), 0)
    is_valid = jnp.arange(capacity, dtype=jnp.int32)[None, :] < filled[:, None]
    row_weight = jnp.sum(jnp.where(route_hits, gates[:, :, None], 0.0), 1)
    slot_weight = jnp.where(
        is_valid, jnp.take_along_axis(jnp.transpose(row_weight), slot_rows, 1), 0.0
    )
    return (route_hits, slot_rows, is_valid, slot_weight)


def forward(
    stream,
    geometry_set,
    is_later,
    prompt_keys,
    gains,
    route_rows,
    matrices,
    router_table,
    first_expert,
    capacity,
):
    query_mat, pairing_matrix, out_mat, gate_up_mat, down_mat = matrices
    q_pos, q_seg, k_pos, k_seg, p_pos, p_seg, angles = geometry_set
    count_of_rows = route_rows.shape[0]
    heads_q = query_mat.shape[1] // HEAD_SIZE
    heads_kv = pairing_matrix.shape[1]
    normalized_input = gather_rows((stream * norm_scale(stream) * gains[0]).astype(jnp.bfloat16))
    query_rows = rotate(
        jnp.dot(normalized_input, query_mat, preferred_element_type=jnp.float32).reshape(
            count_of_rows, heads_q, HEAD_SIZE
        ),
        angles,
    )
    query_rows = query_rows.astype(jnp.bfloat16).reshape(
        count_of_rows, heads_kv, heads_q // heads_kv, HEAD_SIZE
    )
    unnormalized_pairs = jnp.dot(
        normalized_input,
        pairing_matrix.reshape(pairing_matrix.shape[0], -1),
        preferred_element_type=jnp.float32,
    ).reshape(count_of_rows, heads_kv, 2 * HEAD_SIZE)
    own_pairs = jnp.concatenate(
        [rotate(unnormalized_pairs[..., :HEAD_SIZE], angles), unnormalized_pairs[..., HEAD_SIZE:]],
        -1,
    ).astype(jnp.bfloat16)
    all_keys = lax.all_gather(own_pairs, "ctx", axis=0, tiled=True)
    stat_shape = (heads_kv, heads_q // heads_kv, count_of_rows)
    row_stats = (jnp.full(stat_shape, MASKED, jnp.float32), jnp.zeros(stat_shape, jnp.float32))
    row_stats = stat_sweep(row_stats, query_rows, q_pos, q_seg, all_keys, k_pos, k_seg)

    def stats_prompt(current):
        return stat_sweep(current, query_rows, q_pos, q_seg, prompt_keys, p_pos, p_seg)

    def stats_skip(current):
        return current

    row_stats = lax.cond(is_later, stats_prompt, stats_skip, row_stats)
    log_total = row_stats[0] + jnp.log(row_stats[1])
    out_full = value_sweep(
        jnp.zeros(query_rows.shape, jnp.float32),
        query_rows,
        q_pos,
        q_seg,
        all_keys,
        k_pos,
        k_seg,
        log_total,
    )

    def values_prompt(current):
        return value_sweep(current, query_rows, q_pos, q_seg, prompt_keys, p_pos, p_seg, log_total)

    out_full = lax.cond(is_later, values_prompt, stats_skip, out_full)
    out_low = out_full.reshape(count_of_rows, heads_q * HEAD_SIZE).astype(jnp.bfloat16)
    stream_mid = stream + sum_rows(jnp.dot(out_low, out_mat, preferred_element_type=jnp.float32))
    normed_mid = gather_rows((stream_mid * norm_scale(stream_mid) * gains[1]).astype(jnp.bfloat16))
    gates = route_gates(normed_mid, router_table, route_rows)
    route_hits, slot_rows, is_valid, slot_weight = dispatch(
        route_rows, gates, first_expert, gate_up_mat.shape[0], capacity
    )
    picked = normed_mid[slot_rows]
    gate_up = jnp.einsum("ecd,edf->ecf", picked, gate_up_mat, preferred_element_type=jnp.float32)
    hidden = (jax.nn.silu(gate_up[..., :FF]) * gate_up[..., FF:]).astype(jnp.bfloat16)
    expert_out = jnp.einsum("ecf,efd->ecd", hidden, down_mat, preferred_element_type=jnp.float32)
    mixed = (
        jnp.zeros((count_of_rows, MODEL_WIDTH), jnp.float32)
        .at[slot_rows.reshape(-1)]
        .add((expert_out * slot_weight[..., None]).reshape(-1, MODEL_WIDTH))
    )
    stream_out = stream_mid + sum_rows(mixed)
    saved = {
        "stream": stream,
        "stream_mid": stream_mid,
        "normed_in": normalized_input,
        "normed_mid": normed_mid,
        "queries": query_rows,
        "all_keys": all_keys,
        "out_full": out_full,
        "out_low": out_low,
        "log_total": log_total,
        "gates": gates,
        "gate_up": gate_up,
        "expert_out": expert_out,
    }
    return (stream_out.astype(jnp.bfloat16), saved)


def backward(
    upstream,
    saved,
    geometry_set,
    is_later,
    prompt_keys,
    gains,
    route_rows,
    matrices,
    router_table,
    first_expert,
    capacity,
    row_offset,
    share_rows,
    prompt_carry,
):
    query_mat, pairing_matrix, out_mat, gate_up_mat, down_mat = matrices
    q_pos, q_seg, k_pos, k_seg, p_pos, p_seg, angles = geometry_set
    count_of_rows = route_rows.shape[0]
    expert_count = gate_up_mat.shape[0]
    d_mixed = gather_grads(upstream.astype(jnp.bfloat16))
    route_hits, slot_rows, is_valid, slot_weight = dispatch(
        route_rows, saved["gates"], first_expert, expert_count, capacity
    )
    picked_grad = d_mixed[slot_rows].astype(jnp.float32)
    d_expert = (picked_grad * slot_weight[..., None]).astype(jnp.bfloat16)
    d_weight = jnp.where(is_valid, jnp.sum(picked_grad * saved["expert_out"], -1), 0.0)
    gate_up = saved["gate_up"]
    gate_part = gate_up[..., :FF]
    up_part = gate_up[..., FF:]
    sigmoid_val = jax.nn.sigmoid(gate_part)
    activated = gate_part * sigmoid_val
    hidden = (activated * up_part).astype(jnp.bfloat16)
    d_hidden = jnp.einsum("ecd,efd->ecf", d_expert, down_mat, preferred_element_type=jnp.float32)
    d_gate_up = jnp.concatenate(
        [
            d_hidden * up_part * sigmoid_val * (1.0 + gate_part * (1.0 - sigmoid_val)),
            d_hidden * activated,
        ],
        -1,
    ).astype(jnp.bfloat16)
    picked = saved["normed_mid"][slot_rows]
    grad_down = jnp.einsum("ecf,ecd->efd", hidden, d_expert, preferred_element_type=jnp.float32)
    grad_in = jnp.einsum("ecd,ecf->edf", picked, d_gate_up, preferred_element_type=jnp.float32)
    d_picked = jnp.einsum(
        "ecf,edf->ecd", d_gate_up, gate_up_mat, preferred_element_type=jnp.float32
    )
    d_normed = (
        jnp.zeros((count_of_rows, MODEL_WIDTH), jnp.float32)
        .at[slot_rows.reshape(-1)]
        .add(d_picked.reshape(-1, MODEL_WIDTH))
    )
    owner = jnp.broadcast_to(jnp.arange(expert_count, dtype=jnp.int32)[:, None], slot_rows.shape)
    row_grad = (
        jnp.zeros((expert_count, count_of_rows), jnp.float32).at[owner, slot_rows].add(d_weight)
    )
    d_gates = jnp.sum(jnp.where(route_hits, jnp.transpose(row_grad)[:, None, :], 0.0), 2)
    d_normed, d_gate_rows = (
        lax.psum_scatter(
            d_normed.astype(jnp.bfloat16), "wt", scatter_dimension=0, tiled=True
        ).astype(jnp.float32),
        lax.psum_scatter(
            d_gates.astype(jnp.bfloat16), "wt", scatter_dimension=0, tiled=True
        ).astype(jnp.float32),
    )
    normed_rows = lax.dynamic_slice_in_dim(saved["normed_mid"], row_offset, share_rows, 0).astype(
        jnp.float32
    )
    local_routes = lax.dynamic_slice_in_dim(route_rows, row_offset, share_rows, 0)
    local_gates = lax.dynamic_slice_in_dim(saved["gates"], row_offset, share_rows, 0)
    d_choice = local_gates * (d_gate_rows - jnp.sum(local_gates * d_gate_rows, 1, keepdims=True))
    onehot = (
        local_routes[:, :, None]
        == jnp.arange(router_table.shape[1], dtype=jnp.int32)[None, None, :]
    )
    d_logits = jnp.sum(jnp.where(onehot, d_choice[:, :, None], 0.0), 1)
    grad_router = jnp.dot(
        jnp.transpose(normed_rows),
        d_logits,
        precision=lax.Precision.HIGHEST,
        preferred_element_type=jnp.float32,
    )
    d_normed = d_normed + jnp.dot(
        d_logits,
        jnp.transpose(router_table.astype(jnp.float32)),
        precision=lax.Precision.HIGHEST,
        preferred_element_type=jnp.float32,
    )
    d_mid, gain_grad_mid = norm_back(saved["stream_mid"], gains[1], d_normed)
    d_mid = upstream + d_mid
    d_attn = gather_grads(d_mid.astype(jnp.bfloat16))
    query_rows = saved["queries"]
    d_out = (
        jnp.dot(d_attn, jnp.transpose(out_mat), preferred_element_type=jnp.float32)
        .astype(jnp.bfloat16)
        .reshape(query_rows.shape)
    )
    grad_out = jnp.dot(jnp.transpose(saved["out_low"]), d_attn, preferred_element_type=jnp.float32)
    delta_row = jnp.einsum("qhgd,qhgd->hgq", d_out.astype(jnp.float32), saved["out_full"])
    log_total = saved["log_total"]
    d_query, d_pairs = grad_sweep(
        jnp.zeros(query_rows.shape, jnp.float32),
        query_rows,
        q_pos,
        q_seg,
        saved["all_keys"],
        k_pos,
        k_seg,
        log_total,
        d_out,
        delta_row,
    )

    def with_prompt(current):
        return grad_sweep(
            current,
            query_rows,
            q_pos,
            q_seg,
            prompt_keys,
            p_pos,
            p_seg,
            log_total,
            d_out,
            delta_row,
        )

    def without_prompt(current):
        return (current, jnp.zeros(prompt_keys.shape, jnp.float32))

    d_query, d_prompt = lax.cond(is_later, with_prompt, without_prompt, d_query)
    d_rows, d_prompt_rows = (
        lax.psum_scatter(
            d_pairs.astype(jnp.bfloat16), "ctx", scatter_dimension=0, tiled=True
        ).astype(jnp.float32),
        lax.psum_scatter(
            d_prompt.astype(jnp.bfloat16), "ctx", scatter_dimension=0, tiled=True
        ).astype(jnp.float32),
    )
    d_rows = d_rows + jnp.where(is_later, 0.0, prompt_carry)
    heads_q = out_mat.shape[0] // HEAD_SIZE
    d_query_raw = (
        unrotate(d_query.reshape(count_of_rows, heads_q, HEAD_SIZE), angles)
        .astype(jnp.bfloat16)
        .reshape(count_of_rows, -1)
    )
    d_pair_raw = (
        jnp.concatenate([unrotate(d_rows[..., :HEAD_SIZE], angles), d_rows[..., HEAD_SIZE:]], -1)
        .astype(jnp.bfloat16)
        .reshape(count_of_rows, -1)
    )
    normalized_input = saved["normed_in"]
    grad_query = jnp.dot(
        jnp.transpose(normalized_input), d_query_raw, preferred_element_type=jnp.float32
    )
    grad_pair = jnp.dot(
        jnp.transpose(normalized_input), d_pair_raw, preferred_element_type=jnp.float32
    ).reshape(pairing_matrix.shape)
    d_in = jnp.dot(d_query_raw, jnp.transpose(query_mat), preferred_element_type=jnp.float32)
    d_in = d_in + jnp.dot(
        d_pair_raw,
        jnp.transpose(pairing_matrix.reshape(pairing_matrix.shape[0], -1)),
        preferred_element_type=jnp.float32,
    )
    d_in = lax.psum_scatter(
        d_in.astype(jnp.bfloat16), "wt", scatter_dimension=0, tiled=True
    ).astype(jnp.float32)
    d_stream, gain_grad_in = norm_back(saved["stream"], gains[0], d_in)
    grad_set = (
        grad_query,
        grad_pair,
        grad_out,
        grad_in,
        grad_down,
        jnp.stack([gain_grad_in, gain_grad_mid]),
        grad_router,
    )
    return (d_mid + d_stream, grad_set, d_prompt_rows)


def store_slot(buffer, saved, slot_index, slot_count):
    if buffer is None:
        buffer = jax.tree.map(
            lambda member: jnp.zeros((slot_count,) + member.shape, member.dtype), saved
        )
    return jax.tree.map(
        lambda holder, member: lax.dynamic_update_index_in_dim(holder, member, slot_index, 0),
        buffer,
        saved,
    )


def fetch_slot(buffer, slot_index):
    return jax.tree.map(
        lambda holder: lax.dynamic_index_in_dim(holder, slot_index, 0, False), buffer
    )


def shards(
    tokens,
    cotangent,
    blocks,
    routes,
    norm_gain,
    w_query,
    key_value_weight,
    w_attn_out,
    router,
    w_in,
    w_down,
):
    section_count = lax.axis_size("section")
    section_index = lax.axis_index("section")
    micro_count = tokens.shape[0]
    count_of_rows = routes.shape[2]
    seq_len = count_of_rows * lax.axis_size("ctx")
    row_start = lax.axis_index("ctx") * count_of_rows
    expert_count = w_in.shape[1]
    first_expert = lax.axis_index("wt") * expert_count
    capacity = count_of_rows * TOPK * 5 // (4 * expert_count * lax.axis_size("wt"))
    share_rows = count_of_rows // lax.axis_size("wt")
    row_offset = lax.axis_index("wt") * share_rows
    gains = norm_gain[0]
    router_table = router[0]
    route_all = routes[0]
    inverse = inverse_freq(HEAD_SIZE)
    gathered = (
        lax.all_gather(w_query, "ctx", axis=1, tiled=True),
        lax.all_gather(key_value_weight, "ctx", axis=1, tiled=True),
        lax.all_gather(w_attn_out, "ctx", axis=2, tiled=True),
        lax.all_gather(w_in, "ctx", axis=2, tiled=True),
        lax.all_gather(w_down, "ctx", axis=2, tiled=True),
    )
    matrices = tuple((member[0] for member in gathered))
    tick_count = micro_count + section_count - 1
    slot_count = micro_count + 2 * section_count - 2
    p_pos, p_seg = layout(blocks, 0, seq_len)

    def geometry(micro_index):
        k_pos, k_seg = layout(blocks, micro_index, seq_len)
        q_pos = lax.dynamic_slice_in_dim(k_pos, row_start, count_of_rows, 0)
        q_seg = lax.dynamic_slice_in_dim(k_seg, row_start, count_of_rows, 0)
        angles = q_pos.astype(jnp.float32)[:, None] * inverse[None, :]
        return (q_pos, q_seg, k_pos, k_seg, p_pos, p_seg, angles)

    received = jnp.zeros(tokens.shape[1:], jnp.float32)
    outputs = jnp.zeros(tokens.shape, jnp.bfloat16)
    buffer = None
    for tick_index in range(tick_count):
        micro_index = tick_index - section_index
        is_valid = (micro_index >= 0) & (micro_index < micro_count)
        clipped = jnp.clip(micro_index, 0, micro_count - 1)
        own_input = lax.dynamic_index_in_dim(tokens, clipped, 0, False).astype(jnp.float32)
        stream = jnp.where(section_index == 0, own_input, received)
        if buffer is None:
            prompt_keys = jnp.zeros(
                (seq_len, key_value_weight.shape[2], 2 * HEAD_SIZE), jnp.bfloat16
            )
        else:
            prompt_keys = fetch_slot(buffer, section_count - 1)["all_keys"]
        route_rows = lax.dynamic_index_in_dim(route_all, clipped, 0, False)
        section_out, saved = forward(
            stream,
            geometry(clipped),
            clipped > 0,
            prompt_keys,
            gains,
            route_rows,
            matrices,
            router_table,
            first_expert,
            capacity,
        )
        buffer = store_slot(buffer, saved, micro_index + section_count - 1, slot_count)
        previous = lax.dynamic_index_in_dim(outputs, clipped, 0, False)
        outputs = lax.dynamic_update_index_in_dim(
            outputs, jnp.where(is_valid, section_out, previous), clipped, 0
        )
        if tick_index + 1 < tick_count:
            received = passed_along(section_out, "section", 1).astype(jnp.float32)
    regathered = (
        lax.all_gather(w_query, "ctx", axis=1, tiled=True),
        lax.all_gather(key_value_weight, "ctx", axis=1, tiled=True),
        lax.all_gather(w_attn_out, "ctx", axis=2, tiled=True),
        lax.all_gather(w_in, "ctx", axis=2, tiled=True),
        lax.all_gather(w_down, "ctx", axis=2, tiled=True),
    )
    back_matrices = tuple((member[0] for member in regathered))
    prompt_carry = jnp.zeros((count_of_rows, key_value_weight.shape[2], 2 * HEAD_SIZE), jnp.float32)
    incoming = jnp.zeros(tokens.shape[1:], jnp.float32)
    grad_inputs = jnp.zeros(tokens.shape, jnp.bfloat16)
    totals = None
    prompt_keys = fetch_slot(buffer, section_count - 1)["all_keys"]
    for tick_index in range(tick_count):
        micro_index = micro_count + section_count - 2 - tick_index - section_index
        is_valid = (micro_index >= 0) & (micro_index < micro_count)
        clipped = jnp.clip(micro_index, 0, micro_count - 1)
        top_grad = lax.dynamic_index_in_dim(cotangent, clipped, 0, False).astype(jnp.float32)
        upstream = jnp.where(section_index == section_count - 1, top_grad, incoming)
        saved = fetch_slot(buffer, micro_index + section_count - 1)
        route_rows = lax.dynamic_index_in_dim(route_all, clipped, 0, False)
        is_later = clipped > 0
        d_stream, grad_set, carry_next = backward(
            upstream,
            saved,
            geometry(clipped),
            is_later,
            prompt_keys,
            gains,
            route_rows,
            back_matrices,
            router_table,
            first_expert,
            capacity,
            row_offset,
            share_rows,
            prompt_carry,
        )
        grad_set = jax.tree.map(lambda member: jnp.where(is_valid, member, 0.0), grad_set)
        totals = grad_set if totals is None else jax.tree.map(jnp.add, totals, grad_set)
        prompt_carry = jnp.where(is_valid & is_later, carry_next, prompt_carry)
        d_low = d_stream.astype(jnp.bfloat16)
        previous = lax.dynamic_index_in_dim(grad_inputs, clipped, 0, False)
        grad_inputs = lax.dynamic_update_index_in_dim(
            grad_inputs, jnp.where(is_valid, d_low, previous), clipped, 0
        )
        if tick_index + 1 < tick_count:
            incoming = passed_along(d_low, "section", -1).astype(jnp.float32)
    grad_query, grad_pair, grad_out, grad_in, grad_down, gain_grads, grad_router = totals
    reduced = (
        lax.psum_scatter(
            grad_query.astype(jnp.bfloat16), "ctx", scatter_dimension=0, tiled=True
        ).astype(jnp.float32),
        lax.psum_scatter(
            grad_pair.astype(jnp.bfloat16), "ctx", scatter_dimension=0, tiled=True
        ).astype(jnp.float32),
        lax.psum_scatter(
            grad_out.astype(jnp.bfloat16), "ctx", scatter_dimension=1, tiled=True
        ).astype(jnp.float32),
        lax.psum_scatter(
            grad_in.astype(jnp.bfloat16), "ctx", scatter_dimension=1, tiled=True
        ).astype(jnp.float32),
        lax.psum_scatter(
            grad_down.astype(jnp.bfloat16), "ctx", scatter_dimension=1, tiled=True
        ).astype(jnp.float32),
    )
    reduced_small = (
        lax.psum_scatter(gain_grads, ("ctx", "wt"), scatter_dimension=1, tiled=True),
        lax.psum_scatter(grad_router, ("ctx", "wt"), scatter_dimension=0, tiled=True),
    )
    return (
        outputs[None],
        grad_inputs[None],
        reduced_small[0][None],
        reduced[0][None],
        reduced[1][None],
        reduced[2][None],
        reduced_small[1][None],
        reduced[3][None],
        reduced[4][None],
    )


def solution(mesh):
    return jax.shard_map(
        shards,
        mesh=mesh,
        in_specs=(
            P(None, ("ctx", "wt"), None),
            P(None, ("ctx", "wt"), None),
            P(),
            P("section", None, "ctx", None),
            P("section", None, None),
            P("section", "ctx", "wt"),
            P("section", "ctx", "wt", None),
            P("section", "wt", "ctx"),
            P("section", None, None),
            P("section", "wt", "ctx", None),
            P("section", "wt", "ctx", None),
        ),
        out_specs=(
            P("section", None, ("ctx", "wt"), None),
            P("section", None, ("ctx", "wt"), None),
            P("section", None, ("ctx", "wt")),
            P("section", "ctx", "wt"),
            P("section", "ctx", "wt", None),
            P("section", "wt", "ctx"),
            P("section", ("ctx", "wt"), None),
            P("section", "wt", "ctx", None),
            P("section", "wt", "ctx", None),
        ),
        check_vma=False,
    )
```

profile of v0, /device:TPU:0, one launch (start us, length us, event | category | flops | bytes accessed | tf_op | source)
XLA Modules:
  0.0 1960.0 jit_solution(3432736702829028296)
XLA Ops:
  8.8 13.8 all_gather.66
  24.8 19.6 %all_gather.65 = bf16[256,1536]{1,0:T(8,128)(2,1)S(1)} all-gather(bf16[64,1536]{1,0:T(8,128)(2,1)S(1)} %fusion.403), channel_id=1, replica_groups=mesh['section'=2,'ctx'=4,'wt'=4] {'wt'}, dimensions={0}, use_global_device_ids=true | all-gather | bytes 983040 | tf_op jit(solution)/shard_map/all_gather | solution.py:77
  51.4 11.9 all_gather.67
  66.9 14.8 while.243
  119.4 18.5 all_gather.70
  146.9 93.8 %all-gather.9.cloned.1.call-done = bf16[1,4,1536,1024]{3,2,1,0:T(8,128)(2,1)} async-done(((bf16[1,4,384,1024]{3,2,1,0:T(8,128)(2,1)}), bf16[1,4,1536,1024]{3,2,1,0:T(8,128)(2,1)}) %all-gather.9.cloned.1.call-update) | async-done | bytes 12582928 | tf_op jit(solution)/shard_map/all_gather | solution.py:566
  245.9 10.1 bitcast_dynamic-update-slice_fusion.5
  256.0 56.6 %all-gather.11.cloned.1.call-done = bf16[1,4,512,1536]{3,2,1,0:T(8,128)(2,1)} async-done(((bf16[1,4,128,1536]{3,2,1,0:T(8,128)(2,1)}), bf16[1,4,512,1536]{3,2,1,0:T(8,128)(2,1)}) %all-gather.11.cloned.1.call-update) | async-done | bytes 6291472 | tf_op jit(solution)/shard_map/all_gather | solution.py:567
  320.7 12.1 scatter_custom_fusion
  344.6 12.7 reduce-scatter.42.cloned.1.call-done
  361.1 18.1 all_gather.73
  380.3 12.8 all_gather.74
  393.8 17.3 while.245
  413.2 10.3 conditional.11
  413.2 10.3 while.235
  424.9 9.5 while.246
  442.9 22.9 %all_gather.79 = bf16[256,1536]{1,0:T(8,128)(2,1)S(1)} all-gather(bf16[64,1536]{1,0:T(8,128)(2,1)S(1)} %bitcast_convert_fusion.2), channel_id=1, replica_groups=mesh['section'=2,'ctx'=4,'wt'=4] {'wt'}, dimensions={0}, use_global_device_ids=true | all-gather | bytes 983040 | tf_op jit(solution)/shard_map/all_gather | solution.py:87
  477.2 16.6 all_gather.75
  503.6 9.1 bitcast_dynamic-update-slice_fusion.4
  517.3 12.1 scatter_custom_fusion.1
  541.7 11.4 reduce-scatter.46.cloned.1.call-done
  558.9 18.0 all_gather.76
  578.0 12.8 all_gather.77
  591.6 16.6 while.247
  644.8 14.9 reduce-scatter.48.cloned.1.call-done
  661.8 18.2 all_gather.78
  701.1 32.8 %scatter_fusion = f32[4,256]{1,0:T(4,128)S(1)} fusion(f32[4,256]{1,0:T(4,128)S(1)} %broadcast.1086.clone, s32[640]{0:T(1024)S(1)} %reshape.1484, f32[640]{0:T(1024)S(1)} %reshape.1486), kind=kCustom, calls=%fused_computation.19 | custom fusion | flops 640 | bytes 12800 | tf_op jit(solution)/shard_map/scatter-add | solution.py:390
  754.8 11.3 fusion.213
  766.1 12.1 scatter_custom_fusion.3
  789.4 12.5 reduce-scatter.52.cloned.1.call-done
  806.1 18.1 all_gather.80
  827.7 25.7 %while.249 = (s32[]{:T(128)}, f32[256,2,3,64]{0,3,2,1:T(8,128)S(1)}, bf16[2,512,2,128]{1,3,2,0:T(8,128)(2,1)}, s32[2]{0:T(128)S(1)}, bf16[1024,2,128]{0,2,1:T(8,...) while((s32[]{:T(128)}, f32[256,2,3,64]{0,3,2,1:T(8,128)S(1)}, ...), condition=%wide.region_103.105_spmd.clone, body=%wide.region_102.104_spmd.clone.sunk | while | flops 512655872 | bytes 21558636 | solution.py:194
  855.4 25.1 %conditional.15 = (f32[256,2,3,64]{0,3,2,1:T(8,128)S(1)}, bf16[1024,2,128]{2,1,0:T(2,128)(2,1)}) conditional(s32[]{:T(128)} %convert_element_type.613, f32[256,2,3,64]{0,3,2,1:T(8,128)S(1)} %get-tuple-element.1399, (bf16[1024,2,128]{0,2,1:T(8,128)(2,1)}, s32[1024]{0:T(1024)S(1)}, s32[256]{0:T(256)}, s32[1024]{0:T(1024)S(1)}, ...), branch_computations={%region_104.106_spmd, %region_105.109_spmd} | conditional | flops 512557568 | bytes 30991864 | solution.py:466
  855.4 25.1 %while.237 = (s32[]{:T(128)}, f32[256,2,3,64]{0,3,2,1:T(8,128)S(1)}, bf16[2,512,2,128]{3,2,1,0:T(2,128)(2,1)}, s32[2]{0:T(128)S(1)}, bf16[1024,2,128]{0,2,1:T(8,...) while((s32[]{:T(128)}, f32[256,2,3,64]{0,3,2,1:T(8,128)S(1)}, ...), condition=%wide.region_107.108_spmd, body=%wide.region_106.107_spmd.sunk | while | flops 512557568 | bytes 30991688 | solution.py:194
  888.8 22.4 %reduce-scatter.56.cloned.1.call-done = bf16[64,1536]{1,0:T(8,128)(2,1)} async-done(((bf16[256,1536]{1,0:T(8,128)(2,1)}), bf16[64,1536]{1,0:T(8,128)(2,1)}) %reduce-scatter.56.cloned.1.call-update) | async-done | bytes 196624 | tf_op jit(solution)/shard_map/reduce_scatter | solution.py:500
  917.7 18.0 all_gather.81
  942.7 32.8 %scatter_fusion.1 = f32[4,256]{1,0:T(4,128)S(1)} fusion(f32[4,256]{1,0:T(4,128)S(1)} %broadcast.1086.clone.1, s32[640]{0:T(1024)S(1)} %reshape.1498, f32[640]{0:T(1024)S(1)} %reshape.1500), kind=kCustom, calls=%fused_computation.21 | custom fusion | flops 640 | bytes 12800 | tf_op jit(solution)/shard_map/scatter-add | solution.py:390
  987.9 11.3 fusion.211
  999.3 12.9 scatter_custom_fusion.5
  1019.3 18.4 reduce-scatter.58.cloned.1.call-done
  1041.8 18.3 all_gather.82
  1063.7 30.8 %while.250 = (s32[]{:T(128)}, f32[256,2,3,64]{0,3,2,1:T(8,128)S(1)}, bf16[2,512,2,128]{1,3,2,0:T(8,128)(2,1)}, s32[2]{0:T(128)S(1)}, bf16[1024,2,128]{0,2,1:T(8,...) while((s32[]{:T(128)}, f32[256,2,3,64]{0,3,2,1:T(8,128)S(1)}, ...), condition=%wide.region_124.126_spmd.clone, body=%wide.region_123.125_spmd.clone.sunk | while | flops 512655872 | bytes 21529936 | solution.py:194
  1096.6 25.1 %conditional.16 = (f32[256,2,3,64]{0,3,2,1:T(8,128)S(1)}, bf16[1024,2,128]{2,1,0:T(2,128)(2,1)}) conditional(s32[]{:T(128)} %convert_element_type.596, f32[256,2,3,64]{0,3,2,1:T(8,128)S(1)} %get-tuple-element.1402, (bf16[1024,2,128]{0,2,1:T(8,128)(2,1)}, s32[1024]{0:T(1024)S(1)}, s32[256]{0:T(256)}, s32[1024]{0:T(1024)S(1)}, s32[256]{0:T(256)}, ...), branch_computations={%region_125.127_spmd, %region_126.130_spmd} | conditional | flops 512557568 | bytes 30967260 | solution.py:466
  1096.6 25.1 %while.238 = (s32[]{:T(128)}, f32[256,2,3,64]{0,3,2,1:T(8,128)S(1)}, bf16[2,512,2,128]{3,2,1,0:T(2,128)(2,1)}, s32[2]{0:T(128)S(1)}, bf16[1024,2,128]{0,2,1:T(8,...) while((s32[]{:T(128)}, f32[256,2,3,64]{0,3,2,1:T(8,128)S(1)}, ...), condition=%wide.region_128.129_spmd, body=%wide.region_127.128_spmd.sunk | while | flops 512557568 | bytes 30967084 | solution.py:194
  1130.2 21.9 %reduce-scatter.64.cloned.1.call-done = bf16[64,1536]{1,0:T(8,128)(2,1)} async-done(((bf16[256,1536]{1,0:T(8,128)(2,1)}), bf16[64,1536]{1,0:T(8,128)(2,1)}) %reduce-scatter.64.cloned.1.call-update) | async-done | bytes 196624 | tf_op jit(solution)/shard_map/reduce_scatter | solution.py:500
  1158.5 18.0 all_gather.83
  1183.1 32.8 %scatter_fusion.2 = f32[4,256]{1,0:T(4,128)S(1)} fusion(f32[4,256]{1,0:T(4,128)S(1)} %broadcast.1086, s32[640]{0:T(1024)S(1)} %reshape.1512, f32[640]{0:T(1024)S(1)} %reshape.1514), kind=kCustom, calls=%fused_computation.23 | custom fusion | flops 640 | bytes 12800 | tf_op jit(solution)/shard_map/scatter-add | solution.py:390
  1228.0 11.4 fusion.209
  1239.4 12.1 scatter_custom_fusion.7
  1257.2 18.2 reduce-scatter.66.cloned.1.call-done
  1278.5 18.3 all_gather.84
  1300.9 29.6 %while.251 = (s32[]{:T(128)}, f32[256,2,3,64]{0,3,2,1:T(8,128)}, bf16[2,512,2,128]{1,3,2,0:T(8,128)(2,1)S(1)}, s32[2]{0:T(128)S(1)}, bf16[1024,2,128]{0,2,1:T(8,...) while((s32[]{:T(128)}, f32[256,2,3,64]{0,3,2,1:T(8,128)}, ...), condition=%wide.region_146.148_spmd.clone, body=%wide.region_145.147_spmd.clone.sunk | while | flops 512655872 | bytes 17339672 | solution.py:194
  1336.4 19.3 reduce-scatter.68.cloned.1.call-done
  1364.1 12.2 scatter_custom_fusion.2
  1443.4 13.8 fusion.292
  1457.2 10.3 fusion.291
  1467.6 15.9 add_convert_fusion
  1485.9 46.9 %reduce-scatter.92.cloned.1.call-done = f32[96,16]{1,0:T(8,128)} async-done(((f32[1536,16]{1,0:T(8,128)}), f32[96,16]{1,0:T(8,128)}) %reduce-scatter.92.cloned.1.call-update) | async-done | bytes 6160
  1534.2 29.0 %reduce-scatter.90.cloned.1.call-done = bf16[384,384]{1,0:T(8,128)(2,1)} async-done(((bf16[1536,384]{1,0:T(8,128)(2,1)}), bf16[384,384]{1,0:T(8,128)(2,1)}) %reduce-scatter.90.cloned.1.call-update) | async-done | bytes 294928
  1565.2 29.3 %reduce-scatter.74.cloned.1.call-done = bf16[384,384]{1,0:T(8,128)(2,1)} async-done(((bf16[1536,384]{1,0:T(8,128)(2,1)}), bf16[384,384]{1,0:T(8,128)(2,1)}) %reduce-scatter.74.cloned.1.call-update) | async-done | bytes 294928 | tf_op jit(solution)/shard_map/reduce_scatter | solution.py:666
  1596.3 27.2 %reduce-scatter.76.cloned.1.call-done = bf16[384,2,128]{2,0,1:T(8,128)(2,1)} async-done(((bf16[1536,2,128]{2,0,1:T(8,128)(2,1)}), bf16[384,2,128]{2,0,1:T(8,128)(2,1)}) %reduce-scatter.76.cloned.1.call-update) | async-done | bytes 196624 | tf_op jit(solution)/shard_map/reduce_scatter | solution.py:669
  1626.8 123.9 %reduce-scatter.88.cloned.1.call-done = f32[96,2]{1,0:T(8,128)} async-done(((f32[1536,2]{1,0:T(8,128)}), f32[96,2]{1,0:T(8,128)}) %reduce-scatter.88.cloned.1.call-update) | async-done | bytes 784
  1752.1 71.3 %reduce-scatter.80.cloned.1.call-done = bf16[4,128,1536]{2,1,0:T(8,128)(2,1)} async-done(((bf16[4,512,1536]{2,1,0:T(8,128)(2,1)}), bf16[4,128,1536]{2,1,0:T(8,128)(2,1)}) %reduce-scatter.80.cloned.1.call-update) | async-done | bytes 1572880 | tf_op jit(solution)/shard_map/reduce_scatter | solution.py:678
  1827.0 120.4 %reduce-scatter.78.cloned.1.call-done = bf16[4,384,1024]{2,1,0:T(8,128)(2,1)} async-done(((bf16[4,1536,1024]{2,1,0:T(8,128)(2,1)}), bf16[4,384,1024]{2,1,0:T(8,128)(2,1)}) %reduce-scatter.78.cloned.1.call-update) | async-done | bytes 3145744 | tf_op jit(solution)/shard_map/reduce_scatter | solution.py:675
  (1385 shorter events, 692.8 us)
Async XLA Ops:
  7.2 130.7 %copy-start = (bf16[1,1536,16]{1,2,0:T(8,128)(2,1)S(1)}, bf16[1,1536,16]{1,2,0:T(8,128)(2,1)}, u32[]{:S(2)}) copy-start(bf16[1,1536,16]{1,2,0:T(8,128)(2,1)} %param.75) | copy-start | bytes 147460
  7.2 56.8 %all-gather.5.cloned.1.call-start = ((), (), s32[]{:S(2)}) async-start(), calls=%async_computation.27 | async-start | bytes 1474560 | tf_op jit(solution)/shard_map/all_gather | solution.py:563
  7.9 83.8 %all-gather.7.cloned.1.call-start = ((), (), s32[]{:S(2)}) async-start(), calls=%async_computation.28 | async-start | bytes 1474560 | tf_op jit(solution)/shard_map/all_gather | solution.py:565
  8.7 108.5 %reduce-scatter.40.cloned.1.call-start = ((), (), s32[]{:S(2)}) async-start(), calls=%async_computation.29 | async-start | bytes 983040 | tf_op jit(solution)/shard_map/reduce_scatter | solution.py:81
  23.9 40.1 %copy-start.42 = (bf16[1536,256]{0,1:T(8,128)(2,1)}, bf16[1536,256]{0,1:T(8,128)(2,1)S(1)}, u32[]{:S(2)}) copy-start(bf16[1536,256]{0,1:T(8,128)(2,1)S(1)} %copy.286) | copy-start | bytes 2359300
  24.0 94.3 %copy-start.149 = (f32[1536]{0:T(1024)}, f32[1536]{0:T(1024)S(1)}, u32[]{:S(2)}) copy-start(f32[1536]{0:T(1024)S(1)} %get-tuple-element.2028) | copy-start | bytes 18436
  94.7 146.0 %all-gather.9.cloned.1.call-start = ((), (), s32[]{:S(2)}) async-start(), calls=%async_computation.30 | async-start | bytes 15728640 | tf_op jit(solution)/shard_map/all_gather | solution.py:566
  95.3 217.3 %all-gather.11.cloned.1.call-start = ((), (), s32[]{:S(2)}) async-start(), calls=%async_computation.31 | async-start | bytes 7864320 | tf_op jit(solution)/shard_map/all_gather | solution.py:567
  95.8 261.4 %reduce-scatter.42.cloned.1.call-start = ((), (), s32[]{:S(2)}) async-start(), calls=%async_computation.32 | async-start | bytes 983040 | tf_op jit(solution)/shard_map/reduce_scatter | solution.py:81
  95.9 42.4 %copy-start.244 = (s32[4]{0:T(128)}, s32[4]{0:T(128)S(1)}, u32[]{:S(2)}) copy-start(s32[4]{0:T(128)S(1)} %iota_add_fusion.3) | copy-start | bytes 52
  95.9 41.9 %copy-start.204 = (s32[256,8]{0,1:T(8,128)}, s32[256,8]{0,1:T(8,128)S(1)}, u32[]{:S(2)}) copy-start(s32[256,8]{0,1:T(8,128)S(1)} %get-tuple-element.2575) | copy-start | bytes 24580
  96.0 42.4 %copy-start.195 = (s32[256,8]{0,1:T(8,128)}, s32[256,8]{0,1:T(8,128)S(1)}, u32[]{:S(2)}) copy-start(s32[256,8]{0,1:T(8,128)S(1)} %get-tuple-element.2574) | copy-start | bytes 24580
  96.0 42.4 %copy-start.197 = (s32[256,8]{0,1:T(8,128)}, s32[256,8]{0,1:T(8,128)S(1)}, u32[]{:S(2)}) copy-start(s32[256,8]{0,1:T(8,128)S(1)} %get-tuple-element.2576) | copy-start | bytes 24580
  102.5 44.4 %copy-start.272 = (s32[4]{0:T(128)}, s32[4]{0:T(128)S(1)}, u32[]{:S(2)}) copy-start(s32[4]{0:T(128)S(1)} %get-tuple-element.2605) | copy-start | bytes 52
  104.3 34.0 %copy-start.279 = (s32[1024]{0:T(1024)}, s32[1024]{0:T(1024)S(1)}, u32[]{:S(2)}) copy-start(s32[1024]{0:T(1024)S(1)} %reshape.1520) | copy-start | bytes 12292
  108.7 38.2 %copy-start.210 = (s32[4,161]{1,0:T(4,128)}, s32[4,161]{1,0:T(4,128)S(1)}, u32[]{:S(2)}) copy-start(s32[4,161]{1,0:T(4,128)S(1)} %reshape.1318) | copy-start | bytes 7732
  114.3 206.4 %copy-start.281 = (s32[640]{0:T(1024)}, s32[640]{0:T(1024)S(1)}, u32[]{:S(2)}) copy-start(s32[640]{0:T(1024)S(1)} %fusion.541) | copy-start | bytes 7684
  320.7 36.6 %copy-start.90 = (bf16[64,1536]{1,0:T(8,128)(2,1)S(1)}, bf16[64,1536]{1,0:T(8,128)(2,1)}, u32[]{:S(2)}) copy-start(bf16[64,1536]{1,0:T(8,128)(2,1)} %reduce-scatter.40.cloned.1.call-done) | copy-start | bytes 589828
  333.8 141.3 %reduce-scatter.44.cloned.1.call-start = ((), (), s32[]{:S(2)}) async-start(), calls=%async_computation.33 | async-start | bytes 983040 | tf_op jit(solution)/shard_map/reduce_scatter | solution.py:81
  341.0 154.1 %copy-start.9 = (s32[640]{0:T(1024)}, s32[640]{0:T(1024)S(1)}, u32[]{:S(2)}) copy-start(s32[640]{0:T(1024)S(1)} %reshape.1593) | copy-start | bytes 7684
  358.3 35.5 %copy-start.80 = (bf16[2,64,1536]{2,1,0:T(8,128)(2,1)}, bf16[2,64,1536]{2,1,0:T(8,128)(2,1)S(1)}, u32[]{:S(2)}) copy-start(bf16[2,64,1536]{2,1,0:T(8,128)(2,1)S(1)} %get-tuple-element.2494) | copy-start | bytes 1179652
  358.3 2.5 collective-permute-start
  442.8 110.3 %reduce-scatter.46.cloned.1.call-start = ((), (), s32[]{:S(2)}) async-start(), calls=%async_computation.34 | async-start | bytes 983040 | tf_op jit(solution)/shard_map/reduce_scatter | solution.py:81
  470.3 47.0 %copy-start.282 = (s32[640]{0:T(1024)}, s32[640]{0:T(1024)S(1)}, u32[]{:S(2)}) copy-start(s32[640]{0:T(1024)S(1)} %fusion.542) | copy-start | bytes 7684
  530.4 129.2 %reduce-scatter.48.cloned.1.call-start = ((), (), s32[]{:S(2)}) async-start(), calls=%async_computation.35 | async-start | bytes 983040 | tf_op jit(solution)/shard_map/reduce_scatter | solution.py:81
  541.0 36.0 %copy-start.44 = (bf16[1536,256]{0,1:T(8,128)(2,1)S(1)}, bf16[1536,256]{0,1:T(8,128)(2,1)}, u32[]{:S(2)}) copy-start(bf16[1536,256]{0,1:T(8,128)(2,1)} %copy-done.42) | copy-start | bytes 2359300
  554.9 3.2 collective-permute-start.1
  637.7 149.3 %reduce-scatter.82.cloned.1.call-start = ((), (), s32[]{:S(2)}) async-start(), calls=%async_computation.52 | async-start | bytes 81920
  643.3 36.7 %copy-start.230 = (s32[1024]{0:T(1024)S(1)}, s32[1024]{0:T(1024)}, u32[]{:S(2)}) copy-start(s32[1024]{0:T(1024)} %pad_clamp_fusion) | copy-start | bytes 12292
  744.4 57.6 %reduce-scatter.52.cloned.1.call-start = ((), (), s32[]{:S(2)}) async-start(), calls=%async_computation.37 | async-start | bytes 983040 | tf_op jit(solution)/shard_map/reduce_scatter | solution.py:394
  779.2 104.6 %reduce-scatter.54.cloned.1.call-start = ((), (), s32[]{:S(2)}) async-start(), calls=%async_computation.38 | async-start | bytes 655360 | tf_op jit(solution)/shard_map/reduce_scatter | solution.py:468
  784.8 40.3 %copy-start.53 = (bf16[1,384,1536]{2,1,0:T(8,128)(2,1)S(1)}, bf16[1,384,1536]{2,1,0:T(8,128)(2,1)}, u32[]{:S(2)}) copy-start(bf16[1,384,1536]{2,1,0:T(8,128)(2,1)} %all-gather.7.cloned.1.call-done) | copy-start | bytes 3538948
  855.3 55.9 %reduce-scatter.56.cloned.1.call-start = ((), (), s32[]{:S(2)}) async-start(), calls=%async_computation.39 | async-start | bytes 983040 | tf_op jit(solution)/shard_map/reduce_scatter | solution.py:500
  888.5 47.1 %copy-start.233 = (s32[1024]{0:T(1024)S(1)}, s32[1024]{0:T(1024)}, u32[]{:S(2)}) copy-start(s32[1024]{0:T(1024)} %copy-done.232) | copy-start | bytes 12292
  888.6 128.4 %reduce-scatter.84.cloned.1.call-start = ((), (), s32[]{:S(2)}) async-start(), calls=%async_computation.53 | async-start | bytes 81920
  914.3 3.3 collective-permute-start.2
  942.7 34.1 %copy-start.10 = (s32[640]{0:T(1024)S(1)}, s32[640]{0:T(1024)}, u32[]{:S(2)}) copy-start(s32[640]{0:T(1024)} %copy-done.9) | copy-start | bytes 7684
  976.4 61.4 %reduce-scatter.58.cloned.1.call-start = ((), (), s32[]{:S(2)}) async-start(), calls=%async_computation.40 | async-start | bytes 983040 | tf_op jit(solution)/shard_map/reduce_scatter | solution.py:394
  1014.7 110.2 %reduce-scatter.62.cloned.1.call-start = ((), (), s32[]{:S(2)}) async-start(), calls=%async_computation.42 | async-start | bytes 655360 | tf_op jit(solution)/shard_map/reduce_scatter | solution.py:471
  1016.9 108.0 %reduce-scatter.60.cloned.1.call-start = ((), (), s32[]{:S(2)}) async-start(), calls=%async_computation.41 | async-start | bytes 655360 | tf_op jit(solution)/shard_map/reduce_scatter | solution.py:468
  1096.5 55.6 %reduce-scatter.64.cloned.1.call-start = ((), (), s32[]{:S(2)}) async-start(), calls=%async_computation.43 | async-start | bytes 983040 | tf_op jit(solution)/shard_map/reduce_scatter | solution.py:500
  1129.4 47.1 %copy-start.227 = (s32[1024]{0:T(1024)S(1)}, s32[1024]{0:T(1024)}, u32[]{:S(2)}) copy-start(s32[1024]{0:T(1024)} %copy-done.226) | copy-start | bytes 12292
  1129.4 125.5 %reduce-scatter.86.cloned.1.call-start = ((), (), s32[]{:S(2)}) async-start(), calls=%async_computation.54 | async-start | bytes 81920
  1155.0 3.3 collective-permute-start.3
  1179.5 42.6 %copy-start.59 = (bf16[640,1536]{1,0:T(8,128)(2,1)}, bf16[640,1536]{1,0:T(8,128)(2,1)S(1)}, u32[]{:S(2)}) copy-start(bf16[640,1536]{1,0:T(8,128)(2,1)S(1)} %gather_fusion.5) | copy-start | bytes 5898244
  1183.1 34.3 %copy-start.8 = (s32[640]{0:T(1024)S(1)}, s32[640]{0:T(1024)}, u32[]{:S(2)}) copy-start(s32[640]{0:T(1024)} %copy-done.7) | copy-start | bytes 7684
  1216.8 58.7 %reduce-scatter.66.cloned.1.call-start = ((), (), s32[]{:S(2)}) async-start(), calls=%async_computation.44 | async-start | bytes 983040 | tf_op jit(solution)/shard_map/reduce_scatter | solution.py:394
  1252.5 83.8 %reduce-scatter.70.cloned.1.call-start = ((), (), s32[]{:S(2)}) async-start(), calls=%async_computation.46 | async-start | bytes 655360 | tf_op jit(solution)/shard_map/reduce_scatter | solution.py:471
  1252.6 45.0 %copy-start.55 = (bf16[1,384,1536]{2,1,0:T(8,128)(2,1)S(1)}, bf16[1,384,1536]{2,1,0:T(8,128)(2,1)}, u32[]{:S(2)}) copy-start(bf16[1,384,1536]{2,1,0:T(8,128)(2,1)} %all-gather.7.cloned.1.call-done) | copy-start | bytes 3538948
  1254.8 100.9 %reduce-scatter.68.cloned.1.call-start = ((), (), s32[]{:S(2)}) async-start(), calls=%async_computation.45 | async-start | bytes 655360 | tf_op jit(solution)/shard_map/reduce_scatter | solution.py:468
  1257.2 41.0 %copy-start.224 = (f32[64,16]{0,1:T(8,128)}, f32[64,16]{0,1:T(8,128)S(1)}, u32[]{:S(2)}) copy-start(f32[64,16]{0,1:T(8,128)S(1)} %select_reduce_fusion.9) | copy-start | bytes 12292
  1331.4 87.8 %reduce-scatter.72.cloned.1.call-start = ((), (), s32[]{:S(2)}) async-start(), calls=%async_computation.47 | async-start | bytes 983040 | tf_op jit(solution)/shard_map/reduce_scatter | solution.py:500
  1358.2 126.4 %reduce-scatter.50.cloned.1.call-start = ((), (), s32[]{:S(2)}) async-start(), calls=%async_computation.36 | async-start | bytes 983040 | tf_op jit(solution)/shard_map/reduce_scatter | solution.py:81
  1377.3 155.4 %reduce-scatter.92.cloned.1.call-start = ((), (), s32[]{:S(2)}) async-start(), calls=%async_computation.57 | async-start | bytes 835584
  1387.9 175.3 %reduce-scatter.90.cloned.1.call-start = ((), (), s32[]{:S(2)}) async-start(), calls=%async_computation.56 | async-start | bytes 1474560
  1394.4 200.1 %reduce-scatter.74.cloned.1.call-start = ((), (), s32[]{:S(2)}) async-start(), calls=%async_computation.48 | async-start | bytes 1474560 | tf_op jit(solution)/shard_map/reduce_scatter | solution.py:666
  1399.2 224.3 %reduce-scatter.76.cloned.1.call-start = ((), (), s32[]{:S(2)}) async-start(), calls=%async_computation.49 | async-start | bytes 983040 | tf_op jit(solution)/shard_map/reduce_scatter | solution.py:669
  1403.7 347.0 %reduce-scatter.88.cloned.1.call-start = ((), (), s32[]{:S(2)}) async-start(), calls=%async_computation.55 | async-start | bytes 835584
  1421.8 401.7 %reduce-scatter.80.cloned.1.call-start = ((), (), s32[]{:S(2)}) async-start(), calls=%async_computation.51 | async-start | bytes 7864320 | tf_op jit(solution)/shard_map/reduce_scatter | solution.py:678
  1430.7 516.6 %reduce-scatter.78.cloned.1.call-start = ((), (), s32[]{:S(2)}) async-start(), calls=%async_computation.50 | async-start | bytes 15728640 | tf_op jit(solution)/shard_map/reduce_scatter | solution.py:675
  1484.5 141.0 %copy-start.129 = (f32[64,1536]{1,0:T(8,128)S(1)}, f32[64,1536]{1,0:T(8,128)}, u32[]{:S(2)}) copy-start(f32[64,1536]{1,0:T(8,128)} %get-tuple-element.2473) | copy-start | bytes 1179652
  1484.6 141.0 %copy-start.168 = (bf16[64,1536]{1,0:T(8,128)(2,1)S(1)}, bf16[64,1536]{1,0:T(8,128)(2,1)}, u32[]{:S(2)}) copy-start(bf16[64,1536]{1,0:T(8,128)(2,1)} %reduce-scatter.72.cloned.1.call-done) | copy-start | bytes 589828
  1485.8 140.9 %copy-start.175 = (bf16[1,2,64,1536]{3,2,1,0:T(8,128)(2,1)}, bf16[1,2,64,1536]{3,2,1,0:T(8,128)(2,1)S(1)}, u32[]{:S(2)}) copy-start(bf16[1,2,64,1536]{3,2,1,0:T(8,128)(2,1)S(1)} %fusion.409) | copy-start | bytes 1179652
  1626.8 325.9 %copy-start.174 = (bf16[1,2,64,1536]{3,2,1,0:T(8,128)(2,1)}, bf16[1,2,64,1536]{3,2,1,0:T(8,128)(2,1)S(1)}, u32[]{:S(2)}) copy-start(bf16[1,2,64,1536]{3,2,1,0:T(8,128)(2,1)S(1)} %bitcast_dynamic-update-slice_fusion.23) | copy-start | bytes 1179652
  (280 other events, 2669.0 us)
Sparse Core Ops, SparseCore 0:
  9.9 30.4 all-gather.4
  42.2 28.9 all-gather.6
  94.8 22.3 reduce-scatter.39
  118.9 121.7 all-gather.8
  242.4 70.1 all-gather.10
  333.9 23.2 reduce-scatter.41
  442.9 26.0 reduce-scatter.43
  530.5 22.5 reduce-scatter.45
  637.8 21.7 reduce-scatter.47
  744.5 18.2 reduce-scatter.81
  779.3 22.6 reduce-scatter.51
  855.4 24.0 reduce-scatter.53
  888.7 22.4 reduce-scatter.55
  976.5 18.5 reduce-scatter.83
  1014.8 22.8 reduce-scatter.57
  1040.6 24.0 reduce-scatter.61
  1096.6 24.0 reduce-scatter.59
  1129.5 22.5 reduce-scatter.63
  1216.9 18.4 reduce-scatter.85
  1252.7 22.7 reduce-scatter.65
  1278.3 24.0 reduce-scatter.69
  1331.5 24.1 reduce-scatter.67
  1358.3 23.2 reduce-scatter.71
  1383.7 22.6 reduce-scatter.49
  1411.1 121.5 reduce-scatter.91
  1535.5 27.6 reduce-scatter.89
  1565.9 28.5 reduce-scatter.73
  1597.4 26.0 reduce-scatter.75
  1628.2 122.4 reduce-scatter.87
  1754.1 69.3 reduce-scatter.79
  1826.6 120.7 reduce-scatter.77
where the time goes:
time: 1970 us; the launch traced here: 1960 us
  waiting for transfers between devices  761 us (39%)
  matrix products  333 us (17%)
  other arithmetic  317 us (16%)
  blocking collectives  274 us (14%)
  local copies, waits for them, and re-layouts  227 us (12%)
  loops' own time  21.1 us (1%)
    unnamed x37, waiting for transfers between devices  203 us
    reduce_scatter x1, waiting for transfers between devices, shards(): lax.psum_scatter(grad_in.astype(jnp.bfloat16), 'ctx', scatter_dimension=1...  120 us
    all_gather x6, blocking collectives, gather_grads(): return lax.all_gather(values, 'wt', axis=0, tiled=True)  114 us
    all_gather x6, blocking collectives, gather_rows(): return lax.all_gather(values, 'wt', axis=0, tiled=True)  109 us
    scatter-add x3, other arithmetic, backward(): jnp.zeros((expert_count, count_of_rows), jnp.float32).at[owner, slot_rows]  98.4 us
    all_gather x1, waiting for transfers between devices, shards(): lax.all_gather(w_in, 'ctx', axis=2, tiled=True)  93.8 us
    reduce_scatter x1, waiting for transfers between devices, shards(): lax.psum_scatter(grad_down.astype(jnp.bfloat16), 'ctx', scatter_dimension...  71.3 us
    all_gather x1, waiting for transfers between devices, shards(): lax.all_gather(w_down, 'ctx', axis=2, tiled=True)  56.6 us
  transfers between devices with their start and end apart: 35, of which 22 were waited for; matrix products, arithmetic and copies ran while one was open for 26% of the time, Pallas kernels for 0%

commit v1 on v0

v1 whole, which is shorter than its diff:
```python
import functools

import jax
import jax.numpy as jnp
from jax import lax
from jax.experimental import pallas as pl
from jax.experimental.pallas import tpu as pltpu
from jax.sharding import PartitionSpec as P

HEAD_SIZE = 64
FF = 512
CONT_LEN = 1024
EPSILON = 1e-06
ROPE_BASE = 10000.0
MASKED = -1e30
MESH = pl.DeviceIdType.MESH
F32 = jnp.float32
BF16 = jnp.bfloat16


def dot(left, right, contract):
    return lax.dot_general(left, right, (contract, ((), ())), preferred_element_type=F32)


def norm_scale(rows):
    return lax.rsqrt(jnp.mean(rows * rows, -1, keepdims=True) + EPSILON)


def place():
    return lax.axis_index("section"), lax.axis_index("ctx"), lax.axis_index("wt")


def greet(targets):
    barrier = pltpu.get_barrier_semaphore()
    for target in targets:
        pl.semaphore_signal(barrier, inc=1, device_id=target, device_id_type=MESH)
    pl.semaphore_wait(barrier, len(targets))


def remote(source, destination, send_sem, recv_sem, target):
    return pltpu.make_async_remote_copy(
        src_ref=source,
        dst_ref=destination,
        send_sem=send_sem,
        recv_sem=recv_sem,
        device_id=target,
        device_id_type=MESH,
    )


def exchange_kernel(n_wt, reduce, back, spread, rounded, *refs):
    refs = list(refs)
    section, ctx, wt = place()
    sibling = (1 - section, ctx, wt)
    peers = [(section, ctx, lax.rem(wt + k, n_wt)) for k in range(1, n_wt)]
    parts = refs.pop(0) if reduce else None
    rows_ref = refs.pop(0)
    stream_ref = refs.pop(0) if back else None
    gain_ref = refs.pop(0) if (back or spread) else None
    result_ref = refs.pop(0) if reduce else None
    gain_grad_ref = refs.pop(0) if back else None
    all_ref = refs.pop(0) if spread else None
    if reduce:
        from_sibling, from_peers, staged, rs_send, rs_recv = refs[:5]
        refs = refs[5:]
    if spread:
        ag_send, ag_recv = refs
    greet([sibling] + peers)
    own = section * n_wt + wt
    if reduce:
        sends = []
        order = [lax.rem(wt + k, n_wt) for k in range(1, n_wt)] + [wt]
        swaps = []
        for k, block in enumerate(order):
            copy = remote(
                parts.at[(1 - section) * n_wt + block], from_sibling.at[block], rs_send.at[k], rs_recv.at[k], sibling
            )
            copy.start()
            swaps.append(copy)
        for k, block in enumerate(order[:-1]):
            swaps[k].wait_recv()
            staged[k] = (parts[section * n_wt + block].astype(F32) + from_sibling[block].astype(F32)).astype(BF16)
            copy = remote(
                staged.at[k], from_peers.at[k], rs_send.at[n_wt + k], rs_recv.at[n_wt + k], peers[k]
            )
            copy.start()
            sends.append(copy)
        swaps[-1].wait_recv()
        total = parts[own].astype(F32) + from_sibling[wt].astype(F32)
        for k in range(n_wt - 1):
            sends[k].wait_recv()
            total = total + from_peers[k].astype(F32)
        if back:
            stream = stream_ref[...]
            scale = norm_scale(stream)
            weighted = gain_ref[...] * total
            gain_grad_ref[...] = jnp.sum(total * stream * scale, 0, keepdims=True)
            total = scale * weighted - stream * (scale * scale * scale) * jnp.mean(
                weighted * stream, -1, keepdims=True
            )
        total = rows_ref[...].astype(F32) + total
        if rounded:
            total = total.astype(BF16).astype(F32)
        result_ref[...] = total
    else:
        total = rows_ref[...].astype(F32)
    if spread:
        if spread == "norm":
            total = total * norm_scale(total) * gain_ref[...]
        all_ref[own] = total.astype(BF16)
        copies = []
        for k in range(1, n_wt):
            copy = remote(all_ref.at[own], all_ref.at[own], ag_send.at[k], ag_recv.at[k], peers[k - 1])
            copy.start()
            copies.append(copy)
        copy = remote(all_ref.at[own], all_ref.at[own], ag_send.at[0], ag_recv.at[0], sibling)
        copy.start()
        swaps_out = [copy]
        for k in range(1, n_wt):
            copies[k - 1].wait_recv()
            block = section * n_wt + lax.rem(wt + n_wt - k, n_wt)
            copy = remote(all_ref.at[block], all_ref.at[block], ag_send.at[n_wt + k], ag_recv.at[n_wt + k], sibling)
            copy.start()
            swaps_out.append(copy)
        for copy in swaps_out:
            copy.wait()
        for copy in copies:
            copy.wait_send()
    if reduce:
        for copy in swaps + sends:
            copy.wait_send()


VMEM = pl.BlockSpec(memory_space=pltpu.VMEM)


def exchange(number, parts, rows, stream=None, gain=None, spread=None, rounded=False):
    n_wt = lax.axis_size("wt")
    shape = rows.shape
    reduce, back = parts is not None, stream is not None
    operands = [
        member
        for member, wanted in ((parts, reduce), (rows, True), (stream, back), (gain, back or spread))
        if wanted
    ]
    outs = []
    scratch = []
    if reduce:
        outs.append(jax.ShapeDtypeStruct(shape, F32))
        scratch += [
            pltpu.VMEM((n_wt,) + shape, BF16),
            pltpu.VMEM((n_wt - 1,) + shape, BF16),
            pltpu.VMEM((n_wt - 1,) + shape, BF16),
            pltpu.SemaphoreType.DMA((2 * n_wt,)),
            pltpu.SemaphoreType.DMA((2 * n_wt,)),
        ]
    if back:
        outs.append(jax.ShapeDtypeStruct((1, shape[1]), F32))
    if spread:
        outs.append(jax.ShapeDtypeStruct((2 * n_wt,) + shape, BF16))
        scratch += [pltpu.SemaphoreType.DMA((2 * n_wt,)), pltpu.SemaphoreType.DMA((2 * n_wt,))]
    return pl.pallas_call(
        functools.partial(exchange_kernel, n_wt, reduce, back, spread, rounded),
        out_shape=outs,
        in_specs=[VMEM] * len(operands),
        out_specs=[VMEM] * len(outs),
        scratch_shapes=scratch,
        compiler_params=pltpu.CompilerParams(
            collective_id=number, has_side_effects=True, vmem_limit_bytes=40 << 20
        ),
    )(*operands)


def ctx_gather_kernel(n_ctx, own_ref, all_ref, send, recv, local):
    section, ctx, wt = place()
    peers = [(section, lax.rem(ctx + k, n_ctx), wt) for k in range(1, n_ctx)]
    greet(peers)
    keep = pltpu.make_async_copy(own_ref, all_ref.at[ctx], local)
    keep.start()
    copies = [
        remote(own_ref, all_ref.at[ctx], send.at[k], recv.at[k], peers[k]) for k in range(n_ctx - 1)
    ]
    for copy in copies:
        copy.start()
    keep.wait()
    for copy in copies:
        copy.wait()


def ctx_gather(number, own):
    n_ctx = lax.axis_size("ctx")
    return pl.pallas_call(
        functools.partial(ctx_gather_kernel, n_ctx),
        out_shape=jax.ShapeDtypeStruct((n_ctx,) + own.shape, own.dtype),
        in_specs=[VMEM],
        out_specs=VMEM,
        scratch_shapes=[
            pltpu.SemaphoreType.DMA((n_ctx - 1,)),
            pltpu.SemaphoreType.DMA((n_ctx - 1,)),
            pltpu.SemaphoreType.DMA,
        ],
        compiler_params=pltpu.CompilerParams(collective_id=number, has_side_effects=True),
    )(own)


def ctx_sum_kernel(n_ctx, parts_ref, total_ref, landed, send, recv):
    section, ctx, wt = place()
    peers = [(section, lax.rem(ctx + k, n_ctx), wt) for k in range(1, n_ctx)]
    greet(peers)
    copies = [
        remote(parts_ref.at[lax.rem(ctx + k, n_ctx)], landed.at[k - 1], send.at[k - 1], recv.at[k - 1], peers[k - 1])
        for k in range(1, n_ctx)
    ]
    for copy in copies:
        copy.start()
    total = parts_ref[ctx].astype(F32)
    for k, copy in enumerate(copies):
        copy.wait_recv()
        total = total + landed[k].astype(F32)
    total_ref[...] = total
    for copy in copies:
        copy.wait_send()


def ctx_sum(number, parts):
    n_ctx = lax.axis_size("ctx")
    return pl.pallas_call(
        functools.partial(ctx_sum_kernel, n_ctx),
        out_shape=jax.ShapeDtypeStruct(parts.shape[1:], F32),
        in_specs=[VMEM],
        out_specs=VMEM,
        scratch_shapes=[
            pltpu.VMEM((n_ctx - 1,) + parts.shape[1:], BF16),
            pltpu.SemaphoreType.DMA((n_ctx - 1,)),
            pltpu.SemaphoreType.DMA((n_ctx - 1,)),
        ],
        compiler_params=pltpu.CompilerParams(
            collective_id=number, has_side_effects=True, vmem_limit_bytes=40 << 20
        ),
    )(parts)


def turn(values, cosine, sine, heads):
    pieces = []
    for head in range(heads):
        a = values[:, head * 64 : head * 64 + 32]
        b = values[:, head * 64 + 32 : head * 64 + 64]
        pieces += [a * cosine - b * sine, b * cosine + a * sine]
    return jnp.concatenate(pieces, -1)


def allowed_pairs(q_pos, q_seg, k_pos, k_seg):
    return ((k_seg[None, :] == 0) | (k_seg[None, :] == q_seg[:, None])) & (k_pos[None, :] <= q_pos[:, None])


def attend(query, pairs, q_pos, q_seg, k_pos, k_seg):
    logits = jnp.einsum("hqd,kd->hqk", query, pairs[:, :64], preferred_element_type=F32) * (1.0 / HEAD_SIZE)
    allowed = allowed_pairs(q_pos, q_seg, k_pos, k_seg)[None]
    logits = jnp.where(allowed, logits, MASKED)
    largest = jnp.max(logits, -1, keepdims=True)
    expos = jnp.exp(logits - largest)
    total = jnp.sum(expos, -1, keepdims=True)
    probs = (expos / total).astype(BF16)
    out = jnp.einsum("hqk,kd->hqd", probs, pairs[:, 64:], preferred_element_type=F32)
    return out, largest + jnp.log(total)


def attend_back(query, pairs, q_pos, q_seg, k_pos, k_seg, log_total, out, d_out):
    logits = jnp.einsum("hqd,kd->hqk", query, pairs[:, :64], preferred_element_type=F32) * (1.0 / HEAD_SIZE)
    allowed = allowed_pairs(q_pos, q_seg, k_pos, k_seg)[None]
    probs = jnp.where(allowed, jnp.exp(logits - log_total), 0.0)
    delta = jnp.sum(d_out.astype(F32) * out, -1, keepdims=True)
    d_probs = jnp.einsum("hqd,kd->hqk", d_out, pairs[:, 64:], preferred_element_type=F32)
    d_scores = (probs * (d_probs - delta)).astype(BF16)
    d_query = jnp.einsum("hqk,kd->hqd", d_scores, pairs[:, :64], preferred_element_type=F32) * (1.0 / HEAD_SIZE)
    d_keys = jnp.einsum("hqk,hqd->kd", d_scores, query, preferred_element_type=F32) * (1.0 / HEAD_SIZE)
    d_values = jnp.einsum("hqk,hqd->kd", probs.astype(BF16), d_out, preferred_element_type=F32)
    return d_query, jnp.concatenate([d_keys, d_values], -1)


def heads_first(rows, micro_count):
    count = rows.shape[0] // micro_count
    return jnp.transpose(rows.reshape(micro_count, count, -1, HEAD_SIZE), (0, 2, 1, 3))


def rows_first(heads):
    micro_count, h, q, d = heads.shape
    return jnp.transpose(heads, (0, 2, 1, 3)).reshape(micro_count * q, h * d)


def shards(tokens, cotangent, blocks, routes, norm_gain, w_query, key_value_weight, w_attn_out, router, w_in, w_down):
    section, ctx, wt = place()
    n_ctx, n_wt, layers = lax.axis_size("ctx"), lax.axis_size("wt"), lax.axis_size("section")
    micro_count, share, width = tokens.shape
    per_ctx = routes.shape[2]
    seq_len = per_ctx * n_ctx
    experts = w_in.shape[1] // 2
    n_experts = router.shape[2]
    q_cols = w_query.shape[2] // 2
    heads = q_cols // HEAD_SIZE
    depth = w_query.shape[1]

    block_len = seq_len // blocks.shape[1]
    placed = (blocks[:, :, None] * block_len + jnp.arange(block_len, dtype=jnp.int32)[None, None, :]).reshape(
        micro_count, seq_len
    )
    later = (jnp.arange(micro_count) > 0)[:, None]
    k_pos = jnp.where(later, seq_len + placed % CONT_LEN, placed)
    k_seg = jnp.where(later, 1 + placed // CONT_LEN, 0)
    q_pos = lax.dynamic_slice_in_dim(k_pos, ctx * per_ctx, per_ctx, 1)
    q_seg = lax.dynamic_slice_in_dim(k_seg, ctx * per_ctx, per_ctx, 1)
    inverse = jnp.power(ROPE_BASE, -jnp.arange(HEAD_SIZE // 2, dtype=F32) * 2.0 / HEAD_SIZE)
    angles = q_pos.reshape(-1).astype(F32)[:, None] * inverse[None, :]
    cosine, sine = jnp.cos(angles), jnp.sin(angles)

    def swap(values):
        return lax.ppermute(values, "section", [(0, 1), (1, 0)])

    def by_layer(halves):
        mine = lax.dynamic_index_in_dim(halves, section, 0, False)
        other = swap(lax.dynamic_index_in_dim(halves, 1 - section, 0, False))
        return [jnp.where(section == layer, mine, other) for layer in range(2)]

    def to_owner(first, second):
        mine = jnp.where(section == 0, first, second)
        other = swap(jnp.where(section == 0, second, first))
        return jnp.where(section == 0, mine, other), jnp.where(section == 0, other, mine)

    attn_pack = jnp.concatenate(
        [
            jnp.transpose(w_query[0].reshape(depth, 2, q_cols), (1, 0, 2)),
            jnp.transpose(key_value_weight[0], (1, 0, 2)),
            jnp.transpose(w_attn_out[0].reshape(2, q_cols, depth), (0, 2, 1)),
        ],
        -1,
    )
    attn_pack = by_layer(attn_pack)
    in_pack = by_layer(w_in[0].reshape((2, experts) + w_in.shape[2:]))
    down_pack = by_layer(w_down[0].reshape((2, experts) + w_down.shape[2:]))
    route_pack = lax.all_gather(routes[0], "section", axis=0)
    gain_pack = lax.all_gather(norm_gain[0], "section", axis=0)
    router_pack = lax.all_gather(router[0], "section", axis=0)

    attn_full = [lax.all_gather(member, "ctx", axis=0, tiled=True) for member in attn_pack]
    in_full = [lax.all_gather(member, "ctx", axis=1, tiled=True) for member in in_pack]
    down_full = [lax.all_gather(member, "ctx", axis=1, tiled=True) for member in down_pack]

    my_first = wt * 2 * experts + section * experts
    n_rows = micro_count * per_ctx

    def routed(layer):
        names = route_pack[layer].reshape(n_rows, -1)
        return jnp.any(names[:, :, None] == jnp.arange(n_experts, dtype=jnp.int32)[None, None, :], 1)

    def full_rows(values):
        return values.reshape(n_rows, width)

    def blocked(values):
        return values.reshape(2 * n_wt, share, width).astype(BF16)

    stream = lax.dynamic_index_in_dim(tokens, section, 0, False).astype(F32)
    top = lax.dynamic_index_in_dim(cotangent, section, 0, False).astype(F32)

    (normed_in,) = exchange(0, None, stream, gain=gain_pack[0, 0:1], spread="norm")
    (d_mixed,) = exchange(1, None, top, gain=gain_pack[0, 0:1], spread="plain")
    saved = []
    outputs = []
    for layer in range(2):
        rows_in = full_rows(normed_in)
        weights = attn_full[layer]
        mixed_heads = dot(rows_in, weights[:, : q_cols + 2 * HEAD_SIZE], ((1,), (0,)))
        turned = turn(mixed_heads[:, : q_cols + HEAD_SIZE], cosine, sine, heads + 1)
        queries = turned[:, :q_cols].astype(BF16)
        own_pairs = jnp.concatenate([turned[:, q_cols:], mixed_heads[:, q_cols + HEAD_SIZE :]], -1).astype(BF16)
        pairs = ctx_gather(2 + layer, own_pairs)
        pairs = jnp.transpose(
            pairs.reshape(n_ctx, micro_count, per_ctx, 2 * HEAD_SIZE), (1, 0, 2, 3)
        ).reshape(micro_count * seq_len, 2 * HEAD_SIZE)
        by_head = heads_first(queries, micro_count)
        outs = [
            attend(
                by_head[m],
                pairs[: (m + 1) * seq_len],
                q_pos[m],
                q_seg[m],
                k_pos.reshape(-1)[: (m + 1) * seq_len],
                k_seg.reshape(-1)[: (m + 1) * seq_len],
            )
            for m in range(micro_count)
        ]
        out_full = jnp.stack([member[0] for member in outs])
        log_total = [member[1] for member in outs]
        attended = rows_first(out_full).astype(BF16)
        partial = dot(attended, weights[:, q_cols + 2 * HEAD_SIZE :], ((1,), (1,)))
        middle, normed_mid = exchange(
            4 + layer, blocked(partial), stream, gain=gain_pack[layer, 1:2], spread="norm"
        )
        rows_mid = full_rows(normed_mid)
        logits = dot(rows_mid, router_pack[layer], ((1,), (0,)))
        hit = routed(layer)
        masked = jnp.where(hit, logits, MASKED)
        expos = jnp.where(hit, jnp.exp(masked - jnp.max(masked, 1, keepdims=True)), 0.0)
        gates = expos / jnp.sum(expos, 1, keepdims=True)
        my_gates = lax.dynamic_slice_in_dim(gates, my_first, experts, 1)
        gate_up = jnp.einsum("td,edf->etf", rows_mid, in_full[layer], preferred_element_type=F32)
        hidden = jax.nn.silu(gate_up[..., :FF]) * gate_up[..., FF:]
        weighted_hidden = (hidden * jnp.transpose(my_gates)[:, :, None]).astype(BF16)
        partial = jnp.einsum("etf,efd->td", weighted_hidden, down_full[layer], preferred_element_type=F32)
        saved.append(
            dict(
                stream=stream,
                middle=middle,
                rows_in=rows_in,
                rows_mid=rows_mid,
                queries=by_head,
                pairs=pairs,
                out_full=out_full,
                attended=attended,
                log_total=log_total,
                gates=gates,
                my_gates=my_gates,
                gate_up=gate_up,
                weighted_hidden=weighted_hidden,
            )
        )
        if layer == 0:
            stream, normed_in = exchange(
                6, blocked(partial), middle, gain=gain_pack[1, 0:1], spread="norm", rounded=True
            )
        else:
            (stream,) = exchange(7, blocked(partial), middle, rounded=True)
        outputs.append(stream.astype(BF16))

    upstream = top
    grads_in = [None, None]
    attn_grads = [None, None]
    in_grads = [None, None]
    down_grads = [None, None]
    small = [None, None]
    for layer in (1, 0):
        kept = saved[layer]
        rows_d = full_rows(d_mixed)
        d_weighted = jnp.einsum("td,efd->etf", rows_d, down_full[layer], preferred_element_type=F32)
        gate_part, up_part = kept["gate_up"][..., :FF], kept["gate_up"][..., FF:]
        sigmoid = jax.nn.sigmoid(gate_part)
        activated = gate_part * sigmoid
        d_weight = jnp.sum((activated * up_part).astype(BF16).astype(F32) * d_weighted, -1)
        d_hidden = d_weighted * jnp.transpose(kept["my_gates"])[:, :, None]
        d_gate_up = jnp.concatenate(
            [d_hidden * up_part * (sigmoid * (1.0 + gate_part * (1.0 - sigmoid))), d_hidden * activated], -1
        ).astype(BF16)
        down_grad = jnp.einsum("etf,td->efd", kept["weighted_hidden"], rows_d, preferred_element_type=F32)
        in_grad = jnp.einsum("td,etf->edf", kept["rows_mid"], d_gate_up, preferred_element_type=F32)
        down_grads[layer] = lax.psum_scatter(down_grad.astype(BF16), "ctx", scatter_dimension=1, tiled=True)
        in_grads[layer] = lax.psum_scatter(in_grad.astype(BF16), "ctx", scatter_dimension=1, tiled=True)
        partial = jnp.einsum("etf,edf->td", d_gate_up, in_full[layer], preferred_element_type=F32)
        terms = kept["my_gates"] * jnp.transpose(d_weight)
        placed_terms = lax.dynamic_update_slice_in_dim(jnp.zeros_like(kept["gates"]), terms, my_first, 1)
        d_logits = placed_terms - kept["gates"] * jnp.sum(terms, 1, keepdims=True)
        partial = partial + lax.dot_general(
            d_logits,
            router_pack[layer].astype(F32),
            (((1,), (1,)), ((), ())),
            precision=lax.Precision.HIGHEST,
            preferred_element_type=F32,
        )
        router_grad = lax.dot_general(
            d_logits,
            kept["rows_mid"].astype(F32),
            (((0,), (0,)), ((), ())),
            precision=lax.Precision.HIGHEST,
            preferred_element_type=F32,
        )
        d_middle, gain_grad_mid, d_attn = exchange(
            8 + layer, blocked(partial), upstream, kept["middle"], gain_pack[layer, 1:2], spread="plain"
        )
        rows_a = full_rows(d_attn)
        weights = attn_full[layer]
        d_attended = dot(rows_a, weights[:, q_cols + 2 * HEAD_SIZE :], ((1,), (0,))).astype(BF16)
        out_grad = dot(rows_a, kept["attended"], ((0,), (0,)))
        d_heads = heads_first(d_attended, micro_count)
        d_queries = []
        d_pairs = 0.0
        for m in range(micro_count):
            d_query, d_pair = attend_back(
                kept["queries"][m],
                kept["pairs"][: (m + 1) * seq_len],
                q_pos[m],
                q_seg[m],
                k_pos.reshape(-1)[: (m + 1) * seq_len],
                k_seg.reshape(-1)[: (m + 1) * seq_len],
                kept["log_total"][m],
                kept["out_full"][m],
                d_heads[m],
            )
            d_queries.append(d_query)
            d_pairs = d_pairs + jnp.pad(d_pair, ((0, (micro_count - 1 - m) * seq_len), (0, 0)))
        d_pairs = jnp.transpose(
            d_pairs.reshape(micro_count, n_ctx, per_ctx, 2 * HEAD_SIZE), (1, 0, 2, 3)
        ).reshape(n_ctx, n_rows, 2 * HEAD_SIZE)
        d_own = ctx_sum(10 + layer, d_pairs.astype(BF16))
        raw = jnp.concatenate([rows_first(jnp.stack(d_queries)), d_own[:, :HEAD_SIZE]], -1)
        raw = jnp.concatenate([turn(raw, cosine, -sine, heads + 1), d_own[:, HEAD_SIZE:]], -1).astype(BF16)
        heads_grad = dot(kept["rows_in"], raw, ((0,), (0,)))
        attn_grads[layer] = lax.psum_scatter(
            jnp.concatenate([heads_grad, out_grad], -1).astype(BF16), "ctx", scatter_dimension=0, tiled=True
        )
        partial = dot(raw, weights[:, : q_cols + 2 * HEAD_SIZE], ((1,), (1,)))
        if layer == 1:
            upstream, gain_grad_in, d_mixed = exchange(
                12, blocked(partial), d_middle, kept["stream"], gain_pack[1, 0:1], spread="plain", rounded=True
            )
        else:
            upstream, gain_grad_in = exchange(
                13, blocked(partial), d_middle, kept["stream"], gain_pack[0, 0:1], rounded=True
            )
        grads_in[layer] = upstream.astype(BF16)
        small[layer] = jnp.concatenate([gain_grad_in, gain_grad_mid, router_grad], 0)

    small_sum = lax.psum_scatter(
        jnp.transpose(
            jnp.concatenate(small, 0).reshape(-1, n_ctx * n_wt, width // (n_ctx * n_wt)), (1, 0, 2)
        ),
        ("ctx", "wt"),
        scatter_dimension=0,
        tiled=False,
    )
    small_first, small_second = jnp.split(small_sum, 2, 0)
    mine, other = to_owner(small_first, small_second)
    small_total = mine + other
    out_pair = jnp.stack(to_owner(outputs[0], outputs[1]))
    grad_pair = jnp.stack(to_owner(grads_in[0], grads_in[1]))
    attn_first, attn_second = [member.astype(F32) for member in to_owner(attn_grads[0], attn_grads[1])]
    kv_at = q_cols
    out_at = q_cols + 2 * HEAD_SIZE
    grad_query = jnp.concatenate([attn_first[:, :kv_at], attn_second[:, :kv_at]], -1)
    grad_kv = jnp.stack([attn_first[:, kv_at:out_at], attn_second[:, kv_at:out_at]], 1)
    grad_out = jnp.concatenate([jnp.transpose(attn_first[:, out_at:]), jnp.transpose(attn_second[:, out_at:])], 0)
    grad_in = jnp.concatenate(to_owner(in_grads[0], in_grads[1]), 0).astype(F32)
    grad_down = jnp.concatenate(to_owner(down_grads[0], down_grads[1]), 0).astype(F32)
    return (
        out_pair[None],
        grad_pair[None],
        small_total[:2][None],
        grad_query[None],
        grad_kv[None],
        grad_out[None],
        jnp.transpose(small_total[2:])[None],
        grad_in[None],
        grad_down[None],
    )


def solution(mesh):
    return jax.shard_map(
        shards,
        mesh=mesh,
        in_specs=(
            P(None, ("ctx", "wt"), None),
            P(None, ("ctx", "wt"), None),
            P(),
            P("section", None, "ctx", None),
            P("section", None, None),
            P("section", "ctx", "wt"),
            P("section", "ctx", "wt", None),
            P("section", "wt", "ctx"),
            P("section", None, None),
            P("section", "wt", "ctx", None),
            P("section", "wt", "ctx", None),
        ),
        out_specs=(
            P("section", None, ("ctx", "wt"), None),
            P("section", None, ("ctx", "wt"), None),
            P("section", None, ("ctx", "wt")),
            P("section", "ctx", "wt"),
            P("section", "ctx", "wt", None),
            P("section", "wt", "ctx"),
            P("section", ("ctx", "wt"), None),
            P("section", "wt", "ctx", None),
            P("section", "wt", "ctx", None),
        ),
        check_vma=False,
    )
```

time: 1970 us -> 1130 us (0.57)
  waiting for transfers between devices: 761 us -> 299 us
  Pallas kernels: 0 us -> 396 us
  blocking collectives: 274 us -> 5.58 us
  other arithmetic: 317 us -> 60.4 us
  matrix products: 333 us -> 140 us
  local copies, waits for them, and re-layouts: 227 us -> 197 us
  loops' own time: 21.1 us -> 0 us
    pallas_call x0 -> x14, Pallas kernels: none -> 396 us  [the longest x10 342 us: exchange(): pl.pallas_call(functools.partial(exchange_kernel, n_wt, reduce, back, spr...]
    reduce_scatter x21 -> x2, waiting for transfers between devices: 403 us -> 88.9 us  [shards(): lax.psum_scatter(down_grad.astype(BF16), 'ctx', scatter_dimension=1, tile...]
    all_gather x16 -> x3, blocking collectives: 274 us -> 5.58 us  [the longest x1 1.87 us: shards(): gain_pack = lax.all_gather(norm_gain[0], 'section', axis=0)]
    dot_general x124 -> x54, matrix products: 333 us -> 140 us  [the longest x14 25.2 us: dot(): lax.dot_general(left, right, (contract, ((), ())), preferred_element_type...]
    scatter-add x9 -> x0, other arithmetic: 172 us -> none  [the longest x3 98.4 us: backward(): jnp.zeros((expert_count, count_of_rows), jnp.float32).at[owner, slot_rows]]
    all_gather x4 -> x6, waiting for transfers between devices: 150 us -> 0.05 us  [the longest x4 0.03 us: shards(): lax.all_gather(member, 'ctx', axis=1, tiled=True)]
    unnamed x587 -> x320, local copies, waits for them, and re-layouts: 44.3 us -> 135 us
    gather x24 -> x0, local copies, waits for them, and re-layouts: 59.5 us -> none  [the longest x15 28.2 us: dispatch(): jnp.take_along_axis(jnp.transpose(row_weight), slot_rows, 1)]
  transfers between devices with their start and end apart: 35 -> 22, of which waited for: 22 -> 12; matrix products, arithmetic and copies ran while one was open for 26% -> 20% of each run, Pallas kernels for 0% -> 20%
where the time goes in v1:
time: 1130 us; the launch traced here: 1120 us
  Pallas kernels  396 us (35%)
  waiting for transfers between devices  299 us (26%)
  local copies, waits for them, and re-layouts  197 us (17%)
  matrix products  140 us (12%)
  other arithmetic  60.4 us (5%)
  between operations  16.7 us (1%)
    pallas_call x10, Pallas kernels, exchange(): pl.pallas_call(functools.partial(exchange_kernel, n_wt, reduce, back, spr...  342 us
    unnamed x18, waiting for transfers between devices  203 us
    unnamed x320, local copies, waits for them, and re-layouts  135 us
    reduce_scatter x2, waiting for transfers between devices, shards(): lax.psum_scatter(down_grad.astype(BF16), 'ctx', scatter_dimension=1, tile...  88.9 us
    pallas_call x2, Pallas kernels, ctx_gather(): pl.pallas_call(functools.partial(ctx_gather_kernel, n_ctx), out_shape=jax...  34.8 us
    dot_general x14, matrix products, dot(): lax.dot_general(left, right, (contract, ((), ())), preferred_element_type...  25.2 us
  transfers between devices with their start and end apart: 22, of which 12 were waited for; matrix products, arithmetic and copies ran while one was open for 20% of the time, Pallas kernels for 20%

profile of v1, /device:TPU:0, one launch (start us, length us, event | category | flops | bytes accessed | tf_op | source)
XLA Modules:
  0.0 1118.2 jit_solution(1751694562411946994)
XLA Ops:
  18.5 2.5 collective-permute-done
  21.0 3.4 bitcast_select_fusion
  32.4 20.8 %shard_map.178 = bf16[8,64,1536]{2,1,0:T(8,128)(2,1)S(1)} custom-call(f32[64,1536]{1,0:T(8,128)S(1)} %get-tuple-element.237.refs_0_.refs_1_.refs_2_, f32[1,1536]{1,0:T(1,128)S(1)} %get-tuple-element.192.refs_1_.refs_3_), custom_call_target="tpu_custom_call" | custom-call | tf_op jit(solution)/shard_map/pallas_call | solution.py:162
  53.3 22.0 %shard_map.185 = bf16[8,64,1536]{2,1,0:T(8,128)(2,1)S(1)} custom-call(f32[64,1536]{1,0:T(8,128)S(1)} %get-tuple-element.236.refs_0_.refs_1_, f32[1,1536]{1,0:T(1,128)S(1)} %get-tuple-element.192.refs_1_.refs_3_), custom_call_target="tpu_custom_call" | custom-call | tf_op jit(solution)/shard_map/pallas_call | solution.py:162
  86.8 2.3 fusion.178
  89.9 17.4 %shard_map.179 = bf16[4,512,128]{2,1,0:T(8,128)(2,1)} custom-call(bf16[512,128]{1,0:T(8,128)(2,1)} %pad_maximum_fusion.9.own_ref), custom_call_target="tpu_custom_call" | custom-call | tf_op jit(solution)/shard_map/pallas_call | solution.py:192
  124.7 40.4 %shard_map.180 = (f32[64,1536]{1,0:T(8,128)S(1)}, bf16[8,64,1536]{2,1,0:T(8,128)(2,1)S(1)}) custom-call(bf16[8,64,1536]{2,1,0:T(8,128)(2,1)S(1)} %convolution_convert_fusion.5.refs_0_, f32[64,1536]{1,0:T(8,128)S(1)} %get-tuple-element.237.refs_0_.refs_1_.refs_2_, f32[1,1536]{1,0:T(1,128)S(1)} %get-tuple-element.191.refs_2_.refs_3_), custom_call_target="tpu_custom_call" | custom-call | tf_op jit(solution)/shard_map/pallas_call | solution.py:162
  165.8 6.0 convolution_bitcast_fusion.7
  175.5 4.0 fusion.14
  179.6 42.3 %shard_map.181 = (f32[64,1536]{1,0:T(8,128)S(1)}, bf16[8,64,1536]{2,1,0:T(8,128)(2,1)S(1)}) custom-call(bf16[8,64,1536]{2,1,0:T(8,128)(2,1)S(1)} %bitcast.511, f32[64,1536]{1,0:T(8,128)S(1)} %get-tuple-element.27.refs_1_.refs_2_, f32[1,1536]{1,0:T(1,128)S(1)} %get-tuple-element.190.refs_2_.refs_3_), custom_call_target="tpu_custom_call" | custom-call | tf_op jit(solution)/shard_map/pallas_call | solution.py:162
  223.0 2.4 fusion.59
  235.5 3.3 fusion.194
  239.7 17.4 %shard_map.182 = bf16[4,512,128]{2,1,0:T(8,128)(2,1)} custom-call(bf16[512,128]{1,0:T(8,128)(2,1)} %pad_maximum_fusion.10.own_ref), custom_call_target="tpu_custom_call" | custom-call | tf_op jit(solution)/shard_map/pallas_call | solution.py:192
  257.1 2.2 copy.291
  260.3 2.3 reshape.497
  267.5 2.4 select_reduce_fusion
  280.6 42.0 %shard_map.183 = (f32[64,1536]{1,0:T(8,128)S(1)}, bf16[8,64,1536]{2,1,0:T(8,128)(2,1)S(1)}) custom-call(bf16[8,64,1536]{2,1,0:T(8,128)(2,1)S(1)} %convolution_convert_fusion.4.refs_0_, f32[64,1536]{1,0:T(8,128)S(1)} %get-tuple-element.28.refs_1_.refs_2_, f32[1,1536]{1,0:T(1,128)S(1)} %copy-done.28), custom_call_target="tpu_custom_call" | custom-call | tf_op jit(solution)/shard_map/pallas_call | solution.py:162
  327.1 8.0 convolution_bitcast_fusion.6
  335.1 7.5 multiply_convert_fusion.7
  344.3 3.6 fusion.17
  348.0 42.1 %shard_map.186 = (f32[64,1536]{1,0:T(8,128)S(1)}, f32[1,1536]{1,0:T(1,128)S(1)}, bf16[8,64,1536]{2,1,0:T(8,128)(2,1)S(1)}) custom-call(bf16[8,64,1536]{2,1,0:T(8,128)(2,1)S(1)} %bitcast.513, f32[64,1536]{1,0:T(8,128)S(1)} %copy-done.5, f32[64,1536]{1,0:T(8,128)S(1)} %copy-done.18, f32[1,1536]{1,0:T(1,128)S(1)} %copy-done.29), custom_call_target="tpu_custom_call" | custom-call | tf_op jit(solution)/shard_map/pallas_call | solution.py:162
  392.6 2.4 convolution_convert_fusion.11
  398.7 4.4 fusion.22
  403.2 4.5 multiply_convert_fusion.1
  417.4 2.2 copy.305
  420.6 9.6 shard_map.187
  444.9 3.5 fusion.150
  448.4 2.6 concatenate.106
  451.0 2.3 convolution_convert_fusion.3
  454.0 41.8 %shard_map.188 = (f32[64,1536]{1,0:T(8,128)S(1)}, f32[1,1536]{1,0:T(1,128)S(1)}, bf16[8,64,1536]{2,1,0:T(8,128)(2,1)S(1)}) custom-call(bf16[8,64,1536]{2,1,0:T(8,128)(2,1)S(1)} %bitcast.515, f32[64,1536]{1,0:T(8,128)S(1)} %copy-done.25, f32[64,1536]{1,0:T(8,128)S(1)} %get-tuple-element.28.refs_1_.refs_2_, f32[1,1536]{1,0:T(1,128)S(1)} %copy-done.27), custom_call_target="tpu_custom_call" | custom-call | tf_op jit(solution)/shard_map/pallas_call | solution.py:162
  495.9 6.6 multiply_convert_fusion.5
  504.2 3.7 fusion.16
  507.9 42.4 %shard_map.189 = (f32[64,1536]{1,0:T(8,128)S(1)}, f32[1,1536]{1,0:T(1,128)S(1)}, bf16[8,64,1536]{2,1,0:T(8,128)(2,1)S(1)}) custom-call(bf16[8,64,1536]{2,1,0:T(8,128)(2,1)S(1)} %bitcast.514, f32[64,1536]{1,0:T(8,128)S(1)} %get-tuple-element.35.refs_1_, f32[64,1536]{1,0:T(8,128)S(1)} %copy-done.21, f32[1,1536]{1,0:T(1,128)S(1)} %get-tuple-element.191.refs_2_.refs_3_), custom_call_target="tpu_custom_call" | custom-call | tf_op jit(solution)/shard_map/pallas_call | solution.py:162
  552.8 2.4 convolution_convert_fusion.10
  558.9 4.4 fusion.25
  563.4 4.4 multiply_convert_fusion
  586.2 9.6 shard_map.190
  610.4 3.5 fusion.166
  616.2 2.4 convolution_convert_fusion.2
  618.6 24.0 %shard_map.191 = (f32[64,1536]{1,0:T(8,128)S(1)}, f32[1,1536]{1,0:T(1,128)S(1)}) custom-call(bf16[8,64,1536]{2,1,0:T(8,128)(2,1)S(1)} %bitcast.516, f32[64,1536]{1,0:T(8,128)S(1)} %copy-done.23, f32[64,1536]{1,0:T(8,128)S(1)} %copy-done.1, f32[1,1536]{1,0:T(1,128)S(1)} %get-tuple-element.192.refs_1_.refs_3_), custom_call_target="tpu_custom_call" | custom-call | tf_op jit(solution)/shard_map/pallas_call | solution.py:162
  643.9 6.0 concatenate.111
  657.8 2.6 copy.335
  665.9 2.6 copy.333
  668.6 5.2 convolution_convert_fusion
  673.9 5.2 convolution_convert_fusion.1
  679.1 6.9 convert_bitcast_fusion
  686.0 16.4 %copy.339 = bf16[2,1536,1024]{2,0,1:T(2,128)(2,1)} copy(bf16[2,1536,1024]{1,2,0:T(8,128)(2,1)} %convert_bitcast_fusion) | data formatting | bytes 12582912
  702.4 8.1 copy.387
  711.7 6.6 convert_bitcast_fusion.1
  718.3 16.4 %copy.337 = bf16[2,1536,1024]{2,0,1:T(2,128)(2,1)} copy(bf16[2,1536,1024]{1,2,0:T(8,128)(2,1)} %convert_bitcast_fusion.1) | data formatting | bytes 12582912
  734.7 8.0 copy.386
  743.9 3.7 fusion.15
  747.7 24.3 %shard_map.184 = f32[64,1536]{1,0:T(8,128)S(1)} custom-call(bf16[8,64,1536]{2,1,0:T(8,128)(2,1)S(1)} %bitcast.512, f32[64,1536]{1,0:T(8,128)S(1)} %copy-done.19), custom_call_target="tpu_custom_call" | custom-call | tf_op jit(solution)/shard_map/pallas_call | solution.py:162
  778.6 27.7 %reduce-scatter.21.cloned.1.call-done = bf16[384,512]{1,0:T(8,128)(2,1)} async-done(((bf16[1536,512]{1,0:T(8,128)(2,1)}), bf16[384,512]{1,0:T(8,128)(2,1)}) %reduce-scatter.21.cloned.1.call-update) | async-done | bytes 393232
  807.5 33.0 %reduce-scatter.19.cloned.1.call-done = bf16[384,512]{1,0:T(8,128)(2,1)} async-done(((bf16[1536,512]{1,0:T(8,128)(2,1)}), bf16[384,512]{1,0:T(8,128)(2,1)}) %reduce-scatter.19.cloned.1.call-update) | async-done | bytes 393232
  846.5 41.6 %reduce-scatter.17.cloned.1.call-done = bf16[2,128,1536]{2,1,0:T(8,128)(2,1)} async-done(((bf16[2,512,1536]{2,1,0:T(8,128)(2,1)}), bf16[2,128,1536]{2,1,0:T(8,128)(2,1)}) %reduce-scatter.17.cloned.1.call-update) | async-done | bytes 786448 | tf_op jit(solution)/shard_map/reduce_scatter | solution.py:454
  888.2 47.2 %reduce-scatter.15.cloned.1.call-done = bf16[2,128,1536]{2,1,0:T(8,128)(2,1)} async-done(((bf16[2,512,1536]{2,1,0:T(8,128)(2,1)}), bf16[2,128,1536]{2,1,0:T(8,128)(2,1)}) %reduce-scatter.15.cloned.1.call-update) | async-done | bytes 786448 | tf_op jit(solution)/shard_map/reduce_scatter | solution.py:454
  937.6 71.8 %reduce-scatter.25.cloned.1.call-done = bf16[384,2048]{1,0:T(8,128)(2,1)} async-done(((bf16[1536,2048]{1,0:T(8,128)(2,1)}), bf16[384,2048]{1,0:T(8,128)(2,1)}) %reduce-scatter.25.cloned.1.call-update) | async-done | bytes 1572880
  1009.3 2.9 reshape.545
  1013.8 69.0 %reduce-scatter.23.cloned.1.call-done = bf16[384,2048]{1,0:T(8,128)(2,1)} async-done(((bf16[1536,2048]{1,0:T(8,128)(2,1)}), bf16[384,2048]{1,0:T(8,128)(2,1)}) %reduce-scatter.23.cloned.1.call-update) | async-done | bytes 1572880
  1082.8 3.8 reshape.543
  1086.7 3.7 copy.338
  1101.6 3.0 maximum_convert_fusion
  1104.6 6.6 copy.322
  (519 shorter events, 207.9 us)
Async XLA Ops:
  7.2 75.6 %all-gather.9.cloned.1.call-start = ((), (), s32[]{:S(2)}) async-start(), calls=%async_computation.7 | async-start | bytes 1966080 | tf_op jit(solution)/shard_map/all_gather | solution.py:344
  10.6 1.9 collective-permute-start.1
  13.5 152.3 %all-gather.7.cloned.1.call-start = ((), (), s32[]{:S(2)}) async-start(), calls=%async_computation.6 | async-start | bytes 7864320 | tf_op jit(solution)/shard_map/all_gather | solution.py:345
  17.3 3.8 collective-permute-start
  24.4 151.1 %all-gather.11.cloned.1.call-start = ((), (), s32[]{:S(2)}) async-start(), calls=%async_computation.8 | async-start | bytes 3932160 | tf_op jit(solution)/shard_map/all_gather | solution.py:346
  24.6 7.1 copy-start.93
  24.6 7.1 copy-start.94
  24.6 2.4 collective-permute-start.2
  28.2 194.8 %all-gather.15.cloned.1.call-start = ((), (), s32[]{:S(2)}) async-start(), calls=%async_computation.10 | async-start | bytes 1966080 | tf_op jit(solution)/shard_map/all_gather | solution.py:344
  28.8 298.3 %all-gather.13.cloned.1.call-start = ((), (), s32[]{:S(2)}) async-start(), calls=%async_computation.9 | async-start | bytes 7864320 | tf_op jit(solution)/shard_map/all_gather | solution.py:345
  28.8 47.6 %copy-start.106 = (s32[1,2,256,8]{2,3,1,0:T(8,128)S(1)}, s32[1,2,256,8]{2,3,1,0:T(8,128)}, u32[]{:S(2)}) copy-start(s32[1,2,256,8]{2,3,1,0:T(8,128)} %param.14) | copy-start | bytes 49156
  28.9 49.5 %copy-start.97 = (bf16[1,1536,16]{1,2,0:T(8,128)(2,1)S(1)}, bf16[1,1536,16]{1,2,0:T(8,128)(2,1)}, u32[]{:S(2)}) copy-start(bf16[1,1536,16]{1,2,0:T(8,128)(2,1)} %param.19) | copy-start | bytes 147460
  29.4 305.7 %all-gather.17.cloned.1.call-start = ((), (), s32[]{:S(2)}) async-start(), calls=%async_computation.11 | async-start | bytes 3932160 | tf_op jit(solution)/shard_map/all_gather | solution.py:346
  29.8 205.8 %copy-start.95 = (f32[1,2,2,128]{3,1,2,0:T(2,128)}, f32[1,2,2,128]{3,1,2,0:T(2,128)S(1)}, u32[]{:S(2)}) copy-start(f32[1,2,2,128]{3,1,2,0:T(2,128)S(1)} %copy.380) | copy-start | bytes 6148
  31.7 21.5 %copy-start.4 = (f32[64,1536]{1,0:T(8,128)}, f32[64,1536]{1,0:T(8,128)S(1)}, u32[]{:S(2)}) copy-start(f32[64,1536]{1,0:T(8,128)S(1)} %get-tuple-element.236.refs_0_.refs_1_) | copy-start | bytes 1179652
  31.8 92.9 %copy-start = (f32[64,1536]{1,0:T(8,128)}, f32[64,1536]{1,0:T(8,128)S(1)}, u32[]{:S(2)}) copy-start(f32[64,1536]{1,0:T(8,128)S(1)} %get-tuple-element.237.refs_0_.refs_1_.refs_2_) | copy-start | bytes 1179652
  32.4 147.1 %copy-start.26 = (f32[1,1536]{1,0:T(1,128)}, f32[1,1536]{1,0:T(1,128)S(1)}, u32[]{:S(2)}) copy-start(f32[1,1536]{1,0:T(1,128)S(1)} %get-tuple-element.190.refs_2_.refs_3_) | copy-start | bytes 18436
  53.2 31.6 %copy-start.11 = (bf16[8,64,1536]{2,1,0:T(8,128)(2,1)}, bf16[8,64,1536]{2,1,0:T(8,128)(2,1)S(1)}, u32[]{:S(2)}) copy-start(bf16[8,64,1536]{2,1,0:T(8,128)(2,1)S(1)} %shard_map.178) | copy-start | bytes 4718596
  80.2 84.9 %copy-start.70 = (bf16[2,1536,16]{1,2,0:T(8,128)(2,1)}, bf16[2,1536,16]{1,2,0:T(8,128)(2,1)S(1)}, u32[]{:S(2)}) copy-start(bf16[2,1536,16]{1,2,0:T(8,128)(2,1)S(1)} %all_gather.31) | copy-start | bytes 294916
  82.0 191.5 %copy-start.50 = (pred[256,1024]{1,0:T(8,128)(4,1)}, pred[256,1024]{1,0:T(8,128)(4,1)S(1)}, u32[]{:S(2)}) copy-start(pred[256,1024]{1,0:T(8,128)(4,1)S(1)} %compare_and_fusion.1) | copy-start | bytes 786436
  82.7 192.1 %copy-start.40 = (pred[256,2048]{1,0:T(8,128)(4,1)}, pred[256,2048]{1,0:T(8,128)(4,1)S(1)}, u32[]{:S(2)}) copy-start(pred[256,2048]{1,0:T(8,128)(4,1)S(1)} %compare_and_fusion) | copy-start | bytes 1572868
  82.7 691.8 %all-reduce.5.cloned.1.call-start = ((), (), s32[]{:S(2)}) async-start(), calls=%async_computation.18 | async-start | bytes 655360
  114.6 7.8 copy-start.73
  122.4 43.2 %copy-start.53 = (bf16[2,256,3,64]{1,3,2,0:T(8,128)(2,1)}, bf16[2,256,3,64]{1,3,2,0:T(8,128)(2,1)S(1)}, u32[]{:S(2)}) copy-start(bf16[2,256,3,64]{1,3,2,0:T(8,128)(2,1)S(1)} %fusion.206) | copy-start | bytes 589828
  165.1 14.5 %copy-start.20 = (f32[64,1536]{1,0:T(8,128)}, f32[64,1536]{1,0:T(8,128)S(1)}, u32[]{:S(2)}) copy-start(f32[64,1536]{1,0:T(8,128)S(1)} %get-tuple-element.27.refs_1_.refs_2_) | copy-start | bytes 1179652
  165.7 6.1 copy-start.82
  165.7 6.1 copy-start.111
  239.7 22.9 %copy-start.79 = (bf16[512,32]{1,0:T(8,128)(2,1)S(1)}, bf16[512,32]{1,0:T(8,128)(2,1)}, u32[]{:S(2)}) copy-start(bf16[512,32]{1,0:T(8,128)(2,1)} %get-tuple-element.151) | copy-start | bytes 98308
  260.3 13.2 %copy-start.63 = (bf16[1,4,256,128]{3,2,0,1:T(8,128)(2,1)}, bf16[1,4,256,128]{3,2,0,1:T(8,128)(2,1)S(1)}, u32[]{:S(2)}) copy-start(bf16[1,4,256,128]{3,2,0,1:T(8,128)(2,1)S(1)} %slice.479) | copy-start | bytes 786436
  278.2 46.4 %copy-start.92 = (pred[512,16]{0,1:T(8,128)(4,1)S(1)}, pred[512,16]{0,1:T(8,128)(4,1)}, u32[]{:S(2)}) copy-start(pred[512,16]{0,1:T(8,128)(4,1)} %fusion.200) | copy-start | bytes 24580
  278.2 47.7 %copy-start.103 = (f32[3,256]{1,0:T(4,128)S(1)}, f32[3,256]{1,0:T(4,128)}, u32[]{:S(2)}) copy-start(f32[3,256]{1,0:T(4,128)} %copy-done.102) | copy-start | bytes 9220
  278.2 47.7 %copy-start.105 = (f32[3,256]{1,0:T(4,128)S(1)}, f32[3,256]{1,0:T(4,128)}, u32[]{:S(2)}) copy-start(f32[3,256]{1,0:T(4,128)} %copy-done.104) | copy-start | bytes 9220
  278.2 48.3 %copy-start.108 = (f32[3,256]{1,0:T(4,128)S(1)}, f32[3,256]{1,0:T(4,128)}, u32[]{:S(2)}) copy-start(f32[3,256]{1,0:T(4,128)} %copy-done.107) | copy-start | bytes 9220
  278.2 48.3 %copy-start.110 = (f32[3,256]{1,0:T(4,128)S(1)}, f32[3,256]{1,0:T(4,128)}, u32[]{:S(2)}) copy-start(f32[3,256]{1,0:T(4,128)} %copy-done.109) | copy-start | bytes 9220
  335.1 9.1 slice-start.2
  335.1 7.6 copy-start.86
  335.1 7.6 copy-start.71
  335.1 9.1 slice-start.3
  451.0 44.9 %copy-start.112 = (f32[2,512]{1,0:T(2,128)S(1)}, f32[2,512]{1,0:T(2,128)}, u32[]{:S(2)}) copy-start(f32[2,512]{1,0:T(2,128)} %copy-done.111) | copy-start | bytes 12292
  495.8 6.7 copy-start.32
  495.8 6.7 copy-start.37
  495.8 12.0 %copy-start.2 = (f32[64,1536]{1,0:T(8,128)}, f32[64,1536]{1,0:T(8,128)S(1)}, u32[]{:S(2)}) copy-start(f32[64,1536]{1,0:T(8,128)S(1)} %get-tuple-element.35.refs_1_) | copy-start | bytes 1179652
  495.9 8.3 slice-start
  495.9 6.7 copy-start.83
  495.9 6.8 copy-start.72
  495.9 8.2 slice-start.1
  551.6 7.2 copy-start.117
  585.1 25.3 %copy-start.115 = (f32[32]{0:T(128)S(1)}, f32[32]{0:T(128)}, u32[]{:S(2)}) copy-start(f32[32]{0:T(128)} %multiply_power_fusion) | copy-start | bytes 388
  586.2 24.3 %copy-start.96 = (f32[1,2,2,128]{3,1,2,0:T(2,128)S(1)}, f32[1,2,2,128]{3,1,2,0:T(2,128)}, u32[]{:S(2)}) copy-start(f32[1,2,2,128]{3,1,2,0:T(2,128)} %copy-done.95) | copy-start | bytes 6148
  613.9 30.0 %copy-start.31 = (f32[1,1536]{1,0:T(1,128)S(1)}, f32[1,1536]{1,0:T(1,128)}, u32[]{:S(2)}) copy-start(f32[1,1536]{1,0:T(1,128)} %copy-done.30) | copy-start | bytes 18436
  653.5 152.8 %reduce-scatter.21.cloned.1.call-start = ((), (), s32[]{:S(2)}) async-start(), calls=%async_computation.15 | async-start | bytes 1966080
  660.4 180.1 %reduce-scatter.19.cloned.1.call-start = ((), (), s32[]{:S(2)}) async-start(), calls=%async_computation.14 | async-start | bytes 1966080
  668.5 219.6 %reduce-scatter.17.cloned.1.call-start = ((), (), s32[]{:S(2)}) async-start(), calls=%async_computation.13 | async-start | bytes 3932160 | tf_op jit(solution)/shard_map/reduce_scatter | solution.py:454
  673.8 261.6 %reduce-scatter.15.cloned.1.call-start = ((), (), s32[]{:S(2)}) async-start(), calls=%async_computation.12 | async-start | bytes 3932160 | tf_op jit(solution)/shard_map/reduce_scatter | solution.py:454
  679.0 330.3 %reduce-scatter.25.cloned.1.call-start = ((), (), s32[]{:S(2)}) async-start(), calls=%async_computation.17 | async-start | bytes 7864320
  710.5 372.3 %reduce-scatter.23.cloned.1.call-start = ((), (), s32[]{:S(2)}) async-start(), calls=%async_computation.16 | async-start | bytes 7864320
  747.7 24.6 %copy-start.3 = (f32[64,1536]{1,0:T(8,128)S(1)}, f32[64,1536]{1,0:T(8,128)}, u32[]{:S(2)}) copy-start(f32[64,1536]{1,0:T(8,128)} %copy-done.2) | copy-start | bytes 1179652
  747.7 24.6 %copy-start.16 = (f32[64,1536]{1,0:T(8,128)S(1)}, f32[64,1536]{1,0:T(8,128)}, u32[]{:S(2)}) copy-start(f32[64,1536]{1,0:T(8,128)} %copy-done.15) | copy-start | bytes 1179652
  772.1 1.5 collective-permute-start.3
  772.3 2.1 collective-permute-start.4
  776.0 1.2 collective-permute-start.5
  841.8 1.8 collective-permute-start.6
  937.6 158.9 %collective-permute-start.8 = (bf16[2,128,1536]{2,1,0:T(8,128)(2,1)}, bf16[2,128,1536]{2,1,0:T(8,128)(2,1)}, u32[]{:S(2)}, u32[]{:S(2)}) collective-permute-start(bf16[2,128,1536]{2,1,0:T(8,128)(2,1)} %broadcast_select_fusion.2), channel_id=1, source_target_pairs={{0,16},{16,0},{1,17},{17,1},{2,18},{18,2},{3,19},{19,3},{4,20},{20... | collective-permute-start | bytes 2359304 | tf_op jit(solution)/shard_map/ppermute | solution.py:317
  1091.7 8.1 collective-permute-start.7
  (90 other events, 232.5 us)
Sparse Core Ops, SparseCore 0:
  13.6 33.4 all-gather.8
  49.5 75.6 all-gather.6
  127.6 43.9 all-gather.10
  173.8 30.8 all-gather.14
  206.3 75.6 all-gather.12
  283.7 43.9 all-gather.16
  653.6 115.5 all-reduce.4
  772.5 33.7 reduce-scatter.20
  809.6 30.9 reduce-scatter.18
  844.2 43.9 reduce-scatter.16
  891.4 43.9 reduce-scatter.14
  939.1 70.1 reduce-scatter.24
  1012.6 70.1 reduce-scatter.22

commit v2 on v1

--- a/solution.py
+++ b/solution.py
@@ -168,6 +168,7 @@
         compiler_params=pltpu.CompilerParams(
             collective_id=number, has_side_effects=True, vmem_limit_bytes=40 << 20
         ),
+        cost_estimate=pl.CostEstimate(flops=0, bytes_accessed=120 << 20, transcendentals=0),
     )(*operands)
 
 
@@ -240,6 +241,55 @@
     )(parts)
 
 
+def small_sum_kernel(n_ctx, n_wt, parts_ref, total_ref, landed, summed, from_sibling, send, recv):
+    section, ctx, wt = place()
+    count = n_ctx * n_wt
+    own = ctx * n_wt + wt
+    blocks = [lax.rem(own + k, count) for k in range(1, count)]
+    peers = [(section, block // n_wt, lax.rem(block, n_wt)) for block in blocks]
+    sibling = (1 - section, ctx, wt)
+    greet([sibling] + peers)
+    copies = [
+        remote(parts_ref.at[blocks[k]], landed.at[k], send.at[k], recv.at[k], peers[k]) for k in range(count - 1)
+    ]
+    for copy in copies:
+        copy.start()
+    total = parts_ref[own]
+    for k, copy in enumerate(copies):
+        copy.wait_recv()
+        total = total + landed[k]
+    summed[...] = total
+    swap = remote(
+        summed.at[1 - section], from_sibling, send.at[count - 1], recv.at[count - 1], sibling
+    )
+    swap.start()
+    swap.wait()
+    total_ref[...] = summed[section] + from_sibling[...]
+    for copy in copies:
+        copy.wait_send()
+
+
+def small_sum(number, parts):
+    n_ctx, n_wt = lax.axis_size("ctx"), lax.axis_size("wt")
+    count = n_ctx * n_wt
+    return pl.pallas_call(
+        functools.partial(small_sum_kernel, n_ctx, n_wt),
+        out_shape=jax.ShapeDtypeStruct(parts.shape[2:], F32),
+        in_specs=[VMEM],
+        out_specs=VMEM,
+        scratch_shapes=[
+            pltpu.VMEM((count - 1,) + parts.shape[1:], F32),
+            pltpu.VMEM(parts.shape[1:], F32),
+            pltpu.VMEM(parts.shape[2:], F32),
+            pltpu.SemaphoreType.DMA((count,)),
+            pltpu.SemaphoreType.DMA((count,)),
+        ],
+        compiler_params=pltpu.CompilerParams(
+            collective_id=number, has_side_effects=True, vmem_limit_bytes=40 << 20
+        ),
+    )(parts)
+
+
 def turn(values, cosine, sine, heads):
     pieces = []
     for head in range(heads):
@@ -321,6 +371,10 @@
         other = swap(lax.dynamic_index_in_dim(halves, 1 - section, 0, False))
         return [jnp.where(section == layer, mine, other) for layer in range(2)]
 
+    def side_by_side(values):
+        halves = values.reshape((2, experts) + values.shape[1:])
+        return jnp.concatenate([halves[:, e] for e in range(experts)], -1)
+
     def to_owner(first, second):
         mine = jnp.where(section == 0, first, second)
         other = swap(jnp.where(section == 0, second, first))
@@ -335,15 +389,44 @@
         -1,
     )
     attn_pack = by_layer(attn_pack)
-    in_pack = by_layer(w_in[0].reshape((2, experts) + w_in.shape[2:]))
-    down_pack = by_layer(w_down[0].reshape((2, experts) + w_down.shape[2:]))
+    in_pack = by_layer(side_by_side(w_in[0]))
+    down_pack = by_layer(side_by_side(w_down[0]))
     route_pack = lax.all_gather(routes[0], "section", axis=0)
     gain_pack = lax.all_gather(norm_gain[0], "section", axis=0)
     router_pack = lax.all_gather(router[0], "section", axis=0)
 
+    def packed(in_part, down_part):
+        wide = in_part.shape[1]
+        rest = down_part[:, wide:]
+        half = rest.shape[0] // 2
+        return jnp.concatenate(
+            [in_part, down_part[:, :wide], jnp.concatenate([rest[:half], rest[half:]], 1)], 0
+        )
+
+    def unpacked(values, in_rows, down_rows):
+        wide = values.shape[-1]
+        n = values.shape[0]
+        rest = values[:, in_rows + down_rows :]
+        rest = jnp.concatenate([rest[..., : wide // 2], rest[..., wide // 2 :]], 1)
+        down_part = jnp.concatenate([values[:, in_rows : in_rows + down_rows], rest], 2)
+        return values[:, :in_rows].reshape(n * in_rows, wide), down_part.reshape(n * down_rows, -1)
+
+    def after(value, earlier):
+        return value if earlier is None else lax.optimization_barrier((value, earlier))[0]
+
+    in_rows, down_rows = w_in.shape[2], w_down.shape[2]
+    attn_full, in_full, down_full = [], [], []
+    last = None
+
+    def gather_experts(pack):
+        full = lax.all_gather(pack, "ctx", axis=0, tiled=True)
+        one, two = unpacked(full.reshape(n_ctx, -1, full.shape[1]), in_rows, down_rows)
+        in_full.append(one)
+        down_full.append(two)
+
+    moe_pack = [packed(in_pack[layer], down_pack[layer]) for layer in range(2)]
     attn_full = [lax.all_gather(member, "ctx", axis=0, tiled=True) for member in attn_pack]
-    in_full = [lax.all_gather(member, "ctx", axis=1, tiled=True) for member in in_pack]
-    down_full = [lax.all_gather(member, "ctx", axis=1, tiled=True) for member in down_pack]
+    gather_experts(moe_pack[0])
 
     my_first = wt * 2 * experts + section * experts
     n_rows = micro_count * per_ctx
@@ -395,6 +478,9 @@
         middle, normed_mid = exchange(
             4 + layer, blocked(partial), stream, gain=gain_pack[layer, 1:2], spread="norm"
         )
+        if layer == 0:
+            normed_mid, second = lax.optimization_barrier((normed_mid, moe_pack[1]))
+            gather_experts(second)
         rows_mid = full_rows(normed_mid)
         logits = dot(rows_mid, router_pack[layer], ((1,), (0,)))
         hit = routed(layer)
@@ -402,10 +488,16 @@
         expos = jnp.where(hit, jnp.exp(masked - jnp.max(masked, 1, keepdims=True)), 0.0)
         gates = expos / jnp.sum(expos, 1, keepdims=True)
         my_gates = lax.dynamic_slice_in_dim(gates, my_first, experts, 1)
-        gate_up = jnp.einsum("td,edf->etf", rows_mid, in_full[layer], preferred_element_type=F32)
-        hidden = jax.nn.silu(gate_up[..., :FF]) * gate_up[..., FF:]
-        weighted_hidden = (hidden * jnp.transpose(my_gates)[:, :, None]).astype(BF16)
-        partial = jnp.einsum("etf,efd->td", weighted_hidden, down_full[layer], preferred_element_type=F32)
+        gate_up = dot(rows_mid, in_full[layer], ((1,), (0,)))
+        weighted_hidden = []
+        partial = 0.0
+        for e in range(experts):
+            gate_part = gate_up[:, 2 * e * FF : (2 * e + 1) * FF]
+            up_part = gate_up[:, (2 * e + 1) * FF : (2 * e + 2) * FF]
+            weighted_hidden.append((jax.nn.silu(gate_part) * up_part * my_gates[:, e : e + 1]).astype(BF16))
+            partial = partial + dot(
+                weighted_hidden[e], down_full[layer][:, e * width : (e + 1) * width], ((1,), (0,))
+            )
         saved.append(
             dict(
                 stream=stream,
@@ -432,29 +524,48 @@
         outputs.append(stream.astype(BF16))
 
     upstream = top
+    last = None
     grads_in = [None, None]
     attn_grads = [None, None]
-    in_grads = [None, None]
-    down_grads = [None, None]
+    moe_grads = [None, None]
     small = [None, None]
     for layer in (1, 0):
         kept = saved[layer]
         rows_d = full_rows(d_mixed)
-        d_weighted = jnp.einsum("td,efd->etf", rows_d, down_full[layer], preferred_element_type=F32)
-        gate_part, up_part = kept["gate_up"][..., :FF], kept["gate_up"][..., FF:]
-        sigmoid = jax.nn.sigmoid(gate_part)
-        activated = gate_part * sigmoid
-        d_weight = jnp.sum((activated * up_part).astype(BF16).astype(F32) * d_weighted, -1)
-        d_hidden = d_weighted * jnp.transpose(kept["my_gates"])[:, :, None]
-        d_gate_up = jnp.concatenate(
-            [d_hidden * up_part * (sigmoid * (1.0 + gate_part * (1.0 - sigmoid))), d_hidden * activated], -1
-        ).astype(BF16)
-        down_grad = jnp.einsum("etf,td->efd", kept["weighted_hidden"], rows_d, preferred_element_type=F32)
-        in_grad = jnp.einsum("td,etf->edf", kept["rows_mid"], d_gate_up, preferred_element_type=F32)
-        down_grads[layer] = lax.psum_scatter(down_grad.astype(BF16), "ctx", scatter_dimension=1, tiled=True)
-        in_grads[layer] = lax.psum_scatter(in_grad.astype(BF16), "ctx", scatter_dimension=1, tiled=True)
-        partial = jnp.einsum("etf,edf->td", d_gate_up, in_full[layer], preferred_element_type=F32)
-        terms = kept["my_gates"] * jnp.transpose(d_weight)
+        gate_up = kept["gate_up"]
+        d_gate_up = []
+        down_grad = []
+        d_weight = []
+        for e in range(experts):
+            d_weighted = dot(rows_d, down_full[layer][:, e * width : (e + 1) * width], ((1,), (1,)))
+            gate_part = gate_up[:, 2 * e * FF : (2 * e + 1) * FF]
+            up_part = gate_up[:, (2 * e + 1) * FF : (2 * e + 2) * FF]
+            sigmoid = jax.nn.sigmoid(gate_part)
+            activated = gate_part * sigmoid
+            d_weight.append(jnp.sum((activated * up_part).astype(BF16).astype(F32) * d_weighted, -1, keepdims=True))
+            d_hidden = d_weighted * kept["my_gates"][:, e : e + 1]
+            d_gate_up.append(
+                (d_hidden * up_part * (sigmoid * (1.0 + gate_part * (1.0 - sigmoid)))).astype(BF16)
+            )
+            d_gate_up.append((d_hidden * activated).astype(BF16))
+            down_grad.append(dot(kept["weighted_hidden"][e], rows_d, ((0,), (0,))).astype(BF16))
+        d_gate_up = jnp.concatenate(d_gate_up, -1)
+        d_weight = jnp.concatenate(d_weight, -1)
+        down_grad = jnp.concatenate(down_grad, -1)
+        in_grad = dot(kept["rows_mid"], d_gate_up, ((0,), (0,))).astype(BF16)
+        partial = dot(d_gate_up, in_full[layer], ((1,), (1,)))
+        packed_grad = jax.vmap(packed)(
+            in_grad.reshape(n_ctx, in_rows, -1), down_grad.reshape(n_ctx, down_rows, -1)
+        )
+        if layer == 0:
+            partial, packed_grad, moe_grads[1], attn_grads[1] = lax.optimization_barrier(
+                (partial, packed_grad, moe_grads[1], attn_grads[1])
+            )
+        else:
+            partial, packed_grad = lax.optimization_barrier((partial, packed_grad))
+        last = lax.psum_scatter(after(packed_grad, last), "ctx", scatter_dimension=0, tiled=False)
+        moe_grads[layer] = last
+        terms = kept["my_gates"] * d_weight
         placed_terms = lax.dynamic_update_slice_in_dim(jnp.zeros_like(kept["gates"]), terms, my_first, 1)
         d_logits = placed_terms - kept["gates"] * jnp.sum(terms, 1, keepdims=True)
         partial = partial + lax.dot_general(
@@ -502,10 +613,16 @@
         raw = jnp.concatenate([rows_first(jnp.stack(d_queries)), d_own[:, :HEAD_SIZE]], -1)
         raw = jnp.concatenate([turn(raw, cosine, -sine, heads + 1), d_own[:, HEAD_SIZE:]], -1).astype(BF16)
         heads_grad = dot(kept["rows_in"], raw, ((0,), (0,)))
-        attn_grads[layer] = lax.psum_scatter(
-            jnp.concatenate([heads_grad, out_grad], -1).astype(BF16), "ctx", scatter_dimension=0, tiled=True
+        last = lax.psum_scatter(
+            after(jnp.concatenate([heads_grad, out_grad], -1).astype(BF16), last),
+            "ctx",
+            scatter_dimension=0,
+            tiled=True,
         )
+        attn_grads[layer] = last
         partial = dot(raw, weights[:, : q_cols + 2 * HEAD_SIZE], ((1,), (1,)))
+        if layer == 0:
+            partial, moe_grads[0] = lax.optimization_barrier((partial, moe_grads[0]))
         if layer == 1:
             upstream, gain_grad_in, d_mixed = exchange(
                 12, blocked(partial), d_middle, kept["stream"], gain_pack[1, 0:1], spread="plain", rounded=True
@@ -517,17 +634,12 @@
         grads_in[layer] = upstream.astype(BF16)
         small[layer] = jnp.concatenate([gain_grad_in, gain_grad_mid, router_grad], 0)
 
-    small_sum = lax.psum_scatter(
-        jnp.transpose(
-            jnp.concatenate(small, 0).reshape(-1, n_ctx * n_wt, width // (n_ctx * n_wt)), (1, 0, 2)
-        ),
-        ("ctx", "wt"),
-        scatter_dimension=0,
-        tiled=False,
+    piece = width // (n_ctx * n_wt)
+    small_parts = jnp.transpose(
+        jnp.stack(small).reshape(2, small[0].shape[0], n_ctx * n_wt, piece), (2, 0, 1, 3)
     )
-    small_first, small_second = jnp.split(small_sum, 2, 0)
-    mine, other = to_owner(small_first, small_second)
-    small_total = mine + other
+    small_parts = jnp.pad(small_parts, ((0, 0), (0, 0), (0, -small[0].shape[0] % 8), (0, -piece % 128)))
+    small_total = small_sum(14, small_parts)[: small[0].shape[0], :piece]
     out_pair = jnp.stack(to_owner(outputs[0], outputs[1]))
     grad_pair = jnp.stack(to_owner(grads_in[0], grads_in[1]))
     attn_first, attn_second = [member.astype(F32) for member in to_owner(attn_grads[0], attn_grads[1])]
@@ -536,8 +648,16 @@
     grad_query = jnp.concatenate([attn_first[:, :kv_at], attn_second[:, :kv_at]], -1)
     grad_kv = jnp.stack([attn_first[:, kv_at:out_at], attn_second[:, kv_at:out_at]], 1)
     grad_out = jnp.concatenate([jnp.transpose(attn_first[:, out_at:]), jnp.transpose(attn_second[:, out_at:])], 0)
-    grad_in = jnp.concatenate(to_owner(in_grads[0], in_grads[1]), 0).astype(F32)
-    grad_down = jnp.concatenate(to_owner(down_grads[0], down_grads[1]), 0).astype(F32)
+
+    def stacked(halves):
+        columns = halves[0].shape[1] // experts
+        return jnp.stack(
+            [half[:, e * columns : (e + 1) * columns] for half in halves for e in range(experts)]
+        ).astype(F32)
+
+    moe_pair = [unpacked(member[None], in_rows, down_rows) for member in to_owner(moe_grads[0], moe_grads[1])]
+    grad_in = stacked([member[0] for member in moe_pair])
+    grad_down = stacked([member[1] for member in moe_pair])
     return (
         out_pair[None],
         grad_pair[None],

time: 1130 us -> 788 us (0.70)
  waiting for transfers between devices: 299 us -> 11 us
  local copies, waits for them, and re-layouts: 197 us -> 113 us
  other arithmetic: 60.4 us -> 93.4 us
  Pallas kernels: 396 us -> 415 us
  matrix products: 140 us -> 123 us
    unnamed x18 -> x12, waiting for transfers between devices: 203 us -> 10.9 us
    reduce_scatter x2 -> x0, waiting for transfers between devices: 88.9 us -> none  [shards(): lax.psum_scatter(down_grad.astype(BF16), 'ctx', scatter_dimension=1, tile...]
    unnamed x320 -> x337, local copies, waits for them, and re-layouts: 135 us -> 52 us
    dot_general x12 -> x0, matrix products: 67.1 us -> none  [the longest x2 14.2 us: shards(): jnp.einsum('td,efd->etf', rows_d, down_full[layer], preferred_element_typ...]
    dot_general x14 -> x32, matrix products: 25.2 us -> 71.4 us  [dot(): lax.dot_general(left, right, (contract, ((), ())), preferred_element_type...]
    concatenate x2 -> x10, other arithmetic: 3.26 us -> 29.4 us  [the longest x4 26.2 us: packed(): jnp.concatenate([in_part, down_part[:, :wide], jnp.concatenate([rest[:hal...]
    pallas_call x0 -> x1, Pallas kernels: none -> 17.3 us  [small_sum(): pl.pallas_call(functools.partial(small_sum_kernel, n_ctx, n_wt), out_shap...]
    slice x0 -> x20, local copies, waits for them, and re-layouts: none -> 17.1 us  [the longest x2 6.73 us: unpacked(): values[:, :in_rows].reshape(n * in_rows, wide)]
  transfers between devices with their start and end apart: 22 -> 15, of which waited for: 12 -> 1; matrix products, arithmetic and copies ran while one was open for 20% -> 33% of each run, Pallas kernels for 20% -> 53%
where the time goes in v2:
time: 788 us; the launch traced here: 780 us
  Pallas kernels  415 us (53%)
  matrix products  123 us (16%)
  local copies, waits for them, and re-layouts  113 us (14%)
  other arithmetic  93.4 us (12%)
  between operations  17.4 us (2%)
  waiting for transfers between devices  11 us (1%)
    pallas_call x10, Pallas kernels, exchange(): pl.pallas_call(functools.partial(exchange_kernel, n_wt, reduce, back, spr...  337 us
    dot_general x32, matrix products, dot(): lax.dot_general(left, right, (contract, ((), ())), preferred_element_type...  71.4 us
    unnamed x337, local copies, waits for them, and re-layouts  52 us
    pallas_call x2, Pallas kernels, ctx_gather(): pl.pallas_call(functools.partial(ctx_gather_kernel, n_ctx), out_shape=jax...  35.2 us
    concatenate x4, other arithmetic, packed(): jnp.concatenate([in_part, down_part[:, :wide], jnp.concatenate([rest[:hal...  26.2 us
    pallas_call x2, Pallas kernels, ctx_sum(): pl.pallas_call(functools.partial(ctx_sum_kernel, n_ctx), out_shape=jax.Sh...  25 us
    pallas_call x1, Pallas kernels, small_sum(): pl.pallas_call(functools.partial(small_sum_kernel, n_ctx, n_wt), out_shap...  17.3 us
    dot_general x4, matrix products, attend_back(): jnp.einsum('hqd,kd->hqk', d_out, pairs[:, 64:], preferred_element_type=F32)  17.1 us
  transfers between devices with their start and end apart: 15, of which 1 were waited for; matrix products, arithmetic and copies ran while one was open for 33% of the time, Pallas kernels for 53%

profile of v2, /device:TPU:0, one launch (start us, length us, event | category | flops | bytes accessed | tf_op | source)
XLA Modules:
  0.0 780.3 jit_solution(2397171244240889343)
XLA Ops:
  17.8 2.8 broadcast_select_fusion.4
  20.7 3.3 broadcast_select_fusion.2
  27.9 20.6 %shard_map.178 = bf16[8,64,1536]{2,1,0:T(8,128)(2,1)S(1)} custom-call(f32[64,1536]{1,0:T(8,128)S(1)} %bitcast_convert_fusion.1.refs_0_.refs_1_.refs_2_, f32[1,1536]{1,0:T(1,128)S(1)} %get-tuple-element.263.refs_1_.refs_3_), custom_call_target="tpu_custom_call" | custom-call | bytes 125829120 | tf_op jit(solution)/shard_map/pallas_call | solution.py:162
  52.1 3.2 maximum_maximum_fusion.4
  59.2 2.3 fusion.201
  62.2 17.4 %shard_map.179 = bf16[4,512,128]{2,1,0:T(8,128)(2,1)} custom-call(bf16[512,128]{1,0:T(8,128)(2,1)} %pad_maximum_fusion.13.own_ref), custom_call_target="tpu_custom_call" | custom-call | tf_op jit(solution)/shard_map/pallas_call | solution.py:193
  94.8 40.4 %shard_map.180 = (f32[64,1536]{1,0:T(8,128)S(1)}, bf16[8,64,1536]{2,1,0:T(8,128)(2,1)S(1)}) custom-call(bf16[8,64,1536]{2,1,0:T(8,128)(2,1)S(1)} %convolution_convert_fusion.8.refs_0_, f32[64,1536]{1,0:T(8,128)S(1)} %bitcast_convert_fusion.1.refs_0_.refs_1_.refs_2_, f32[1,1536]{1,0:T(1,128)S(1)} %get-tuple-element.262.refs_2_.refs_3_), custom_call_target="tpu_custom_call" | custom-call | bytes 125829120 | tf_op jit(solution)/shard_map/pallas_call | solution.py:162
  136.4 24.1 %shard_map.185 = bf16[8,64,1536]{2,1,0:T(8,128)(2,1)S(1)} custom-call(f32[64,1536]{1,0:T(8,128)S(1)} %bitcast_convert_fusion.refs_0_.refs_1_, f32[1,1536]{1,0:T(1,128)S(1)} %get-tuple-element.263.refs_1_.refs_3_), custom_call_target="tpu_custom_call" | custom-call | bytes 125829120 | tf_op jit(solution)/shard_map/pallas_call | solution.py:162
  164.3 2.1 all_gather.25
  169.5 3.4 slice.718
  172.9 2.1 fusion.272
  175.5 3.4 fusion.286
  182.2 40.4 %shard_map.181 = (f32[64,1536]{1,0:T(8,128)S(1)}, bf16[8,64,1536]{2,1,0:T(8,128)(2,1)S(1)}) custom-call(bf16[8,64,1536]{2,1,0:T(8,128)(2,1)S(1)} %bitcast.476, f32[64,1536]{1,0:T(8,128)S(1)} %get-tuple-element.41.refs_1_.refs_2_, f32[1,1536]{1,0:T(1,128)S(1)} %get-tuple-element.261.refs_2_.refs_3_), custom_call_target="tpu_custom_call" | custom-call | bytes 125829120 | tf_op jit(solution)/shard_map/pallas_call | solution.py:162
  223.7 2.4 fusion.75
  238.2 3.3 fusion.217
  243.2 17.8 %shard_map.182 = bf16[4,512,128]{2,1,0:T(8,128)(2,1)} custom-call(bf16[512,128]{1,0:T(8,128)(2,1)} %pad_maximum_fusion.14.own_ref), custom_call_target="tpu_custom_call" | custom-call | tf_op jit(solution)/shard_map/pallas_call | solution.py:193
  262.0 2.3 copy.296
  267.6 2.3 reshape.596
  280.9 42.1 %shard_map.183 = (f32[64,1536]{1,0:T(8,128)S(1)}, bf16[8,64,1536]{2,1,0:T(8,128)(2,1)S(1)}) custom-call(bf16[8,64,1536]{2,1,0:T(8,128)(2,1)S(1)} %convolution_convert_fusion.7.refs_0_, f32[64,1536]{1,0:T(8,128)S(1)} %get-tuple-element.42.refs_1_.refs_2_, f32[1,1536]{1,0:T(1,128)S(1)} %get-tuple-element.260.refs_2_.refs_3_), custom_call_target="tpu_custom_call" | custom-call | bytes 125829120 | tf_op jit(solution)/shard_map/pallas_call | solution.py:162
  329.4 3.4 slice.750
  332.8 3.6 fusion.287
  339.3 2.8 multiply_reduce_fusion.3
  344.8 5.1 fusion.157
  349.9 4.0 convolution_convert_fusion.1
  354.0 10.8 %maximum_maximum_fusion = bf16[4,576,2048]{2,1,0:T(8,128)(2,1)} fusion(bf16[4,64,1024]{2,1,0:T(8,128)(2,1)S(1)} %get-tuple-element.159, bf16[4,64,1024]{2,1,0:T(8,128)(2,1)S(1)} %get-tuple-element.158, bf16[4,128,2048]{2,1,0:T(8,128)(2,1)S(1)} %slice.762, bf16[4,384,2048]{2,1,0:T(8,128)(2,1)S(1)} %bitcast.528), kind=kLoop, calls=%fused_computation | loop fusion | flops 37748736 | bytes 18874368 | tf_op jit(solution)/shard_map/vmap()/concatenate | solution.py:402
  370.1 3.4 fusion.14
  373.6 42.0 %shard_map.186 = (f32[64,1536]{1,0:T(8,128)S(1)}, f32[1,1536]{1,0:T(1,128)S(1)}, bf16[8,64,1536]{2,1,0:T(8,128)(2,1)S(1)}) custom-call(bf16[8,64,1536]{2,1,0:T(8,128)(2,1)S(1)} %bitcast.475, f32[64,1536]{1,0:T(8,128)S(1)} %copy-done.6, f32[64,1536]{1,0:T(8,128)S(1)} %copy-done.17, f32[1,1536]{1,0:T(1,128)S(1)} %get-tuple-element.260.refs_2_.refs_3_), custom_call_target="tpu_custom_call" | custom-call | bytes 125829120 | tf_op jit(solution)/shard_map/pallas_call | solution.py:162
  418.1 2.4 convolution_convert_fusion.14
  424.3 3.6 multiply_convert_fusion.3
  429.7 5.2 multiply_convert_fusion.1
  438.1 2.2 convert_element_type.348
  440.4 2.2 copy.311
  443.6 15.5 %shard_map.187 = f32[512,128]{1,0:T(8,128)S(1)} custom-call(bf16[4,512,128]{2,1,0:T(8,128)(2,1)S(1)} %bitcast.478), custom_call_target="tpu_custom_call" | custom-call | tf_op jit(solution)/shard_map/pallas_call | solution.py:228
  459.2 2.1 fusion.62
  461.3 3.1 fusion.63
  476.4 3.5 fusion.173
  479.8 2.2 concatenate.174
  482.1 2.4 convolution_convert_fusion.6
  484.5 42.7 %shard_map.188 = (f32[64,1536]{1,0:T(8,128)S(1)}, f32[1,1536]{1,0:T(1,128)S(1)}, bf16[8,64,1536]{2,1,0:T(8,128)(2,1)S(1)}) custom-call(bf16[8,64,1536]{2,1,0:T(8,128)(2,1)S(1)} %bitcast.491, f32[64,1536]{1,0:T(8,128)S(1)} %copy-done.22, f32[64,1536]{1,0:T(8,128)S(1)} %get-tuple-element.42.refs_1_.refs_2_, f32[1,1536]{1,0:T(1,128)S(1)} %get-tuple-element.261.refs_2_.refs_3_), custom_call_target="tpu_custom_call" | custom-call | bytes 125829120 | tf_op jit(solution)/shard_map/pallas_call | solution.py:162
  529.8 2.1 convolution_convert_fusion.2
  531.9 2.2 convolution_convert_fusion.3
  535.2 5.6 multiply_reduce_fusion.1
  540.8 2.6 copy.339
  543.4 2.2 pad_maximum_fusion.1
  547.1 7.9 %fusion.156 = f32[512,1536]{1,0:T(8,128)} fusion(bf16[1536,2048]{1,0:T(8,128)(2,1)} %bitcast.521, bf16[512,512]{1,0:T(8,128)(2,1)S(1)} %copy-done.139, bf16[512,512]{1,0:T(8,128)(2,1)S(1)} %copy-done.140, bf16[512,512]{1,0:T(8,128)(2,1)S(1)} %copy-done.141, bf16[512,512]{1,0:T(8,128)(2,1)S(1)} %copy-done.142), kind=kOutput, calls=%fused_computation.288 | convolution fusion | flops 3229614080 | bytes 11534336 | tf_op jit(solution)/shard_map/dot_general | solution.py:22
  555.0 4.0 convolution_convert_fusion
  559.1 10.6 %maximum_maximum_fusion.1 = bf16[4,576,2048]{2,1,0:T(8,128)(2,1)} fusion(bf16[4,64,1024]{2,1,0:T(8,128)(2,1)S(1)} %get-tuple-element.157, bf16[4,64,1024]{2,1,0:T(8,128)(2,1)S(1)} %get-tuple-element.156, bf16[4,128,2048]{2,1,0:T(8,128)(2,1)S(1)} %slice.774, bf16[4,384,2048]{2,1,0:T(8,128)(2,1)S(1)} %bitcast.529), kind=kLoop, calls=%fused_computation.1 | loop fusion | flops 37748736 | bytes 18874368 | tf_op jit(solution)/shard_map/vmap()/concatenate | solution.py:402
  569.7 10.8 %reduce-scatter.13.cloned.1.call-done = bf16[384,512]{1,0:T(8,128)(2,1)} async-done(((bf16[1536,512]{1,0:T(8,128)(2,1)}), bf16[384,512]{1,0:T(8,128)(2,1)}) %reduce-scatter.13.cloned.1.call-update) | async-done | bytes 393232
  586.4 2.7 fusion.45
  590.2 19.2 %shard_map.184 = f32[64,1536]{1,0:T(8,128)S(1)} custom-call(bf16[8,64,1536]{2,1,0:T(8,128)(2,1)S(1)} %bitcast.477, f32[64,1536]{1,0:T(8,128)S(1)} %copy-done.18), custom_call_target="tpu_custom_call" | custom-call | bytes 125829120 | tf_op jit(solution)/shard_map/pallas_call | solution.py:162
  613.0 2.1 fusion.235
  619.7 40.1 %shard_map.189 = (f32[64,1536]{1,0:T(8,128)S(1)}, f32[1,1536]{1,0:T(1,128)S(1)}, bf16[8,64,1536]{2,1,0:T(8,128)(2,1)S(1)}) custom-call(bf16[8,64,1536]{2,1,0:T(8,128)(2,1)S(1)} %bitcast.474, f32[64,1536]{1,0:T(8,128)S(1)} %copy-done.4, f32[64,1536]{1,0:T(8,128)S(1)} %copy-done.20, f32[1,1536]{1,0:T(1,128)S(1)} %copy-done.26), custom_call_target="tpu_custom_call" | custom-call | bytes 125829120 | tf_op jit(solution)/shard_map/pallas_call | solution.py:162
  662.9 3.4 multiply_convert_fusion.2
  667.7 4.9 multiply_convert_fusion
  677.6 9.5 %shard_map.190 = f32[512,128]{1,0:T(8,128)S(1)} custom-call(bf16[4,512,128]{2,1,0:T(8,128)(2,1)S(1)} %bitcast.479), custom_call_target="tpu_custom_call" | custom-call | tf_op jit(solution)/shard_map/pallas_call | solution.py:228
  687.7 3.0 fusion.65
  694.8 3.3 fusion.189
  699.6 2.0 convolution_convert_fusion.11
  704.6 2.9 copy.341
  707.5 3.4 broadcast_select_fusion
  710.9 25.4 %shard_map.191 = (f32[64,1536]{1,0:T(8,128)S(1)}, f32[1,1536]{1,0:T(1,128)S(1)}) custom-call(bf16[8,64,1536]{2,1,0:T(8,128)(2,1)S(1)} %bitcast.490, f32[64,1536]{1,0:T(8,128)S(1)} %get-tuple-element.59.refs_1_, f32[64,1536]{1,0:T(8,128)S(1)} %copy-done.1, f32[1,1536]{1,0:T(1,128)S(1)} %copy-done.24), custom_call_target="tpu_custom_call" | custom-call | bytes 125829120 | tf_op jit(solution)/shard_map/pallas_call | solution.py:162
  736.6 17.3 %shard_map.192 = f32[24,128]{1,0:T(8,128)S(1)} custom-call(f32[16,2,24,128]{3,2,1,0:T(8,128)S(1)} %pad.13.parts_ref), custom_call_target="tpu_custom_call" | custom-call | tf_op jit(solution)/shard_map/pallas_call | solution.py:275
  756.5 2.3 select_bitcast_fusion.1
  763.8 4.1 maximum_convert_fusion
  (563 shorter events, 171.2 us)
Async XLA Ops:
  7.2 48.2 %all-gather.5.cloned.1.call-start = ((), (), s32[]{:S(2)}) async-start(), calls=%async_computation.4 | async-start | bytes 1966080 | tf_op jit(solution)/shard_map/all_gather | solution.py:428
  11.5 4.2 collective-permute-start
  13.1 4.7 collective-permute-start.2
  15.1 5.6 collective-permute-start.1
  17.7 150.0 %all-gather.7.cloned.1.call-start = ((), (), s32[]{:S(2)}) async-start(), calls=%async_computation.5 | async-start | bytes 11796480 | tf_op jit(solution)/shard_map/all_gather | solution.py:422
  25.6 198.2 %all-gather.9.cloned.1.call-start = ((), (), s32[]{:S(2)}) async-start(), calls=%async_computation.6 | async-start | bytes 1966080 | tf_op jit(solution)/shard_map/all_gather | solution.py:428
  25.9 212.2 %copy-start.107 = (f32[1,2,2,128]{3,1,2,0:T(2,128)}, f32[1,2,2,128]{3,1,2,0:T(2,128)S(1)}, u32[]{:S(2)}) copy-start(f32[1,2,2,128]{3,1,2,0:T(2,128)S(1)} %copy.382) | copy-start | bytes 6148
  27.8 67.0 %copy-start = (f32[64,1536]{1,0:T(8,128)}, f32[64,1536]{1,0:T(8,128)S(1)}, u32[]{:S(2)}) copy-start(f32[64,1536]{1,0:T(8,128)S(1)} %bitcast_convert_fusion.1.refs_0_.refs_1_.refs_2_) | copy-start | bytes 1179652
  27.9 66.9 %copy-start.25 = (f32[1,1536]{1,0:T(1,128)}, f32[1,1536]{1,0:T(1,128)S(1)}, u32[]{:S(2)}) copy-start(f32[1,1536]{1,0:T(1,128)S(1)} %get-tuple-element.262.refs_2_.refs_3_) | copy-start | bytes 18436
  27.9 108.5 %copy-start.23 = (f32[1,1536]{1,0:T(1,128)}, f32[1,1536]{1,0:T(1,128)S(1)}, u32[]{:S(2)}) copy-start(f32[1,1536]{1,0:T(1,128)S(1)} %get-tuple-element.263.refs_1_.refs_3_) | copy-start | bytes 18436
  48.5 6.9 copy-start.9
  48.5 189.7 %copy-start.125 = (f32[32]{0:T(128)}, f32[32]{0:T(128)S(1)}, u32[]{:S(2)}) copy-start(f32[32]{0:T(128)S(1)} %multiply_power_fusion) | copy-start | bytes 388
  49.2 225.6 %copy-start.59 = (pred[256,1024]{1,0:T(8,128)(4,1)}, pred[256,1024]{1,0:T(8,128)(4,1)S(1)}, u32[]{:S(2)}) copy-start(pred[256,1024]{1,0:T(8,128)(4,1)S(1)} %compare_and_fusion.1) | copy-start | bytes 786436
  49.8 226.2 %copy-start.45 = (pred[256,2048]{1,0:T(8,128)(4,1)}, pred[256,2048]{1,0:T(8,128)(4,1)S(1)}, u32[]{:S(2)}) copy-start(pred[256,2048]{1,0:T(8,128)(4,1)S(1)} %compare_and_fusion) | copy-start | bytes 1572868
  49.9 276.6 %all-gather.11.cloned.1.call-start = ((), (), s32[]{:S(2)}) async-start(), calls=%async_computation.7 | async-start | bytes 11796480 | tf_op jit(solution)/shard_map/all_gather | solution.py:422
  80.7 8.6 %copy-start.75 = (bf16[1,4,256,128]{3,2,0,1:T(8,128)(2,1)}, bf16[1,4,256,128]{3,2,0,1:T(8,128)(2,1)S(1)}, u32[]{:S(2)}) copy-start(bf16[1,4,256,128]{3,2,0,1:T(8,128)(2,1)S(1)} %slice.700) | copy-start | bytes 786436
  84.3 6.2 copy-start.71
  94.8 67.6 %copy-start.119 = (s32[1,2,256,8]{2,3,1,0:T(8,128)S(1)}, s32[1,2,256,8]{2,3,1,0:T(8,128)}, u32[]{:S(2)}) copy-start(s32[1,2,256,8]{2,3,1,0:T(8,128)} %param.14) | copy-start | bytes 49156
  94.8 69.4 %copy-start.110 = (bf16[1,1536,16]{1,2,0:T(8,128)(2,1)S(1)}, bf16[1,1536,16]{1,2,0:T(8,128)(2,1)}, u32[]{:S(2)}) copy-start(bf16[1,1536,16]{1,2,0:T(8,128)(2,1)} %param.19) | copy-start | bytes 147460
  135.3 46.9 %copy-start.19 = (f32[64,1536]{1,0:T(8,128)}, f32[64,1536]{1,0:T(8,128)S(1)}, u32[]{:S(2)}) copy-start(f32[64,1536]{1,0:T(8,128)S(1)} %get-tuple-element.41.refs_1_.refs_2_) | copy-start | bytes 1179652
  135.3 405.5 %reduce-scatter.17.cloned.1.call-start = ((), (), s32[]{:S(2)}) async-start(), calls=%async_computation.10 | async-start | bytes 11796480
  166.4 6.5 copy-start.82
  167.7 11.2 %copy-start.128 = (f32[512,1]{0,1:T(1,128)}, f32[512,1]{0,1:T(1,128)S(1)}, u32[]{:S(2)}) copy-start(f32[512,1]{0,1:T(1,128)S(1)} %get-tuple-element.256) | copy-start | bytes 6148
  167.7 11.2 %copy-start.130 = (f32[512,1]{0,1:T(1,128)}, f32[512,1]{0,1:T(1,128)S(1)}, u32[]{:S(2)}) copy-start(f32[512,1]{0,1:T(1,128)S(1)} %get-tuple-element.257) | copy-start | bytes 6148
  175.3 5.7 copy-start.33
  261.9 12.9 %copy-start.77 = (bf16[1,4,256,128]{3,2,0,1:T(8,128)(2,1)}, bf16[1,4,256,128]{3,2,0,1:T(8,128)(2,1)S(1)}, u32[]{:S(2)}) copy-start(bf16[1,4,256,128]{3,2,0,1:T(8,128)(2,1)S(1)} %slice.742) | copy-start | bytes 786436
  279.3 45.9 %copy-start.105 = (pred[512,16]{0,1:T(8,128)(4,1)S(1)}, pred[512,16]{0,1:T(8,128)(4,1)}, u32[]{:S(2)}) copy-start(pred[512,16]{0,1:T(8,128)(4,1)} %fusion.223) | copy-start | bytes 24580
  364.8 215.6 %reduce-scatter.13.cloned.1.call-start = ((), (), s32[]{:S(2)}) async-start(), calls=%async_computation.8 | async-start | bytes 1966080
  364.8 8.8 %copy-start.6 = (f32[64,1536]{1,0:T(8,128)S(1)}, f32[64,1536]{1,0:T(8,128)}, u32[]{:S(2)}) copy-start(f32[64,1536]{1,0:T(8,128)} %copy-done.5) | copy-start | bytes 1179652
  364.8 8.8 %copy-start.17 = (f32[64,1536]{1,0:T(8,128)S(1)}, f32[64,1536]{1,0:T(8,128)}, u32[]{:S(2)}) copy-start(f32[64,1536]{1,0:T(8,128)} %copy-done.16) | copy-start | bytes 1179652
  428.4 7.2 slice-start.2
  429.7 5.9 slice-start.3
  459.1 5.6 copy-start.7
  464.4 12.0 %copy-start.108 = (f32[1,2,2,128]{3,1,2,0:T(2,128)S(1)}, f32[1,2,2,128]{3,1,2,0:T(2,128)}, u32[]{:S(2)}) copy-start(f32[1,2,2,128]{3,1,2,0:T(2,128)} %copy-done.107) | copy-start | bytes 6148
  464.4 12.0 %copy-start.126 = (f32[32]{0:T(128)S(1)}, f32[32]{0:T(128)}, u32[]{:S(2)}) copy-start(f32[32]{0:T(128)} %copy-done.125) | copy-start | bytes 388
  482.0 45.2 %copy-start.14 = (bf16[8,64,1536]{2,1,0:T(8,128)(2,1)S(1)}, bf16[8,64,1536]{2,1,0:T(8,128)(2,1)}, u32[]{:S(2)}) copy-start(bf16[8,64,1536]{2,1,0:T(8,128)(2,1)} %copy-done.13) | copy-start | bytes 4718596
  482.0 45.2 %copy-start.84 = (bf16[24,8,2,256]{3,1,2,0:T(8,128)(2,1)S(1)}, bf16[24,8,2,256]{3,1,2,0:T(8,128)(2,1)}, u32[]{:S(2)}) copy-start(bf16[24,8,2,256]{3,1,2,0:T(8,128)(2,1)} %copy.385) | copy-start | bytes 589828
  482.1 45.7 %copy-start.30 = (bf16[8,64,1536]{2,1,0:T(8,128)(2,1)S(1)}, bf16[8,64,1536]{2,1,0:T(8,128)(2,1)}, u32[]{:S(2)}) copy-start(bf16[8,64,1536]{2,1,0:T(8,128)(2,1)} %copy-done.29) | copy-start | bytes 4718596
  482.1 45.7 %copy-start.96 = (bf16[512,320]{1,0:T(8,128)(2,1)S(1)}, bf16[512,320]{1,0:T(8,128)(2,1)}, u32[]{:S(2)}) copy-start(bf16[512,320]{1,0:T(8,128)(2,1)} %concatenate.174) | copy-start | bytes 983044
  543.4 161.2 %reduce-scatter.19.cloned.1.call-start = ((), (), s32[]{:S(2)}) async-start(), calls=%async_computation.11 | async-start | bytes 11796480
  582.4 179.8 %reduce-scatter.15.cloned.1.call-start = ((), (), s32[]{:S(2)}) async-start(), calls=%async_computation.9 | async-start | bytes 1966080
  590.1 20.2 %copy-start.101 = (f32[512,16]{0,1:T(8,128)S(1)}, f32[512,16]{0,1:T(8,128)}, u32[]{:S(2)}) copy-start(f32[512,16]{0,1:T(8,128)} %copy-done.100) | copy-start | bytes 98308
  590.1 20.2 %copy-start.103 = (f32[512,16]{0,1:T(8,128)S(1)}, f32[512,16]{0,1:T(8,128)}, u32[]{:S(2)}) copy-start(f32[512,16]{0,1:T(8,128)} %copy-done.102) | copy-start | bytes 98308
  590.1 20.2 %copy-start.112 = (f32[512]{0:T(512)S(1)}, f32[512]{0:T(512)}, u32[]{:S(2)}) copy-start(f32[512]{0:T(512)} %copy-done.111) | copy-start | bytes 6148
  590.1 20.9 %copy-start.28 = (f32[1,1536]{1,0:T(1,128)S(1)}, f32[1,1536]{1,0:T(1,128)}, u32[]{:S(2)}) copy-start(f32[1,1536]{1,0:T(1,128)} %copy-done.27) | copy-start | bytes 18436
  610.2 5.0 collective-permute-start.3
  611.0 7.1 copy-start.83
  611.0 7.1 copy-start.99
  611.2 6.9 copy-start.57
  619.6 43.1 %copy-start.86 = (f32[3,256,64]{1,2,0:T(8,128)S(1)}, f32[3,256,64]{1,2,0:T(8,128)}, u32[]{:S(2)}) copy-start(f32[3,256,64]{1,2,0:T(8,128)} %copy-done.85) | copy-start | bytes 589828
  619.6 43.1 %copy-start.88 = (f32[3,256,64]{1,2,0:T(8,128)S(1)}, f32[3,256,64]{1,2,0:T(8,128)}, u32[]{:S(2)}) copy-start(f32[3,256,64]{1,2,0:T(8,128)} %copy-done.87) | copy-start | bytes 589828
  619.7 43.2 %copy-start.61 = (pred[256,1024]{1,0:T(8,128)(4,1)S(1)}, pred[256,1024]{1,0:T(8,128)(4,1)}, u32[]{:S(2)}) copy-start(pred[256,1024]{1,0:T(8,128)(4,1)} %copy-done.59) | copy-start | bytes 786436
  619.7 43.2 %copy-start.76 = (bf16[1,4,256,128]{3,2,0,1:T(8,128)(2,1)S(1)}, bf16[1,4,256,128]{3,2,0,1:T(8,128)(2,1)}, u32[]{:S(2)}) copy-start(bf16[1,4,256,128]{3,2,0,1:T(8,128)(2,1)} %copy-done.75) | copy-start | bytes 786436
  619.7 43.2 %copy-start.133 = (f32[3,256]{1,0:T(4,128)S(1)}, f32[3,256]{1,0:T(4,128)}, u32[]{:S(2)}) copy-start(f32[3,256]{1,0:T(4,128)} %log_add_fusion.3) | copy-start | bytes 9220
  666.4 6.9 slice-start
  667.7 5.6 slice-start.1
  694.8 6.9 copy-start.10
  707.5 28.8 %copy-start.97 = (f32[16,1536]{1,0:T(8,128)S(1)}, f32[16,1536]{1,0:T(8,128)}, u32[]{:S(2)}) copy-start(f32[16,1536]{1,0:T(8,128)} %fusion.235) | copy-start | bytes 294916
  710.9 25.6 %copy-start.89 = (f32[1,18,16,96]{3,1,0,2:T(8,128)S(1)}, f32[1,18,16,96]{3,1,0,2:T(8,128)}, u32[]{:S(2)}) copy-start(f32[1,18,16,96]{3,1,0,2:T(8,128)} %copy.327) | copy-start | bytes 331780
  710.9 45.5 %collective-permute-start.6 = (bf16[576,2048]{1,0:T(8,128)(2,1)}, bf16[576,2048]{1,0:T(8,128)(2,1)}, u32[]{:S(2)}, u32[]{:S(2)}) collective-permute-start(bf16[576,2048]{1,0:T(8,128)(2,1)} %broadcast_select_fusion), channel_id=1, source_target_pairs={{0,16},{16,0},{1,17},{17,1},{2,18},{18,2},{3,19},{19,3},{4,20},{20... | collective-permute-start | bytes 7077896 | tf_op jit(solution)/shard_map/ppermute | solution.py:367
  736.5 20.0 %copy-start.37 = (bf16[1,576,2048]{2,1,0:T(8,128)(2,1)S(1)}, bf16[1,576,2048]{2,1,0:T(8,128)(2,1)}, u32[]{:S(2)}) copy-start(bf16[1,576,2048]{2,1,0:T(8,128)(2,1)} %reduce-scatter.17.cloned.1.call-done) | copy-start | bytes 7077892
  736.5 20.0 %copy-start.38 = (bf16[1,576,2048]{2,1,0:T(8,128)(2,1)S(1)}, bf16[1,576,2048]{2,1,0:T(8,128)(2,1)}, u32[]{:S(2)}) copy-start(bf16[1,576,2048]{2,1,0:T(8,128)(2,1)} %reduce-scatter.19.cloned.1.call-done) | copy-start | bytes 7077892
  754.0 1.6 collective-permute-start.4
  763.4 6.4 collective-permute-start.5
  (98 other events, 227.7 us)
Sparse Core Ops, SparseCore 0:
  17.8 33.2 all-gather.4
  53.5 101.9 all-gather.6
  157.9 30.8 all-gather.8
  190.5 101.9 all-gather.10
  364.9 106.5 reduce-scatter.16
  543.5 36.8 reduce-scatter.12
  583.5 95.0 reduce-scatter.18
  707.6 36.3 reduce-scatter.14

commit v3 on v2

--- a/solution.py
+++ b/solution.py
@@ -48,48 +48,121 @@
     )
 
 
-def exchange_kernel(n_wt, reduce, back, spread, rounded, *refs):
+def exchange_kernel(n_ctx, n_wt, reduce, back, spread, rounded, ride, *refs):
     refs = list(refs)
     section, ctx, wt = place()
     sibling = (1 - section, ctx, wt)
-    peers = [(section, ctx, lax.rem(wt + k, n_wt)) for k in range(1, n_wt)]
+    right = (section, ctx, jnp.minimum(wt + 1, n_wt - 1))
+    left = (section, ctx, jnp.maximum(wt - 1, 0))
+    has_right, has_left = wt < n_wt - 1, wt > 0
+    peers = [(section, lax.rem(ctx + k, n_ctx), wt) for k in range(1, n_ctx)]
     parts = refs.pop(0) if reduce else None
     rows_ref = refs.pop(0)
     stream_ref = refs.pop(0) if back else None
     gain_ref = refs.pop(0) if (back or spread) else None
+    ride_ref = refs.pop(0) if ride else None
     result_ref = refs.pop(0) if reduce else None
     gain_grad_ref = refs.pop(0) if back else None
     all_ref = refs.pop(0) if spread else None
+    rode_ref = refs.pop(0) if ride else None
     if reduce:
-        from_sibling, from_peers, staged, rs_send, rs_recv = refs[:5]
-        refs = refs[5:]
+        from_sibling, in_right, in_left, out_right, out_left, swap_send, swap_recv, rs_send, rs_recv = refs[:9]
+        refs = refs[9:]
     if spread:
-        ag_send, ag_recv = refs
-    greet([sibling] + peers)
-    own = section * n_wt + wt
+        ag_send, ag_recv, pass_send, pass_recv = refs[:4]
+        refs = refs[4:]
+    if ride:
+        landed, ride_send, ride_recv, ride_local = refs
+
+    barrier = pltpu.get_barrier_semaphore()
+
+    def hail(target):
+        pl.semaphore_signal(barrier, inc=1, device_id=target, device_id_type=MESH)
+
+    hail(sibling)
+    pl.when(has_right)(lambda: hail(right))
+    pl.when(has_left)(lambda: hail(left))
+    if ride:
+        for peer in peers:
+            hail(peer)
+    met = 1 + (n_ctx - 1 if ride else 0)
+    pl.semaphore_wait(barrier, met + has_right.astype(jnp.int32) + has_left.astype(jnp.int32))
+
+    finish = []
+
+    def launch(condition, copy):
+        pl.when(condition)(copy.start)
+        finish.append((condition, copy))
+
     if reduce:
-        sends = []
-        order = [lax.rem(wt + k, n_wt) for k in range(1, n_wt)] + [wt]
-        swaps = []
-        for k, block in enumerate(order):
-            copy = remote(
-                parts.at[(1 - section) * n_wt + block], from_sibling.at[block], rs_send.at[k], rs_recv.at[k], sibling
+        order = []
+        for step in range(n_wt - 1):
+            order += [n_wt - 1 - step, step]
+        order = list(dict.fromkeys(order))
+        swaps = {}
+        for block in order:
+            swaps[block] = remote(
+                parts.at[(1 - section) * n_wt + block],
+                from_sibling.at[block],
+                swap_send.at[block],
+                swap_recv.at[block],
+                sibling,
             )
+            swaps[block].start()
+    if ride == "gather":
+        keep = pltpu.make_async_copy(ride_ref, rode_ref.at[ctx], ride_local)
+        keep.start()
+        riders = [
+            remote(ride_ref, rode_ref.at[ctx], ride_send.at[k], ride_recv.at[k], peers[k]) for k in range(n_ctx - 1)
+        ]
+    elif ride == "sum":
+        riders = [
+            remote(
+                ride_ref.at[lax.rem(ctx + 1 + k, n_ctx)], landed.at[k], ride_send.at[k], ride_recv.at[k], peers[k]
+            )
+            for k in range(n_ctx - 1)
+        ]
+    if ride:
+        for copy in riders:
             copy.start()
-            swaps.append(copy)
-        for k, block in enumerate(order[:-1]):
-            swaps[k].wait_recv()
-            staged[k] = (parts[section * n_wt + block].astype(F32) + from_sibling[block].astype(F32)).astype(BF16)
-            copy = remote(
-                staged.at[k], from_peers.at[k], rs_send.at[n_wt + k], rs_recv.at[n_wt + k], peers[k]
-            )
-            copy.start()
-            sends.append(copy)
-        swaps[-1].wait_recv()
-        total = parts[own].astype(F32) + from_sibling[wt].astype(F32)
-        for k in range(n_wt - 1):
-            sends[k].wait_recv()
-            total = total + from_peers[k].astype(F32)
+
+    if reduce:
+
+        def chip_sum(block):
+            return parts[section * n_wt + block].astype(F32) + from_sibling[block].astype(F32)
+
+        def send_on(block, inward, outward, first, target, number):
+            swaps[block].wait_recv()
+            outward[block] = chip_sum(block).astype(BF16)
+
+            @pl.when(first)
+            def _():
+                remote(outward.at[block], inward.at[block], rs_send.at[number], rs_recv.at[number], target).wait_recv()
+                outward[block] = (chip_sum(block) + inward[block].astype(F32)).astype(BF16)
+
+            remote(outward.at[block], inward.at[block], rs_send.at[number], rs_recv.at[number], target).start()
+
+        for step in range(n_wt - 1):
+            far, near = n_wt - 1 - step, step
+            pl.when(wt < far)(functools.partial(send_on, far, in_right, out_right, has_left, right, far))
+            pl.when(wt > near)(functools.partial(send_on, near, in_left, out_left, has_right, left, n_wt + near))
+        swap = remote(
+            parts.at[(1 - section) * n_wt + wt], from_sibling.at[wt], swap_send.at[wt], swap_recv.at[wt], sibling
+        )
+        swap.wait_recv()
+        result_ref[...] = chip_sum(wt)
+
+        @pl.when(has_left)
+        def _():
+            remote(out_right.at[wt], in_right.at[wt], rs_send.at[wt], rs_recv.at[wt], right).wait_recv()
+            result_ref[...] += in_right[wt].astype(F32)
+
+        @pl.when(has_right)
+        def _():
+            remote(out_left.at[wt], in_left.at[wt], rs_send.at[n_wt + wt], rs_recv.at[n_wt + wt], left).wait_recv()
+            result_ref[...] += in_left[wt].astype(F32)
+
+        total = result_ref[...]
         if back:
             stream = stream_ref[...]
             scale = norm_scale(stream)
@@ -107,60 +180,105 @@
     if spread:
         if spread == "norm":
             total = total * norm_scale(total) * gain_ref[...]
+        own = section * n_wt + wt
         all_ref[own] = total.astype(BF16)
-        copies = []
-        for k in range(1, n_wt):
-            copy = remote(all_ref.at[own], all_ref.at[own], ag_send.at[k], ag_recv.at[k], peers[k - 1])
-            copy.start()
-            copies.append(copy)
-        copy = remote(all_ref.at[own], all_ref.at[own], ag_send.at[0], ag_recv.at[0], sibling)
-        copy.start()
-        swaps_out = [copy]
-        for k in range(1, n_wt):
-            copies[k - 1].wait_recv()
-            block = section * n_wt + lax.rem(wt + n_wt - k, n_wt)
-            copy = remote(all_ref.at[block], all_ref.at[block], ag_send.at[n_wt + k], ag_recv.at[n_wt + k], sibling)
-            copy.start()
-            swaps_out.append(copy)
-        for copy in swaps_out:
+
+        def along(block, number, target):
+            return remote(all_ref.at[block], all_ref.at[block], ag_send.at[number], ag_recv.at[number], target)
+
+        def across(block, number):
+            return remote(all_ref.at[block], all_ref.at[block], pass_send.at[number], pass_recv.at[number], sibling)
+
+        always = wt >= 0
+        launch(has_right, along(own, 1, right))
+        launch(has_left, along(own, n_wt + 1, left))
+        launch(always, across(own, 0))
+        arrivals = [(always, across(own, 0))]
+        for hop in range(1, n_wt):
+            came_right = wt >= hop
+            block = jnp.maximum(own - hop, 0)
+            pl.when(came_right)(along(block, hop, right).wait_recv)
+            if hop + 1 < n_wt:
+                launch(came_right & has_right, along(block, hop + 1, right))
+            launch(came_right, across(block, hop))
+            arrivals.append((came_right, across(block, hop)))
+            came_left = wt + hop < n_wt
+            block = jnp.minimum(own + hop, 2 * n_wt - 1)
+            pl.when(came_left)(along(block, n_wt + hop, left).wait_recv)
+            if hop + 1 < n_wt:
+                launch(came_left & has_left, along(block, n_wt + hop + 1, left))
+            launch(came_left, across(block, n_wt + hop))
+            arrivals.append((came_left, across(block, n_wt + hop)))
+        for condition, copy in arrivals:
+            pl.when(condition)(copy.wait_recv)
+    if ride == "gather":
+        keep.wait()
+        for copy in riders:
             copy.wait()
-        for copy in copies:
-            copy.wait_send()
+    elif ride == "sum":
+        total = ride_ref[ctx].astype(F32)
+        for k, copy in enumerate(riders):
+            copy.wait()
+            total = total + landed[k].astype(F32)
+        rode_ref[...] = total
+    for condition, copy in finish:
+        pl.when(condition)(copy.wait_send)
     if reduce:
-        for copy in swaps + sends:
-            copy.wait_send()
+        for block in order:
+            swaps[block].wait_send()
+        for block in range(n_wt):
+            if block > 0:
+                pl.when(wt < block)(
+                    remote(out_right.at[block], in_right.at[block], rs_send.at[block], rs_recv.at[block], right).wait_send
+                )
+            if block < n_wt - 1:
+                pl.when(wt > block)(
+                    remote(
+                        out_left.at[block], in_left.at[block], rs_send.at[n_wt + block], rs_recv.at[n_wt + block], left
+                    ).wait_send
+                )
 
 
 VMEM = pl.BlockSpec(memory_space=pltpu.VMEM)
 
 
-def exchange(number, parts, rows, stream=None, gain=None, spread=None, rounded=False):
-    n_wt = lax.axis_size("wt")
+def exchange(number, parts, rows, stream=None, gain=None, spread=None, rounded=False, gather=None, add=None):
+    n_ctx, n_wt = lax.axis_size("ctx"), lax.axis_size("wt")
     shape = rows.shape
     reduce, back = parts is not None, stream is not None
+    ride = "gather" if gather is not None else "sum" if add is not None else None
+    rider = gather if gather is not None else add
     operands = [
         member
-        for member, wanted in ((parts, reduce), (rows, True), (stream, back), (gain, back or spread))
+        for member, wanted in (
+            (parts, reduce),
+            (rows, True),
+            (stream, back),
+            (gain, back or spread),
+            (rider, ride),
+        )
         if wanted
     ]
     outs = []
     scratch = []
+    dma = pltpu.SemaphoreType.DMA
     if reduce:
         outs.append(jax.ShapeDtypeStruct(shape, F32))
-        scratch += [
-            pltpu.VMEM((n_wt,) + shape, BF16),
-            pltpu.VMEM((n_wt - 1,) + shape, BF16),
-            pltpu.VMEM((n_wt - 1,) + shape, BF16),
-            pltpu.SemaphoreType.DMA((2 * n_wt,)),
-            pltpu.SemaphoreType.DMA((2 * n_wt,)),
-        ]
+        scratch += [pltpu.VMEM((n_wt,) + shape, BF16)] * 5
+        scratch += [dma((n_wt,)), dma((n_wt,)), dma((2 * n_wt,)), dma((2 * n_wt,))]
     if back:
         outs.append(jax.ShapeDtypeStruct((1, shape[1]), F32))
     if spread:
         outs.append(jax.ShapeDtypeStruct((2 * n_wt,) + shape, BF16))
-        scratch += [pltpu.SemaphoreType.DMA((2 * n_wt,)), pltpu.SemaphoreType.DMA((2 * n_wt,))]
+        scratch += [dma((2 * n_wt,))] * 4
+    if ride == "gather":
+        outs.append(jax.ShapeDtypeStruct((n_ctx,) + rider.shape, BF16))
+        scratch += [pltpu.VMEM((8, 128), BF16), dma((n_ctx - 1,)), dma((n_ctx - 1,)), dma]
+    elif ride == "sum":
+        outs.append(jax.ShapeDtypeStruct(rider.shape[1:], F32))
+        scratch += [pltpu.VMEM((n_ctx - 1,) + rider.shape[1:], BF16), dma((n_ctx - 1,)), dma((n_ctx - 1,)), dma]
     return pl.pallas_call(
-        functools.partial(exchange_kernel, n_wt, reduce, back, spread, rounded),
+        functools.partial(exchange_kernel, n_ctx, n_wt, reduce, back, spread, rounded, ride),
         out_shape=outs,
         in_specs=[VMEM] * len(operands),
         out_specs=[VMEM] * len(outs),
@@ -168,7 +286,7 @@
         compiler_params=pltpu.CompilerParams(
             collective_id=number, has_side_effects=True, vmem_limit_bytes=40 << 20
         ),
-        cost_estimate=pl.CostEstimate(flops=0, bytes_accessed=120 << 20, transcendentals=0),
+        cost_estimate=pl.CostEstimate(flops=0, bytes_accessed=110 << 20, transcendentals=0),
     )(*operands)
 
 
@@ -290,52 +408,266 @@
     )(parts)
 
 
-def turn(values, cosine, sine, heads):
-    pieces = []
-    for head in range(heads):
-        a = values[:, head * 64 : head * 64 + 32]
-        b = values[:, head * 64 + 32 : head * 64 + 64]
-        pieces += [a * cosine - b * sine, b * cosine + a * sine]
-    return jnp.concatenate(pieces, -1)
-
-
-def allowed_pairs(q_pos, q_seg, k_pos, k_seg):
-    return ((k_seg[None, :] == 0) | (k_seg[None, :] == q_seg[:, None])) & (k_pos[None, :] <= q_pos[:, None])
-
-
-def attend(query, pairs, q_pos, q_seg, k_pos, k_seg):
-    logits = jnp.einsum("hqd,kd->hqk", query, pairs[:, :64], preferred_element_type=F32) * (1.0 / HEAD_SIZE)
-    allowed = allowed_pairs(q_pos, q_seg, k_pos, k_seg)[None]
-    logits = jnp.where(allowed, logits, MASKED)
-    largest = jnp.max(logits, -1, keepdims=True)
-    expos = jnp.exp(logits - largest)
-    total = jnp.sum(expos, -1, keepdims=True)
-    probs = (expos / total).astype(BF16)
-    out = jnp.einsum("hqk,kd->hqd", probs, pairs[:, 64:], preferred_element_type=F32)
-    return out, largest + jnp.log(total)
-
-
-def attend_back(query, pairs, q_pos, q_seg, k_pos, k_seg, log_total, out, d_out):
-    logits = jnp.einsum("hqd,kd->hqk", query, pairs[:, :64], preferred_element_type=F32) * (1.0 / HEAD_SIZE)
-    allowed = allowed_pairs(q_pos, q_seg, k_pos, k_seg)[None]
-    probs = jnp.where(allowed, jnp.exp(logits - log_total), 0.0)
-    delta = jnp.sum(d_out.astype(F32) * out, -1, keepdims=True)
-    d_probs = jnp.einsum("hqd,kd->hqk", d_out, pairs[:, 64:], preferred_element_type=F32)
-    d_scores = (probs * (d_probs - delta)).astype(BF16)
-    d_query = jnp.einsum("hqk,kd->hqd", d_scores, pairs[:, :64], preferred_element_type=F32) * (1.0 / HEAD_SIZE)
-    d_keys = jnp.einsum("hqk,hqd->kd", d_scores, query, preferred_element_type=F32) * (1.0 / HEAD_SIZE)
-    d_values = jnp.einsum("hqk,hqd->kd", probs.astype(BF16), d_out, preferred_element_type=F32)
-    return d_query, jnp.concatenate([d_keys, d_values], -1)
-
-
-def heads_first(rows, micro_count):
-    count = rows.shape[0] // micro_count
-    return jnp.transpose(rows.reshape(micro_count, count, -1, HEAD_SIZE), (0, 2, 1, 3))
-
-
-def rows_first(heads):
-    micro_count, h, q, d = heads.shape
-    return jnp.transpose(heads, (0, 2, 1, 3)).reshape(micro_count * q, h * d)
+LANES = 2 * HEAD_SIZE
+HEADS = 3
+
+
+def roll(values, by):
+    return pltpu.roll(values, by, 1)
+
+
+def lower_half(shape):
+    return lax.broadcasted_iota(jnp.int32, shape, 1) < HEAD_SIZE
+
+
+def turned(values, cosine, sine):
+    first = lax.rem(lax.broadcasted_iota(jnp.int32, values.shape, 1), HEAD_SIZE) < HEAD_SIZE // 2
+    half = HEAD_SIZE // 2
+    return values * cosine + jnp.where(first, roll(values, LANES - half), roll(values, half)) * sine
+
+
+def visible(key_place, query_place, query_start):
+    return (key_place <= query_place) & (key_place >= query_start)
+
+
+def attend_kernel(
+    n_ctx,
+    x_ref,
+    w_ref,
+    cos_ref,
+    sin_ref,
+    key_place,
+    query_place,
+    query_start,
+    part_ref,
+    q_ref,
+    pairs_ref,
+    out_ref,
+    lse_ref,
+    att_ref,
+    top_ref,
+    sum_ref,
+    acc_ref,
+    send,
+    recv,
+):
+    section, ctx, wt = place()
+    peers = [(section, lax.rem(ctx + k, n_ctx), wt) for k in range(1, n_ctx)]
+    greet(peers)
+    rows = x_ref.shape[0] // 2
+    low = lower_half((2 * rows, LANES))
+    mixed = dot(x_ref[...], w_ref[:, : 3 * LANES], ((1,), (0,)))
+    cosine, sine = cos_ref[...], sin_ref[...]
+    first = turned(mixed[:, :LANES], cosine, sine)
+    second = turned(mixed[:, LANES : 2 * LANES], cosine, sine)
+    pairs_ref[ctx] = jnp.where(low, roll(second, HEAD_SIZE), roll(mixed[:, 2 * LANES :], HEAD_SIZE)).astype(BF16)
+
+    def passing(k):
+        return remote(
+            pairs_ref.at[ctx], pairs_ref.at[ctx], send.at[k], recv.at[k], (section, lax.rem(ctx + k, n_ctx), wt)
+        )
+
+    for k in range(1, n_ctx):
+        passing(k).start()
+    for h, part in enumerate((first, roll(first, HEAD_SIZE), second)):
+        scaled = jnp.where(low, part * (1.0 / HEAD_SIZE), 0.0).astype(BF16)
+        q_ref[0, h] = scaled[:rows]
+        q_ref[1, h] = scaled[rows:]
+    top_ref[...] = jnp.full(top_ref.shape, MASKED, F32)
+    sum_ref[...] = jnp.zeros(sum_ref.shape, F32)
+    acc_ref[...] = jnp.zeros(acc_ref.shape, F32)
+
+    def block(c, m, j):
+        keys = pairs_ref[c, j * rows : (j + 1) * rows, :]
+        if m == j:
+            seen = visible(key_place[c, j * rows : (j + 1) * rows, :], query_place[m], query_start[m])
+        for h in range(HEADS):
+            logits = dot(keys, q_ref[m, h], ((1,), (1,)))
+            if m == j:
+                logits = jnp.where(seen, logits, MASKED)
+            before = top_ref[m, h]
+            top = jnp.maximum(before, jnp.max(logits, 0, keepdims=True))
+            expos = jnp.exp(logits - top)
+            shrink = jnp.exp(before - top)
+            top_ref[m, h] = top
+            sum_ref[m, h] = sum_ref[m, h] * shrink + jnp.sum(expos, 0, keepdims=True)
+            acc_ref[m, h] = acc_ref[m, h] * shrink + dot(keys, expos.astype(BF16), ((0,), (0,)))
+
+    def blocks_of(c):
+        block(c, 0, 0)
+        block(c, 1, 1)
+        block(c, 1, 0)
+
+    blocks_of(ctx)
+
+    @pl.loop(1, n_ctx)
+    def _(k):
+        passing(k).wait_recv()
+        blocks_of(lax.rem(ctx + n_ctx - k, n_ctx))
+
+    low = lower_half((rows, LANES))
+    for m in range(2):
+        outs = []
+        for h in range(HEADS):
+            lse_ref[m, h] = top_ref[m, h] + jnp.log(sum_ref[m, h])
+            outs.append(jnp.transpose(acc_ref[m, h] / sum_ref[m, h]))
+            out_ref[m, h] = outs[h]
+        att_ref[m * rows : (m + 1) * rows, :LANES] = jnp.where(low, 0.0, outs[0]).astype(BF16)
+        att_ref[m * rows : (m + 1) * rows, LANES:] = jnp.where(low, roll(outs[1], HEAD_SIZE), outs[2]).astype(BF16)
+    part_ref[...] = dot(att_ref[...], w_ref[:, 2 * LANES :], ((1,), (1,))).astype(BF16)
+    for k in range(1, n_ctx):
+        passing(k).wait_send()
+
+
+def attend(number, rows_in, weights, tables):
+    n_ctx = lax.axis_size("ctx")
+    n_rows, width = rows_in.shape
+    rows = n_rows // 2
+    dma = pltpu.SemaphoreType.DMA
+    return pl.pallas_call(
+        functools.partial(attend_kernel, n_ctx),
+        out_shape=[
+            jax.ShapeDtypeStruct((n_rows, width), BF16),
+            jax.ShapeDtypeStruct((2, HEADS, rows, LANES), BF16),
+            jax.ShapeDtypeStruct((n_ctx, n_rows, LANES), BF16),
+            jax.ShapeDtypeStruct((2, HEADS, rows, LANES), F32),
+            jax.ShapeDtypeStruct((2, HEADS, 1, rows), F32),
+            jax.ShapeDtypeStruct((n_rows, 2 * LANES), BF16),
+        ],
+        in_specs=[VMEM] * 7,
+        out_specs=[VMEM] * 6,
+        scratch_shapes=[
+            pltpu.VMEM((2, HEADS, 1, rows), F32),
+            pltpu.VMEM((2, HEADS, 1, rows), F32),
+            pltpu.VMEM((2, HEADS, LANES, rows), F32),
+            dma((n_ctx,)),
+            dma((n_ctx,)),
+        ],
+        compiler_params=pltpu.CompilerParams(
+            collective_id=number, has_side_effects=True, vmem_limit_bytes=40 << 20
+        ),
+        cost_estimate=pl.CostEstimate(flops=0, bytes_accessed=70 << 20, transcendentals=0),
+    )(rows_in, weights, *tables)
+
+
+def attend_back_kernel(
+    n_ctx,
+    a_ref,
+    w_ref,
+    cos_ref,
+    sin_ref,
+    key_place,
+    query_place,
+    query_start,
+    q_ref,
+    pairs_ref,
+    out_ref,
+    lse_ref,
+    part_ref,
+    raw_ref,
+    do_ref,
+    delta_ref,
+    dq_ref,
+    dkv_ref,
+    own_ref,
+    landed,
+    send,
+    recv,
+):
+    section, ctx, wt = place()
+    peers = [(section, lax.rem(ctx + k, n_ctx), wt) for k in range(1, n_ctx)]
+    greet(peers)
+    rows = a_ref.shape[0] // 2
+    low = lower_half((2 * rows, LANES))
+    d_att = dot(a_ref[...], w_ref[:, 2 * LANES :], ((1,), (0,)))
+    for h, part in enumerate((d_att[:, :LANES], roll(d_att[:, LANES:], HEAD_SIZE), d_att[:, LANES:])):
+        d_out = jnp.where(low, 0.0, part).astype(BF16)
+        for m in range(2):
+            do_ref[m, h] = d_out[m * rows : (m + 1) * rows]
+            product = do_ref[m, h].astype(F32) * out_ref[m, h]
+            delta_ref[m, h] = jnp.sum(jnp.transpose(product), 0, keepdims=True)
+    dq_ref[...] = jnp.zeros(dq_ref.shape, F32)
+
+    def block(c, j):
+        keys = pairs_ref[c, j * rows : (j + 1) * rows, :]
+        total = jnp.zeros((rows, LANES), F32)
+        for m in range(j, 2):
+            if m == j:
+                seen = visible(key_place[c, j * rows : (j + 1) * rows, :], query_place[m], query_start[m])
+            for h in range(HEADS):
+                probs = jnp.exp(dot(keys, q_ref[m, h], ((1,), (1,))) - lse_ref[m, h])
+                if m == j:
+                    probs = jnp.where(seen, probs, 0.0)
+                d_probs = dot(keys, do_ref[m, h], ((1,), (1,)))
+                d_scores = (probs * (d_probs - delta_ref[m, h])).astype(BF16)
+                total = total + dot(d_scores, q_ref[m, h], ((1,), (0,)))
+                total = total + dot(probs.astype(BF16), do_ref[m, h], ((1,), (0,)))
+                dq_ref[m, h] += dot(keys, d_scores, ((0,), (0,)))
+        return total
+
+    def passing(k):
+        target = lax.rem(ctx + k, n_ctx)
+        return remote(dkv_ref.at[target], landed.at[k - 1], send.at[k], recv.at[k], (section, target, wt))
+
+    @pl.loop(1, n_ctx)
+    def _(k):
+        c = lax.rem(ctx + k, n_ctx)
+        for j in range(2):
+            dkv_ref[c, j * rows : (j + 1) * rows, :] = block(c, j).astype(BF16)
+        passing(k).start()
+
+    for j in range(2):
+        own_ref[j * rows : (j + 1) * rows, :] = block(ctx, j)
+
+    @pl.loop(1, n_ctx)
+    def _(k):
+        passing(k).wait_recv()
+        own_ref[...] += landed[k - 1].astype(F32)
+
+    cosine, sine = cos_ref[...], sin_ref[...]
+    d_own = own_ref[...]
+    over = roll(d_own, HEAD_SIZE)
+    d_query = [
+        jnp.concatenate([jnp.transpose(dq_ref[m, h]) for m in range(2)], 0) * (1.0 / HEAD_SIZE) for h in range(HEADS)
+    ]
+    first = jnp.where(low, d_query[0], roll(d_query[1], HEAD_SIZE))
+    second = jnp.where(low, d_query[2], over)
+    raw_ref[:, :LANES] = turned(first, cosine, -sine).astype(BF16)
+    raw_ref[:, LANES : 2 * LANES] = turned(second, cosine, -sine).astype(BF16)
+    raw_ref[:, 2 * LANES :] = jnp.where(low, over, 0.0).astype(BF16)
+    part_ref[...] = dot(raw_ref[...], w_ref[:, : 3 * LANES], ((1,), (1,))).astype(BF16)
+    for k in range(1, n_ctx):
+        passing(k).wait_send()
+
+
+def attend_back(number, rows_a, weights, tables, kept):
+    n_ctx = lax.axis_size("ctx")
+    n_rows, width = rows_a.shape
+    rows = n_rows // 2
+    dma = pltpu.SemaphoreType.DMA
+    return pl.pallas_call(
+        functools.partial(attend_back_kernel, n_ctx),
+        out_shape=[
+            jax.ShapeDtypeStruct((n_rows, width), BF16),
+            jax.ShapeDtypeStruct((n_rows, 3 * LANES), BF16),
+        ],
+        in_specs=[VMEM] * 11,
+        out_specs=[VMEM] * 2,
+        scratch_shapes=[
+            pltpu.VMEM((2, HEADS, rows, LANES), BF16),
+            pltpu.VMEM((2, HEADS, 1, rows), F32),
+            pltpu.VMEM((2, HEADS, LANES, rows), F32),
+            pltpu.VMEM((n_ctx, n_rows, LANES), BF16),
+            pltpu.VMEM((n_rows, LANES), F32),
+            pltpu.VMEM((n_ctx - 1, n_rows, LANES), BF16),
+            dma((n_ctx,)),
+            dma((n_ctx,)),
+        ],
+        compiler_params=pltpu.CompilerParams(
+            collective_id=number, has_side_effects=True, vmem_limit_bytes=40 << 20
+        ),
+        cost_estimate=pl.CostEstimate(flops=0, bytes_accessed=100 << 20, transcendentals=0),
+    )(rows_a, weights, *tables, *kept)
 
 
 def shards(tokens, cotangent, blocks, routes, norm_gain, w_query, key_value_weight, w_attn_out, router, w_in, w_down):
@@ -347,21 +679,26 @@
     experts = w_in.shape[1] // 2
     n_experts = router.shape[2]
     q_cols = w_query.shape[2] // 2
-    heads = q_cols // HEAD_SIZE
     depth = w_query.shape[1]
 
     block_len = seq_len // blocks.shape[1]
     placed = (blocks[:, :, None] * block_len + jnp.arange(block_len, dtype=jnp.int32)[None, None, :]).reshape(
         micro_count, seq_len
     )
+    query_place = lax.dynamic_slice_in_dim(placed, ctx * per_ctx, per_ctx, 1)
     later = (jnp.arange(micro_count) > 0)[:, None]
-    k_pos = jnp.where(later, seq_len + placed % CONT_LEN, placed)
-    k_seg = jnp.where(later, 1 + placed // CONT_LEN, 0)
-    q_pos = lax.dynamic_slice_in_dim(k_pos, ctx * per_ctx, per_ctx, 1)
-    q_seg = lax.dynamic_slice_in_dim(k_seg, ctx * per_ctx, per_ctx, 1)
+    query_start = jnp.where(later, query_place - query_place % CONT_LEN, 0)
+    query_pos = jnp.where(later, seq_len + query_place % CONT_LEN, query_place)
     inverse = jnp.power(ROPE_BASE, -jnp.arange(HEAD_SIZE // 2, dtype=F32) * 2.0 / HEAD_SIZE)
-    angles = q_pos.reshape(-1).astype(F32)[:, None] * inverse[None, :]
+    angles = query_pos.reshape(-1).astype(F32)[:, None] * inverse[None, :]
     cosine, sine = jnp.cos(angles), jnp.sin(angles)
+    tables = (
+        jnp.tile(cosine, (1, 4)),
+        jnp.concatenate([-sine, sine, -sine, sine], 1),
+        jnp.transpose(placed.reshape(micro_count, n_ctx, per_ctx), (1, 0, 2)).reshape(n_ctx, -1, 1),
+        query_place[:, None, :],
+        query_start[:, None, :],
+    )
 
     def swap(values):
         return lax.ppermute(values, "section", [(0, 1), (1, 0)])
@@ -418,15 +755,16 @@
     attn_full, in_full, down_full = [], [], []
     last = None
 
-    def gather_experts(pack):
-        full = lax.all_gather(pack, "ctx", axis=0, tiled=True)
+    def unpack_experts(full):
         one, two = unpacked(full.reshape(n_ctx, -1, full.shape[1]), in_rows, down_rows)
         in_full.append(one)
         down_full.append(two)
 
+    def gather_experts(pack):
+        return lax.all_gather(pack, "ctx", axis=0, tiled=True)
+
     moe_pack = [packed(in_pack[layer], down_pack[layer]) for layer in range(2)]
-    attn_full = [lax.all_gather(member, "ctx", axis=0, tiled=True) for member in attn_pack]
-    gather_experts(moe_pack[0])
+    attn_full = [None, None]
 
     my_first = wt * 2 * experts + section * experts
     n_rows = micro_count * per_ctx
@@ -444,43 +782,25 @@
     stream = lax.dynamic_index_in_dim(tokens, section, 0, False).astype(F32)
     top = lax.dynamic_index_in_dim(cotangent, section, 0, False).astype(F32)
 
-    (normed_in,) = exchange(0, None, stream, gain=gain_pack[0, 0:1], spread="norm")
+    normed_in, full = exchange(0, None, stream, gain=gain_pack[0, 0:1], spread="norm", gather=attn_pack[0])
+    attn_full[0] = full.reshape(-1, full.shape[2])
+    normed_in, first = lax.optimization_barrier((normed_in, moe_pack[0]))
+    moe_full = [gather_experts(first), None]
     (d_mixed,) = exchange(1, None, top, gain=gain_pack[0, 0:1], spread="plain")
     saved = []
     outputs = []
     for layer in range(2):
         rows_in = full_rows(normed_in)
         weights = attn_full[layer]
-        mixed_heads = dot(rows_in, weights[:, : q_cols + 2 * HEAD_SIZE], ((1,), (0,)))
-        turned = turn(mixed_heads[:, : q_cols + HEAD_SIZE], cosine, sine, heads + 1)
-        queries = turned[:, :q_cols].astype(BF16)
-        own_pairs = jnp.concatenate([turned[:, q_cols:], mixed_heads[:, q_cols + HEAD_SIZE :]], -1).astype(BF16)
-        pairs = ctx_gather(2 + layer, own_pairs)
-        pairs = jnp.transpose(
-            pairs.reshape(n_ctx, micro_count, per_ctx, 2 * HEAD_SIZE), (1, 0, 2, 3)
-        ).reshape(micro_count * seq_len, 2 * HEAD_SIZE)
-        by_head = heads_first(queries, micro_count)
-        outs = [
-            attend(
-                by_head[m],
-                pairs[: (m + 1) * seq_len],
-                q_pos[m],
-                q_seg[m],
-                k_pos.reshape(-1)[: (m + 1) * seq_len],
-                k_seg.reshape(-1)[: (m + 1) * seq_len],
-            )
-            for m in range(micro_count)
-        ]
-        out_full = jnp.stack([member[0] for member in outs])
-        log_total = [member[1] for member in outs]
-        attended = rows_first(out_full).astype(BF16)
-        partial = dot(attended, weights[:, q_cols + 2 * HEAD_SIZE :], ((1,), (1,)))
+        partial, queries, pairs, out_full, log_total, attended = attend(2 + layer, rows_in, weights, tables)
         middle, normed_mid = exchange(
             4 + layer, blocked(partial), stream, gain=gain_pack[layer, 1:2], spread="norm"
         )
         if layer == 0:
             normed_mid, second = lax.optimization_barrier((normed_mid, moe_pack[1]))
-            gather_experts(second)
+            moe_full[1] = gather_experts(second)
+        normed_mid, full = lax.optimization_barrier((normed_mid, moe_full[layer]))
+        unpack_experts(full)
         rows_mid = full_rows(normed_mid)
         logits = dot(rows_mid, router_pack[layer], ((1,), (0,)))
         hit = routed(layer)
@@ -504,11 +824,8 @@
                 middle=middle,
                 rows_in=rows_in,
                 rows_mid=rows_mid,
-                queries=by_head,
-                pairs=pairs,
-                out_full=out_full,
+                heads=(queries, pairs, out_full, log_total),
                 attended=attended,
-                log_total=log_total,
                 gates=gates,
                 my_gates=my_gates,
                 gate_up=gate_up,
@@ -516,9 +833,10 @@
             )
         )
         if layer == 0:
-            stream, normed_in = exchange(
-                6, blocked(partial), middle, gain=gain_pack[1, 0:1], spread="norm", rounded=True
+            stream, normed_in, full = exchange(
+                6, blocked(partial), middle, gain=gain_pack[1, 0:1], spread="norm", rounded=True, gather=attn_pack[1]
             )
+            attn_full[1] = full.reshape(-1, full.shape[2])
         else:
             (stream,) = exchange(7, blocked(partial), middle, rounded=True)
         outputs.append(stream.astype(BF16))
@@ -558,9 +876,7 @@
             in_grad.reshape(n_ctx, in_rows, -1), down_grad.reshape(n_ctx, down_rows, -1)
         )
         if layer == 0:
-            partial, packed_grad, moe_grads[1], attn_grads[1] = lax.optimization_barrier(
-                (partial, packed_grad, moe_grads[1], attn_grads[1])
-            )
+            partial, packed_grad, moe_grads[1] = lax.optimization_barrier((partial, packed_grad, moe_grads[1]))
         else:
             partial, packed_grad = lax.optimization_barrier((partial, packed_grad))
         last = lax.psum_scatter(after(packed_grad, last), "ctx", scatter_dimension=0, tiled=False)
@@ -587,49 +903,28 @@
         )
         rows_a = full_rows(d_attn)
         weights = attn_full[layer]
-        d_attended = dot(rows_a, weights[:, q_cols + 2 * HEAD_SIZE :], ((1,), (0,))).astype(BF16)
-        out_grad = dot(rows_a, kept["attended"], ((0,), (0,)))
-        d_heads = heads_first(d_attended, micro_count)
-        d_queries = []
-        d_pairs = 0.0
-        for m in range(micro_count):
-            d_query, d_pair = attend_back(
-                kept["queries"][m],
-                kept["pairs"][: (m + 1) * seq_len],
-                q_pos[m],
-                q_seg[m],
-                k_pos.reshape(-1)[: (m + 1) * seq_len],
-                k_seg.reshape(-1)[: (m + 1) * seq_len],
-                kept["log_total"][m],
-                kept["out_full"][m],
-                d_heads[m],
-            )
-            d_queries.append(d_query)
-            d_pairs = d_pairs + jnp.pad(d_pair, ((0, (micro_count - 1 - m) * seq_len), (0, 0)))
-        d_pairs = jnp.transpose(
-            d_pairs.reshape(micro_count, n_ctx, per_ctx, 2 * HEAD_SIZE), (1, 0, 2, 3)
-        ).reshape(n_ctx, n_rows, 2 * HEAD_SIZE)
-        d_own = ctx_sum(10 + layer, d_pairs.astype(BF16))
-        raw = jnp.concatenate([rows_first(jnp.stack(d_queries)), d_own[:, :HEAD_SIZE]], -1)
-        raw = jnp.concatenate([turn(raw, cosine, -sine, heads + 1), d_own[:, HEAD_SIZE:]], -1).astype(BF16)
-        heads_grad = dot(kept["rows_in"], raw, ((0,), (0,)))
-        last = lax.psum_scatter(
-            after(jnp.concatenate([heads_grad, out_grad], -1).astype(BF16), last),
-            "ctx",
-            scatter_dimension=0,
-            tiled=True,
-        )
-        attn_grads[layer] = last
-        partial = dot(raw, weights[:, : q_cols + 2 * HEAD_SIZE], ((1,), (1,)))
+        partial, raw = attend_back(10 + layer, rows_a, weights, tables, kept["heads"])
+        attn_parts = dot(kept["rows_in"], jnp.pad(raw, ((0, 0), (0, weights.shape[1] - raw.shape[1]))), ((0,), (0,)))
+        attn_parts = attn_parts + dot(
+            rows_a, jnp.pad(kept["attended"], ((0, 0), (weights.shape[1] - kept["attended"].shape[1], 0))), ((0,), (0,))
+        )
+        attn_parts = attn_parts.astype(BF16).reshape(n_ctx, depth, -1)
         if layer == 0:
             partial, moe_grads[0] = lax.optimization_barrier((partial, moe_grads[0]))
         if layer == 1:
-            upstream, gain_grad_in, d_mixed = exchange(
-                12, blocked(partial), d_middle, kept["stream"], gain_pack[1, 0:1], spread="plain", rounded=True
+            upstream, gain_grad_in, d_mixed, attn_grads[1] = exchange(
+                12,
+                blocked(partial),
+                d_middle,
+                kept["stream"],
+                gain_pack[1, 0:1],
+                spread="plain",
+                rounded=True,
+                add=attn_parts,
             )
         else:
-            upstream, gain_grad_in = exchange(
-                13, blocked(partial), d_middle, kept["stream"], gain_pack[0, 0:1], rounded=True
+            upstream, gain_grad_in, attn_grads[0] = exchange(
+                13, blocked(partial), d_middle, kept["stream"], gain_pack[0, 0:1], rounded=True, add=attn_parts
             )
         grads_in[layer] = upstream.astype(BF16)
         small[layer] = jnp.concatenate([gain_grad_in, gain_grad_mid, router_grad], 0)

time: 788 us -> 664 us (0.84)
  matrix products: 123 us -> 58.5 us
  local copies, waits for them, and re-layouts: 113 us -> 57 us
  Pallas kernels: 415 us -> 449 us
  other arithmetic: 93.4 us -> 62.7 us
  waiting for transfers between devices: 11 us -> 0.11 us
    dot_general x24 -> x0, matrix products: 43.5 us -> none  [the longest x4 17.1 us: attend_back(): jnp.einsum('hqd,kd->hqk', d_out, pairs[:, 64:], preferred_element_type=F32)]
    pallas_call x14, Pallas kernels: 397 us -> 435 us  [the longest x10 362 us: exchange(): pl.pallas_call(functools.partial(exchange_kernel, n_ctx, n_wt, reduce, ba...]
    unnamed x337 -> x263, local copies, waits for them, and re-layouts: 52 us -> 29.3 us
    dot_general x32 -> x24, matrix products: 71.4 us -> 49.6 us  [dot(): lax.dot_general(left, right, (contract, ((), ())), preferred_element_type...]
    another operation x4 -> x0, other arithmetic: 12.4 us -> none
    convert_element_type x14 -> x0, local copies, waits for them, and re-layouts: 11.7 us -> none  [the longest x4 7.09 us: shards(): d_own = ctx_sum(10 + layer, d_pairs.astype(BF16))]
    unnamed x12 -> x6, waiting for transfers between devices: 10.9 us -> 0.09 us
  transfers between devices with their start and end apart: 15 -> 11, of which waited for: 1 -> 0; matrix products, arithmetic and copies ran while one was open for 33% -> 15% of each run, Pallas kernels for 53% -> 62%
where the time goes in v3:
time: 664 us; the launch traced here: 654 us
  Pallas kernels  449 us (68%)
  other arithmetic  62.7 us (9%)
  matrix products  58.5 us (9%)
  local copies, waits for them, and re-layouts  57 us (9%)
  between operations  16.3 us (2%)
  blocking collectives  8.89 us (1%)
    pallas_call x10, Pallas kernels, exchange(): pl.pallas_call(functools.partial(exchange_kernel, n_ctx, n_wt, reduce, ba...  362 us
    dot_general x24, matrix products, dot(): lax.dot_general(left, right, (contract, ((), ())), preferred_element_type...  49.6 us
    pallas_call x2, Pallas kernels, attend(): pl.pallas_call(functools.partial(attend_kernel, n_ctx), out_shape=[jax.Sh...  40.5 us
    pallas_call x2, Pallas kernels, attend_back(): pl.pallas_call(functools.partial(attend_back_kernel, n_ctx), out_shape=[j...  32.8 us
    unnamed x263, local copies, waits for them, and re-layouts  29.3 us
    concatenate x4, other arithmetic, packed(): jnp.concatenate([in_part, down_part[:, :wide], jnp.concatenate([rest[:hal...  24.3 us
    pallas_call x1, Pallas kernels, small_sum(): pl.pallas_call(functools.partial(small_sum_kernel, n_ctx, n_wt), out_shap...  13.4 us
  transfers between devices with their start and end apart: 11, of which 0 were waited for; matrix products, arithmetic and copies ran while one was open for 15% of the time, Pallas kernels for 62%

profile of v3, /device:TPU:0, one launch (start us, length us, event | category | flops | bytes accessed | tf_op | source)
XLA Modules:
  0.0 654.4 jit_solution(3739144093607031531)
XLA Ops:
  7.2 1.1 copy.151
  8.3 1.3 copy.150
  13.0 1.2 copy-done.95
  14.6 1.3 fusion.7
  16.8 3.4 all_gather.15
  21.9 23.8 %shard_map.178 = (bf16[8,64,1536]{2,1,0:T(8,128)(2,1)S(1)}, bf16[4,384,512]{2,1,0:T(8,128)(2,1)S(1)}) custom-call(f32[64,1536]{1,0:T(8,128)S(1)} %bitcast_convert_fusion.1.refs_0_.refs_1_.refs_2_, f32[1,1536]{1,0:T(1,128)S(1)} %get-tuple-element.258.refs_1_.refs_3_, bf16[384,512]{1,0:T(8,128)(2,1)S(1)} %get-tuple-element.238.refs_2_), custom_call_target="tpu_custom_call" | custom-call | bytes 115343360 | tf_op jit(solution)/shard_map/pallas_call | solution.py:280
  45.8 2.6 broadcast_select_fusion.4
  49.3 3.3 broadcast_select_fusion.2
  52.7 1.6 maximum_maximum_fusion.4
  56.5 1.8 fusion.42
  59.0 1.6 pad_maximum_fusion.9.sin_ref
  60.6 1.2 slice.347
  63.1 20.1 %shard_map.179 = (bf16[512,1536]{1,0:T(8,128)(2,1)S(1)}, bf16[2,3,256,128]{3,2,1,0:T(8,128)(2,1)S(1)}, bf16[4,512,128]{2,1,0:T(8,128)(2,1)S(1)}, f32[2,3,256,128...) custom-call(bf16[512,1536]{1,0:T(8,128)(2,1)S(1)} %bitcast.222, ...), custom_call_target="tpu_custom_call" | custom-call | bytes 73400320 | tf_op jit(solution)/shard_map/pallas_call | solution.py:527
  86.4 41.9 %shard_map.180 = (f32[64,1536]{1,0:T(8,128)S(1)}, bf16[8,64,1536]{2,1,0:T(8,128)(2,1)S(1)}) custom-call(bf16[8,64,1536]{2,1,0:T(8,128)(2,1)S(1)} %bitcast.255, f32[64,1536]{1,0:T(8,128)S(1)} %bitcast_convert_fusion.1.refs_0_.refs_1_.refs_2_, f32[1,1536]{1,0:T(1,128)S(1)} %get-tuple-element.257.refs_2_.refs_3_), custom_call_target="tpu_custom_call" | custom-call | bytes 115343360 | tf_op jit(solution)/shard_map/pallas_call | solution.py:280
  128.4 1.1 copy-done
  130.3 1.6 maximum_maximum_fusion.5
  133.0 20.0 %shard_map.185 = bf16[8,64,1536]{2,1,0:T(8,128)(2,1)S(1)} custom-call(f32[64,1536]{1,0:T(8,128)S(1)} %bitcast_convert_fusion.refs_0_.refs_1_, f32[1,1536]{1,0:T(1,128)S(1)} %get-tuple-element.258.refs_1_.refs_3_), custom_call_target="tpu_custom_call" | custom-call | bytes 115343360 | tf_op jit(solution)/shard_map/pallas_call | solution.py:280
  153.8 1.2 copy-done.26
  154.9 2.1 all_gather.17
  157.0 3.5 all_gather.18
  161.7 1.7 slice.355
  163.5 4.7 slice.350
  168.8 1.1 copy-done.109
  169.9 2.1 fusion.65
  172.4 3.4 fusion.75
  176.4 1.4 copy-done.92
  179.9 46.3 %shard_map.181 = (f32[64,1536]{1,0:T(8,128)S(1)}, bf16[8,64,1536]{2,1,0:T(8,128)(2,1)S(1)}, bf16[4,384,512]{2,1,0:T(8,128)(2,1)S(1)}) custom-call(bf16[8,64,1536]{2,1,0:T(8,128)(2,1)S(1)} %bitcast.247, f32[64,1536]{1,0:T(8,128)S(1)} %copy-done.35, f32[1,1536]{1,0:T(1,128)S(1)} %copy-done.55, bf16[384,512]{1,0:T(8,128)(2,1)S(1)} %copy-done.33), custom_call_target="tpu_custom_call" | custom-call | bytes 115343360 | tf_op jit(solution)/shard_map/pallas_call | solution.py:280
  226.3 20.4 %shard_map.182 = (bf16[512,1536]{1,0:T(8,128)(2,1)S(1)}, bf16[2,3,256,128]{3,2,1,0:T(8,128)(2,1)S(1)}, bf16[4,512,128]{2,1,0:T(8,128)(2,1)S(1)}, f32[2,3,256,128...) custom-call(bf16[512,1536]{1,0:T(8,128)(2,1)S(1)} %bitcast.238, ...), custom_call_target="tpu_custom_call" | custom-call | bytes 73400320 | tf_op jit(solution)/shard_map/pallas_call | solution.py:527
  250.4 41.0 %shard_map.183 = (f32[64,1536]{1,0:T(8,128)S(1)}, bf16[8,64,1536]{2,1,0:T(8,128)(2,1)S(1)}) custom-call(bf16[8,64,1536]{2,1,0:T(8,128)(2,1)S(1)} %bitcast.254, f32[64,1536]{1,0:T(8,128)S(1)} %get-tuple-element.73.refs_1_.refs_2_, f32[1,1536]{1,0:T(1,128)S(1)} %copy-done.57), custom_call_target="tpu_custom_call" | custom-call | bytes 115343360 | tf_op jit(solution)/shard_map/pallas_call | solution.py:280
  291.5 1.2 copy-done.3
  293.4 1.3 fusion.64
  294.6 1.7 slice.369
  296.4 3.5 slice.364
  300.6 3.4 fusion.76
  306.4 2.7 multiply_reduce_fusion.3
  311.9 5.2 fusion.39
  317.0 4.0 convolution_convert_fusion.1
  321.1 10.6 %maximum_maximum_fusion = bf16[4,576,2048]{2,1,0:T(8,128)(2,1)} fusion(bf16[4,64,1024]{2,1,0:T(8,128)(2,1)S(1)} %get-tuple-element.212, bf16[4,64,1024]{2,1,0:T(8,128)(2,1)S(1)} %get-tuple-element.211, bf16[4,128,2048]{2,1,0:T(8,128)(2,1)S(1)} %slice.376, bf16[4,384,2048]{2,1,0:T(8,128)(2,1)S(1)} %bitcast.288), kind=kLoop, calls=%fused_computation | loop fusion | flops 37748736 | bytes 18874368 | tf_op jit(solution)/shard_map/vmap()/concatenate | solution.py:739
  333.0 3.6 fusion.4
  336.7 44.7 %shard_map.186 = (f32[64,1536]{1,0:T(8,128)S(1)}, f32[1,1536]{1,0:T(1,128)S(1)}, bf16[8,64,1536]{2,1,0:T(8,128)(2,1)S(1)}) custom-call(bf16[8,64,1536]{2,1,0:T(8,128)(2,1)S(1)} %bitcast.245, f32[64,1536]{1,0:T(8,128)S(1)} %copy-done.23, f32[64,1536]{1,0:T(8,128)S(1)} %copy-done.31, f32[1,1536]{1,0:T(1,128)S(1)} %copy-done.58), custom_call_target="tpu_custom_call" | custom-call | bytes 115343360 | tf_op jit(solution)/shard_map/pallas_call | solution.py:280
  381.5 16.2 %shard_map.187 = (bf16[512,1536]{1,0:T(8,128)(2,1)S(1)}, bf16[512,384]{1,0:T(8,128)(2,1)S(1)}) custom-call(bf16[512,1536]{1,0:T(8,128)(2,1)S(1)} %bitcast.224, bf16[1536,512]{1,0:T(8,128)(2,1)S(1)} %bitcast.241, f32[512,128]{1,0:T(8,128)S(1)} %copy.158.cos_ref, f32[512,128]{1,0:T(8,128)S(1)} %pad_maximum_fusion.9.sin_ref, s32[4,512,1]{2,1,0:T(8,128)S(1)} %copy.159.key_place, ...), custom_call_target="tpu_custom_call" | custom-call | bytes 104857600 | tf_op jit(solution)/shard_map/pallas_call | solution.py:648
  400.2 44.2 %shard_map.188 = (f32[64,1536]{1,0:T(8,128)S(1)}, f32[1,1536]{1,0:T(1,128)S(1)}, bf16[8,64,1536]{2,1,0:T(8,128)(2,1)S(1)}, f32[384,512]{1,0:T(8,128)S(1)}) custom-call(bf16[8,64,1536]{2,1,0:T(8,128)(2,1)S(1)} %bitcast.253, f32[64,1536]{1,0:T(8,128)S(1)} %get-tuple-element.89.refs_1_, f32[64,1536]{1,0:T(8,128)S(1)} %copy-done.7, f32[1,1536]{1,0:T(1,128)S(1)} %copy-done.56, ...), custom_call_target="tpu_custom_call" | custom-call | bytes 115343360 | tf_op jit(solution)/shard_map/pallas_call | solution.py:280
  447.6 1.6 copy-done.82
  450.3 4.8 multiply_reduce_fusion.1
  455.1 5.1 fusion.38
  460.3 4.0 convolution_convert_fusion
  464.3 10.5 %maximum_maximum_fusion.1 = bf16[4,576,2048]{2,1,0:T(8,128)(2,1)} fusion(bf16[4,64,1024]{2,1,0:T(8,128)(2,1)S(1)} %get-tuple-element.210, bf16[4,64,1024]{2,1,0:T(8,128)(2,1)S(1)} %get-tuple-element.209, bf16[4,128,2048]{2,1,0:T(8,128)(2,1)S(1)} %slice.379, bf16[4,384,2048]{2,1,0:T(8,128)(2,1)S(1)} %bitcast.289), kind=kLoop, calls=%fused_computation.1 | loop fusion | flops 37748736 | bytes 18874368 | tf_op jit(solution)/shard_map/vmap()/concatenate | solution.py:739
  474.9 2.7 fusion.15
  478.7 26.7 %shard_map.184 = f32[64,1536]{1,0:T(8,128)S(1)} custom-call(bf16[8,64,1536]{2,1,0:T(8,128)(2,1)S(1)} %bitcast.246, f32[64,1536]{1,0:T(8,128)S(1)} %copy-done.32), custom_call_target="tpu_custom_call" | custom-call | bytes 115343360 | tf_op jit(solution)/shard_map/pallas_call | solution.py:280
  507.7 1.7 stack.73
  509.4 1.7 copy.175
  512.0 3.2 fusion.48
  517.1 1.5 fusion.5
  518.7 44.6 %shard_map.189 = (f32[64,1536]{1,0:T(8,128)S(1)}, f32[1,1536]{1,0:T(1,128)S(1)}, bf16[8,64,1536]{2,1,0:T(8,128)(2,1)S(1)}) custom-call(bf16[8,64,1536]{2,1,0:T(8,128)(2,1)S(1)} %bitcast.244, f32[64,1536]{1,0:T(8,128)S(1)} %copy-done.20, f32[64,1536]{1,0:T(8,128)S(1)} %copy-done.36, f32[1,1536]{1,0:T(1,128)S(1)} %get-tuple-element.257.refs_2_.refs_3_), custom_call_target="tpu_custom_call" | custom-call | bytes 115343360 | tf_op jit(solution)/shard_map/pallas_call | solution.py:280
  563.4 16.5 %shard_map.190 = (bf16[512,1536]{1,0:T(8,128)(2,1)S(1)}, bf16[512,384]{1,0:T(8,128)(2,1)S(1)}) custom-call(bf16[512,1536]{1,0:T(8,128)(2,1)S(1)} %bitcast.242, bf16[1536,512]{1,0:T(8,128)(2,1)S(1)} %bitcast.237, f32[512,128]{1,0:T(8,128)S(1)} %copy.158.cos_ref, f32[512,128]{1,0:T(8,128)S(1)} %pad_maximum_fusion.9.sin_ref, s32[4,512,1]{2,1,0:T(8,128)S(1)} %copy.159.key_place, ...), custom_call_target="tpu_custom_call" | custom-call | bytes 104857600 | tf_op jit(solution)/shard_map/pallas_call | solution.py:648
  582.2 1.4 copy-done.29
  583.6 28.8 %shard_map.191 = (f32[64,1536]{1,0:T(8,128)S(1)}, f32[1,1536]{1,0:T(1,128)S(1)}, f32[384,512]{1,0:T(8,128)S(1)}) custom-call(bf16[8,64,1536]{2,1,0:T(8,128)(2,1)S(1)} %bitcast.252, f32[64,1536]{1,0:T(8,128)S(1)} %copy-done.50, f32[64,1536]{1,0:T(8,128)S(1)} %bitcast_convert_fusion.1.refs_0_.refs_1_.refs_2_, ...), custom_call_target="tpu_custom_call" | custom-call | bytes 115343360 | tf_op jit(solution)/shard_map/pallas_call | solution.py:280
  613.6 1.1 maximum_bitcast_fusion.6
  614.7 13.4 %shard_map.192 = f32[24,128]{1,0:T(8,128)S(1)} custom-call(f32[16,2,24,128]{3,2,1,0:T(8,128)S(1)} %pad.22.parts_ref), custom_call_target="tpu_custom_call" | custom-call | tf_op jit(solution)/shard_map/pallas_call | solution.py:393
  629.6 1.7 broadcast_select_fusion
  636.9 2.0 maximum_bitcast_fusion.2
  638.9 2.8 select_bitcast_fusion.1
  642.6 1.9 maximum_convert_fusion.1
  644.5 3.0 maximum_convert_fusion
  (383 shorter events, 57.3 us)
Async XLA Ops:
  7.2 154.6 %all-gather.3.cloned.1.call-start = ((), (), s32[]{:S(2)}) async-start(), calls=%async_computation.2 | async-start | bytes 11796480 | tf_op jit(solution)/shard_map/all_gather | solution.py:764
  11.0 10.1 %collective-permute-start = (bf16[384,512]{1,0:T(8,128)(2,1)S(1)}, bf16[384,512]{1,0:T(8,128)(2,1)S(1)}, u32[]{:S(2)}, u32[]{:S(2)}) collective-permute-start(bf16[384,512]{1,0:T(8,128)(2,1)S(1)} %bitcast.295), channel_id=1, source_target_pairs={{0,16},{16,0},{1,17},{17,1},{2,18},{18,2},{3,19},{19,3},{4,20},{20... | collective-permute-start | bytes 1179656 | tf_op jit(solution)/shard_map/ppermute | solution.py:704
  12.7 33.0 %collective-permute-start.2 = (bf16[128,3072]{1,0:T(8,128)(2,1)}, bf16[128,3072]{1,0:T(8,128)(2,1)}, u32[]{:S(2)}, u32[]{:S(2)}) collective-permute-start(bf16[128,3072]{1,0:T(8,128)(2,1)} %fusion.29), channel_id=1, source_target_pairs={{0,16},{16,0},{1,17},{17,1},{2,18},{18,2},{3,19},{19,3},{4,20},{20... | collective-permute-start | bytes 2359304 | tf_op jit(solution)/shard_map/ppermute | solution.py:704
  14.6 6.4 copy-start.117
  16.8 32.6 %collective-permute-start.1 = (bf16[384,2048]{1,0:T(8,128)(2,1)}, bf16[384,2048]{1,0:T(8,128)(2,1)}, u32[]{:S(2)}, u32[]{:S(2)}) collective-permute-start(bf16[384,2048]{1,0:T(8,128)(2,1)} %fusion.7), channel_id=1, source_target_pairs={{0,16},{16,0},{1,17},{17,1},{2,18},{18,2},{3,19},{19,3},{4,20},{20... | collective-permute-start | bytes 4718600 | tf_op jit(solution)/shard_map/ppermute | solution.py:704
  54.3 239.1 %all-gather.5.cloned.1.call-start = ((), (), s32[]{:S(2)}) async-start(), calls=%async_computation.3 | async-start | bytes 11796480 | tf_op jit(solution)/shard_map/all_gather | solution.py:764
  63.1 67.2 %copy-start.91 = (bf16[384,2048]{1,0:T(8,128)(2,1)S(1)}, bf16[384,2048]{1,0:T(8,128)(2,1)}, u32[]{:S(2)}) copy-start(bf16[384,2048]{1,0:T(8,128)(2,1)} %get-tuple-element.203) | copy-start | bytes 4718596
  63.1 67.2 %copy-start.105 = (bf16[64,1024]{1,0:T(8,128)(2,1)S(1)}, bf16[64,1024]{1,0:T(8,128)(2,1)}, u32[]{:S(2)}) copy-start(bf16[64,1024]{1,0:T(8,128)(2,1)} %get-tuple-element.239) | copy-start | bytes 393220
  63.1 67.2 %copy-start.106 = (bf16[64,1024]{1,0:T(8,128)(2,1)S(1)}, bf16[64,1024]{1,0:T(8,128)(2,1)}, u32[]{:S(2)}) copy-start(bf16[64,1024]{1,0:T(8,128)(2,1)} %get-tuple-element.240) | copy-start | bytes 393220
  86.4 41.9 %copy-start.67 = (f32[2,3,1,256]{3,2,1,0:T(1,128)}, f32[2,3,1,256]{3,2,1,0:T(1,128)S(1)}, u32[]{:S(2)}) copy-start(f32[2,3,1,256]{3,2,1,0:T(1,128)S(1)} %get-tuple-element.100.lse_ref) | copy-start | bytes 18436
  131.9 342.9 %reduce-scatter.7.cloned.1.call-start = ((), (), s32[]{:S(2)}) async-start(), calls=%async_computation.4 | async-start | bytes 11796480
  169.9 5.9 copy-start.121
  169.9 5.9 copy-start.123
  172.3 6.4 copy-start.81
  179.8 46.4 %copy-start.60 = (s32[2,1,256]{2,1,0:T(1,128)S(1)}, s32[2,1,256]{2,1,0:T(1,128)}, u32[]{:S(2)}) copy-start(s32[2,1,256]{2,1,0:T(1,128)} %broadcast_in_dim.89.query_start) | copy-start | bytes 6148
  179.8 46.4 %copy-start.64 = (s32[2,1,256]{2,1,0:T(1,128)S(1)}, s32[2,1,256]{2,1,0:T(1,128)}, u32[]{:S(2)}) copy-start(s32[2,1,256]{2,1,0:T(1,128)} %broadcast_in_dim.88.query_place) | copy-start | bytes 6148
  226.2 20.4 %copy-start.13 = (bf16[8,64,1536]{2,1,0:T(8,128)(2,1)}, bf16[8,64,1536]{2,1,0:T(8,128)(2,1)S(1)}, u32[]{:S(2)}) copy-start(bf16[8,64,1536]{2,1,0:T(8,128)(2,1)S(1)} %get-tuple-element.74) | copy-start | bytes 4718596
  226.2 20.4 %copy-start.15 = (bf16[4,384,512]{2,1,0:T(8,128)(2,1)}, bf16[4,384,512]{2,1,0:T(8,128)(2,1)S(1)}, u32[]{:S(2)}) copy-start(bf16[4,384,512]{2,1,0:T(8,128)(2,1)S(1)} %get-tuple-element.75) | copy-start | bytes 4718596
  226.2 24.2 %copy-start.6 = (f32[64,1536]{1,0:T(8,128)}, f32[64,1536]{1,0:T(8,128)S(1)}, u32[]{:S(2)}) copy-start(f32[64,1536]{1,0:T(8,128)S(1)} %get-tuple-element.73.refs_1_.refs_2_) | copy-start | bytes 1179652
  226.2 24.1 %copy-start.57 = (f32[1,1536]{1,0:T(1,128)S(1)}, f32[1,1536]{1,0:T(1,128)}, u32[]{:S(2)}) copy-start(f32[1,1536]{1,0:T(1,128)} %get-tuple-element.255.refs_2_.refs_3_) | copy-start | bytes 18436
  331.7 250.4 %reduce-scatter.9.cloned.1.call-start = ((), (), s32[]{:S(2)}) async-start(), calls=%async_computation.5 | async-start | bytes 11796480
  333.0 48.4 %copy-start.44 = (bf16[4,512,128]{2,1,0:T(8,128)(2,1)S(1)}, bf16[4,512,128]{2,1,0:T(8,128)(2,1)}, u32[]{:S(2)}) copy-start(bf16[4,512,128]{2,1,0:T(8,128)(2,1)} %copy-done.43) | copy-start | bytes 1572868
  333.0 48.4 %copy-start.48 = (bf16[2,3,256,128]{3,2,1,0:T(8,128)(2,1)S(1)}, bf16[2,3,256,128]{3,2,1,0:T(8,128)(2,1)}, u32[]{:S(2)}) copy-start(bf16[2,3,256,128]{3,2,1,0:T(8,128)(2,1)} %copy-done.47) | copy-start | bytes 1179652
  336.6 44.9 %copy-start.16 = (bf16[4,384,512]{2,1,0:T(8,128)(2,1)S(1)}, bf16[4,384,512]{2,1,0:T(8,128)(2,1)}, u32[]{:S(2)}) copy-start(bf16[4,384,512]{2,1,0:T(8,128)(2,1)} %copy-done.15) | copy-start | bytes 4718596
  336.6 44.9 %copy-start.40 = (f32[2,3,256,128]{3,2,1,0:T(8,128)S(1)}, f32[2,3,256,128]{3,2,1,0:T(8,128)}, u32[]{:S(2)}) copy-start(f32[2,3,256,128]{3,2,1,0:T(8,128)} %copy-done.39) | copy-start | bytes 2359300
  336.6 44.9 %copy-start.61 = (s32[2,1,256]{2,1,0:T(1,128)S(1)}, s32[2,1,256]{2,1,0:T(1,128)}, u32[]{:S(2)}) copy-start(s32[2,1,256]{2,1,0:T(1,128)} %broadcast_in_dim.89.query_start) | copy-start | bytes 6148
  336.6 44.9 %copy-start.65 = (s32[2,1,256]{2,1,0:T(1,128)S(1)}, s32[2,1,256]{2,1,0:T(1,128)}, u32[]{:S(2)}) copy-start(s32[2,1,256]{2,1,0:T(1,128)} %broadcast_in_dim.88.query_place) | copy-start | bytes 6148
  336.6 44.9 %copy-start.70 = (f32[2,3,1,256]{3,2,1,0:T(1,128)S(1)}, f32[2,3,1,256]{3,2,1,0:T(1,128)}, u32[]{:S(2)}) copy-start(f32[2,3,1,256]{3,2,1,0:T(1,128)} %copy-done.69) | copy-start | bytes 18436
  381.4 16.3 %copy-start.71 = (f32[1,1536]{1,0:T(1,128)}, f32[1,1536]{1,0:T(1,128)S(1)}, u32[]{:S(2)}) copy-start(f32[1,1536]{1,0:T(1,128)S(1)} %get-tuple-element.112) | copy-start | bytes 18436
  381.5 16.3 %copy-start.54 = (bf16[512,256]{1,0:T(8,128)(2,1)S(1)}, bf16[512,256]{1,0:T(8,128)(2,1)}, u32[]{:S(2)}) copy-start(bf16[512,256]{1,0:T(8,128)(2,1)} %copy-done.53) | copy-start | bytes 786436
  400.2 44.3 %copy-start.99 = (bf16[512,512]{1,0:T(8,128)(2,1)S(1)}, bf16[512,512]{1,0:T(8,128)(2,1)}, u32[]{:S(2)}) copy-start(bf16[512,512]{1,0:T(8,128)(2,1)} %copy-done.98) | copy-start | bytes 1572868
  449.3 5.9 slice-start
  450.3 4.8 slice-start.1
  455.1 5.1 copy-start.2
  478.6 26.8 %copy-start.8 = (f32[64,1536]{1,0:T(8,128)S(1)}, f32[64,1536]{1,0:T(8,128)}, u32[]{:S(2)}) copy-start(f32[64,1536]{1,0:T(8,128)} %copy-done.6) | copy-start | bytes 1179652
  478.6 27.6 %copy-start.5 = (bf16[8,64,1536]{2,1,0:T(8,128)(2,1)S(1)}, bf16[8,64,1536]{2,1,0:T(8,128)(2,1)}, u32[]{:S(2)}) copy-start(bf16[8,64,1536]{2,1,0:T(8,128)(2,1)} %copy-done.3) | copy-start | bytes 4718596
  478.6 27.6 %copy-start.112 = (f32[512,16]{0,1:T(8,128)S(1)}, f32[512,16]{0,1:T(8,128)}, u32[]{:S(2)}) copy-start(f32[512,16]{0,1:T(8,128)} %copy-done.111) | copy-start | bytes 98308
  478.6 27.6 %copy-start.114 = (f32[512,16]{0,1:T(8,128)S(1)}, f32[512,16]{0,1:T(8,128)}, u32[]{:S(2)}) copy-start(f32[512,16]{0,1:T(8,128)} %copy-done.113) | copy-start | bytes 98308
  478.7 27.6 %copy-start.119 = (f32[512]{0:T(512)S(1)}, f32[512]{0:T(512)}, u32[]{:S(2)}) copy-start(f32[512]{0:T(512)} %copy-done.118) | copy-start | bytes 6148
  478.7 28.3 %copy-start.72 = (f32[1,1536]{1,0:T(1,128)S(1)}, f32[1,1536]{1,0:T(1,128)}, u32[]{:S(2)}) copy-start(f32[1,1536]{1,0:T(1,128)} %copy-done.71) | copy-start | bytes 18436
  478.7 28.3 %copy-start.74 = (f32[1,1536]{1,0:T(1,128)S(1)}, f32[1,1536]{1,0:T(1,128)}, u32[]{:S(2)}) copy-start(f32[1,1536]{1,0:T(1,128)} %copy-done.73) | copy-start | bytes 18436
  506.2 9.0 %collective-permute-start.3 = (bf16[64,1536]{1,0:T(8,128)(2,1)}, bf16[64,1536]{1,0:T(8,128)(2,1)}, u32[]{:S(2)}, u32[]{:S(2)}) collective-permute-start(bf16[64,1536]{1,0:T(8,128)(2,1)} %broadcast_select_fusion.12), channel_id=1, source_target_pairs={{0,16},{16,0},{1,17},{17,1},{2,18},{18,2},{3,19},{19,3},{4,20},{20... | collective-permute-start | bytes 589832 | tf_op jit(solution)/shard_map/ppermute | solution.py:704
  509.4 5.8 copy-start.9
  509.4 5.8 copy-start.18
  511.1 6.0 copy-start.96
  511.1 6.0 copy-start.104
  511.1 6.0 copy-start.110
  517.1 46.2 %copy-start.42 = (bf16[4,512,128]{2,1,0:T(8,128)(2,1)S(1)}, bf16[4,512,128]{2,1,0:T(8,128)(2,1)}, u32[]{:S(2)}) copy-start(bf16[4,512,128]{2,1,0:T(8,128)(2,1)} %copy-done.41) | copy-start | bytes 1572868
  517.1 46.2 %copy-start.46 = (bf16[2,3,256,128]{3,2,1,0:T(8,128)(2,1)S(1)}, bf16[2,3,256,128]{3,2,1,0:T(8,128)(2,1)}, u32[]{:S(2)}) copy-start(bf16[2,3,256,128]{3,2,1,0:T(8,128)(2,1)} %copy-done.45) | copy-start | bytes 1179652
  518.6 44.7 %copy-start.12 = (bf16[4,384,512]{2,1,0:T(8,128)(2,1)S(1)}, bf16[4,384,512]{2,1,0:T(8,128)(2,1)}, u32[]{:S(2)}) copy-start(bf16[4,384,512]{2,1,0:T(8,128)(2,1)} %copy-done.10) | copy-start | bytes 4718596
  518.6 44.7 %copy-start.38 = (f32[2,3,256,128]{3,2,1,0:T(8,128)S(1)}, f32[2,3,256,128]{3,2,1,0:T(8,128)}, u32[]{:S(2)}) copy-start(f32[2,3,256,128]{3,2,1,0:T(8,128)} %copy-done.37) | copy-start | bytes 2359300
  518.6 44.7 %copy-start.62 = (s32[2,1,256]{2,1,0:T(1,128)S(1)}, s32[2,1,256]{2,1,0:T(1,128)}, u32[]{:S(2)}) copy-start(s32[2,1,256]{2,1,0:T(1,128)} %broadcast_in_dim.89.query_start) | copy-start | bytes 6148
  518.7 44.7 %copy-start.66 = (s32[2,1,256]{2,1,0:T(1,128)S(1)}, s32[2,1,256]{2,1,0:T(1,128)}, u32[]{:S(2)}) copy-start(s32[2,1,256]{2,1,0:T(1,128)} %broadcast_in_dim.88.query_place) | copy-start | bytes 6148
  518.7 44.7 %copy-start.68 = (f32[2,3,1,256]{3,2,1,0:T(1,128)S(1)}, f32[2,3,1,256]{3,2,1,0:T(1,128)}, u32[]{:S(2)}) copy-start(f32[2,3,1,256]{3,2,1,0:T(1,128)} %copy-done.67) | copy-start | bytes 18436
  563.3 16.6 %copy-start.49 = (f32[64,1536]{1,0:T(8,128)}, f32[64,1536]{1,0:T(8,128)S(1)}, u32[]{:S(2)}) copy-start(f32[64,1536]{1,0:T(8,128)S(1)} %get-tuple-element.105.refs_1_) | copy-start | bytes 1179652
  563.3 16.6 %copy-start.75 = (f32[1,1536]{1,0:T(1,128)}, f32[1,1536]{1,0:T(1,128)S(1)}, u32[]{:S(2)}) copy-start(f32[1,1536]{1,0:T(1,128)S(1)} %get-tuple-element.110) | copy-start | bytes 18436
  582.1 30.3 %copy-start.76 = (f32[1,1536]{1,0:T(1,128)S(1)}, f32[1,1536]{1,0:T(1,128)}, u32[]{:S(2)}) copy-start(f32[1,1536]{1,0:T(1,128)} %copy-done.75) | copy-start | bytes 18436
  612.4 16.4 %copy-start.21 = (f32[64,1536]{1,0:T(8,128)S(1)}, f32[64,1536]{1,0:T(8,128)}, u32[]{:S(2)}) copy-start(f32[64,1536]{1,0:T(8,128)} %copy-done.19) | copy-start | bytes 1179652
  612.4 16.9 %copy-start.25 = (f32[384,512]{1,0:T(8,128)S(1)}, f32[384,512]{1,0:T(8,128)}, u32[]{:S(2)}) copy-start(f32[384,512]{1,0:T(8,128)} %copy-done.24) | copy-start | bytes 2359300
  613.6 16.1 %copy-start.87 = (bf16[1,576,2048]{2,1,0:T(8,128)(2,1)S(1)}, bf16[1,576,2048]{2,1,0:T(8,128)(2,1)}, u32[]{:S(2)}) copy-start(bf16[1,576,2048]{2,1,0:T(8,128)(2,1)} %reduce-scatter.9.cloned.1.call-done) | copy-start | bytes 7077892
  614.7 14.9 %copy-start.85 = (bf16[1,576,2048]{2,1,0:T(8,128)(2,1)S(1)}, bf16[1,576,2048]{2,1,0:T(8,128)(2,1)}, u32[]{:S(2)}) copy-start(bf16[1,576,2048]{2,1,0:T(8,128)(2,1)} %reduce-scatter.7.cloned.1.call-done) | copy-start | bytes 7077892
  628.8 3.4 collective-permute-start.4
  629.4 3.7 collective-permute-start.5
  631.3 7.6 %collective-permute-start.6 = (bf16[576,2048]{1,0:T(8,128)(2,1)}, bf16[576,2048]{1,0:T(8,128)(2,1)}, u32[]{:S(2)}, u32[]{:S(2)}) collective-permute-start(bf16[576,2048]{1,0:T(8,128)(2,1)} %broadcast_select_fusion), channel_id=1, source_target_pairs={{0,16},{16,0},{1,17},{17,1},{2,18},{18,2},{3,19},{19,3},{4,20},{20... | collective-permute-start | bytes 7077896 | tf_op jit(solution)/shard_map/ppermute | solution.py:704
  (75 other events, 141.3 us)
Sparse Core Ops, SparseCore 0:
  54.4 101.6 all-gather.2
  157.9 118.7 all-gather.4
  331.8 115.5 reduce-scatter.6
  475.0 93.7 reduce-scatter.8

commit v4 on v3

v4 whole, which is shorter than its diff:
```python
import functools

import jax
import jax.numpy as jnp
from jax import lax
from jax.experimental import pallas as pl
from jax.experimental.pallas import tpu as pltpu
from jax.sharding import PartitionSpec as P

HEAD_SIZE = 64
FF = 512
CONT_LEN = 1024
EPSILON = 1e-06
ROPE_BASE = 10000.0
MASKED = -1e30
CHUNKS = 2
LANES = 2 * HEAD_SIZE
MESH = pl.DeviceIdType.MESH
F32 = jnp.float32
BF16 = jnp.bfloat16


def dot(left, right, contract):
    return lax.dot_general(left, right, (contract, ((), ())), preferred_element_type=F32)


def norm_scale(rows):
    return lax.rsqrt(jnp.mean(rows * rows, -1, keepdims=True) + EPSILON)


def place():
    return lax.axis_index("section"), lax.axis_index("ctx"), lax.axis_index("wt")


def greet(targets):
    barrier = pltpu.get_barrier_semaphore()
    for target in targets:
        pl.semaphore_signal(barrier, inc=1, device_id=target, device_id_type=MESH)
    pl.semaphore_wait(barrier, len(targets))


def remote(source, destination, send_sem, recv_sem, target):
    return pltpu.make_async_remote_copy(
        src_ref=source,
        dst_ref=destination,
        send_sem=send_sem,
        recv_sem=recv_sem,
        device_id=target,
        device_id_type=MESH,
    )


class Near:
    def __init__(self, n_wt):
        self.section, self.ctx, self.wt = place()
        self.n_wt = n_wt
        self.sibling = (1 - self.section, self.ctx, self.wt)
        self.right = (self.section, self.ctx, jnp.minimum(self.wt + 1, n_wt - 1))
        self.left = (self.section, self.ctx, jnp.maximum(self.wt - 1, 0))
        self.has_right, self.has_left = self.wt < n_wt - 1, self.wt > 0
        self.own = self.section * n_wt + self.wt

    def greet(self, others=()):
        barrier = pltpu.get_barrier_semaphore()

        def hail(target):
            pl.semaphore_signal(barrier, inc=1, device_id=target, device_id_type=MESH)

        hail(self.sibling)
        pl.when(self.has_right)(lambda: hail(self.right))
        pl.when(self.has_left)(lambda: hail(self.left))
        for other in others:
            hail(other)
        pl.semaphore_wait(
            barrier, 1 + len(others) + self.has_right.astype(jnp.int32) + self.has_left.astype(jnp.int32)
        )


def rows_of(chunk, rows):
    return slice(chunk * rows, (chunk + 1) * rows)


class RowSum:
    def __init__(self, near, chunks, parts, scratch):
        self.near, self.chunks, self.parts = near, chunks, parts
        self.rows = parts.shape[1] // chunks
        self.from_sibling, self.in_right, self.in_left, self.out_right, self.out_left = scratch[:5]
        self.swap_send, self.swap_recv, self.send, self.recv = scratch[5:]

    @staticmethod
    def scratch(n_wt, shape, chunks):
        dma = pltpu.SemaphoreType.DMA
        return [pltpu.VMEM((n_wt,) + shape, BF16)] * 5 + [dma((chunks * n_wt,))] * 2 + [dma((2 * chunks * n_wt,))] * 2

    def swap(self, chunk, block):
        at = rows_of(chunk, self.rows)
        number = chunk * self.near.n_wt + block
        return remote(
            self.parts.at[(1 - self.near.section) * self.near.n_wt + block, at],
            self.from_sibling.at[block, at],
            self.swap_send.at[number],
            self.swap_recv.at[number],
            self.near.sibling,
        )

    def begin(self):
        n_wt = self.near.n_wt
        order = []
        for step in range(n_wt - 1):
            order += [n_wt - 1 - step, step]
        for chunk in range(self.chunks):
            for block in dict.fromkeys(order):
                self.swap(chunk, block).start()

    def chip_sum(self, chunk, block):
        at = rows_of(chunk, self.rows)
        mine = self.parts[self.near.section * self.near.n_wt + block, at, :]
        return mine.astype(F32) + self.from_sibling[block, at, :].astype(F32)

    def toward(self, chunk, block, rightward):
        at = rows_of(chunk, self.rows)
        number = (2 * chunk + (0 if rightward else 1)) * self.near.n_wt + block
        source, target = (self.out_right, self.in_right) if rightward else (self.out_left, self.in_left)
        return remote(
            source.at[block, at],
            target.at[block, at],
            self.send.at[number],
            self.recv.at[number],
            self.near.right if rightward else self.near.left,
        )

    def send_on(self, chunk, block, rightward):
        at = rows_of(chunk, self.rows)
        self.swap(chunk, block).wait_recv()
        outward, inward = (self.out_right, self.in_right) if rightward else (self.out_left, self.in_left)
        behind = self.near.has_left if rightward else self.near.has_right

        @pl.when(jnp.logical_not(behind))
        def _():
            outward[block, at, :] = self.chip_sum(chunk, block).astype(BF16)

        @pl.when(behind)
        def _():
            self.toward(chunk, block, rightward).wait_recv()
            outward[block, at, :] = (self.chip_sum(chunk, block) + inward[block, at, :].astype(F32)).astype(BF16)

        self.toward(chunk, block, rightward).start()

    def step(self, chunk, step):
        wt, n_wt = self.near.wt, self.near.n_wt
        far, near = n_wt - 1 - step, step
        lower = 2 * wt < n_wt
        pl.when((wt < far) & lower)(lambda: self.send_on(chunk, far, True))
        pl.when(wt > near)(lambda: self.send_on(chunk, near, False))
        pl.when((wt < far) & jnp.logical_not(lower))(lambda: self.send_on(chunk, far, True))

    def collect(self, chunk, result):
        at, wt = rows_of(chunk, self.rows), self.near.wt
        self.swap(chunk, wt).wait_recv()
        result[at, :] = self.chip_sum(chunk, wt)

        @pl.when(self.near.has_left)
        def _():
            self.toward(chunk, wt, True).wait_recv()
            result[at, :] += self.in_right[wt, at, :].astype(F32)

        @pl.when(self.near.has_right)
        def _():
            self.toward(chunk, wt, False).wait_recv()
            result[at, :] += self.in_left[wt, at, :].astype(F32)

    def end(self):
        wt, n_wt = self.near.wt, self.near.n_wt
        for chunk in range(self.chunks):
            for block in range(n_wt):
                self.swap(chunk, block).wait_send()
                if block > 0:
                    pl.when(wt < block)(self.toward(chunk, block, True).wait_send)
                if block < n_wt - 1:
                    pl.when(wt > block)(self.toward(chunk, block, False).wait_send)


class RowGather:
    def __init__(self, near, chunks, all_ref, scratch):
        self.near, self.chunks, self.all = near, chunks, all_ref
        self.rows = all_ref.shape[1] // chunks
        self.send, self.recv, self.pass_send, self.pass_recv = scratch
        self.sent, self.arrivals = [], []

    @staticmethod
    def scratch(n_wt, chunks):
        return [pltpu.SemaphoreType.DMA((2 * chunks * n_wt,))] * 4

    def along(self, chunk, block, hop, rightward):
        at = rows_of(chunk, self.rows)
        number = (2 * chunk + (0 if rightward else 1)) * self.near.n_wt + hop
        return remote(
            self.all.at[block, at],
            self.all.at[block, at],
            self.send.at[number],
            self.recv.at[number],
            self.near.right if rightward else self.near.left,
        )

    def across(self, chunk, block, number):
        at = rows_of(chunk, self.rows)
        number = 2 * chunk * self.near.n_wt + number
        return remote(
            self.all.at[block, at],
            self.all.at[block, at],
            self.pass_send.at[number],
            self.pass_recv.at[number],
            self.near.sibling,
        )

    def launch(self, condition, copy):
        pl.when(condition)(copy.start)
        self.sent.append((condition, copy))

    def first(self, chunk):
        near = self.near
        always = near.wt >= 0
        self.launch(near.has_right, self.along(chunk, near.own, 1, True))
        self.launch(near.has_left, self.along(chunk, near.own, 1, False))
        self.launch(always, self.across(chunk, near.own, 0))
        self.arrivals.append((always, self.across(chunk, near.own, 0)))

    def hop(self, chunk, hop):
        near, n_wt = self.near, self.near.n_wt
        for rightward, came, more, block, number in (
            (True, near.wt >= hop, near.has_right, jnp.maximum(near.own - hop, 0), hop),
            (False, near.wt + hop < n_wt, near.has_left, jnp.minimum(near.own + hop, 2 * n_wt - 1), n_wt + hop),
        ):
            pl.when(came)(self.along(chunk, block, hop, rightward).wait_recv)
            if hop + 1 < n_wt:
                self.launch(came & more, self.along(chunk, block, hop + 1, rightward))
            self.launch(came, self.across(chunk, block, number))
            self.arrivals.append((came, self.across(chunk, block, number)))

    def arrive(self):
        for condition, copy in self.arrivals:
            pl.when(condition)(copy.wait_recv)

    def end(self):
        for condition, copy in self.sent:
            pl.when(condition)(copy.wait_send)


def exchange_kernel(n_ctx, n_wt, reduce, back, spread, rounded, ride, *refs):
    refs = list(refs)
    near = Near(n_wt)
    section, ctx, wt = near.section, near.ctx, near.wt
    peers = [(section, lax.rem(ctx + k, n_ctx), wt) for k in range(1, n_ctx)]
    parts = refs.pop(0) if reduce else None
    rows_ref = refs.pop(0)
    stream_ref = refs.pop(0) if back else None
    gain_ref = refs.pop(0) if (back or spread) else None
    ride_ref = refs.pop(0) if ride else None
    result_ref = refs.pop(0) if reduce else None
    gain_grad_ref = refs.pop(0) if back else None
    all_ref = refs.pop(0) if spread else None
    rode_ref = refs.pop(0) if ride else None
    if reduce:
        sums = RowSum(near, CHUNKS, parts, refs[:9])
        refs = refs[9:]
    if spread:
        gathers = RowGather(near, CHUNKS, all_ref, refs[:4])
        refs = refs[4:]
    if ride:
        landed, ride_send, ride_recv, ride_local = refs
    chunk_rows = rows_ref.shape[0] // CHUNKS
    near.greet(peers if ride else ())
    if reduce:
        sums.begin()
    if ride == "gather":
        keep = pltpu.make_async_copy(ride_ref, rode_ref.at[ctx], ride_local)
        keep.start()
        riders = [
            remote(ride_ref, rode_ref.at[ctx], ride_send.at[k], ride_recv.at[k], peers[k]) for k in range(n_ctx - 1)
        ]
    elif ride == "sum":
        riders = [
            remote(
                ride_ref.at[lax.rem(ctx + 1 + k, n_ctx)], landed.at[k], ride_send.at[k], ride_recv.at[k], peers[k]
            )
            for k in range(n_ctx - 1)
        ]
    if ride:
        for copy in riders:
            copy.start()

    def settle(chunk):
        at = rows_of(chunk, chunk_rows)
        if reduce:
            sums.collect(chunk, result_ref)
            total = result_ref[at, :]
            if back:
                stream = stream_ref[at, :]
                scale = norm_scale(stream)
                weighted = gain_ref[...] * total
                gain_part = jnp.sum(total * stream * scale, 0, keepdims=True)
                gain_grad_ref[...] = gain_part if chunk == 0 else gain_grad_ref[...] + gain_part
                total = scale * weighted - stream * (scale * scale * scale) * jnp.mean(
                    weighted * stream, -1, keepdims=True
                )
            total = rows_ref[at, :].astype(F32) + total
            if rounded:
                total = total.astype(BF16).astype(F32)
            result_ref[at, :] = total
        else:
            total = rows_ref[at, :].astype(F32)
        if spread:
            if spread == "norm":
                total = total * norm_scale(total) * gain_ref[...]
            all_ref[near.own, at, :] = total.astype(BF16)
            gathers.first(chunk)

    stages = []
    if reduce:
        stages += [functools.partial(sums.step, step=step) for step in range(n_wt - 1)]
    stages.append(settle)
    if spread:
        stages += [functools.partial(gathers.hop, hop=hop) for hop in range(1, n_wt)]
    for slot in range(CHUNKS + len(stages) - 1):
        for chunk in reversed(range(CHUNKS)):
            if 0 <= slot - chunk < len(stages):
                stages[slot - chunk](chunk)

    if spread:
        gathers.arrive()
    if ride == "gather":
        keep.wait()
        for copy in riders:
            copy.wait()
    elif ride == "sum":
        total = ride_ref[ctx].astype(F32)
        for k, copy in enumerate(riders):
            copy.wait()
            total = total + landed[k].astype(F32)
        rode_ref[...] = total
    if spread:
        gathers.end()
    if reduce:
        sums.end()


VMEM = pl.BlockSpec(memory_space=pltpu.VMEM)


def exchange(number, parts, rows, stream=None, gain=None, spread=None, rounded=False, gather=None, add=None):
    n_ctx, n_wt = lax.axis_size("ctx"), lax.axis_size("wt")
    shape = rows.shape
    reduce, back = parts is not None, stream is not None
    ride = "gather" if gather is not None else "sum" if add is not None else None
    rider = gather if gather is not None else add
    operands = [
        member
        for member, wanted in (
            (parts, reduce),
            (rows, True),
            (stream, back),
            (gain, back or spread),
            (rider, ride),
        )
        if wanted
    ]
    outs = []
    scratch = []
    dma = pltpu.SemaphoreType.DMA
    if reduce:
        outs.append(jax.ShapeDtypeStruct(shape, F32))
        scratch += RowSum.scratch(n_wt, shape, CHUNKS)
    if back:
        outs.append(jax.ShapeDtypeStruct((1, shape[1]), F32))
    if spread:
        outs.append(jax.ShapeDtypeStruct((2 * n_wt,) + shape, BF16))
        scratch += RowGather.scratch(n_wt, CHUNKS)
    if ride == "gather":
        outs.append(jax.ShapeDtypeStruct((n_ctx,) + rider.shape, BF16))
        scratch += [pltpu.VMEM((8, 128), BF16), dma((n_ctx - 1,)), dma((n_ctx - 1,)), dma]
    elif ride == "sum":
        outs.append(jax.ShapeDtypeStruct(rider.shape[1:], F32))
        scratch += [pltpu.VMEM((n_ctx - 1,) + rider.shape[1:], BF16), dma((n_ctx - 1,)), dma((n_ctx - 1,)), dma]
    return pl.pallas_call(
        functools.partial(exchange_kernel, n_ctx, n_wt, reduce, back, spread, rounded, ride),
        out_shape=outs,
        in_specs=[VMEM] * len(operands),
        out_specs=[VMEM] * len(outs),
        scratch_shapes=scratch,
        compiler_params=pltpu.CompilerParams(
            collective_id=number, has_side_effects=True, vmem_limit_bytes=40 << 20
        ),
        cost_estimate=pl.CostEstimate(flops=0, bytes_accessed=110 << 20, transcendentals=0),
    )(*operands)


def small_sum_kernel(n_ctx, n_wt, *refs):
    small, kept = refs[:6], refs[6:12]
    total_ref, attn_ref, out_ref, grad_ref = refs[12:16]
    parts, landed, summed, from_sibling, send, recv, swap_send, swap_recv = refs[16:]
    section, ctx, wt = place()
    count = n_ctx * n_wt
    own = ctx * n_wt + wt
    blocks = [lax.rem(own + k, count) for k in range(1, count)]
    peers = [(section, block // n_wt, lax.rem(block, n_wt)) for block in blocks]
    sibling = (1 - section, ctx, wt)
    greet([sibling] + peers)
    members = list(zip(kept[0::2], kept[1::2], (attn_ref, out_ref, grad_ref)))
    swaps = swap_copies(section, sibling, members, swap_send, swap_recv)
    start_swaps(section, swaps)
    piece = small[0].shape[1] // count
    parts[...] = jnp.zeros(parts.shape, F32)
    for block in range(count):
        for layer in range(2):
            at = 0
            for ref in small[3 * layer : 3 * layer + 3]:
                end = at + ref.shape[0]
                parts[block, layer, at:end, :piece] = ref[:, block * piece : (block + 1) * piece]
                at = end
    copies = [
        remote(parts.at[blocks[k]], landed.at[k], send.at[k], recv.at[k], peers[k]) for k in range(count - 1)
    ]
    for copy in copies:
        copy.start()
    total = parts[own]
    for k, copy in enumerate(copies):
        copy.wait_recv()
        total = total + landed[k]
    summed[...] = total
    swap = remote(summed.at[1 - section], from_sibling, send.at[count - 1], recv.at[count - 1], sibling)
    swap.start()
    swap.wait()
    total_ref[...] = summed[section] + from_sibling[...]
    for copy in copies:
        copy.wait_send()
    wait_swaps(section, swaps)


def swap_copies(section, sibling, members, send, recv):
    return [
        [remote(pair[1 - layer], pair[2], send.at[k], recv.at[k], sibling) for k, pair in enumerate(members)]
        for layer in range(2)
    ]


def start_swaps(section, swaps):
    for layer in range(2):

        @pl.when(section == layer)
        def _():
            for copy in swaps[layer]:
                copy.start()


def wait_swaps(section, swaps):
    for layer in range(2):

        @pl.when(section == layer)
        def _():
            for copy in swaps[layer]:
                copy.wait()


def small_sum(number, small, kept):
    n_ctx, n_wt = lax.axis_size("ctx"), lax.axis_size("wt")
    count = n_ctx * n_wt
    rows = sum(member.shape[0] for member in small[:3])
    shape = (2, rows + -rows % 8, LANES)
    dma = pltpu.SemaphoreType.DMA
    any_place = pl.BlockSpec(memory_space=pl.ANY)
    return pl.pallas_call(
        functools.partial(small_sum_kernel, n_ctx, n_wt),
        out_shape=[jax.ShapeDtypeStruct(shape[1:], F32)]
        + [jax.ShapeDtypeStruct(member.shape, member.dtype) for member in kept[0::2]],
        in_specs=[VMEM] * 6 + [any_place] * 6,
        out_specs=[VMEM] + [any_place] * 3,
        scratch_shapes=[
            pltpu.VMEM((count,) + shape, F32),
            pltpu.VMEM((count - 1,) + shape, F32),
            pltpu.VMEM(shape, F32),
            pltpu.VMEM(shape[1:], F32),
            dma((count,)),
            dma((count,)),
            dma((3,)),
            dma((3,)),
        ],
        compiler_params=pltpu.CompilerParams(
            collective_id=number, has_side_effects=True, vmem_limit_bytes=40 << 20
        ),
        cost_estimate=pl.CostEstimate(flops=0, bytes_accessed=40 << 20, transcendentals=0),
    )(*small, *kept)


def hand_over_kernel(first, second, result, send, recv):
    section, ctx, wt = place()
    sibling = (1 - section, ctx, wt)
    greet([sibling])
    swaps = swap_copies(section, sibling, [(first, second, result)], send, recv)
    start_swaps(section, swaps)
    wait_swaps(section, swaps)


def hand_over(number, first, second):
    any_place = pl.BlockSpec(memory_space=pl.ANY)
    return pl.pallas_call(
        hand_over_kernel,
        out_shape=jax.ShapeDtypeStruct(first.shape, first.dtype),
        in_specs=[any_place] * 2,
        out_specs=any_place,
        scratch_shapes=[pltpu.SemaphoreType.DMA((1,))] * 2,
        compiler_params=pltpu.CompilerParams(collective_id=number, has_side_effects=True),
    )(first, second)


HEADS = 3


def roll(values, by):
    return pltpu.roll(values, by, 1)


def lower_half(shape):
    return lax.broadcasted_iota(jnp.int32, shape, 1) < HEAD_SIZE


def turned(values, cosine, sine):
    first = lax.rem(lax.broadcasted_iota(jnp.int32, values.shape, 1), HEAD_SIZE) < HEAD_SIZE // 2
    half = HEAD_SIZE // 2
    return values * cosine + jnp.where(first, roll(values, LANES - half), roll(values, half)) * sine


def visible(key_place, query_place, query_start):
    return (key_place <= query_place) & (key_place >= query_start)


def attend_kernel(
    n_ctx,
    n_wt,
    ride,
    x_ref,
    w_ref,
    cos_ref,
    sin_ref,
    key_place,
    query_place,
    query_start,
    *refs,
):
    refs = list(refs)
    ride_ref = refs.pop(0) if ride else None
    part_ref, q_ref, pairs_ref, out_ref, lse_ref, att_ref = [refs.pop(0) for _ in range(6)]
    all_ref = refs.pop(0) if ride else None
    top_ref, sum_ref, acc_ref, send, recv = refs[:5]
    near = Near(n_wt)
    section, ctx, wt = near.section, near.ctx, near.wt
    peers = [(section, lax.rem(ctx + k, n_ctx), wt) for k in range(1, n_ctx)]
    waiting = []
    if ride:
        gathers = RowGather(near, 1, all_ref, refs[5:])
        waiting = [functools.partial(gathers.hop, 0, hop) for hop in range(1, n_wt)]
        all_ref[near.own] = ride_ref[...]
        near.greet(peers)
        gathers.first(0)
    else:
        greet(peers)

    def ride_on():
        if waiting:
            waiting.pop(0)()

    rows = x_ref.shape[0] // 2
    low = lower_half((2 * rows, LANES))
    mixed = dot(x_ref[...], w_ref[:, : 3 * LANES], ((1,), (0,)))
    cosine, sine = cos_ref[...], sin_ref[...]
    first = turned(mixed[:, :LANES], cosine, sine)
    second = turned(mixed[:, LANES : 2 * LANES], cosine, sine)
    pairs_ref[ctx] = jnp.where(low, roll(second, HEAD_SIZE), roll(mixed[:, 2 * LANES :], HEAD_SIZE)).astype(BF16)

    def passing(k):
        return remote(
            pairs_ref.at[ctx], pairs_ref.at[ctx], send.at[k], recv.at[k], (section, lax.rem(ctx + k, n_ctx), wt)
        )

    for k in range(1, n_ctx):
        passing(k).start()
    for h, part in enumerate((first, roll(first, HEAD_SIZE), second)):
        scaled = jnp.where(low, part * (1.0 / HEAD_SIZE), 0.0).astype(BF16)
        q_ref[0, h] = scaled[:rows]
        q_ref[1, h] = scaled[rows:]
    ride_on()
    top_ref[...] = jnp.full(top_ref.shape, MASKED, F32)
    sum_ref[...] = jnp.zeros(sum_ref.shape, F32)
    acc_ref[...] = jnp.zeros(acc_ref.shape, F32)

    def block(c, m, j):
        keys = pairs_ref[c, j * rows : (j + 1) * rows, :]
        if m == j:
            seen = visible(key_place[c, j * rows : (j + 1) * rows, :], query_place[m], query_start[m])
        for h in range(HEADS):
            logits = dot(keys, q_ref[m, h], ((1,), (1,)))
            if m == j:
                logits = jnp.where(seen, logits, MASKED)
            before = top_ref[m, h]
            top = jnp.maximum(before, jnp.max(logits, 0, keepdims=True))
            expos = jnp.exp(logits - top)
            shrink = jnp.exp(before - top)
            top_ref[m, h] = top
            sum_ref[m, h] = sum_ref[m, h] * shrink + jnp.sum(expos, 0, keepdims=True)
            acc_ref[m, h] = acc_ref[m, h] * shrink + dot(keys, expos.astype(BF16), ((0,), (0,)))

    def blocks_of(c):
        block(c, 0, 0)
        block(c, 1, 1)
        block(c, 1, 0)

    blocks_of(ctx)
    ride_on()

    def arrived(k):
        passing(k).wait_recv()
        blocks_of(lax.rem(ctx + n_ctx - k, n_ctx))

    arrived(1)
    ride_on()
    pl.loop(2, n_ctx)(arrived)
    while waiting:
        ride_on()
    low = lower_half((rows, LANES))
    for m in range(2):
        outs = []
        for h in range(HEADS):
            lse_ref[m, h] = top_ref[m, h] + jnp.log(sum_ref[m, h])
            outs.append(jnp.transpose(acc_ref[m, h] / sum_ref[m, h]))
            out_ref[m, h] = outs[h]
        att_ref[m * rows : (m + 1) * rows, :LANES] = jnp.where(low, 0.0, outs[0]).astype(BF16)
        att_ref[m * rows : (m + 1) * rows, LANES:] = jnp.where(low, roll(outs[1], HEAD_SIZE), outs[2]).astype(BF16)
    part_ref[...] = dot(att_ref[...], w_ref[:, 2 * LANES :], ((1,), (1,))).astype(BF16)
    if ride:
        gathers.arrive()
        gathers.end()
    for k in range(1, n_ctx):
        passing(k).wait_send()


def attend(number, rows_in, weights, tables, ride=None):
    n_ctx, n_wt = lax.axis_size("ctx"), lax.axis_size("wt")
    riders = [] if ride is None else [ride]
    n_rows, width = rows_in.shape
    rows = n_rows // 2
    dma = pltpu.SemaphoreType.DMA
    return pl.pallas_call(
        functools.partial(attend_kernel, n_ctx, n_wt, bool(riders)),
        out_shape=[
            jax.ShapeDtypeStruct((n_rows, width), BF16),
            jax.ShapeDtypeStruct((2, HEADS, rows, LANES), BF16),
            jax.ShapeDtypeStruct((n_ctx, n_rows, LANES), BF16),
            jax.ShapeDtypeStruct((2, HEADS, rows, LANES), F32),
            jax.ShapeDtypeStruct((2, HEADS, 1, rows), F32),
            jax.ShapeDtypeStruct((n_rows, 2 * LANES), BF16),
        ]
        + [jax.ShapeDtypeStruct((2 * n_wt,) + member.shape, BF16) for member in riders],
        in_specs=[VMEM] * (7 + len(riders)),
        out_specs=[VMEM] * (6 + len(riders)),
        scratch_shapes=[
            pltpu.VMEM((2, HEADS, 1, rows), F32),
            pltpu.VMEM((2, HEADS, 1, rows), F32),
            pltpu.VMEM((2, HEADS, LANES, rows), F32),
            dma((n_ctx,)),
            dma((n_ctx,)),
        ]
        + (RowGather.scratch(n_wt, 1) if riders else []),
        compiler_params=pltpu.CompilerParams(
            collective_id=number, has_side_effects=True, vmem_limit_bytes=40 << 20
        ),
        cost_estimate=pl.CostEstimate(flops=0, bytes_accessed=70 << 20, transcendentals=0),
    )(rows_in, weights, *tables, *riders)


def attend_back_kernel(
    n_ctx,
    n_wt,
    ride,
    a_ref,
    w_ref,
    cos_ref,
    sin_ref,
    key_place,
    query_place,
    query_start,
    q_ref,
    pairs_ref,
    out_ref,
    lse_ref,
    *refs,
):
    refs = list(refs)
    ride_refs = [refs.pop(0), refs.pop(0)] if ride else None
    part_ref, raw_ref = refs.pop(0), refs.pop(0)
    rode_ref = refs.pop(0) if ride else None
    do_ref, delta_ref, dq_ref, dkv_ref, own_ref, landed, send, recv = refs[:8]
    near = Near(n_wt)
    section, ctx, wt = near.section, near.ctx, near.wt
    peers = [(section, lax.rem(ctx + k, n_ctx), wt) for k in range(1, n_ctx)]
    waiting = []
    if ride:
        sums = RowSum(near, 1, ride_refs[0], refs[8:])
        waiting = [functools.partial(sums.step, 0, step) for step in range(n_wt - 1)]
        near.greet(peers)
        sums.begin()
    else:
        greet(peers)

    def ride_on():
        if waiting:
            waiting.pop(0)()

    rows = a_ref.shape[0] // 2
    low = lower_half((2 * rows, LANES))
    d_att = dot(a_ref[...], w_ref[:, 2 * LANES :], ((1,), (0,)))
    for h, part in enumerate((d_att[:, :LANES], roll(d_att[:, LANES:], HEAD_SIZE), d_att[:, LANES:])):
        d_out = jnp.where(low, 0.0, part).astype(BF16)
        for m in range(2):
            do_ref[m, h] = d_out[m * rows : (m + 1) * rows]
            product = do_ref[m, h].astype(F32) * out_ref[m, h]
            delta_ref[m, h] = jnp.sum(jnp.transpose(product), 0, keepdims=True)
    dq_ref[...] = jnp.zeros(dq_ref.shape, F32)
    ride_on()

    def block(c, j):
        keys = pairs_ref[c, j * rows : (j + 1) * rows, :]
        total = jnp.zeros((rows, LANES), F32)
        for m in range(j, 2):
            if m == j:
                seen = visible(key_place[c, j * rows : (j + 1) * rows, :], query_place[m], query_start[m])
            for h in range(HEADS):
                probs = jnp.exp(dot(keys, q_ref[m, h], ((1,), (1,))) - lse_ref[m, h])
                if m == j:
                    probs = jnp.where(seen, probs, 0.0)
                d_probs = dot(keys, do_ref[m, h], ((1,), (1,)))
                d_scores = (probs * (d_probs - delta_ref[m, h])).astype(BF16)
                total = total + dot(d_scores, q_ref[m, h], ((1,), (0,)))
                total = total + dot(probs.astype(BF16), do_ref[m, h], ((1,), (0,)))
                dq_ref[m, h] += dot(keys, d_scores, ((0,), (0,)))
        return total

    def passing(k):
        target = lax.rem(ctx + k, n_ctx)
        return remote(dkv_ref.at[target], landed.at[k - 1], send.at[k], recv.at[k], (section, target, wt))

    def sent(k):
        c = lax.rem(ctx + k, n_ctx)
        for j in range(2):
            dkv_ref[c, j * rows : (j + 1) * rows, :] = block(c, j).astype(BF16)
        passing(k).start()

    sent(1)
    ride_on()
    pl.loop(2, n_ctx)(sent)
    ride_on()

    for j in range(2):
        own_ref[j * rows : (j + 1) * rows, :] = block(ctx, j)

    while waiting:
        ride_on()
    if ride:
        sums.collect(0, rode_ref)
        rode_ref[...] += ride_refs[1][...]

    @pl.loop(1, n_ctx)
    def _(k):
        passing(k).wait_recv()
        own_ref[...] += landed[k - 1].astype(F32)

    cosine, sine = cos_ref[...], sin_ref[...]
    d_own = own_ref[...]
    over = roll(d_own, HEAD_SIZE)
    d_query = [
        jnp.concatenate([jnp.transpose(dq_ref[m, h]) for m in range(2)], 0) * (1.0 / HEAD_SIZE) for h in range(HEADS)
    ]
    first = jnp.where(low, d_query[0], roll(d_query[1], HEAD_SIZE))
    second = jnp.where(low, d_query[2], over)
    raw_ref[:, :LANES] = turned(first, cosine, -sine).astype(BF16)
    raw_ref[:, LANES : 2 * LANES] = turned(second, cosine, -sine).astype(BF16)
    raw_ref[:, 2 * LANES :] = jnp.where(low, over, 0.0).astype(BF16)
    part_ref[...] = dot(raw_ref[...], w_ref[:, : 3 * LANES], ((1,), (1,))).astype(BF16)
    if ride:
        sums.end()
    for k in range(1, n_ctx):
        passing(k).wait_send()


def attend_back(number, rows_a, weights, tables, kept, ride=()):
    n_ctx, n_wt = lax.axis_size("ctx"), lax.axis_size("wt")
    n_rows, width = rows_a.shape
    rows = n_rows // 2
    dma = pltpu.SemaphoreType.DMA
    return pl.pallas_call(
        functools.partial(attend_back_kernel, n_ctx, n_wt, bool(ride)),
        out_shape=[
            jax.ShapeDtypeStruct((n_rows, width), BF16),
            jax.ShapeDtypeStruct((n_rows, 3 * LANES), BF16),
        ]
        + [jax.ShapeDtypeStruct(member.shape, F32) for member in ride[1:]],
        in_specs=[VMEM] * (11 + len(ride)),
        out_specs=[VMEM] * (2 + len(ride) // 2),
        scratch_shapes=[
            pltpu.VMEM((2, HEADS, rows, LANES), BF16),
            pltpu.VMEM((2, HEADS, 1, rows), F32),
            pltpu.VMEM((2, HEADS, LANES, rows), F32),
            pltpu.VMEM((n_ctx, n_rows, LANES), BF16),
            pltpu.VMEM((n_rows, LANES), F32),
            pltpu.VMEM((n_ctx - 1, n_rows, LANES), BF16),
            dma((n_ctx,)),
            dma((n_ctx,)),
        ]
        + (RowSum.scratch(n_wt, ride[1].shape, 1) if ride else []),
        compiler_params=pltpu.CompilerParams(
            collective_id=number, has_side_effects=True, vmem_limit_bytes=40 << 20
        ),
        cost_estimate=pl.CostEstimate(flops=0, bytes_accessed=100 << 20, transcendentals=0),
    )(rows_a, weights, *tables, *kept, *ride)


def expert_halves(inward, down, packed, half, per_core):
    depth, down_rows = inward.shape[1], down.shape[1]
    wide, width = packed.shape[1], down.shape[2]
    column, second = inward.shape[2], depth + down_rows
    first, middle = wide - width, down_rows // 2
    a, b = half * per_core, half * per_core + 1
    return [
        (inward.at[a], packed.at[:depth, :column]),
        (inward.at[b], packed.at[:depth, column:]),
        (down.at[a], packed.at[depth:second, :width]),
        (down.at[b, :, :first], packed.at[depth:second, width:]),
        (down.at[b, :middle, first:], packed.at[second:, : wide // 2]),
        (down.at[b, middle:, first:], packed.at[second:, wide // 2 :]),
    ]


def prepare_kernel(query, pair, out, inward, down, routes, gains, router, *refs):
    attn, moe = refs[:2], refs[2:4]
    all_routes, all_gains, all_router, halves, keep_sem, send, recv = refs[4:]
    section, ctx, wt = place()
    sibling = (1 - section, ctx, wt)
    greet([sibling])
    per_core = inward.shape[0] // 2
    q_cols = query.shape[1] // 2
    outward = jnp.transpose(out[...].astype(F32))
    for half in range(2):
        halves[half] = jnp.concatenate(
            [
                query[:, half * q_cols : (half + 1) * q_cols].astype(F32),
                pair[:, half * LANES : (half + 1) * LANES].astype(F32),
                outward[:, half * q_cols : (half + 1) * q_cols],
            ],
            1,
        ).astype(BF16)
    for layer in range(2):

        @pl.when(section == layer)
        def _():
            own = expert_halves(inward, down, moe[layer], layer, per_core)
            other = expert_halves(inward, down, moe[layer], 1 - layer, per_core)
            own += [
                (halves.at[layer], attn[layer]),
                (routes, all_routes.at[layer]),
                (gains, all_gains.at[layer]),
                (router, all_router.at[layer]),
            ]
            other += [
                (halves.at[1 - layer], attn[layer]),
                (routes, all_routes.at[layer]),
                (gains, all_gains.at[layer]),
                (router, all_router.at[layer]),
            ]
            copies = [pltpu.make_async_copy(a, b, keep_sem.at[k]) for k, (a, b) in enumerate(own)]
            moves = [remote(a, b, send.at[k], recv.at[k], sibling) for k, (a, b) in enumerate(other)]
            for copy in moves + copies:
                copy.start()
            for copy in moves:
                copy.wait_send()
            for copy in copies:
                copy.wait()
            arrive = expert_halves(inward, down, moe[1 - layer], layer, per_core)
            arrive += [
                (halves.at[layer], attn[1 - layer]),
                (routes, all_routes.at[1 - layer]),
                (gains, all_gains.at[1 - layer]),
                (router, all_router.at[1 - layer]),
            ]
            for k, (a, b) in enumerate(arrive):
                remote(a, b, send.at[k], recv.at[k], sibling).wait_recv()


def prepare(number, query, pair, out, inward, down, routes, gains, router):
    depth, down_rows = inward.shape[1], down.shape[1]
    any_place = pl.BlockSpec(memory_space=pl.ANY)
    columns = query.shape[1] + LANES
    wide = inward.shape[0] // 2 * inward.shape[2]
    packed = jax.ShapeDtypeStruct((depth + down_rows + down_rows // 2, wide), BF16)
    attn = jax.ShapeDtypeStruct((depth, columns), BF16)
    both = [jax.ShapeDtypeStruct((2,) + member.shape, member.dtype) for member in (routes, gains, router)]
    dma = pltpu.SemaphoreType.DMA
    return pl.pallas_call(
        prepare_kernel,
        out_shape=[attn, attn, packed, packed] + both,
        in_specs=[VMEM] * 3 + [any_place] * 5,
        out_specs=[any_place] * 7,
        scratch_shapes=[pltpu.VMEM((2, depth, columns), BF16), dma((10,)), dma((10,)), dma((10,))],
        compiler_params=pltpu.CompilerParams(
            collective_id=number, has_side_effects=True, vmem_limit_bytes=40 << 20
        ),
    )(query, pair, out, inward, down, routes, gains, router)


TILE = 256


def expert_pieces(packed, inward, down, depth, down_rows):
    n, wide, width = packed.shape[0], packed.shape[2], down.shape[2]
    half = down_rows // 2
    first = wide - width
    pairs = []
    for c in range(n):
        at = c * down_rows
        second = depth + down_rows
        pairs += [
            (packed.at[c, depth:second, :width], down.at[0, at : at + down_rows, :]),
            (packed.at[c, depth:second, width:], down.at[1, at : at + down_rows, :first]),
            (packed.at[c, second:, : wide // 2], down.at[1, at : at + half, first:]),
            (packed.at[c, second:, wide // 2 :], down.at[1, at + half : at + down_rows, first:]),
        ]
    for c in range(n):
        pairs.append((packed.at[c, :depth, :], inward.at[c * depth : (c + 1) * depth, :]))
    return pairs


def gate_rows(x, router, routes):
    lane = lax.broadcasted_iota(jnp.int32, (x.shape[0], LANES), 1)
    named = routes[:, 0:1] == lane
    for t in range(1, routes.shape[1]):
        named = named | (routes[:, t : t + 1] == lane)
    logits = jnp.where(named, dot(x, router, ((1,), (0,))), MASKED)
    expos = jnp.where(named, jnp.exp(logits - jnp.max(logits, 1, keepdims=True)), 0.0)
    return expos / jnp.sum(expos, 1, keepdims=True)


def experts_kernel(forward, backward, depth, down_rows, *refs):
    refs = list(refs)
    x_ref, packed_ref, router_ref, pick_ref = [refs.pop(0) for _ in range(4)]
    if forward:
        hit_ref = refs.pop(0)
    else:
        gates_ref, gate_up_ref = refs.pop(0), refs.pop(0)
    d_ref = refs.pop(0) if backward else None
    part_ref = refs.pop(0) if forward else None
    if forward and not backward:
        gates_ref, gate_up_ref = refs.pop(0), refs.pop(0)
    if backward:
        back_ref, grads_ref, router_grad_ref = [refs.pop(0) for _ in range(3)]
    inward, down, weighted, load = [refs.pop(0) for _ in range(4)]
    if forward and backward:
        gates_ref, gate_up_ref = refs.pop(0), refs.pop(0)
    if backward:
        d_gate_up, x_turned, in_grad, down_grad, store = refs

    pieces = expert_pieces(packed_ref, inward, down, depth, down_rows)
    loads = [pltpu.make_async_copy(source, target, load.at[k]) for k, (source, target) in enumerate(pieces)]
    n_down = 4 * packed_ref.shape[0]
    for copy in (loads[n_down:] + loads[:n_down]) if forward else loads:
        copy.start()
    columns = [slice(t * TILE, (t + 1) * TILE) for t in range(2 * FF // TILE)]
    per_expert = FF // TILE
    width = x_ref.shape[1]

    def gate_at(t):
        return slice(2 * FF * (t // per_expert) + TILE * (t % per_expert), 2 * FF * (t // per_expert) + TILE * (t % per_expert + 1))

    def up_at(t):
        return slice(gate_at(t).start + FF, gate_at(t).stop + FF)

    def weight_of(e):
        return jnp.sum(gates_ref[...] * pick_ref[e : e + 1, :], 1, keepdims=True)

    if forward:
        gates_ref[...] = gate_rows(x_ref[...], router_ref[...], hit_ref[...])
        for copy in loads[n_down:]:
            copy.wait()
        for t, place_of in enumerate(columns):
            gate = dot(x_ref[...], inward[:, gate_at(t)], ((1,), (0,)))
            up = dot(x_ref[...], inward[:, up_at(t)], ((1,), (0,)))
            gate_up_ref[:, gate_at(t)] = gate.astype(BF16)
            gate_up_ref[:, up_at(t)] = up.astype(BF16)
            weighted[:, place_of] = (gate / (1.0 + jnp.exp(-gate)) * up * weight_of(t // per_expert)).astype(BF16)
        for copy in loads[:n_down]:
            copy.wait()
        for n in range(width // TILE):
            at = slice(n * TILE, (n + 1) * TILE)
            part_ref[:, at] = (
                dot(weighted[:, :FF], down[0, :, at], ((1,), (0,)))
                + dot(weighted[:, FF:], down[1, :, at], ((1,), (0,)))
            ).astype(BF16)
    else:
        for copy in loads[:n_down]:
            copy.wait()
    if backward:
        d_weight = [0.0, 0.0]
        for t, place_of in enumerate(columns):
            e = t // per_expert
            rows_of = slice(TILE * (t % per_expert), TILE * (t % per_expert + 1))
            weight = weight_of(e)
            d_weighted = dot(d_ref[...], down[e, rows_of, :], ((1,), (1,)))
            gate = gate_up_ref[:, gate_at(t)].astype(F32)
            up = gate_up_ref[:, up_at(t)].astype(F32)
            sigmoid = 1.0 / (1.0 + jnp.exp(-gate))
            activated = gate * sigmoid
            hidden = activated * up
            d_weight[e] = d_weight[e] + jnp.sum(hidden * d_weighted, 1, keepdims=True)
            weighted[:, place_of] = (hidden * weight).astype(BF16)
            d_hidden = d_weighted * weight
            d_gate_up[:, gate_at(t)] = (d_hidden * up * (sigmoid * (1.0 + gate * (1.0 - sigmoid)))).astype(BF16)
            d_gate_up[:, up_at(t)] = (d_hidden * activated).astype(BF16)
        gates = gates_ref[...]
        terms = gates * (pick_ref[0:1, :] * d_weight[0] + pick_ref[1:2, :] * d_weight[1])
        d_logits = terms - gates * jnp.sum(terms, 1, keepdims=True)
        high = d_logits.astype(BF16)
        low = (d_logits - high.astype(F32)).astype(BF16)
        both = jnp.concatenate([high, low], 1)
        if not forward:
            for copy in loads[n_down:]:
                copy.wait()
        for n in range(width // TILE):
            at = slice(n * TILE, (n + 1) * TILE)
            table = router_ref[at, :]
            back_ref[:, at] = (
                dot(d_gate_up[...], inward[at, :], ((1,), (1,)))
                + dot(both, jnp.concatenate([table, table], 1), ((1,), (1,)))
            ).astype(BF16)
        x_turned[...] = jnp.transpose(x_ref[...])
        router_grad = dot(both, x_ref[...], ((0,), (0,)))
        named = router_grad_ref.shape[0]
        router_grad_ref[...] = router_grad[:named] + router_grad[LANES : LANES + named]
        for n in range(2 * 2 * FF // TILE):
            at = slice(n * TILE, (n + 1) * TILE)
            in_grad[:, at] = dot(x_turned[...], d_gate_up[:, at], ((1,), (0,))).astype(BF16)
        for e in range(2):
            turned_hidden = jnp.transpose(weighted[:, e * FF : (e + 1) * FF])
            for n in range(width // TILE):
                at = slice(n * TILE, (n + 1) * TILE)
                down_grad[e, :, at] = dot(turned_hidden, d_ref[:, at], ((1,), (0,))).astype(BF16)
        stores = [
            pltpu.make_async_copy(source, target, store.at[k])
            for k, (target, source) in enumerate(expert_pieces(grads_ref, in_grad, down_grad, depth, down_rows))
        ]
        for copy in stores:
            copy.start()
        for copy in stores:
            copy.wait()


def experts(x, packed, router, pick, n_experts, depth, down_rows, hit=None, kept=None, d_rows=None):
    forward, backward = hit is not None, d_rows is not None
    n_rows, width = x.shape
    any_place = pl.BlockSpec(memory_space=pl.ANY)
    operands = [x, packed, router, pick]
    operands += [hit] if forward else list(kept)
    operands += [d_rows] if backward else []
    in_specs = [VMEM, any_place] + [VMEM] * (len(operands) - 2)
    rows_out = jax.ShapeDtypeStruct((n_rows, width), BF16)
    inner = [jax.ShapeDtypeStruct((n_rows, LANES), F32), jax.ShapeDtypeStruct((n_rows, 4 * FF), BF16)]
    n_pieces = 5 * packed.shape[0]
    scratch = [
        pltpu.VMEM((width, 4 * FF), BF16),
        pltpu.VMEM((2, FF, width), BF16),
        pltpu.VMEM((n_rows, 2 * FF), BF16),
        pltpu.SemaphoreType.DMA((n_pieces,)),
    ]
    outs = []
    out_specs = []
    if forward:
        outs += [rows_out]
        out_specs += [VMEM]
    if forward and not backward:
        outs += inner
        out_specs += [VMEM] * 2
    if backward:
        outs += [rows_out, jax.ShapeDtypeStruct(packed.shape, BF16), jax.ShapeDtypeStruct((n_experts, width), F32)]
        out_specs += [VMEM, any_place, VMEM]
        if forward:
            scratch += [pltpu.VMEM(member.shape, member.dtype) for member in inner]
        scratch += [
            pltpu.VMEM((n_rows, 4 * FF), BF16),
            pltpu.VMEM((width, n_rows), BF16),
            pltpu.VMEM((width, 4 * FF), BF16),
            pltpu.VMEM((2, FF, width), BF16),
            pltpu.SemaphoreType.DMA((n_pieces,)),
        ]
    work = n_rows * 6 * width * FF * 2 * ((1 if forward else 0) + (2 if backward else 0))
    return pl.pallas_call(
        functools.partial(experts_kernel, forward, backward, depth, down_rows),
        out_shape=outs,
        in_specs=in_specs,
        out_specs=out_specs,
        scratch_shapes=scratch,
        compiler_params=pltpu.CompilerParams(vmem_limit_bytes=56 << 20),
        cost_estimate=pl.CostEstimate(flops=2 * work, bytes_accessed=40 << 20, transcendentals=0),
    )(*operands)


def shards(tokens, cotangent, blocks, routes, norm_gain, w_query, key_value_weight, w_attn_out, router, w_in, w_down):
    section, ctx, wt = place()
    n_ctx, n_wt, layers = lax.axis_size("ctx"), lax.axis_size("wt"), lax.axis_size("section")
    micro_count, share, width = tokens.shape
    per_ctx = routes.shape[2]
    seq_len = per_ctx * n_ctx
    per_core = w_in.shape[1] // 2
    n_experts = router.shape[2]
    q_cols = w_query.shape[2] // 2
    depth = w_query.shape[1]

    block_len = seq_len // blocks.shape[1]
    placed = (blocks[:, :, None] * block_len + jnp.arange(block_len, dtype=jnp.int32)[None, None, :]).reshape(
        micro_count, seq_len
    )
    query_place = lax.dynamic_slice_in_dim(placed, ctx * per_ctx, per_ctx, 1)
    later = (jnp.arange(micro_count) > 0)[:, None]
    query_start = jnp.where(later, query_place - query_place % CONT_LEN, 0)
    query_pos = jnp.where(later, seq_len + query_place % CONT_LEN, query_place)
    inverse = jnp.power(ROPE_BASE, -jnp.arange(HEAD_SIZE // 2, dtype=F32) * 2.0 / HEAD_SIZE)
    angles = query_pos.reshape(-1).astype(F32)[:, None] * inverse[None, :]
    cosine, sine = jnp.cos(angles), jnp.sin(angles)
    tables = (
        jnp.tile(cosine, (1, 4)),
        jnp.concatenate([-sine, sine, -sine, sine], 1),
        jnp.transpose(placed.reshape(micro_count, n_ctx, per_ctx), (1, 0, 2)).reshape(n_ctx, -1, 1),
        query_place[:, None, :],
        query_start[:, None, :],
    )

    prepared = prepare(
        15,
        w_query[0],
        key_value_weight[0].reshape(depth, -1),
        w_attn_out[0],
        w_in[0],
        w_down[0],
        routes[0],
        norm_gain[0],
        router[0],
    )
    attn_pack, moe_pack = prepared[:2], prepared[2:4]
    route_pack, gain_pack, router_pack = prepared[4:]

    def unpacked(values, in_rows, down_rows):
        wide = values.shape[-1]
        n = values.shape[0]
        rest = values[:, in_rows + down_rows :]
        rest = jnp.concatenate([rest[..., : wide // 2], rest[..., wide // 2 :]], 1)
        down_part = jnp.concatenate([values[:, in_rows : in_rows + down_rows], rest], 2)
        return values[:, :in_rows].reshape(n * in_rows, wide), down_part.reshape(n * down_rows, -1)

    in_rows, down_rows = w_in.shape[2], w_down.shape[2]

    def gather_experts(pack):
        return lax.all_gather(pack, "ctx", axis=0, tiled=True).reshape((n_ctx,) + pack.shape)

    attn_full = [None, None]

    my_first = wt * 2 * per_core + section * per_core
    n_rows = micro_count * per_ctx

    hits = [route_pack[layer].reshape(n_rows, -1) for layer in range(2)]
    pick = (jnp.arange(LANES)[None, :] == my_first + jnp.arange(8)[:, None]).astype(F32)
    router_wide = [jnp.pad(router_pack[layer], ((0, 0), (0, LANES - n_experts))) for layer in range(2)]

    def full_rows(values):
        return values.reshape(n_rows, width)

    def blocked(values):
        return values.reshape(2 * n_wt, share, width).astype(BF16)

    stream = lax.dynamic_index_in_dim(tokens, section, 0, False).astype(F32)
    top = lax.dynamic_index_in_dim(cotangent, section, 0, False).astype(F32)

    normed_in, full = exchange(0, None, stream, gain=gain_pack[0, 0:1], spread="norm", gather=attn_pack[0])
    attn_full[0] = full.reshape(-1, full.shape[2])
    moe_full = [gather_experts(moe_pack[0]), None]
    saved = []
    outputs = []
    for layer in range(2):
        rows_in = full_rows(normed_in)
        weights = attn_full[layer]
        if layer == 0:
            top_low = lax.dynamic_index_in_dim(cotangent, section, 0, False)
            partial, *heads, attended, d_mixed = attend(2, rows_in, weights, tables, top_low)
        else:
            partial, *heads, attended = attend(3, rows_in, weights, tables)
        middle, normed_mid = exchange(
            4 + layer, blocked(partial), stream, gain=gain_pack[layer, 1:2], spread="norm"
        )
        if layer == 0:
            normed_mid, second = lax.optimization_barrier((normed_mid, moe_pack[1]))
            moe_full[1] = gather_experts(second)
        normed_mid, moe_full[layer] = lax.optimization_barrier((normed_mid, moe_full[layer]))
        rows_mid = full_rows(normed_mid)
        if layer == 0:
            partial, gates, gate_up = experts(
                rows_mid, moe_full[0], router_wide[0], pick, n_experts, in_rows, down_rows, hit=hits[0]
            )
            inner = (gates, gate_up)
        else:
            partial, *back_parts = experts(
                rows_mid, moe_full[1], router_wide[1], pick, n_experts, in_rows, down_rows, hit=hits[1], d_rows=full_rows(d_mixed)
            )
            inner = None
        saved.append(
            dict(
                stream=stream,
                middle=middle,
                rows_in=rows_in,
                rows_mid=rows_mid,
                heads=heads,
                attended=attended,
                inner=inner,
            )
        )
        if layer == 0:
            stream, normed_in, full = exchange(
                6, blocked(partial), middle, gain=gain_pack[1, 0:1], spread="norm", rounded=True, gather=attn_pack[1]
            )
            attn_full[1] = full.reshape(-1, full.shape[2])
            outputs.append(stream.astype(BF16))
        else:
            last_rows = (blocked(partial), middle)
    upstream = top
    grads_in = [None, None]
    attn_grads = [None, None]
    moe_grads = [None, None]
    small = [None, None]
    for layer in (1, 0):
        kept = saved[layer]
        if layer == 0:
            back_parts = experts(
                kept["rows_mid"],
                moe_full[0],
                router_wide[0],
                pick,
                n_experts,
                in_rows,
                down_rows,
                kept=kept["inner"],
                d_rows=full_rows(d_mixed),
            )
        partial, packed_grad, router_grad = back_parts
        if layer == 0:
            partial, packed_grad, moe_grads[1] = lax.optimization_barrier((partial, packed_grad, moe_grads[1]))
        else:
            partial, packed_grad = lax.optimization_barrier((partial, packed_grad))
        moe_grads[layer] = lax.psum_scatter(packed_grad, "ctx", scatter_dimension=0, tiled=False)
        d_middle, gain_grad_mid, d_attn = exchange(
            8 + layer, blocked(partial), upstream, kept["middle"], gain_pack[layer, 1:2], spread="plain"
        )
        rows_a = full_rows(d_attn)
        weights = attn_full[layer]
        if layer == 1:
            partial, raw, last = attend_back(11, rows_a, weights, tables, kept["heads"], last_rows)
            outputs.append(last.astype(BF16))
        else:
            partial, raw = attend_back(10, rows_a, weights, tables, kept["heads"])
        attn_parts = dot(kept["rows_in"], jnp.pad(raw, ((0, 0), (0, weights.shape[1] - raw.shape[1]))), ((0,), (0,)))
        attn_parts = attn_parts + dot(
            rows_a, jnp.pad(kept["attended"], ((0, 0), (weights.shape[1] - kept["attended"].shape[1], 0))), ((0,), (0,))
        )
        attn_parts = attn_parts.astype(BF16).reshape(n_ctx, depth, -1)
        if layer == 1:
            upstream, gain_grad_in, d_mixed, attn_grads[1] = exchange(
                12,
                blocked(partial),
                d_middle,
                kept["stream"],
                gain_pack[1, 0:1],
                spread="plain",
                rounded=True,
                add=attn_parts,
            )
        else:
            upstream, gain_grad_in, attn_grads[0] = exchange(
                1, blocked(partial), d_middle, kept["stream"], gain_pack[0, 0:1], rounded=True, add=attn_parts
            )
        grads_in[layer] = upstream.astype(BF16)
        small[layer] = [router_grad, gain_grad_in, gain_grad_mid]

    def by_core(parts, received):
        return jnp.where(section == 0, parts[0], received), jnp.where(section == 0, received, parts[1])

    small_total, *received = small_sum(14, small[0] + small[1], attn_grads + outputs + grads_in)
    out_pair = jnp.stack(by_core(outputs, received[1]))
    grad_pair = jnp.stack(by_core(grads_in, received[2]))
    piece = width // (n_ctx * n_wt)
    router_total = small_total[:n_experts, :piece]
    gain_total = small_total[n_experts : n_experts + 2, :piece]
    attn_first, attn_second = by_core(attn_grads, received[0])
    kv_at = q_cols
    out_at = q_cols + 2 * HEAD_SIZE
    grad_query = jnp.concatenate([attn_first[:, :kv_at], attn_second[:, :kv_at]], -1)
    grad_kv = jnp.stack([attn_first[:, kv_at:out_at], attn_second[:, kv_at:out_at]], 1)
    grad_out = jnp.concatenate([jnp.transpose(attn_first[:, out_at:]), jnp.transpose(attn_second[:, out_at:])], 0)

    def stacked(halves):
        columns = halves[0].shape[1] // per_core
        return jnp.stack(
            [half[:, e * columns : (e + 1) * columns] for half in halves for e in range(per_core)]
        ).astype(F32)

    moe_grads = [member.reshape(member.shape[-2:]) for member in moe_grads]
    moe_pair = by_core(moe_grads, hand_over(13, moe_grads[0], moe_grads[1]))
    moe_pair = [unpacked(member[None], in_rows, down_rows) for member in moe_pair]
    grad_in = stacked([member[0] for member in moe_pair])
    grad_down = stacked([member[1] for member in moe_pair])
    return (
        out_pair[None],
        grad_pair[None],
        gain_total[None],
        grad_query[None],
        grad_kv[None],
        grad_out[None],
        jnp.transpose(router_total)[None],
        grad_in[None],
        grad_down[None],
    )


def solution(mesh):
    return jax.shard_map(
        shards,
        mesh=mesh,
        in_specs=(
            P(None, ("ctx", "wt"), None),
            P(None, ("ctx", "wt"), None),
            P(),
            P("section", None, "ctx", None),
            P("section", None, None),
            P("section", "ctx", "wt"),
            P("section", "ctx", "wt", None),
            P("section", "wt", "ctx"),
            P("section", None, None),
            P("section", "wt", "ctx", None),
            P("section", "wt", "ctx", None),
        ),
        out_specs=(
            P("section", None, ("ctx", "wt"), None),
            P("section", None, ("ctx", "wt"), None),
            P("section", None, ("ctx", "wt")),
            P("section", "ctx", "wt"),
            P("section", "ctx", "wt", None),
            P("section", "wt", "ctx"),
            P("section", ("ctx", "wt"), None),
            P("section", "wt", "ctx", None),
            P("section", "wt", "ctx", None),
        ),
        check_vma=False,
    )
```

time: 664 us -> 577 us (0.87)
  matrix products: 58.5 us -> 4.08 us
  other arithmetic: 62.7 us -> 19.7 us
  Pallas kernels: 449 us -> 468 us
  blocking collectives: 8.89 us -> 0 us
  waiting for transfers between devices: 0.11 us -> 7.91 us
    pallas_call x4 -> x9, Pallas kernels: 73.3 us -> 160 us  [the longest x3 61.5 us: experts(): pl.pallas_call(functools.partial(experts_kernel, forward, backward, depth...]
    pallas_call x10 -> x8, Pallas kernels: 362 us -> 294 us  [exchange(): pl.pallas_call(functools.partial(exchange_kernel, n_ctx, n_wt, reduce, ba...]
    dot_general x24 -> x4, matrix products: 49.6 us -> 4.08 us  [dot(): lax.dot_general(left, right, (contract, ((), ())), preferred_element_type...]
    concatenate x11 -> x0, other arithmetic: 28.7 us -> none  [the longest x4 24.3 us: packed(): jnp.concatenate([in_part, down_part[:, :wide], jnp.concatenate([rest[:hal...]
    unnamed x263 -> x178, local copies, waits for them, and re-layouts: 29.3 us -> 43 us
    select_n x8 -> x1, other arithmetic: 9.61 us -> 0.25 us  [by_core(): jnp.where(section == 0, parts[0], received)]
    dot_general x4 -> x0, matrix products: 8.94 us -> none  [the longest x2 5.05 us: shards(): lax.dot_general(d_logits, router_pack[layer].astype(F32), (((1,), (1,)),...]
    all_gather x3 -> x0, blocking collectives: 8.89 us -> none  [the longest x1 3.46 us: shards(): router_pack = lax.all_gather(router[0], 'section', axis=0)]
  transfers between devices with their start and end apart: 11 -> 4, of which waited for: 0 -> 2; matrix products, arithmetic and copies ran while one was open for 15% -> 5% of each run, Pallas kernels for 62% -> 75%
where the time goes in v4:
time: 577 us; the launch traced here: 567 us
  Pallas kernels  468 us (81%)
  local copies, waits for them, and re-layouts  52.7 us (9%)
  other arithmetic  19.7 us (3%)
  between operations  15.2 us (3%)
  waiting for transfers between devices  7.91 us (1%)
    pallas_call x8, Pallas kernels, exchange(): pl.pallas_call(functools.partial(exchange_kernel, n_ctx, n_wt, reduce, ba...  294 us
    pallas_call x3, Pallas kernels, experts(): pl.pallas_call(functools.partial(experts_kernel, forward, backward, depth...  61.5 us
    pallas_call x2, Pallas kernels, attend(): pl.pallas_call(functools.partial(attend_kernel, n_ctx, n_wt, bool(riders)...  43.7 us
    pallas_call x2, Pallas kernels, attend_back(): pl.pallas_call(functools.partial(attend_back_kernel, n_ctx, n_wt, bool(ri...  43.2 us
    unnamed x178, local copies, waits for them, and re-layouts  43 us
    pallas_call x1, Pallas kernels, small_sum(): pl.pallas_call(functools.partial(small_sum_kernel, n_ctx, n_wt), out_shap...  12.9 us
  transfers between devices with their start and end apart: 4, of which 2 were waited for; matrix products, arithmetic and copies ran while one was open for 5% of the time, Pallas kernels for 75%

profile of v4, /device:TPU:0, one launch (start us, length us, event | category | flops | bytes accessed | tf_op | source)
XLA Modules:
  0.0 567.3 jit_solution(16581069208987627026)
XLA Ops:
  7.2 1.0 copy.83
  8.2 0.8 copy.64
  9.0 1.0 copy.65
  10.1 1.9 copy-done.12
  12.0 1.4 copy-done.21
  13.4 1.0 copy-done.48
  14.3 1.0 copy-done.49
  16.0 6.9 %shard_map.178 = (bf16[384,512]{1,0:T(8,128)(2,1)S(1)}, bf16[384,512]{1,0:T(8,128)(2,1)S(1)}, bf16[576,2048]{1,0:T(8,128)(2,1)}, bf16[576,2048]{1,0:T(8,128)(2,1...) custom-call(bf16[384,384]{1,0:T(8,128)(2,1)S(1)} %bitcast.165, ...), custom_call_target="tpu_custom_call" | custom-call | tf_op jit(solution)/shard_map/pallas_call | solution.py:905
  22.9 1.4 copy-done.15
  24.3 0.9 copy-done.30
  29.1 1.8 fusion.8
  32.3 0.8 fusion.15
  33.8 1.0 copy-done.45
  34.8 38.1 %shard_map.179 = (bf16[8,64,1536]{2,1,0:T(8,128)(2,1)S(1)}, bf16[4,384,512]{2,1,0:T(8,128)(2,1)S(1)}) custom-call(f32[64,1536]{1,0:T(8,128)S(1)} %get-tuple-element.237.refs_0_.refs_1_.refs_2_, f32[1,1536]{1,0:T(1,128)S(1)} %get-tuple-element.233.refs_1_.refs_3_, bf16[384,512]{1,0:T(8,128)(2,1)S(1)} %copy-done.45), custom_call_target="tpu_custom_call" | custom-call | bytes 115343360 | tf_op jit(solution)/shard_map/pallas_call | solution.py:384
  72.9 2.0 pad_maximum_fusion.sin_ref
  75.6 26.1 %shard_map.180 = (bf16[512,1536]{1,0:T(8,128)(2,1)S(1)}, bf16[2,3,256,128]{3,2,1,0:T(8,128)(2,1)S(1)}, bf16[4,512,128]{2,1,0:T(8,128)(2,1)S(1)}, f32[2,3,256,128...) custom-call(bf16[512,1536]{1,0:T(8,128)(2,1)S(1)} %bitcast.138, ...), custom_call_target="tpu_custom_call" | custom-call | bytes 73400320 | tf_op jit(solution)/shard_map/pallas_call | solution.py:651
  101.7 1.2 copy-done.78
  102.9 33.6 %shard_map.181 = (f32[64,1536]{1,0:T(8,128)S(1)}, bf16[8,64,1536]{2,1,0:T(8,128)(2,1)S(1)}) custom-call(bf16[8,64,1536]{2,1,0:T(8,128)(2,1)S(1)} %bitcast.155, f32[64,1536]{1,0:T(8,128)S(1)} %get-tuple-element.237.refs_0_.refs_1_.refs_2_, f32[1,1536]{1,0:T(1,128)S(1)} %get-tuple-element.232.refs_2_.refs_3_), custom_call_target="tpu_custom_call" | custom-call | bytes 115343360 | tf_op jit(solution)/shard_map/pallas_call | solution.py:384
  137.2 1.2 copy-done.77
  138.5 1.2 slice_bitcast_fusion.12
  139.7 0.8 pad.21.refs_2_
  140.5 0.8 pad.22.refs_2_
  142.0 1.9 fusion.18
  143.8 1.8 all-gather.3.cloned.1.call-done
  145.6 11.7 %shard_map.182 = (bf16[512,1536]{1,0:T(8,128)(2,1)}, f32[512,128]{1,0:T(8,128)}, bf16[512,2048]{1,0:T(8,128)(2,1)}) custom-call(bf16[512,1536]{1,0:T(8,128)(2,1)} %bitcast.168, bf16[4,576,2048]{2,1,0:T(8,128)(2,1)} %bitcast.183, bf16[1536,128]{1,0:T(8,128)(2,1)} %pad.21.refs_2_, f32[8,128]{1,0:T(8,128)} %fusion.9.refs_3_, s32[512,8]{1,0:T(8,128)} %bitcast.178), custom_call_target="tpu_custom_call" | custom-call | flops 9663676416 | bytes 41943040 | tf_op jit(solution)/shard_map/pallas_call | solution.py:1100
  157.4 1.6 copy-done.24
  158.9 39.3 %shard_map.183 = (f32[64,1536]{1,0:T(8,128)S(1)}, bf16[8,64,1536]{2,1,0:T(8,128)(2,1)S(1)}, bf16[4,384,512]{2,1,0:T(8,128)(2,1)S(1)}) custom-call(bf16[8,64,1536]{2,1,0:T(8,128)(2,1)S(1)} %bitcast.160, f32[64,1536]{1,0:T(8,128)S(1)} %copy-done.28, f32[1,1536]{1,0:T(1,128)S(1)} %copy-done.56, bf16[384,512]{1,0:T(8,128)(2,1)S(1)} %copy-done.47), custom_call_target="tpu_custom_call" | custom-call | bytes 115343360 | tf_op jit(solution)/shard_map/pallas_call | solution.py:384
  198.3 17.6 %shard_map.184 = (bf16[512,1536]{1,0:T(8,128)(2,1)S(1)}, bf16[2,3,256,128]{3,2,1,0:T(8,128)(2,1)S(1)}, bf16[4,512,128]{2,1,0:T(8,128)(2,1)S(1)}, f32[2,3,256,128...) custom-call(bf16[512,1536]{1,0:T(8,128)(2,1)S(1)} %bitcast.140, ...), custom_call_target="tpu_custom_call" | custom-call | bytes 73400320 | tf_op jit(solution)/shard_map/pallas_call | solution.py:651
  215.9 0.9 copy-done.33
  219.7 35.5 %shard_map.185 = (f32[64,1536]{1,0:T(8,128)S(1)}, bf16[8,64,1536]{2,1,0:T(8,128)(2,1)S(1)}) custom-call(bf16[8,64,1536]{2,1,0:T(8,128)(2,1)S(1)} %bitcast.156, f32[64,1536]{1,0:T(8,128)S(1)} %get-tuple-element.97.refs_1_.refs_2_, f32[1,1536]{1,0:T(1,128)S(1)} %copy-done.58), custom_call_target="tpu_custom_call" | custom-call | bytes 115343360 | tf_op jit(solution)/shard_map/pallas_call | solution.py:384
  255.9 1.2 copy-done.80
  257.1 6.1 %all-gather.5.cloned.1.call-done = bf16[2304,2048]{1,0:T(8,128)(2,1)} async-done(((bf16[576,2048]{1,0:T(8,128)(2,1)}), bf16[2304,2048]{1,0:T(8,128)(2,1)}) %all-gather.5.cloned.1.call-update) | async-done | bytes 9437200 | tf_op jit(solution)/shard_map/all_gather | solution.py:1166
  263.2 28.1 %shard_map.186 = (bf16[512,1536]{1,0:T(8,128)(2,1)}, bf16[512,1536]{1,0:T(8,128)(2,1)}, bf16[4,576,2048]{2,1,0:T(8,128)(2,1)}, f32[16,1536]{1,0:T(8,128)}) custom-call(bf16[512,1536]{1,0:T(8,128)(2,1)} %bitcast.172, bf16[4,576,2048]{2,1,0:T(8,128)(2,1)} %bitcast.185, bf16[1536,128]{1,0:T(8,128)(2,1)} %pad.22.refs_2_, f32[8,128]{1,0:T(8,128)} %fusion.9.refs_3_, ...), custom_call_target="tpu_custom_call" | custom-call | flops 28991029248 | bytes 41943040 | tf_op jit(solution)/shard_map/pallas_call | solution.py:1100
  291.4 1.1 copy-done.17
  292.5 1.4 copy-done.23
  293.9 1.0 copy-done.25
  295.6 36.3 %shard_map.187 = (f32[64,1536]{1,0:T(8,128)S(1)}, f32[1,1536]{1,0:T(1,128)S(1)}, bf16[8,64,1536]{2,1,0:T(8,128)(2,1)S(1)}) custom-call(bf16[8,64,1536]{2,1,0:T(8,128)(2,1)S(1)} %bitcast.159, f32[64,1536]{1,0:T(8,128)S(1)} %copy-done.25, f32[64,1536]{1,0:T(8,128)S(1)} %copy-done.17, f32[1,1536]{1,0:T(1,128)S(1)} %copy-done.59), custom_call_target="tpu_custom_call" | custom-call | bytes 115343360 | tf_op jit(solution)/shard_map/pallas_call | solution.py:384
  332.5 1.6 copy-done.26
  334.1 1.1 copy-done.34
  335.2 1.0 copy-done.39
  337.6 22.8 %shard_map.188 = (bf16[512,1536]{1,0:T(8,128)(2,1)S(1)}, bf16[512,384]{1,0:T(8,128)(2,1)S(1)}, f32[64,1536]{1,0:T(8,128)S(1)}) custom-call(bf16[512,1536]{1,0:T(8,128)(2,1)S(1)} %bitcast.150, bf16[1536,512]{1,0:T(8,128)(2,1)S(1)} %bitcast.149, f32[512,128]{1,0:T(8,128)S(1)} %copy.68.cos_ref, f32[512,128]{1,0:T(8,128)S(1)} %pad_maximum_fusion.sin_ref, ...), custom_call_target="tpu_custom_call" | custom-call | bytes 104857600 | tf_op jit(solution)/shard_map/pallas_call | solution.py:798
  360.5 1.0 fusion.6
  361.6 1.0 fusion
  362.6 44.7 %shard_map.189 = (f32[64,1536]{1,0:T(8,128)S(1)}, f32[1,1536]{1,0:T(1,128)S(1)}, bf16[8,64,1536]{2,1,0:T(8,128)(2,1)S(1)}, f32[384,512]{1,0:T(8,128)S(1)}) custom-call(bf16[8,64,1536]{2,1,0:T(8,128)(2,1)S(1)} %bitcast.154, f32[64,1536]{1,0:T(8,128)S(1)} %get-tuple-element.119.refs_1_, f32[64,1536]{1,0:T(8,128)S(1)} %copy-done.3, f32[1,1536]{1,0:T(1,128)S(1)} %copy-done.57, ...), custom_call_target="tpu_custom_call" | custom-call | bytes 115343360 | tf_op jit(solution)/shard_map/pallas_call | solution.py:384
  408.1 0.9 copy-done.13
  409.6 1.1 copy-done.79
  410.8 21.7 %shard_map.190 = (bf16[512,1536]{1,0:T(8,128)(2,1)}, bf16[4,576,2048]{2,1,0:T(8,128)(2,1)}, f32[16,1536]{1,0:T(8,128)}) custom-call(bf16[512,1536]{1,0:T(8,128)(2,1)} %bitcast.169, bf16[4,576,2048]{2,1,0:T(8,128)(2,1)} %bitcast.184, bf16[1536,128]{1,0:T(8,128)(2,1)} %pad.21.refs_2_, f32[8,128]{1,0:T(8,128)} %fusion.9.refs_3_, ...), custom_call_target="tpu_custom_call" | custom-call | flops 19327352832 | bytes 41943040 | tf_op jit(solution)/shard_map/pallas_call | solution.py:1100
  432.5 1.1 convert_element_type.73.refs_8_
  433.6 1.1 convert_element_type.77.refs_9_
  434.7 1.1 convert_element_type.79.refs_11_
  435.9 1.4 copy-done.22
  437.3 35.2 %shard_map.191 = (f32[64,1536]{1,0:T(8,128)S(1)}, f32[1,1536]{1,0:T(1,128)S(1)}, bf16[8,64,1536]{2,1,0:T(8,128)(2,1)S(1)}) custom-call(bf16[8,64,1536]{2,1,0:T(8,128)(2,1)S(1)} %bitcast.158, f32[64,1536]{1,0:T(8,128)S(1)} %copy-done.10, f32[64,1536]{1,0:T(8,128)S(1)} %copy-done.29, f32[1,1536]{1,0:T(1,128)S(1)} %get-tuple-element.232.refs_2_.refs_3_), custom_call_target="tpu_custom_call" | custom-call | bytes 115343360 | tf_op jit(solution)/shard_map/pallas_call | solution.py:384
  472.6 20.4 %shard_map.192 = (bf16[512,1536]{1,0:T(8,128)(2,1)S(1)}, bf16[512,384]{1,0:T(8,128)(2,1)S(1)}) custom-call(bf16[512,1536]{1,0:T(8,128)(2,1)S(1)} %bitcast.146, bf16[1536,512]{1,0:T(8,128)(2,1)S(1)} %bitcast.145, f32[512,128]{1,0:T(8,128)S(1)} %copy.68.cos_ref, f32[512,128]{1,0:T(8,128)S(1)} %pad_maximum_fusion.sin_ref, s32[4,512,1]{2,1,0:T(8,128)S(1)} %copy.69.key_place, ...), custom_call_target="tpu_custom_call" | custom-call | bytes 104857600 | tf_op jit(solution)/shard_map/pallas_call | solution.py:798
  493.0 1.0 fusion.3
  494.0 1.0 fusion.1
  495.1 31.8 %shard_map.193 = (f32[64,1536]{1,0:T(8,128)S(1)}, f32[1,1536]{1,0:T(1,128)S(1)}, f32[384,512]{1,0:T(8,128)S(1)}) custom-call(bf16[8,64,1536]{2,1,0:T(8,128)(2,1)S(1)} %bitcast.153, f32[64,1536]{1,0:T(8,128)S(1)} %get-tuple-element.135.refs_1_, f32[64,1536]{1,0:T(8,128)S(1)} %get-tuple-element.237.refs_0_.refs_1_.refs_2_, ...), custom_call_target="tpu_custom_call" | custom-call | bytes 115343360 | tf_op jit(solution)/shard_map/pallas_call | solution.py:384
  526.9 12.9 %shard_map.194 = (f32[24,128]{1,0:T(8,128)S(1)}, f32[384,512]{1,0:T(8,128)S(1)}, bf16[64,1536]{1,0:T(8,128)(2,1)S(1)}, bf16[64,1536]{1,0:T(8,128)(2,1)S(1)}) custom-call(f32[16,1536]{1,0:T(8,128)S(1)} %copy-done.55, f32[1,1536]{1,0:T(1,128)S(1)} %get-tuple-element.138.refs_1_, f32[1,1536]{1,0:T(1,128)S(1)} %get-tuple-element.139.refs_2_, ...), custom_call_target="tpu_custom_call" | custom-call | bytes 41943040 | tf_op jit(solution)/shard_map/pallas_call | solution.py:471
  540.4 1.1 copy.76
  542.0 1.1 copy.77
  543.0 1.0 maximum_bitcast_fusion.2
  546.8 4.9 shard_map.195
  551.7 2.8 select_bitcast_fusion.1
  555.4 3.0 maximum_convert_fusion
  558.4 1.9 maximum_convert_fusion.1
  (208 shorter events, 21.3 us)
Async XLA Ops:
  7.2 138.4 %all-gather.3.cloned.1.call-start = ((), (), s32[]{:S(2)}) async-start(), calls=%async_computation.2 | async-start | bytes 11796480 | tf_op jit(solution)/shard_map/all_gather | solution.py:1166
  10.1 1.9 copy-start.12
  12.0 1.4 copy-start.21
  22.9 1.4 copy-start.15
  27.6 235.6 %all-gather.5.cloned.1.call-start = ((), (), s32[]{:S(2)}) async-start(), calls=%async_computation.3 | async-start | bytes 11796480 | tf_op jit(solution)/shard_map/all_gather | solution.py:1166
  28.2 4.1 copy-start.82
  28.2 4.1 copy-start.83
  32.3 42.6 %copy-start.64 = (s32[2,1,256]{2,1,0:T(1,128)S(1)}, s32[2,1,256]{2,1,0:T(1,128)}, u32[]{:S(2)}) copy-start(s32[2,1,256]{2,1,0:T(1,128)} %broadcast_in_dim.62.query_start) | copy-start | bytes 6148
  72.9 28.8 %copy-start.5 = (bf16[4,384,512]{2,1,0:T(8,128)(2,1)}, bf16[4,384,512]{2,1,0:T(8,128)(2,1)S(1)}, u32[]{:S(2)}) copy-start(bf16[4,384,512]{2,1,0:T(8,128)(2,1)S(1)} %get-tuple-element.84) | copy-start | bytes 4718596
  101.7 1.2 copy-start.78
  102.9 33.6 %copy-start.31 = (f32[2,3,256,128]{3,2,1,0:T(8,128)}, f32[2,3,256,128]{3,2,1,0:T(8,128)S(1)}, u32[]{:S(2)}) copy-start(f32[2,3,256,128]{3,2,1,0:T(8,128)S(1)} %get-tuple-element.132.out_ref) | copy-start | bytes 2359300
  102.9 35.5 %copy-start.35 = (bf16[4,512,128]{2,1,0:T(8,128)(2,1)}, bf16[4,512,128]{2,1,0:T(8,128)(2,1)S(1)}, u32[]{:S(2)}) copy-start(bf16[4,512,128]{2,1,0:T(8,128)(2,1)S(1)} %get-tuple-element.131.pairs_ref) | copy-start | bytes 1572868
  102.9 35.5 %copy-start.42 = (bf16[2,3,256,128]{3,2,1,0:T(8,128)(2,1)}, bf16[2,3,256,128]{3,2,1,0:T(8,128)(2,1)S(1)}, u32[]{:S(2)}) copy-start(bf16[2,3,256,128]{3,2,1,0:T(8,128)(2,1)S(1)} %get-tuple-element.130.q_ref) | copy-start | bytes 1179652
  102.9 35.5 %copy-start.50 = (bf16[512,256]{1,0:T(8,128)(2,1)}, bf16[512,256]{1,0:T(8,128)(2,1)S(1)}, u32[]{:S(2)}) copy-start(bf16[512,256]{1,0:T(8,128)(2,1)S(1)} %get-tuple-element.137) | copy-start | bytes 786436
  102.9 35.5 %copy-start.69 = (f32[2,3,1,256]{3,2,1,0:T(1,128)}, f32[2,3,1,256]{3,2,1,0:T(1,128)S(1)}, u32[]{:S(2)}) copy-start(f32[2,3,1,256]{3,2,1,0:T(1,128)S(1)} %get-tuple-element.133.lse_ref) | copy-start | bytes 18436
  137.2 1.2 copy-start.77
  138.4 294.0 %reduce-scatter.7.cloned.1.call-start = ((), (), s32[]{:S(2)}) async-start(), calls=%async_computation.4 | async-start | bytes 11796480
  145.6 11.7 %copy-start.28 = (f32[64,1536]{1,0:T(8,128)S(1)}, f32[64,1536]{1,0:T(8,128)}, u32[]{:S(2)}) copy-start(f32[64,1536]{1,0:T(8,128)} %copy-done.27) | copy-start | bytes 1179652
  145.6 11.8 %copy-start.47 = (bf16[384,512]{1,0:T(8,128)(2,1)S(1)}, bf16[384,512]{1,0:T(8,128)(2,1)}, u32[]{:S(2)}) copy-start(bf16[384,512]{1,0:T(8,128)(2,1)} %copy-done.46) | copy-start | bytes 1179652
  145.6 11.8 %copy-start.56 = (f32[1,1536]{1,0:T(1,128)S(1)}, f32[1,1536]{1,0:T(1,128)}, u32[]{:S(2)}) copy-start(f32[1,1536]{1,0:T(1,128)} %get-tuple-element.231.refs_2_.refs_3_) | copy-start | bytes 18436
  157.3 41.0 %copy-start.61 = (s32[2,1,256]{2,1,0:T(1,128)S(1)}, s32[2,1,256]{2,1,0:T(1,128)}, u32[]{:S(2)}) copy-start(s32[2,1,256]{2,1,0:T(1,128)} %broadcast_in_dim.61.query_place) | copy-start | bytes 6148
  157.3 41.0 %copy-start.65 = (s32[2,1,256]{2,1,0:T(1,128)S(1)}, s32[2,1,256]{2,1,0:T(1,128)}, u32[]{:S(2)}) copy-start(s32[2,1,256]{2,1,0:T(1,128)} %broadcast_in_dim.62.query_start) | copy-start | bytes 6148
  157.4 1.6 copy-start.24
  198.2 17.7 %copy-start = (bf16[8,64,1536]{2,1,0:T(8,128)(2,1)}, bf16[8,64,1536]{2,1,0:T(8,128)(2,1)S(1)}, u32[]{:S(2)}) copy-start(bf16[8,64,1536]{2,1,0:T(8,128)(2,1)S(1)} %get-tuple-element.100) | copy-start | bytes 4718596
  198.2 17.7 %copy-start.7 = (bf16[4,384,512]{2,1,0:T(8,128)(2,1)}, bf16[4,384,512]{2,1,0:T(8,128)(2,1)S(1)}, u32[]{:S(2)}) copy-start(bf16[4,384,512]{2,1,0:T(8,128)(2,1)S(1)} %get-tuple-element.101) | copy-start | bytes 4718596
  198.3 21.4 %copy-start.2 = (f32[64,1536]{1,0:T(8,128)}, f32[64,1536]{1,0:T(8,128)S(1)}, u32[]{:S(2)}) copy-start(f32[64,1536]{1,0:T(8,128)S(1)} %get-tuple-element.97.refs_1_.refs_2_) | copy-start | bytes 1179652
  198.3 21.4 %copy-start.58 = (f32[1,1536]{1,0:T(1,128)S(1)}, f32[1,1536]{1,0:T(1,128)}, u32[]{:S(2)}) copy-start(f32[1,1536]{1,0:T(1,128)} %get-tuple-element.230.refs_2_.refs_3_) | copy-start | bytes 18436
  255.9 1.2 copy-start.80
  291.4 255.5 %reduce-scatter.9.cloned.1.call-start = ((), (), s32[]{:S(2)}) async-start(), calls=%async_computation.5 | async-start | bytes 11796480
  291.4 41.1 %copy-start.8 = (bf16[4,384,512]{2,1,0:T(8,128)(2,1)S(1)}, bf16[4,384,512]{2,1,0:T(8,128)(2,1)}, u32[]{:S(2)}) copy-start(bf16[4,384,512]{2,1,0:T(8,128)(2,1)} %copy-done.7) | copy-start | bytes 4718596
  291.4 1.1 copy-start.17
  292.5 1.4 copy-start.23
  295.6 36.9 %copy-start.18 = (f32[64,1536]{1,0:T(8,128)S(1)}, f32[64,1536]{1,0:T(8,128)}, u32[]{:S(2)}) copy-start(f32[64,1536]{1,0:T(8,128)} %copy-done.16) | copy-start | bytes 1179652
  295.6 36.9 %copy-start.41 = (bf16[2,3,256,128]{3,2,1,0:T(8,128)(2,1)S(1)}, bf16[2,3,256,128]{3,2,1,0:T(8,128)(2,1)}, u32[]{:S(2)}) copy-start(bf16[2,3,256,128]{3,2,1,0:T(8,128)(2,1)} %copy-done.40) | copy-start | bytes 1179652
  295.6 36.9 %copy-start.76 = (f32[2,3,1,256]{3,2,1,0:T(1,128)S(1)}, f32[2,3,1,256]{3,2,1,0:T(1,128)}, u32[]{:S(2)}) copy-start(f32[2,3,1,256]{3,2,1,0:T(1,128)} %copy-done.75) | copy-start | bytes 18436
  332.5 1.6 copy-start.26
  334.1 1.1 copy-start.34
  335.2 1.0 copy-start.39
  337.6 22.8 %copy-start.1 = (bf16[8,64,1536]{2,1,0:T(8,128)(2,1)S(1)}, bf16[8,64,1536]{2,1,0:T(8,128)(2,1)}, u32[]{:S(2)}) copy-start(bf16[8,64,1536]{2,1,0:T(8,128)(2,1)} %copy-done) | copy-start | bytes 4718596
  360.5 1.0 copy-start.19
  360.5 1.1 copy-start.53
  361.6 1.0 copy-start.3
  361.6 1.0 copy-start.57
  409.6 1.1 copy-start.79
  432.5 3.3 copy-start.10
  432.5 3.3 copy-start.29
  433.6 38.9 %copy-start.43 = (bf16[2,3,256,128]{3,2,1,0:T(8,128)(2,1)S(1)}, bf16[2,3,256,128]{3,2,1,0:T(8,128)(2,1)}, u32[]{:S(2)}) copy-start(bf16[2,3,256,128]{3,2,1,0:T(8,128)(2,1)} %copy-done.42) | copy-start | bytes 1179652
  434.7 37.8 %copy-start.6 = (bf16[4,384,512]{2,1,0:T(8,128)(2,1)S(1)}, bf16[4,384,512]{2,1,0:T(8,128)(2,1)}, u32[]{:S(2)}) copy-start(bf16[4,384,512]{2,1,0:T(8,128)(2,1)} %copy-done.5) | copy-start | bytes 4718596
  435.9 1.4 copy-start.22
  437.3 35.2 %copy-start.32 = (f32[2,3,256,128]{3,2,1,0:T(8,128)S(1)}, f32[2,3,256,128]{3,2,1,0:T(8,128)}, u32[]{:S(2)}) copy-start(f32[2,3,256,128]{3,2,1,0:T(8,128)} %copy-done.31) | copy-start | bytes 2359300
  437.3 35.2 %copy-start.36 = (bf16[4,512,128]{2,1,0:T(8,128)(2,1)S(1)}, bf16[4,512,128]{2,1,0:T(8,128)(2,1)}, u32[]{:S(2)}) copy-start(bf16[4,512,128]{2,1,0:T(8,128)(2,1)} %copy-done.35) | copy-start | bytes 1572868
  437.3 35.2 %copy-start.63 = (s32[2,1,256]{2,1,0:T(1,128)S(1)}, s32[2,1,256]{2,1,0:T(1,128)}, u32[]{:S(2)}) copy-start(s32[2,1,256]{2,1,0:T(1,128)} %broadcast_in_dim.61.query_place) | copy-start | bytes 6148
  437.3 35.2 %copy-start.67 = (s32[2,1,256]{2,1,0:T(1,128)S(1)}, s32[2,1,256]{2,1,0:T(1,128)}, u32[]{:S(2)}) copy-start(s32[2,1,256]{2,1,0:T(1,128)} %broadcast_in_dim.62.query_start) | copy-start | bytes 6148
  437.3 35.2 %copy-start.70 = (f32[2,3,1,256]{3,2,1,0:T(1,128)S(1)}, f32[2,3,1,256]{3,2,1,0:T(1,128)}, u32[]{:S(2)}) copy-start(f32[2,3,1,256]{3,2,1,0:T(1,128)} %copy-done.69) | copy-start | bytes 18436
  492.9 1.0 copy-start.51
  495.0 31.9 %copy-start.14 = (f32[384,512]{1,0:T(8,128)S(1)}, f32[384,512]{1,0:T(8,128)}, u32[]{:S(2)}) copy-start(f32[384,512]{1,0:T(8,128)} %copy-done.13) | copy-start | bytes 2359300
  495.0 31.9 %copy-start.54 = (f32[16,1536]{1,0:T(8,128)S(1)}, f32[16,1536]{1,0:T(8,128)}, u32[]{:S(2)}) copy-start(f32[16,1536]{1,0:T(8,128)} %get-tuple-element.140.refs_3_) | copy-start | bytes 294916
  495.0 31.9 %copy-start.55 = (f32[16,1536]{1,0:T(8,128)S(1)}, f32[16,1536]{1,0:T(8,128)}, u32[]{:S(2)}) copy-start(f32[16,1536]{1,0:T(8,128)} %get-tuple-element.123.refs_0_) | copy-start | bytes 294916
  495.0 31.9 %copy-start.72 = (f32[1,1536]{1,0:T(1,128)S(1)}, f32[1,1536]{1,0:T(1,128)}, u32[]{:S(2)}) copy-start(f32[1,1536]{1,0:T(1,128)} %copy-done.71) | copy-start | bytes 18436
  495.1 31.9 %copy-start.74 = (f32[1,1536]{1,0:T(1,128)S(1)}, f32[1,1536]{1,0:T(1,128)}, u32[]{:S(2)}) copy-start(f32[1,1536]{1,0:T(1,128)} %copy-done.73) | copy-start | bytes 18436
  541.9 3.2 copy-start.4
  541.9 3.2 copy-start.20
  543.0 3.0 copy-start.11
  546.8 4.9 copy-start.81
  (25 other events, 19.3 us)
Sparse Core Ops, SparseCore 0:
  27.7 117.8 all-gather.2
  148.0 115.1 all-gather.4
  291.5 117.4 reduce-scatter.6
  432.6 113.6 reduce-scatter.8

commit v5 on v4

--- a/solution.py
+++ b/solution.py
@@ -80,6 +80,10 @@
     return slice(chunk * rows, (chunk + 1) * rows)
 
 
+def block_at(last, block, rightward):
+    return last + 1 - block if rightward else block - 1
+
+
 class RowSum:
     def __init__(self, near, chunks, parts, scratch):
         self.near, self.chunks, self.parts = near, chunks, parts
@@ -153,6 +157,17 @@
         pl.when((wt < far) & lower)(lambda: self.send_on(chunk, far, True))
         pl.when(wt > near)(lambda: self.send_on(chunk, near, False))
         pl.when((wt < far) & jnp.logical_not(lower))(lambda: self.send_on(chunk, far, True))
+
+    def point(self, chunk, number):
+        wt, last = self.near.wt, self.near.n_wt - 1
+        for block in range(1, last + 1):
+            turn = last - block
+            if number == 0:
+                pl.when(wt == 0)(functools.partial(self.send_on, chunk, block_at(last, block, True), True))
+                pl.when(wt == last)(functools.partial(self.send_on, chunk, block_at(last, block, False), False))
+            elif 1 <= number - turn < block:
+                pl.when(wt == number - turn)(functools.partial(self.send_on, chunk, block, True))
+                pl.when(wt == last - (number - turn))(functools.partial(self.send_on, chunk, last - block, False))
 
     def collect(self, chunk, result):
         at, wt = rows_of(chunk, self.rows), self.near.wt
@@ -260,9 +275,12 @@
     gain_grad_ref = refs.pop(0) if back else None
     all_ref = refs.pop(0) if spread else None
     rode_ref = refs.pop(0) if ride else None
+    token_ref = refs.pop(0)
+    token_ref[...] = jnp.zeros(token_ref.shape, F32)
     if reduce:
         sums = RowSum(near, CHUNKS, parts, refs[:9])
         refs = refs[9:]
+        sum_ref = refs.pop(0) if rounded else result_ref
     if spread:
         gathers = RowGather(near, CHUNKS, all_ref, refs[:4])
         refs = refs[4:]
@@ -292,10 +310,10 @@
     def settle(chunk):
         at = rows_of(chunk, chunk_rows)
         if reduce:
-            sums.collect(chunk, result_ref)
-            total = result_ref[at, :]
+            sums.collect(chunk, sum_ref)
+            total = sum_ref[at, :]
             if back:
-                stream = stream_ref[at, :]
+                stream = stream_ref[at, :].astype(F32)
                 scale = norm_scale(stream)
                 weighted = gain_ref[...] * total
                 gain_part = jnp.sum(total * stream * scale, 0, keepdims=True)
@@ -305,8 +323,9 @@
                 )
             total = rows_ref[at, :].astype(F32) + total
             if rounded:
-                total = total.astype(BF16).astype(F32)
+                total = total.astype(BF16)
             result_ref[at, :] = total
+            total = total.astype(F32)
         else:
             total = rows_ref[at, :].astype(F32)
         if spread:
@@ -368,8 +387,9 @@
     scratch = []
     dma = pltpu.SemaphoreType.DMA
     if reduce:
-        outs.append(jax.ShapeDtypeStruct(shape, F32))
+        outs.append(jax.ShapeDtypeStruct(shape, BF16 if rounded else F32))
         scratch += RowSum.scratch(n_wt, shape, CHUNKS)
+        scratch += [pltpu.VMEM(shape, F32)] if rounded else []
     if back:
         outs.append(jax.ShapeDtypeStruct((1, shape[1]), F32))
     if spread:
@@ -381,6 +401,7 @@
     elif ride == "sum":
         outs.append(jax.ShapeDtypeStruct(rider.shape[1:], F32))
         scratch += [pltpu.VMEM((n_ctx - 1,) + rider.shape[1:], BF16), dma((n_ctx - 1,)), dma((n_ctx - 1,)), dma]
+    outs.append(jax.ShapeDtypeStruct((8, LANES), F32))
     return pl.pallas_call(
         functools.partial(exchange_kernel, n_ctx, n_wt, reduce, back, spread, rounded, ride),
         out_shape=outs,
@@ -388,16 +409,16 @@
         out_specs=[VMEM] * len(outs),
         scratch_shapes=scratch,
         compiler_params=pltpu.CompilerParams(
-            collective_id=number, has_side_effects=True, vmem_limit_bytes=40 << 20
+            collective_id=number, has_side_effects=True, vmem_limit_bytes=16 << 20
         ),
         cost_estimate=pl.CostEstimate(flops=0, bytes_accessed=110 << 20, transcendentals=0),
     )(*operands)
 
 
-def small_sum_kernel(n_ctx, n_wt, *refs):
-    small, kept = refs[:6], refs[6:12]
-    total_ref, attn_ref, out_ref, grad_ref = refs[12:16]
-    parts, landed, summed, from_sibling, send, recv, swap_send, swap_recv = refs[16:]
+def finish_kernel(n_ctx, n_wt, *refs):
+    small, attn, rows = refs[:6], refs[6:8], refs[8:12]
+    gain_ref, router_ref, query_ref, pair_ref, out_ref, rows_ref, grads_ref = refs[12:19]
+    parts, landed, summed, from_sibling, received, send, recv, swap_send, swap_recv = refs[19:]
     section, ctx, wt = place()
     count = n_ctx * n_wt
     own = ctx * n_wt + wt
@@ -405,9 +426,19 @@
     peers = [(section, block // n_wt, lax.rem(block, n_wt)) for block in blocks]
     sibling = (1 - section, ctx, wt)
     greet([sibling] + peers)
-    members = list(zip(kept[0::2], kept[1::2], (attn_ref, out_ref, grad_ref)))
-    swaps = swap_copies(section, sibling, members, swap_send, swap_recv)
-    start_swaps(section, swaps)
+    members = [(attn[0], attn[1], received)]
+    members += [(rows[0], rows[1], rows_ref.at[section]), (rows[2], rows[3], grads_ref.at[section])]
+    swaps = [
+        [remote(member[1 - layer], member[2], swap_send.at[k], swap_recv.at[k], sibling) for k, member in enumerate(members)]
+        for layer in range(2)
+    ]
+    for layer in range(2):
+
+        @pl.when(section == layer)
+        def _():
+            for copy in swaps[layer]:
+                copy.start()
+
     piece = small[0].shape[1] // count
     parts[...] = jnp.zeros(parts.shape, F32)
     for block in range(count):
@@ -422,6 +453,19 @@
     ]
     for copy in copies:
         copy.start()
+    mine = section == 0
+    rows_ref[section] = jnp.where(mine, rows[0][...], rows[1][...])
+    grads_ref[section] = jnp.where(mine, rows[2][...], rows[3][...])
+    for copy in swaps[0]:
+        copy.wait_recv()
+    held = jnp.where(mine, attn[0][...], attn[1][...])
+    came = received[...]
+    first, second = jnp.where(mine, held, came), jnp.where(mine, came, held)
+    q_cols = query_ref.shape[1] // 2
+    at = q_cols + LANES
+    query_ref[...] = jnp.concatenate([first[:, :q_cols], second[:, :q_cols]], 1)
+    pair_ref[...] = jnp.concatenate([first[:, q_cols:at], second[:, q_cols:at]], 1)
+    out_ref[...] = jnp.transpose(jnp.concatenate([first[:, at:], second[:, at:]], 1))
     total = parts[own]
     for k, copy in enumerate(copies):
         copy.wait_recv()
@@ -430,86 +474,103 @@
     swap = remote(summed.at[1 - section], from_sibling, send.at[count - 1], recv.at[count - 1], sibling)
     swap.start()
     swap.wait()
-    total_ref[...] = summed[section] + from_sibling[...]
+    total = summed[section] + from_sibling[...]
+    named = small[0].shape[0]
+    gain_ref[...] = total[named : named + 2, :]
+    router_ref[...] = total[:named, :]
     for copy in copies:
         copy.wait_send()
-    wait_swaps(section, swaps)
-
-
-def swap_copies(section, sibling, members, send, recv):
-    return [
-        [remote(pair[1 - layer], pair[2], send.at[k], recv.at[k], sibling) for k, pair in enumerate(members)]
-        for layer in range(2)
-    ]
-
-
-def start_swaps(section, swaps):
-    for layer in range(2):
-
-        @pl.when(section == layer)
-        def _():
-            for copy in swaps[layer]:
-                copy.start()
-
-
-def wait_swaps(section, swaps):
-    for layer in range(2):
-
-        @pl.when(section == layer)
-        def _():
-            for copy in swaps[layer]:
-                copy.wait()
-
-
-def small_sum(number, small, kept):
+    for copy in swaps[0]:
+        copy.wait_send()
+
+
+def finish(number, small, attn, rows, q_cols):
     n_ctx, n_wt = lax.axis_size("ctx"), lax.axis_size("wt")
     count = n_ctx * n_wt
-    rows = sum(member.shape[0] for member in small[:3])
-    shape = (2, rows + -rows % 8, LANES)
+    named = small[0].shape[0]
+    shape = (2, named + 2 + -(named + 2) % 8, LANES)
     dma = pltpu.SemaphoreType.DMA
-    any_place = pl.BlockSpec(memory_space=pl.ANY)
+    depth = attn[0].shape[0]
+    pair = jax.ShapeDtypeStruct((2,) + rows[0].shape, BF16)
     return pl.pallas_call(
-        functools.partial(small_sum_kernel, n_ctx, n_wt),
-        out_shape=[jax.ShapeDtypeStruct(shape[1:], F32)]
-        + [jax.ShapeDtypeStruct(member.shape, member.dtype) for member in kept[0::2]],
-        in_specs=[VMEM] * 6 + [any_place] * 6,
-        out_specs=[VMEM] + [any_place] * 3,
+        functools.partial(finish_kernel, n_ctx, n_wt),
+        out_shape=[
+            jax.ShapeDtypeStruct((2, LANES), F32),
+            jax.ShapeDtypeStruct((named, LANES), F32),
+            jax.ShapeDtypeStruct((depth, 2 * q_cols), F32),
+            jax.ShapeDtypeStruct((depth, 2 * LANES), F32),
+            jax.ShapeDtypeStruct((2 * q_cols, depth), F32),
+            pair,
+            pair,
+        ],
+        in_specs=[VMEM] * 12,
+        out_specs=[VMEM] * 7,
         scratch_shapes=[
             pltpu.VMEM((count,) + shape, F32),
             pltpu.VMEM((count - 1,) + shape, F32),
             pltpu.VMEM(shape, F32),
             pltpu.VMEM(shape[1:], F32),
+            pltpu.VMEM(attn[0].shape, F32),
             dma((count,)),
             dma((count,)),
             dma((3,)),
             dma((3,)),
         ],
         compiler_params=pltpu.CompilerParams(
-            collective_id=number, has_side_effects=True, vmem_limit_bytes=40 << 20
+            collective_id=number, has_side_effects=True, vmem_limit_bytes=16 << 20
         ),
         cost_estimate=pl.CostEstimate(flops=0, bytes_accessed=40 << 20, transcendentals=0),
-    )(*small, *kept)
-
-
-def hand_over_kernel(first, second, result, send, recv):
+    )(*small, *attn, *rows)
+
+
+def hand_over_kernel(per_core, first, second, after, inward, down, held, send, recv, load, keep):
     section, ctx, wt = place()
     sibling = (1 - section, ctx, wt)
+    for layer, own in enumerate((first, second)):
+
+        @pl.when(section == layer)
+        def _():
+            pltpu.make_async_copy(own, held, load).start()
+
+    def moves(source):
+        pieces = expert_halves(inward, down, source, section, per_core)
+        return [remote(piece, target, send.at[k], recv.at[k], sibling) for k, (target, piece) in enumerate(pieces)]
+
     greet([sibling])
-    swaps = swap_copies(section, sibling, [(first, second, result)], send, recv)
-    start_swaps(section, swaps)
-    wait_swaps(section, swaps)
-
-
-def hand_over(number, first, second):
+    for layer, other in enumerate((second, first)):
+
+        @pl.when(section == layer)
+        def _():
+            for copy in moves(other):
+                copy.start()
+
+    pltpu.make_async_copy(first, held, load).wait()
+    pieces = expert_halves(inward, down, held, section, per_core)
+    copies = [pltpu.make_async_copy(piece, target, keep.at[k]) for k, (target, piece) in enumerate(pieces)]
+    for copy in copies:
+        copy.start()
+    for copy in copies:
+        copy.wait()
+    for copy in moves(first):
+        copy.wait()
+
+
+def hand_over(number, first, second, after, depth, down_rows, per_core, width):
     any_place = pl.BlockSpec(memory_space=pl.ANY)
+    dma = pltpu.SemaphoreType.DMA
     return pl.pallas_call(
-        hand_over_kernel,
-        out_shape=jax.ShapeDtypeStruct(first.shape, first.dtype),
-        in_specs=[any_place] * 2,
-        out_specs=any_place,
-        scratch_shapes=[pltpu.SemaphoreType.DMA((1,))] * 2,
-        compiler_params=pltpu.CompilerParams(collective_id=number, has_side_effects=True),
-    )(first, second)
+        functools.partial(hand_over_kernel, per_core),
+        out_shape=[
+            jax.ShapeDtypeStruct((2 * per_core, depth, first.shape[1] // per_core), first.dtype),
+            jax.ShapeDtypeStruct((2 * per_core, down_rows, width), first.dtype),
+        ],
+        in_specs=[any_place] * 3,
+        out_specs=[any_place] * 2,
+        scratch_shapes=[pltpu.VMEM(first.shape, first.dtype), dma((6,)), dma((6,)), dma, dma((6,))],
+        compiler_params=pltpu.CompilerParams(
+            collective_id=number, has_side_effects=True, vmem_limit_bytes=60 << 20
+        ),
+    )(first, second, after)
 
 
 HEADS = 3
@@ -670,7 +731,7 @@
         ]
         + (RowGather.scratch(n_wt, 1) if riders else []),
         compiler_params=pltpu.CompilerParams(
-            collective_id=number, has_side_effects=True, vmem_limit_bytes=40 << 20
+            collective_id=number, has_side_effects=True, vmem_limit_bytes=20 << 20
         ),
         cost_estimate=pl.CostEstimate(flops=0, bytes_accessed=70 << 20, transcendentals=0),
     )(rows_in, weights, *tables, *riders)
@@ -703,8 +764,9 @@
     peers = [(section, lax.rem(ctx + k, n_ctx), wt) for k in range(1, n_ctx)]
     waiting = []
     if ride:
-        sums = RowSum(near, 1, ride_refs[0], refs[8:])
-        waiting = [functools.partial(sums.step, 0, step) for step in range(n_wt - 1)]
+        sums = RowSum(near, 1, ride_refs[0], refs[8:17])
+        rode_sum = refs[17]
+        waiting = [functools.partial(sums.point, 0, number) for number in range(n_wt - 1)]
         near.greet(peers)
         sums.begin()
     else:
@@ -754,18 +816,15 @@
         passing(k).start()
 
     sent(1)
+    sent(2)
     ride_on()
-    pl.loop(2, n_ctx)(sent)
-    ride_on()
+    pl.loop(3, n_ctx)(sent)
 
     for j in range(2):
         own_ref[j * rows : (j + 1) * rows, :] = block(ctx, j)
 
     while waiting:
         ride_on()
-    if ride:
-        sums.collect(0, rode_ref)
-        rode_ref[...] += ride_refs[1][...]
 
     @pl.loop(1, n_ctx)
     def _(k):
@@ -785,6 +844,8 @@
     raw_ref[:, 2 * LANES :] = jnp.where(low, over, 0.0).astype(BF16)
     part_ref[...] = dot(raw_ref[...], w_ref[:, : 3 * LANES], ((1,), (1,))).astype(BF16)
     if ride:
+        sums.collect(0, rode_sum)
+        rode_ref[...] = (rode_sum[...] + ride_refs[1][...]).astype(BF16)
         sums.end()
     for k in range(1, n_ctx):
         passing(k).wait_send()
@@ -801,7 +862,7 @@
             jax.ShapeDtypeStruct((n_rows, width), BF16),
             jax.ShapeDtypeStruct((n_rows, 3 * LANES), BF16),
         ]
-        + [jax.ShapeDtypeStruct(member.shape, F32) for member in ride[1:]],
+        + [jax.ShapeDtypeStruct(member.shape, BF16) for member in ride[1:]],
         in_specs=[VMEM] * (11 + len(ride)),
         out_specs=[VMEM] * (2 + len(ride) // 2),
         scratch_shapes=[
@@ -814,9 +875,9 @@
             dma((n_ctx,)),
             dma((n_ctx,)),
         ]
-        + (RowSum.scratch(n_wt, ride[1].shape, 1) if ride else []),
+        + (RowSum.scratch(n_wt, ride[1].shape, 1) + [pltpu.VMEM(ride[1].shape, F32)] if ride else []),
         compiler_params=pltpu.CompilerParams(
-            collective_id=number, has_side_effects=True, vmem_limit_bytes=40 << 20
+            collective_id=number, has_side_effects=True, vmem_limit_bytes=24 << 20
         ),
         cost_estimate=pl.CostEstimate(flops=0, bytes_accessed=100 << 20, transcendentals=0),
     )(rows_a, weights, *tables, *kept, *ride)
@@ -838,13 +899,80 @@
     ]
 
 
-def prepare_kernel(query, pair, out, inward, down, routes, gains, router, *refs):
-    attn, moe = refs[:2], refs[2:4]
-    all_routes, all_gains, all_router, halves, keep_sem, send, recv = refs[4:]
+def prepare_kernel(inward, down, first, second, halves, load, send, recv, keep):
+    packed = (first, second)
     section, ctx, wt = place()
     sibling = (1 - section, ctx, wt)
+    per_core = inward.shape[0] // 2
+    loads = []
+    for half in range(2):
+        for source, target in expert_halves(inward, down, halves.at[half], half, per_core):
+            loads.append(pltpu.make_async_copy(source, target, load.at[len(loads)]))
+    for copy in loads:
+        copy.start()
     greet([sibling])
-    per_core = inward.shape[0] // 2
+    for copy in loads:
+        copy.wait()
+    for layer in range(2):
+
+        @pl.when(section == layer)
+        def _():
+            move = remote(halves.at[1 - layer], packed[layer], send, recv, sibling)
+            move.start()
+            own = pltpu.make_async_copy(halves.at[layer], packed[layer], keep)
+            own.start()
+            own.wait()
+            move.wait_send()
+            remote(halves.at[layer], packed[1 - layer], send, recv, sibling).wait_recv()
+
+
+def prepare(number, inward, down):
+    depth, down_rows = inward.shape[1], down.shape[1]
+    in_place = pl.BlockSpec(memory_space=pltpu.HBM)
+    shape = (depth + down_rows + down_rows // 2, inward.shape[0] // 2 * inward.shape[2])
+    packed = jax.ShapeDtypeStruct(shape, BF16)
+    dma = pltpu.SemaphoreType.DMA
+    return pl.pallas_call(
+        prepare_kernel,
+        out_shape=[packed, packed],
+        in_specs=[in_place] * 2,
+        out_specs=[in_place] * 2,
+        scratch_shapes=[pltpu.VMEM((2,) + shape, BF16), dma((12,)), dma, dma, dma],
+        compiler_params=pltpu.CompilerParams(
+            collective_id=number, has_side_effects=True, vmem_limit_bytes=12 << 20
+        ),
+    )(inward, down)
+
+
+def begin_kernel(n_ctx, n_wt, *refs):
+    given = refs[:7]
+    all_ref, rode_ref, pack, all_gains, all_router, all_routes = refs[7:13]
+    tokens, query, pair, out, gains, router, routes = refs[13:20]
+    halves, first_pack, load, keep, send, recv, ride_send, ride_recv = refs[20:28]
+    near = Near(n_wt)
+    loads = [
+        pltpu.make_async_copy(source.at[near.section] if k == 0 else source, target, load.at[k])
+        for k, (source, target) in enumerate(zip(given, refs[13:20]))
+    ]
+    for copy in loads:
+        copy.start()
+    section, ctx, wt = near.section, near.ctx, near.wt
+    peers = [(section, lax.rem(ctx + k, n_ctx), wt) for k in range(1, n_ctx)]
+    gathers = RowGather(near, CHUNKS, all_ref, refs[28:])
+    near.greet(peers)
+    for copy in loads:
+        copy.wait()
+    named = router.shape[0]
+    all_gains[section] = gains[...]
+    all_routes[section] = routes[...]
+    all_router[section] = jnp.zeros(all_router.shape[1:], BF16)
+    all_router[section, :named, :] = router[...]
+    shared = [
+        remote(ref.at[section], ref.at[section], send.at[k], recv.at[k], near.sibling)
+        for k, ref in enumerate((all_gains, all_router, all_routes))
+    ]
+    for copy in shared:
+        copy.start()
     q_cols = query.shape[1] // 2
     outward = jnp.transpose(out[...].astype(F32))
     for half in range(2):
@@ -856,62 +984,81 @@
             ],
             1,
         ).astype(BF16)
+    packs = (first_pack, pack)
     for layer in range(2):
 
         @pl.when(section == layer)
         def _():
-            own = expert_halves(inward, down, moe[layer], layer, per_core)
-            other = expert_halves(inward, down, moe[layer], 1 - layer, per_core)
-            own += [
-                (halves.at[layer], attn[layer]),
-                (routes, all_routes.at[layer]),
-                (gains, all_gains.at[layer]),
-                (router, all_router.at[layer]),
-            ]
-            other += [
-                (halves.at[1 - layer], attn[layer]),
-                (routes, all_routes.at[layer]),
-                (gains, all_gains.at[layer]),
-                (router, all_router.at[layer]),
-            ]
-            copies = [pltpu.make_async_copy(a, b, keep_sem.at[k]) for k, (a, b) in enumerate(own)]
-            moves = [remote(a, b, send.at[k], recv.at[k], sibling) for k, (a, b) in enumerate(other)]
-            for copy in moves + copies:
-                copy.start()
-            for copy in moves:
-                copy.wait_send()
-            for copy in copies:
-                copy.wait()
-            arrive = expert_halves(inward, down, moe[1 - layer], layer, per_core)
-            arrive += [
-                (halves.at[layer], attn[1 - layer]),
-                (routes, all_routes.at[1 - layer]),
-                (gains, all_gains.at[1 - layer]),
-                (router, all_router.at[1 - layer]),
-            ]
-            for k, (a, b) in enumerate(arrive):
-                remote(a, b, send.at[k], recv.at[k], sibling).wait_recv()
-
-
-def prepare(number, query, pair, out, inward, down, routes, gains, router):
-    depth, down_rows = inward.shape[1], down.shape[1]
-    any_place = pl.BlockSpec(memory_space=pl.ANY)
-    columns = query.shape[1] + LANES
-    wide = inward.shape[0] // 2 * inward.shape[2]
-    packed = jax.ShapeDtypeStruct((depth + down_rows + down_rows // 2, wide), BF16)
-    attn = jax.ShapeDtypeStruct((depth, columns), BF16)
-    both = [jax.ShapeDtypeStruct((2,) + member.shape, member.dtype) for member in (routes, gains, router)]
+            remote(halves.at[1 - layer], packs[layer], send.at[3], recv.at[3], near.sibling).start()
+            packs[layer][...] = halves[layer]
+
+    rows = tokens[...].astype(F32)
+    scaled = rows * norm_scale(rows)
+    shared[0].wait_recv()
+    all_ref[near.own] = (scaled * all_gains[0, 0:1, :]).astype(BF16)
+    for chunk in range(CHUNKS):
+        gathers.first(chunk)
+    for layer in range(2):
+
+        @pl.when(section == layer)
+        def _():
+            remote(halves.at[layer], packs[1 - layer], send.at[3], recv.at[3], near.sibling).wait_recv()
+
+    own = pltpu.make_async_copy(first_pack, rode_ref.at[ctx], keep)
+    riders = [
+        remote(first_pack, rode_ref.at[ctx], ride_send.at[k], ride_recv.at[k], peers[k]) for k in range(n_ctx - 1)
+    ]
+    for copy in riders + [own]:
+        copy.start()
+    for hop in range(1, n_wt):
+        for chunk in range(CHUNKS):
+            gathers.hop(chunk, hop)
+    gathers.arrive()
+    own.wait()
+    for copy in riders:
+        copy.wait()
+    gathers.end()
+    shared[0].wait_send()
+    for copy in shared[1:]:
+        copy.wait()
+    remote(halves.at[0], first_pack, send.at[3], recv.at[3], near.sibling).wait_send()
+
+
+def begin(number, tokens, query, pair, out, gains, router, routes):
+    n_ctx, n_wt = lax.axis_size("ctx"), lax.axis_size("wt")
+    depth, columns = query.shape[0], query.shape[1] + LANES
     dma = pltpu.SemaphoreType.DMA
+    pack = (depth, columns)
     return pl.pallas_call(
-        prepare_kernel,
-        out_shape=[attn, attn, packed, packed] + both,
-        in_specs=[VMEM] * 3 + [any_place] * 5,
-        out_specs=[any_place] * 7,
-        scratch_shapes=[pltpu.VMEM((2, depth, columns), BF16), dma((10,)), dma((10,)), dma((10,))],
+        functools.partial(begin_kernel, n_ctx, n_wt),
+        out_shape=[
+            jax.ShapeDtypeStruct((2 * n_wt,) + tokens.shape[1:], BF16),
+            jax.ShapeDtypeStruct((n_ctx,) + pack, BF16),
+            jax.ShapeDtypeStruct(pack, BF16),
+            jax.ShapeDtypeStruct((2,) + gains.shape, gains.dtype),
+            jax.ShapeDtypeStruct((2, LANES, router.shape[1]), BF16),
+            jax.ShapeDtypeStruct((2,) + routes.shape, routes.dtype),
+        ],
+        in_specs=[pl.BlockSpec(memory_space=pltpu.HBM)] * 7,
+        out_specs=[VMEM] * 6,
+        scratch_shapes=[pltpu.VMEM(tokens.shape[1:], BF16)]
+        + [pltpu.VMEM(member.shape, member.dtype) for member in (query, pair, out, gains, router, routes)]
+        + [
+            pltpu.VMEM((2,) + pack, BF16),
+            pltpu.VMEM(pack, BF16),
+            dma((7,)),
+            dma,
+            dma((4,)),
+            dma((4,)),
+            dma((n_ctx - 1,)),
+            dma((n_ctx - 1,)),
+        ]
+        + RowGather.scratch(n_wt, CHUNKS),
         compiler_params=pltpu.CompilerParams(
-            collective_id=number, has_side_effects=True, vmem_limit_bytes=40 << 20
+            collective_id=number, has_side_effects=True, vmem_limit_bytes=16 << 20
         ),
-    )(query, pair, out, inward, down, routes, gains, router)
+        cost_estimate=pl.CostEstimate(flops=0, bytes_accessed=90 << 20, transcendentals=0),
+    )(tokens, query, pair, out, gains, router, routes)
 
 
 TILE = 256
@@ -941,12 +1088,12 @@
     named = routes[:, 0:1] == lane
     for t in range(1, routes.shape[1]):
         named = named | (routes[:, t : t + 1] == lane)
-    logits = jnp.where(named, dot(x, router, ((1,), (0,))), MASKED)
+    logits = jnp.where(named, dot(x, router, ((1,), (1,))), MASKED)
     expos = jnp.where(named, jnp.exp(logits - jnp.max(logits, 1, keepdims=True)), 0.0)
     return expos / jnp.sum(expos, 1, keepdims=True)
 
 
-def experts_kernel(forward, backward, depth, down_rows, *refs):
+def experts_kernel(n_ctx, layer, forward, backward, depth, down_rows, ride, *refs):
     refs = list(refs)
     x_ref, packed_ref, router_ref, pick_ref = [refs.pop(0) for _ in range(4)]
     if forward:
@@ -954,22 +1101,38 @@
     else:
         gates_ref, gate_up_ref = refs.pop(0), refs.pop(0)
     d_ref = refs.pop(0) if backward else None
+    ride_ref = refs.pop(0) if ride else None
     part_ref = refs.pop(0) if forward else None
     if forward and not backward:
         gates_ref, gate_up_ref = refs.pop(0), refs.pop(0)
     if backward:
         back_ref, grads_ref, router_grad_ref = [refs.pop(0) for _ in range(3)]
+    rode_ref = refs.pop(0) if ride else None
     inward, down, weighted, load = [refs.pop(0) for _ in range(4)]
     if forward and backward:
         gates_ref, gate_up_ref = refs.pop(0), refs.pop(0)
     if backward:
-        d_gate_up, x_turned, in_grad, down_grad, store = refs
+        d_gate_up, x_turned, in_grad, down_grad, store = refs[:5]
+        refs = refs[5:]
 
     pieces = expert_pieces(packed_ref, inward, down, depth, down_rows)
     loads = [pltpu.make_async_copy(source, target, load.at[k]) for k, (source, target) in enumerate(pieces)]
     n_down = 4 * packed_ref.shape[0]
     for copy in (loads[n_down:] + loads[:n_down]) if forward else loads:
         copy.start()
+    if ride:
+        landed, ride_send, ride_recv = refs
+        section, ctx, wt = place()
+        peers = [(section, lax.rem(ctx + k, n_ctx), wt) for k in range(1, n_ctx)]
+        greet(peers)
+        riders = [
+            remote(
+                ride_ref.at[lax.rem(ctx + 1 + k, n_ctx)], landed.at[k], ride_send.at[k], ride_recv.at[k], peers[k]
+            )
+            for k in range(n_ctx - 1)
+        ]
+        for copy in riders:
+            copy.start()
     columns = [slice(t * TILE, (t + 1) * TILE) for t in range(2 * FF // TILE)]
     per_expert = FF // TILE
     width = x_ref.shape[1]
@@ -984,7 +1147,9 @@
         return jnp.sum(gates_ref[...] * pick_ref[e : e + 1, :], 1, keepdims=True)
 
     if forward:
-        gates_ref[...] = gate_rows(x_ref[...], router_ref[...], hit_ref[...])
+        routes = hit_ref[layer]
+        routes = routes.reshape(routes.shape[0] * routes.shape[1], routes.shape[2])
+        gates_ref[...] = gate_rows(x_ref[...], router_ref[layer], routes)
         for copy in loads[n_down:]:
             copy.wait()
         for t, place_of in enumerate(columns):
@@ -1032,40 +1197,53 @@
                 copy.wait()
         for n in range(width // TILE):
             at = slice(n * TILE, (n + 1) * TILE)
-            table = router_ref[at, :]
+            table = router_ref[layer, :, at]
             back_ref[:, at] = (
                 dot(d_gate_up[...], inward[at, :], ((1,), (1,)))
-                + dot(both, jnp.concatenate([table, table], 1), ((1,), (1,)))
+                + dot(both, jnp.concatenate([table, table], 0), ((1,), (0,)))
             ).astype(BF16)
         x_turned[...] = jnp.transpose(x_ref[...])
         router_grad = dot(both, x_ref[...], ((0,), (0,)))
         named = router_grad_ref.shape[0]
         router_grad_ref[...] = router_grad[:named] + router_grad[LANES : LANES + named]
-        for n in range(2 * 2 * FF // TILE):
-            at = slice(n * TILE, (n + 1) * TILE)
-            in_grad[:, at] = dot(x_turned[...], d_gate_up[:, at], ((1,), (0,))).astype(BF16)
+        pieces = expert_pieces(grads_ref, in_grad, down_grad, depth, down_rows)
+        stores = [
+            pltpu.make_async_copy(source, target, store.at[k]) for k, (target, source) in enumerate(pieces)
+        ]
         for e in range(2):
             turned_hidden = jnp.transpose(weighted[:, e * FF : (e + 1) * FF])
             for n in range(width // TILE):
                 at = slice(n * TILE, (n + 1) * TILE)
                 down_grad[e, :, at] = dot(turned_hidden, d_ref[:, at], ((1,), (0,))).astype(BF16)
-        stores = [
-            pltpu.make_async_copy(source, target, store.at[k])
-            for k, (target, source) in enumerate(expert_pieces(grads_ref, in_grad, down_grad, depth, down_rows))
-        ]
-        for copy in stores:
+        for copy in stores[:n_down]:
             copy.start()
+        for c in range(n_ctx):
+            at = slice(c * depth, (c + 1) * depth)
+            for n in range(2):
+                wide = slice(n * 2 * FF, (n + 1) * 2 * FF)
+                in_grad[at, wide] = dot(x_turned[at, :], d_gate_up[:, wide], ((1,), (0,))).astype(BF16)
+            stores[n_down + c].start()
         for copy in stores:
             copy.wait()
-
-
-def experts(x, packed, router, pick, n_experts, depth, down_rows, hit=None, kept=None, d_rows=None):
+    if ride:
+        total = ride_ref[ctx].astype(F32)
+        for k, copy in enumerate(riders):
+            copy.wait()
+            total = total + landed[k].astype(F32)
+        rode_ref[...] = total
+
+
+def experts(
+    layer, x, packed, router, pick, n_experts, depth, down_rows, hit=None, kept=None, d_rows=None, number=None, add=None
+):
+    n_ctx = lax.axis_size("ctx")
     forward, backward = hit is not None, d_rows is not None
     n_rows, width = x.shape
     any_place = pl.BlockSpec(memory_space=pl.ANY)
     operands = [x, packed, router, pick]
     operands += [hit] if forward else list(kept)
     operands += [d_rows] if backward else []
+    operands += [add] if add is not None else []
     in_specs = [VMEM, any_place] + [VMEM] * (len(operands) - 2)
     rows_out = jax.ShapeDtypeStruct((n_rows, width), BF16)
     inner = [jax.ShapeDtypeStruct((n_rows, LANES), F32), jax.ShapeDtypeStruct((n_rows, 4 * FF), BF16)]
@@ -1096,14 +1274,24 @@
             pltpu.VMEM((2, FF, width), BF16),
             pltpu.SemaphoreType.DMA((n_pieces,)),
         ]
+    params = {}
+    if add is not None:
+        outs.append(jax.ShapeDtypeStruct(add.shape[1:], F32))
+        out_specs.append(VMEM)
+        scratch += [
+            pltpu.VMEM((n_ctx - 1,) + add.shape[1:], BF16),
+            pltpu.SemaphoreType.DMA((n_ctx - 1,)),
+            pltpu.SemaphoreType.DMA((n_ctx - 1,)),
+        ]
+        params = dict(collective_id=number, has_side_effects=True)
     work = n_rows * 6 * width * FF * 2 * ((1 if forward else 0) + (2 if backward else 0))
     return pl.pallas_call(
-        functools.partial(experts_kernel, forward, backward, depth, down_rows),
+        functools.partial(experts_kernel, n_ctx, layer, forward, backward, depth, down_rows, add is not None),
         out_shape=outs,
         in_specs=in_specs,
         out_specs=out_specs,
         scratch_shapes=scratch,
-        compiler_params=pltpu.CompilerParams(vmem_limit_bytes=56 << 20),
+        compiler_params=pltpu.CompilerParams(vmem_limit_bytes=(44 if backward else 28) << 20, **params),
         cost_estimate=pl.CostEstimate(flops=2 * work, bytes_accessed=40 << 20, transcendentals=0),
     )(*operands)
 
@@ -1127,38 +1315,29 @@
     later = (jnp.arange(micro_count) > 0)[:, None]
     query_start = jnp.where(later, query_place - query_place % CONT_LEN, 0)
     query_pos = jnp.where(later, seq_len + query_place % CONT_LEN, query_place)
-    inverse = jnp.power(ROPE_BASE, -jnp.arange(HEAD_SIZE // 2, dtype=F32) * 2.0 / HEAD_SIZE)
+    half = HEAD_SIZE // 2
+    inverse = jnp.power(ROPE_BASE, -(jnp.arange(LANES, dtype=jnp.int32) % half).astype(F32) * 2.0 / HEAD_SIZE)
     angles = query_pos.reshape(-1).astype(F32)[:, None] * inverse[None, :]
-    cosine, sine = jnp.cos(angles), jnp.sin(angles)
+    sign = jnp.where(jnp.arange(LANES) % HEAD_SIZE < half, -1.0, 1.0)
     tables = (
-        jnp.tile(cosine, (1, 4)),
-        jnp.concatenate([-sine, sine, -sine, sine], 1),
+        jnp.cos(angles),
+        jnp.sin(angles) * sign[None, :],
         jnp.transpose(placed.reshape(micro_count, n_ctx, per_ctx), (1, 0, 2)).reshape(n_ctx, -1, 1),
         query_place[:, None, :],
         query_start[:, None, :],
     )
 
-    prepared = prepare(
-        15,
+    moe_pack = prepare(15, w_in[0], w_down[0])
+    normed_in, full, attn_pack, gain_pack, router_pack, route_pack = begin(
+        0,
+        tokens,
         w_query[0],
         key_value_weight[0].reshape(depth, -1),
         w_attn_out[0],
-        w_in[0],
-        w_down[0],
+        norm_gain[0],
+        jnp.transpose(router[0]),
         routes[0],
-        norm_gain[0],
-        router[0],
     )
-    attn_pack, moe_pack = prepared[:2], prepared[2:4]
-    route_pack, gain_pack, router_pack = prepared[4:]
-
-    def unpacked(values, in_rows, down_rows):
-        wide = values.shape[-1]
-        n = values.shape[0]
-        rest = values[:, in_rows + down_rows :]
-        rest = jnp.concatenate([rest[..., : wide // 2], rest[..., wide // 2 :]], 1)
-        down_part = jnp.concatenate([values[:, in_rows : in_rows + down_rows], rest], 2)
-        return values[:, :in_rows].reshape(n * in_rows, wide), down_part.reshape(n * down_rows, -1)
 
     in_rows, down_rows = w_in.shape[2], w_down.shape[2]
 
@@ -1170,20 +1349,16 @@
     my_first = wt * 2 * per_core + section * per_core
     n_rows = micro_count * per_ctx
 
-    hits = [route_pack[layer].reshape(n_rows, -1) for layer in range(2)]
     pick = (jnp.arange(LANES)[None, :] == my_first + jnp.arange(8)[:, None]).astype(F32)
-    router_wide = [jnp.pad(router_pack[layer], ((0, 0), (0, LANES - n_experts))) for layer in range(2)]
-
     def full_rows(values):
         return values.reshape(n_rows, width)
 
     def blocked(values):
         return values.reshape(2 * n_wt, share, width).astype(BF16)
 
-    stream = lax.dynamic_index_in_dim(tokens, section, 0, False).astype(F32)
-    top = lax.dynamic_index_in_dim(cotangent, section, 0, False).astype(F32)
-
-    normed_in, full = exchange(0, None, stream, gain=gain_pack[0, 0:1], spread="norm", gather=attn_pack[0])
+    stream = lax.dynamic_index_in_dim(tokens, section, 0, False)
+    top = lax.dynamic_index_in_dim(cotangent, section, 0, False)
+
     attn_full[0] = full.reshape(-1, full.shape[2])
     moe_full = [gather_experts(moe_pack[0]), None]
     saved = []
@@ -1192,26 +1367,35 @@
         rows_in = full_rows(normed_in)
         weights = attn_full[layer]
         if layer == 0:
-            top_low = lax.dynamic_index_in_dim(cotangent, section, 0, False)
-            partial, *heads, attended, d_mixed = attend(2, rows_in, weights, tables, top_low)
+            partial, *heads, attended, d_mixed = attend(2, rows_in, weights, tables, top)
         else:
             partial, *heads, attended = attend(3, rows_in, weights, tables)
-        middle, normed_mid = exchange(
+        middle, normed_mid, token = exchange(
             4 + layer, blocked(partial), stream, gain=gain_pack[layer, 1:2], spread="norm"
         )
         if layer == 0:
-            normed_mid, second = lax.optimization_barrier((normed_mid, moe_pack[1]))
+            token, second = lax.optimization_barrier((token, moe_pack[1]))
             moe_full[1] = gather_experts(second)
-        normed_mid, moe_full[layer] = lax.optimization_barrier((normed_mid, moe_full[layer]))
+        token, moe_full[layer] = lax.optimization_barrier((token, moe_full[layer]))
+        pick_now = pick + token
         rows_mid = full_rows(normed_mid)
         if layer == 0:
             partial, gates, gate_up = experts(
-                rows_mid, moe_full[0], router_wide[0], pick, n_experts, in_rows, down_rows, hit=hits[0]
+                0, rows_mid, moe_full[0], router_pack, pick_now, n_experts, in_rows, down_rows, hit=route_pack
             )
             inner = (gates, gate_up)
         else:
             partial, *back_parts = experts(
-                rows_mid, moe_full[1], router_wide[1], pick, n_experts, in_rows, down_rows, hit=hits[1], d_rows=full_rows(d_mixed)
+                1,
+                rows_mid,
+                moe_full[1],
+                router_pack,
+                pick_now,
+                n_experts,
+                in_rows,
+                down_rows,
+                hit=route_pack,
+                d_rows=full_rows(d_mixed),
             )
             inner = None
         saved.append(
@@ -1226,11 +1410,11 @@
             )
         )
         if layer == 0:
-            stream, normed_in, full = exchange(
-                6, blocked(partial), middle, gain=gain_pack[1, 0:1], spread="norm", rounded=True, gather=attn_pack[1]
+            stream, normed_in, full, token = exchange(
+                6, blocked(partial), middle, gain=gain_pack[1, 0:1], spread="norm", rounded=True, gather=attn_pack
             )
             attn_full[1] = full.reshape(-1, full.shape[2])
-            outputs.append(stream.astype(BF16))
+            outputs.append(stream)
         else:
             last_rows = (blocked(partial), middle)
     upstream = top
@@ -1242,30 +1426,33 @@
         kept = saved[layer]
         if layer == 0:
             back_parts = experts(
+                0,
                 kept["rows_mid"],
                 moe_full[0],
-                router_wide[0],
+                router_pack,
                 pick,
                 n_experts,
                 in_rows,
                 down_rows,
                 kept=kept["inner"],
                 d_rows=full_rows(d_mixed),
+                number=7,
+                add=attn_parts,
             )
+            *back_parts, attn_grads[1] = back_parts
         partial, packed_grad, router_grad = back_parts
+        gain = gain_pack[layer, 1:2]
         if layer == 0:
-            partial, packed_grad, moe_grads[1] = lax.optimization_barrier((partial, packed_grad, moe_grads[1]))
-        else:
-            partial, packed_grad = lax.optimization_barrier((partial, packed_grad))
+            gain, moe_grads[1] = lax.optimization_barrier((gain, moe_grads[1]))
         moe_grads[layer] = lax.psum_scatter(packed_grad, "ctx", scatter_dimension=0, tiled=False)
-        d_middle, gain_grad_mid, d_attn = exchange(
-            8 + layer, blocked(partial), upstream, kept["middle"], gain_pack[layer, 1:2], spread="plain"
+        d_middle, gain_grad_mid, d_attn, token = exchange(
+            8 + layer, blocked(partial), upstream, kept["middle"], gain, spread="plain"
         )
         rows_a = full_rows(d_attn)
         weights = attn_full[layer]
         if layer == 1:
             partial, raw, last = attend_back(11, rows_a, weights, tables, kept["heads"], last_rows)
-            outputs.append(last.astype(BF16))
+            outputs.append(last)
         else:
             partial, raw = attend_back(10, rows_a, weights, tables, kept["heads"])
         attn_parts = dot(kept["rows_in"], jnp.pad(raw, ((0, 0), (0, weights.shape[1] - raw.shape[1]))), ((0,), (0,)))
@@ -1274,7 +1461,7 @@
         )
         attn_parts = attn_parts.astype(BF16).reshape(n_ctx, depth, -1)
         if layer == 1:
-            upstream, gain_grad_in, d_mixed, attn_grads[1] = exchange(
+            upstream, gain_grad_in, d_mixed, token = exchange(
                 12,
                 blocked(partial),
                 d_middle,
@@ -1282,52 +1469,30 @@
                 gain_pack[1, 0:1],
                 spread="plain",
                 rounded=True,
-                add=attn_parts,
             )
         else:
-            upstream, gain_grad_in, attn_grads[0] = exchange(
+            upstream, gain_grad_in, attn_grads[0], token = exchange(
                 1, blocked(partial), d_middle, kept["stream"], gain_pack[0, 0:1], rounded=True, add=attn_parts
             )
-        grads_in[layer] = upstream.astype(BF16)
+        grads_in[layer] = upstream
         small[layer] = [router_grad, gain_grad_in, gain_grad_mid]
 
-    def by_core(parts, received):
-        return jnp.where(section == 0, parts[0], received), jnp.where(section == 0, received, parts[1])
-
-    small_total, *received = small_sum(14, small[0] + small[1], attn_grads + outputs + grads_in)
-    out_pair = jnp.stack(by_core(outputs, received[1]))
-    grad_pair = jnp.stack(by_core(grads_in, received[2]))
+    gain_total, router_total, grad_query, grad_kv, grad_out, out_pair, grad_pair = finish(
+        14, small[0] + small[1], attn_grads, outputs + grads_in, q_cols
+    )
     piece = width // (n_ctx * n_wt)
-    router_total = small_total[:n_experts, :piece]
-    gain_total = small_total[n_experts : n_experts + 2, :piece]
-    attn_first, attn_second = by_core(attn_grads, received[0])
-    kv_at = q_cols
-    out_at = q_cols + 2 * HEAD_SIZE
-    grad_query = jnp.concatenate([attn_first[:, :kv_at], attn_second[:, :kv_at]], -1)
-    grad_kv = jnp.stack([attn_first[:, kv_at:out_at], attn_second[:, kv_at:out_at]], 1)
-    grad_out = jnp.concatenate([jnp.transpose(attn_first[:, out_at:]), jnp.transpose(attn_second[:, out_at:])], 0)
-
-    def stacked(halves):
-        columns = halves[0].shape[1] // per_core
-        return jnp.stack(
-            [half[:, e * columns : (e + 1) * columns] for half in halves for e in range(per_core)]
-        ).astype(F32)
-
     moe_grads = [member.reshape(member.shape[-2:]) for member in moe_grads]
-    moe_pair = by_core(moe_grads, hand_over(13, moe_grads[0], moe_grads[1]))
-    moe_pair = [unpacked(member[None], in_rows, down_rows) for member in moe_pair]
-    grad_in = stacked([member[0] for member in moe_pair])
-    grad_down = stacked([member[1] for member in moe_pair])
+    grad_in, grad_down = hand_over(13, moe_grads[0], moe_grads[1], gain_total, in_rows, down_rows, per_core, width)
     return (
         out_pair[None],
         grad_pair[None],
-        gain_total[None],
+        gain_total[None, :, :piece],
         grad_query[None],
-        grad_kv[None],
+        grad_kv.reshape(depth, 2, LANES)[None],
         grad_out[None],
-        jnp.transpose(router_total)[None],
-        grad_in[None],
-        grad_down[None],
+        jnp.transpose(router_total[:, :piece])[None],
+        grad_in.astype(F32)[None],
+        grad_down.astype(F32)[None],
     )
 
 

time: 577 us -> 560 us (0.971)
  Pallas kernels: 468 us -> 450 us
  local copies, waits for them, and re-layouts: 52.7 us -> 64.4 us
  other arithmetic: 19.7 us -> 11.6 us
    pallas_call x8 -> x7, Pallas kernels: 294 us -> 247 us  [exchange(): pl.pallas_call(functools.partial(exchange_kernel, n_ctx, n_wt, reduce, ba...]
    pallas_call x6 -> x7, Pallas kernels: 86.3 us -> 115 us  [the longest x3 50.6 us: experts(): pl.pallas_call(functools.partial(experts_kernel, n_ctx, layer, forward, b...]
    unnamed x178 -> x213, local copies, waits for them, and re-layouts: 43 us -> 59.5 us
    convert_element_type x7 -> x0, other arithmetic: 9.08 us -> none  [the longest x2 4.92 us: stacked(): return jnp.stack([half[:, e * columns:(e + 1) * columns] for half in halv...]
    all_gather x2, waiting for transfers between devices: 7.82 us -> 0.01 us  [gather_experts(): lax.all_gather(pack, 'ctx', axis=0, tiled=True)]
  transfers between devices with their start and end apart: 4 -> 4, of which waited for: 2 -> 1; matrix products, arithmetic and copies ran while one was open for 5% -> 2% of each run, Pallas kernels for 75% -> 76%
where the time goes in v5:
time: 560 us; the launch traced here: 550 us
  Pallas kernels  450 us (80%)
  local copies, waits for them, and re-layouts  64.4 us (12%)
  between operations  15.1 us (3%)
  other arithmetic  11.6 us (2%)
    pallas_call x7, Pallas kernels, exchange(): pl.pallas_call(functools.partial(exchange_kernel, n_ctx, n_wt, reduce, ba...  247 us
    unnamed x213, local copies, waits for them, and re-layouts  59.5 us
    pallas_call x3, Pallas kernels, experts(): pl.pallas_call(functools.partial(experts_kernel, n_ctx, layer, forward, b...  50.6 us
    pallas_call x2, Pallas kernels, attend(): pl.pallas_call(functools.partial(attend_kernel, n_ctx, n_wt, bool(riders)...  46.9 us
    pallas_call x2, Pallas kernels, attend_back(): pl.pallas_call(functools.partial(attend_back_kernel, n_ctx, n_wt, bool(ri...  40.8 us
    pallas_call x1, Pallas kernels, begin(): pl.pallas_call(functools.partial(begin_kernel, n_ctx, n_wt), out_shape=[j...  40.6 us
    pallas_call x1, Pallas kernels, finish(): pl.pallas_call(functools.partial(finish_kernel, n_ctx, n_wt), out_shape=[...  12.9 us
  transfers between devices with their start and end apart: 4, of which 1 were waited for; matrix products, arithmetic and copies ran while one was open for 2% of the time, Pallas kernels for 76%

profile of v5, /device:TPU:0, one launch (start us, length us, event | category | flops | bytes accessed | tf_op | source)
XLA Modules:
  0.0 550.0 jit_solution(803172568173330945)
XLA Ops:
  7.2 1.9 copy-done.6
  9.1 1.4 copy-done.17
  10.5 5.3 shard_map.181
  15.9 1.4 copy-done.7
  19.0 1.0 copy-done.43
  19.9 1.0 copy-done.44
  20.9 40.6 %shard_map.178 = (bf16[8,64,1536]{2,1,0:T(8,128)(2,1)S(1)}, bf16[4,384,512]{2,1,0:T(8,128)(2,1)S(1)}, bf16[384,512]{1,0:T(8,128)(2,1)S(1)}, f32[2,2,1536]{2,1,0:...) custom-call(bf16[2,64,1536]{2,1,0:T(8,128)(2,1)S(1)} %copy-done.23, ...), custom_call_target="tpu_custom_call" | custom-call | bytes 94371840 | tf_op jit(solution)/shard_map/pallas_call | solution.py:1032
  62.3 0.9 copy-done.87
  64.0 1.5 dynamic-slice_bitcast_fusion
  65.5 1.0 fusion.8
  66.6 27.4 %shard_map.179 = (bf16[512,1536]{1,0:T(8,128)(2,1)S(1)}, bf16[2,3,256,128]{3,2,1,0:T(8,128)(2,1)S(1)}, bf16[4,512,128]{2,1,0:T(8,128)(2,1)S(1)}, f32[2,3,256,128...) custom-call(bf16[512,1536]{1,0:T(8,128)(2,1)S(1)} %bitcast.86, ...), custom_call_target="tpu_custom_call" | custom-call | bytes 73400320 | tf_op jit(solution)/shard_map/pallas_call | solution.py:712
  94.7 1.1 copy-done.83
  96.6 34.5 %shard_map.180 = (f32[64,1536]{1,0:T(8,128)S(1)}, bf16[8,64,1536]{2,1,0:T(8,128)(2,1)S(1)}, f32[8,128]{1,0:T(8,128)S(1)}) custom-call(bf16[8,64,1536]{2,1,0:T(8,128)(2,1)S(1)} %bitcast.103, bf16[64,1536]{1,0:T(8,128)(2,1)S(1)} %get-tuple-element.169.refs_1_.refs_2_, f32[1,1536]{1,0:T(1,128)S(1)} %get-tuple-element.129.refs_2_.refs_3_), custom_call_target="tpu_custom_call" | custom-call | bytes 115343360 | tf_op jit(solution)/shard_map/pallas_call | solution.py:405
  131.8 1.2 copy-done.80
  135.0 3.7 copy-done.79
  138.7 1.7 copy-done.81
  140.4 1.3 copy-done.88
  141.7 1.1 copy-done.92
  142.8 8.1 %shard_map.182 = (bf16[512,1536]{1,0:T(8,128)(2,1)S(1)}, f32[512,128]{1,0:T(8,128)S(1)}, bf16[512,2048]{1,0:T(8,128)(2,1)S(1)}) custom-call(bf16[512,1536]{1,0:T(8,128)(2,1)S(1)} %bitcast.122, bf16[4,576,2048]{2,1,0:T(8,128)(2,1)S(1)} %bitcast.121, bf16[2,128,1536]{2,1,0:T(8,128)(2,1)S(1)} %copy-done.88, f32[8,128]{1,0:T(8,128)S(1)} %fusion.11.refs_3_, ...), custom_call_target="tpu_custom_call" | custom-call | flops 9663676416 | bytes 41943040 | tf_op jit(solution)/shard_map/pallas_call | solution.py:1288
  151.0 37.7 %shard_map.183 = (bf16[64,1536]{1,0:T(8,128)(2,1)S(1)}, bf16[8,64,1536]{2,1,0:T(8,128)(2,1)S(1)}, bf16[4,384,512]{2,1,0:T(8,128)(2,1)S(1)}, f32[8,128]{1,0:T(8,128)}) custom-call(bf16[8,64,1536]{2,1,0:T(8,128)(2,1)S(1)} %bitcast.108, f32[64,1536]{1,0:T(8,128)S(1)} %copy-done.19, f32[1,1536]{1,0:T(1,128)S(1)} %get-tuple-element.163.refs_2_.refs_3_, ...), custom_call_target="tpu_custom_call" | custom-call | bytes 115343360 | tf_op jit(solution)/shard_map/pallas_call | solution.py:405
  188.8 19.4 %shard_map.184 = (bf16[512,1536]{1,0:T(8,128)(2,1)S(1)}, bf16[2,3,256,128]{3,2,1,0:T(8,128)(2,1)S(1)}, bf16[4,512,128]{2,1,0:T(8,128)(2,1)S(1)}, f32[2,3,256,128...) custom-call(bf16[512,1536]{1,0:T(8,128)(2,1)S(1)} %bitcast.88, ...), custom_call_target="tpu_custom_call" | custom-call | bytes 73400320 | tf_op jit(solution)/shard_map/pallas_call | solution.py:712
  208.3 0.9 copy-done.31
  212.0 35.8 %shard_map.185 = (f32[64,1536]{1,0:T(8,128)S(1)}, bf16[8,64,1536]{2,1,0:T(8,128)(2,1)S(1)}, f32[8,128]{1,0:T(8,128)S(1)}) custom-call(bf16[8,64,1536]{2,1,0:T(8,128)(2,1)S(1)} %bitcast.104, bf16[64,1536]{1,0:T(8,128)(2,1)S(1)} %get-tuple-element.105.refs_1_.refs_2_.refs_8_, f32[1,1536]{1,0:T(1,128)S(1)} %copy-done.55), custom_call_target="tpu_custom_call" | custom-call | bytes 115343360 | tf_op jit(solution)/shard_map/pallas_call | solution.py:405
  249.1 1.2 copy-done.85
  251.1 1.4 copy-done.84
  252.5 1.4 copy-done.86
  253.9 1.1 copy-done.89
  255.0 1.0 copy-done.93
  256.1 22.1 %shard_map.186 = (bf16[512,1536]{1,0:T(8,128)(2,1)S(1)}, bf16[512,1536]{1,0:T(8,128)(2,1)S(1)}, bf16[4,576,2048]{2,1,0:T(8,128)(2,1)}, f32[16,1536]{1,0:T(8,128)S(1)}) custom-call(bf16[512,1536]{1,0:T(8,128)(2,1)S(1)} %bitcast.126, bf16[4,576,2048]{2,1,0:T(8,128)(2,1)} %bitcast.133, bf16[2,128,1536]{2,1,0:T(8,128)(2,1)S(1)} %copy-done.89, ...), custom_call_target="tpu_custom_call" | custom-call | flops 28991029248 | bytes 41943040 | tf_op jit(solution)/shard_map/pallas_call | solution.py:1288
  278.2 1.1 copy-done.15
  279.3 1.2 copy-done.21
  281.2 0.8 fusion.9.refs_3_
  282.1 1.0 copy-done.11
  283.1 1.4 copy-done.16
  285.2 36.4 %shard_map.187 = (f32[64,1536]{1,0:T(8,128)S(1)}, f32[1,1536]{1,0:T(1,128)S(1)}, bf16[8,64,1536]{2,1,0:T(8,128)(2,1)S(1)}, f32[8,128]{1,0:T(8,128)}) custom-call(bf16[8,64,1536]{2,1,0:T(8,128)(2,1)S(1)} %bitcast.101, bf16[64,1536]{1,0:T(8,128)(2,1)S(1)} %get-tuple-element.170.refs_0_.refs_1_, f32[64,1536]{1,0:T(8,128)S(1)} %copy-done.11, ...), custom_call_target="tpu_custom_call" | custom-call | bytes 115343360 | tf_op jit(solution)/shard_map/pallas_call | solution.py:405
  322.2 1.4 copy-done.22
  323.6 1.1 copy-done.32
  324.8 1.1 copy-done.36
  325.9 1.0 copy-done.38
  328.2 20.3 %shard_map.188 = (bf16[512,1536]{1,0:T(8,128)(2,1)S(1)}, bf16[512,384]{1,0:T(8,128)(2,1)S(1)}, bf16[64,1536]{1,0:T(8,128)(2,1)S(1)}) custom-call(bf16[512,1536]{1,0:T(8,128)(2,1)S(1)} %bitcast.97, bf16[1536,512]{1,0:T(8,128)(2,1)S(1)} %bitcast.96, f32[512,128]{1,0:T(8,128)S(1)} %get-tuple-element.166.cos_ref, f32[512,128]{1,0:T(8,128)S(1)} %get-tuple-element.165.sin_ref, ...), custom_call_target="tpu_custom_call" | custom-call | bytes 104857600 | tf_op jit(solution)/shard_map/pallas_call | solution.py:859
  348.6 36.4 %shard_map.189 = (bf16[64,1536]{1,0:T(8,128)(2,1)S(1)}, f32[1,1536]{1,0:T(1,128)S(1)}, bf16[8,64,1536]{2,1,0:T(8,128)(2,1)S(1)}, f32[8,128]{1,0:T(8,128)}) custom-call(bf16[8,64,1536]{2,1,0:T(8,128)(2,1)S(1)} %bitcast.102, f32[64,1536]{1,0:T(8,128)S(1)} %get-tuple-element.121.refs_1_, bf16[64,1536]{1,0:T(8,128)(2,1)S(1)} %copy-done.9, ...), custom_call_target="tpu_custom_call" | custom-call | bytes 115343360 | tf_op jit(solution)/shard_map/pallas_call | solution.py:405
  385.0 1.0 fusion.6
  386.1 1.0 fusion
  388.4 20.4 %shard_map.190 = (bf16[512,1536]{1,0:T(8,128)(2,1)S(1)}, bf16[4,576,2048]{2,1,0:T(8,128)(2,1)}, f32[16,1536]{1,0:T(8,128)S(1)}, f32[384,512]{1,0:T(8,128)S(1)}) custom-call(bf16[512,1536]{1,0:T(8,128)(2,1)S(1)} %bitcast.123, bf16[4,576,2048]{2,1,0:T(8,128)(2,1)} %bitcast.120, bf16[2,128,1536]{2,1,0:T(8,128)(2,1)S(1)} %copy-done.90, ...), custom_call_target="tpu_custom_call" | custom-call | flops 19327352832 | bytes 41943040 | tf_op jit(solution)/shard_map/pallas_call | solution.py:1288
  408.8 1.1 copy-done.13
  409.9 0.9 copy-done.27
  411.5 1.5 copy-done.14
  413.1 1.0 copy-done.20
  414.1 0.9 copy-done.25
  415.0 34.2 %shard_map.191 = (f32[64,1536]{1,0:T(8,128)S(1)}, f32[1,1536]{1,0:T(1,128)S(1)}, bf16[8,64,1536]{2,1,0:T(8,128)(2,1)S(1)}, f32[8,128]{1,0:T(8,128)}) custom-call(bf16[8,64,1536]{2,1,0:T(8,128)(2,1)S(1)} %bitcast.100, bf16[64,1536]{1,0:T(8,128)(2,1)S(1)} %copy-done.25, f32[64,1536]{1,0:T(8,128)S(1)} %copy-done.20, ...), custom_call_target="tpu_custom_call" | custom-call | bytes 115343360 | tf_op jit(solution)/shard_map/pallas_call | solution.py:405
  449.2 1.3 copy-done.30
  450.5 1.0 copy-done.40
  452.2 20.5 %shard_map.192 = (bf16[512,1536]{1,0:T(8,128)(2,1)S(1)}, bf16[512,384]{1,0:T(8,128)(2,1)S(1)}) custom-call(bf16[512,1536]{1,0:T(8,128)(2,1)S(1)} %bitcast.92, bf16[1536,512]{1,0:T(8,128)(2,1)S(1)} %bitcast.91, f32[512,128]{1,0:T(8,128)S(1)} %get-tuple-element.166.cos_ref, f32[512,128]{1,0:T(8,128)S(1)} %get-tuple-element.165.sin_ref, ...), custom_call_target="tpu_custom_call" | custom-call | bytes 104857600 | tf_op jit(solution)/shard_map/pallas_call | solution.py:859
  472.7 1.0 fusion.3
  473.7 1.0 fusion.1
  474.9 32.3 %shard_map.193 = (bf16[64,1536]{1,0:T(8,128)(2,1)S(1)}, f32[1,1536]{1,0:T(1,128)S(1)}, f32[384,512]{1,0:T(8,128)S(1)}, f32[8,128]{1,0:T(8,128)}) custom-call(bf16[8,64,1536]{2,1,0:T(8,128)(2,1)S(1)} %bitcast.106, f32[64,1536]{1,0:T(8,128)S(1)} %get-tuple-element.136.refs_1_, bf16[64,1536]{1,0:T(8,128)(2,1)S(1)} %get-tuple-element.169.refs_1_.refs_2_, ...), custom_call_target="tpu_custom_call" | custom-call | bytes 115343360 | tf_op jit(solution)/shard_map/pallas_call | solution.py:405
  507.2 12.9 %shard_map.194 = (f32[2,128]{1,0:T(2,128)S(1)}, f32[16,128]{1,0:T(8,128)S(1)}, f32[384,384]{1,0:T(8,128)S(1)}, f32[384,256]{1,0:T(8,128)S(1)}, f32[384,384]{1,0:...) custom-call(f32[16,1536]{1,0:T(8,128)S(1)} %copy-done.54, ...), custom_call_target="tpu_custom_call" | custom-call | bytes 41943040 | tf_op jit(solution)/shard_map/pallas_call | solution.py:495
  520.7 5.1 reduce-scatter.9.cloned.1.call-done
  525.8 5.0 shard_map.195
  530.9 5.5 bitcast_convert_fusion
  536.3 2.1 bitcast_convert_fusion.1
  538.4 0.9 broadcast_in_dim_reshape.3
  541.4 0.8 copy.50
  542.3 0.8 copy.51
  (209 shorter events, 20.9 us)
Async XLA Ops:
  7.2 127.0 %all-gather.3.cloned.1.call-start = ((), (), s32[]{:S(2)}) async-start(), calls=%async_computation.2 | async-start | bytes 11796480 | tf_op jit(solution)/shard_map/all_gather | solution.py:1345
  7.2 1.9 copy-start.6
  9.1 1.4 copy-start.17
  15.9 1.4 copy-start.7
  17.3 1.1 copy-start.99
  17.3 1.7 copy-start.23
  17.3 1.7 copy-start.65
  17.3 1.7 copy-start.67
  17.3 233.0 %all-gather.5.cloned.1.call-start = ((), (), s32[]{:S(2)}) async-start(), calls=%async_computation.3 | async-start | bytes 11796480 | tf_op jit(solution)/shard_map/all_gather | solution.py:1345
  18.2 48.3 %copy-start.57 = (s32[2,1,256]{2,1,0:T(1,128)}, s32[2,1,256]{2,1,0:T(1,128)S(1)}, u32[]{:S(2)}) copy-start(s32[2,1,256]{2,1,0:T(1,128)S(1)} %broadcast_in_dim.73.query_place) | copy-start | bytes 6148
  18.3 48.3 %copy-start.61 = (s32[2,1,256]{2,1,0:T(1,128)}, s32[2,1,256]{2,1,0:T(1,128)S(1)}, u32[]{:S(2)}) copy-start(s32[2,1,256]{2,1,0:T(1,128)S(1)} %broadcast_in_dim.74.query_start) | copy-start | bytes 6148
  64.0 30.0 %copy-start.2 = (bf16[4,384,512]{2,1,0:T(8,128)(2,1)}, bf16[4,384,512]{2,1,0:T(8,128)(2,1)S(1)}, u32[]{:S(2)}) copy-start(bf16[4,384,512]{2,1,0:T(8,128)(2,1)S(1)} %get-tuple-element.85) | copy-start | bytes 4718596
  94.7 1.1 copy-start.83
  95.9 35.2 %copy-start.29 = (f32[2,3,256,128]{3,2,1,0:T(8,128)}, f32[2,3,256,128]{3,2,1,0:T(8,128)S(1)}, u32[]{:S(2)}) copy-start(f32[2,3,256,128]{3,2,1,0:T(8,128)S(1)} %get-tuple-element.133.out_ref) | copy-start | bytes 2359300
  95.9 37.1 %copy-start.33 = (bf16[4,512,128]{2,1,0:T(8,128)(2,1)}, bf16[4,512,128]{2,1,0:T(8,128)(2,1)S(1)}, u32[]{:S(2)}) copy-start(bf16[4,512,128]{2,1,0:T(8,128)(2,1)S(1)} %get-tuple-element.132.pairs_ref) | copy-start | bytes 1572868
  95.9 37.1 %copy-start.39 = (bf16[2,3,256,128]{3,2,1,0:T(8,128)(2,1)}, bf16[2,3,256,128]{3,2,1,0:T(8,128)(2,1)S(1)}, u32[]{:S(2)}) copy-start(bf16[2,3,256,128]{3,2,1,0:T(8,128)(2,1)S(1)} %get-tuple-element.131.q_ref) | copy-start | bytes 1179652
  95.9 37.1 %copy-start.68 = (f32[2,3,1,256]{3,2,1,0:T(1,128)}, f32[2,3,1,256]{3,2,1,0:T(1,128)S(1)}, u32[]{:S(2)}) copy-start(f32[2,3,1,256]{3,2,1,0:T(1,128)S(1)} %get-tuple-element.134.lse_ref) | copy-start | bytes 18436
  131.8 1.2 copy-start.80
  133.6 277.9 %reduce-scatter.7.cloned.1.call-start = ((), (), s32[]{:S(2)}) async-start(), calls=%async_computation.4 | async-start | bytes 11796480
  134.9 3.7 copy-start.79
  138.7 1.7 copy-start.81
  140.4 1.3 copy-start.88
  142.8 8.2 %copy-start.19 = (f32[64,1536]{1,0:T(8,128)S(1)}, f32[64,1536]{1,0:T(8,128)}, u32[]{:S(2)}) copy-start(f32[64,1536]{1,0:T(8,128)} %copy-done.18) | copy-start | bytes 1179652
  142.8 8.2 %copy-start.42 = (bf16[384,512]{1,0:T(8,128)(2,1)S(1)}, bf16[384,512]{1,0:T(8,128)(2,1)}, u32[]{:S(2)}) copy-start(bf16[384,512]{1,0:T(8,128)(2,1)} %copy-done.41) | copy-start | bytes 1179652
  151.0 57.3 %copy-start.94 = (bf16[512,2048]{1,0:T(8,128)(2,1)}, bf16[512,2048]{1,0:T(8,128)(2,1)S(1)}, u32[]{:S(2)}) copy-start(bf16[512,2048]{1,0:T(8,128)(2,1)S(1)} %get-tuple-element.98.refs_5_) | copy-start | bytes 6291460
  151.0 57.3 %copy-start.96 = (f32[512,128]{1,0:T(8,128)}, f32[512,128]{1,0:T(8,128)S(1)}, u32[]{:S(2)}) copy-start(f32[512,128]{1,0:T(8,128)S(1)} %get-tuple-element.97.refs_4_) | copy-start | bytes 786436
  151.0 37.8 %copy-start.58 = (s32[2,1,256]{2,1,0:T(1,128)S(1)}, s32[2,1,256]{2,1,0:T(1,128)}, u32[]{:S(2)}) copy-start(s32[2,1,256]{2,1,0:T(1,128)} %copy-done.57) | copy-start | bytes 6148
  151.0 37.8 %copy-start.62 = (s32[2,1,256]{2,1,0:T(1,128)S(1)}, s32[2,1,256]{2,1,0:T(1,128)}, u32[]{:S(2)}) copy-start(s32[2,1,256]{2,1,0:T(1,128)} %copy-done.61) | copy-start | bytes 6148
  188.8 19.5 %copy-start = (bf16[8,64,1536]{2,1,0:T(8,128)(2,1)}, bf16[8,64,1536]{2,1,0:T(8,128)(2,1)S(1)}, u32[]{:S(2)}) copy-start(bf16[8,64,1536]{2,1,0:T(8,128)(2,1)S(1)} %get-tuple-element.102) | copy-start | bytes 4718596
  188.8 19.5 %copy-start.4 = (bf16[4,384,512]{2,1,0:T(8,128)(2,1)}, bf16[4,384,512]{2,1,0:T(8,128)(2,1)S(1)}, u32[]{:S(2)}) copy-start(bf16[4,384,512]{2,1,0:T(8,128)(2,1)S(1)} %get-tuple-element.103) | copy-start | bytes 4718596
  188.8 23.2 %copy-start.8 = (bf16[64,1536]{1,0:T(8,128)(2,1)}, bf16[64,1536]{1,0:T(8,128)(2,1)S(1)}, u32[]{:S(2)}) copy-start(bf16[64,1536]{1,0:T(8,128)(2,1)S(1)} %get-tuple-element.105.refs_1_.refs_2_.refs_8_) | copy-start | bytes 589828
  188.8 23.2 %copy-start.55 = (f32[1,1536]{1,0:T(1,128)S(1)}, f32[1,1536]{1,0:T(1,128)}, u32[]{:S(2)}) copy-start(f32[1,1536]{1,0:T(1,128)} %get-tuple-element.162.refs_2_.refs_3_) | copy-start | bytes 18436
  249.1 1.2 copy-start.85
  251.1 1.4 copy-start.84
  252.5 1.4 copy-start.86
  279.3 1.2 copy-start.21
  281.2 244.6 %reduce-scatter.9.cloned.1.call-start = ((), (), s32[]{:S(2)}) async-start(), calls=%async_computation.5 | async-start | bytes 11796480
  281.2 41.0 %copy-start.5 = (bf16[4,384,512]{2,1,0:T(8,128)(2,1)S(1)}, bf16[4,384,512]{2,1,0:T(8,128)(2,1)}, u32[]{:S(2)}) copy-start(bf16[4,384,512]{2,1,0:T(8,128)(2,1)} %copy-done.4) | copy-start | bytes 4718596
  283.1 1.4 copy-start.16
  285.2 37.0 %copy-start.12 = (f32[64,1536]{1,0:T(8,128)S(1)}, f32[64,1536]{1,0:T(8,128)}, u32[]{:S(2)}) copy-start(f32[64,1536]{1,0:T(8,128)} %copy-done.10) | copy-start | bytes 1179652
  285.2 37.0 %copy-start.75 = (f32[2,3,1,256]{3,2,1,0:T(1,128)S(1)}, f32[2,3,1,256]{3,2,1,0:T(1,128)}, u32[]{:S(2)}) copy-start(f32[2,3,1,256]{3,2,1,0:T(1,128)} %copy-done.74) | copy-start | bytes 18436
  322.2 1.4 copy-start.22
  328.2 20.4 %copy-start.9 = (bf16[64,1536]{1,0:T(8,128)(2,1)S(1)}, bf16[64,1536]{1,0:T(8,128)(2,1)}, u32[]{:S(2)}) copy-start(bf16[64,1536]{1,0:T(8,128)(2,1)} %copy-done.8) | copy-start | bytes 589828
  348.5 37.5 %copy-start.49 = (bf16[64,1536]{1,0:T(8,128)(2,1)}, bf16[64,1536]{1,0:T(8,128)(2,1)S(1)}, u32[]{:S(2)}) copy-start(bf16[64,1536]{1,0:T(8,128)(2,1)S(1)} %get-tuple-element.146.refs_9_) | copy-start | bytes 589828
  348.5 36.4 %copy-start.1 = (bf16[8,64,1536]{2,1,0:T(8,128)(2,1)S(1)}, bf16[8,64,1536]{2,1,0:T(8,128)(2,1)}, u32[]{:S(2)}) copy-start(bf16[8,64,1536]{2,1,0:T(8,128)(2,1)} %copy-done) | copy-start | bytes 4718596
  386.0 1.4 copy-start.82
  386.1 1.6 copy-start.90
  386.1 2.3 copy-start.95
  386.1 2.3 copy-start.97
  411.5 37.7 %copy-start.60 = (s32[2,1,256]{2,1,0:T(1,128)S(1)}, s32[2,1,256]{2,1,0:T(1,128)}, u32[]{:S(2)}) copy-start(s32[2,1,256]{2,1,0:T(1,128)} %copy-done.57) | copy-start | bytes 6148
  411.5 37.7 %copy-start.64 = (s32[2,1,256]{2,1,0:T(1,128)S(1)}, s32[2,1,256]{2,1,0:T(1,128)}, u32[]{:S(2)}) copy-start(s32[2,1,256]{2,1,0:T(1,128)} %copy-done.61) | copy-start | bytes 6148
  411.5 37.7 %copy-start.3 = (bf16[4,384,512]{2,1,0:T(8,128)(2,1)S(1)}, bf16[4,384,512]{2,1,0:T(8,128)(2,1)}, u32[]{:S(2)}) copy-start(bf16[4,384,512]{2,1,0:T(8,128)(2,1)} %copy-done.2) | copy-start | bytes 4718596
  411.5 1.5 copy-start.14
  415.0 34.2 %copy-start.34 = (bf16[4,512,128]{2,1,0:T(8,128)(2,1)S(1)}, bf16[4,512,128]{2,1,0:T(8,128)(2,1)}, u32[]{:S(2)}) copy-start(bf16[4,512,128]{2,1,0:T(8,128)(2,1)} %copy-done.33) | copy-start | bytes 1572868
  449.2 1.3 copy-start.30
  474.8 32.4 %copy-start.26 = (bf16[64,1536]{1,0:T(8,128)(2,1)S(1)}, bf16[64,1536]{1,0:T(8,128)(2,1)}, u32[]{:S(2)}) copy-start(bf16[64,1536]{1,0:T(8,128)(2,1)} %copy-done.24) | copy-start | bytes 589828
  474.8 32.4 %copy-start.28 = (f32[384,512]{1,0:T(8,128)S(1)}, f32[384,512]{1,0:T(8,128)}, u32[]{:S(2)}) copy-start(f32[384,512]{1,0:T(8,128)} %copy-done.27) | copy-start | bytes 2359300
  474.8 32.4 %copy-start.50 = (bf16[64,1536]{1,0:T(8,128)(2,1)S(1)}, bf16[64,1536]{1,0:T(8,128)(2,1)}, u32[]{:S(2)}) copy-start(bf16[64,1536]{1,0:T(8,128)(2,1)} %copy-done.49) | copy-start | bytes 589828
  474.8 32.4 %copy-start.52 = (f32[16,1536]{1,0:T(8,128)S(1)}, f32[16,1536]{1,0:T(8,128)}, u32[]{:S(2)}) copy-start(f32[16,1536]{1,0:T(8,128)} %copy-done.51) | copy-start | bytes 294916
  474.8 32.4 %copy-start.54 = (f32[16,1536]{1,0:T(8,128)S(1)}, f32[16,1536]{1,0:T(8,128)}, u32[]{:S(2)}) copy-start(f32[16,1536]{1,0:T(8,128)} %copy-done.53) | copy-start | bytes 294916
  474.8 32.4 %copy-start.71 = (f32[1,1536]{1,0:T(1,128)S(1)}, f32[1,1536]{1,0:T(1,128)}, u32[]{:S(2)}) copy-start(f32[1,1536]{1,0:T(1,128)} %copy-done.70) | copy-start | bytes 18436
  474.8 32.4 %copy-start.73 = (f32[1,1536]{1,0:T(1,128)S(1)}, f32[1,1536]{1,0:T(1,128)}, u32[]{:S(2)}) copy-start(f32[1,1536]{1,0:T(1,128)} %copy-done.72) | copy-start | bytes 18436
  520.1 5.7 %copy-start.76 = (f32[2,128]{1,0:T(2,128)}, f32[2,128]{1,0:T(2,128)S(1)}, u32[]{:S(2)}) copy-start(f32[2,128]{1,0:T(2,128)S(1)} %get-tuple-element.150.after) | copy-start | bytes 3076
  530.9 5.5 copy-start.98
  (42 other events, 36.7 us)
Sparse Core Ops, SparseCore 0:
  17.5 112.9 all-gather.2
  133.7 116.2 all-gather.4
  281.3 98.5 reduce-scatter.6
  411.6 114.1 reduce-scatter.8

commit v6 on v5

--- a/solution.py
+++ b/solution.py
@@ -50,6 +50,30 @@
     )
 
 
+def loaded(kernel, operands, whole, **call):
+    n = len(operands)
+
+    def body(*refs):
+        held, sems = refs[-n - 1 : -1], refs[-1]
+        copies = [pltpu.make_async_copy(refs[k], held[k], sems.at[k]) for k in range(n)]
+        for copy in copies:
+            copy.start()
+
+        def ready():
+            for copy in copies:
+                copy.wait()
+
+        kernel(ready, *held, *refs[n : -n - 1])
+
+    call["scratch_shapes"] = (
+        list(call["scratch_shapes"])
+        + [pltpu.VMEM(member.shape, member.dtype) for member in operands]
+        + [pltpu.SemaphoreType.DMA((n,))]
+    )
+    call["in_specs"] = [pl.BlockSpec(memory_space=pl.ANY)] * (n + len(whole))
+    return pl.pallas_call(body, **call)(*operands, *whole)
+
+
 class Near:
     def __init__(self, n_wt):
         self.section, self.ctx, self.wt = place()
@@ -261,82 +285,143 @@
             pl.when(condition)(copy.wait_send)
 
 
-def exchange_kernel(n_ctx, n_wt, reduce, back, spread, rounded, ride, *refs):
-    refs = list(refs)
-    near = Near(n_wt)
-    section, ctx, wt = near.section, near.ctx, near.wt
+class CtxGather:
+    def __init__(self, near, n_ctx, source, target, sems):
+        self.n_ctx, self.source, self.target = n_ctx, source, target
+        self.send, self.recv, self.local = sems
+        self.ctx = near.ctx
+        x, y = lax.rem(near.ctx, 2), near.ctx // 2
+        self.at_x, self.at_y = 2 * y + 1 - x, 2 * (1 - y) + x
+        self.device = lambda index: (near.section, index, near.wt)
+        self.half = source.shape[0] // 2
+
+    @staticmethod
+    def scratch(n_ctx):
+        dma = pltpu.SemaphoreType.DMA
+        return [dma((max(4, n_ctx - 1),)), dma((max(4, n_ctx - 1),)), dma]
+
+    def copy(self, source, target, number, index):
+        return remote(source, target, self.send.at[number], self.recv.at[number], self.device(index))
+
+    def near_copies(self):
+        if self.n_ctx != 4:
+            return [
+                self.copy(self.source, self.target.at[self.ctx], k, lax.rem(self.ctx + 1 + k, self.n_ctx))
+                for k in range(self.n_ctx - 1)
+            ]
+        return [
+            self.copy(self.source, self.target.at[self.ctx], k, index)
+            for k, index in enumerate((self.at_x, self.at_y))
+        ]
+
+    def far_copies(self):
+        if self.n_ctx != 4:
+            return []
+        parts = []
+        for number, block, at, index in (
+            (2, self.at_x, slice(0, self.half), self.at_y),
+            (3, self.at_y, slice(self.half, 2 * self.half), self.at_x),
+        ):
+            ref = self.target.at[block, at]
+            parts.append(self.copy(ref, ref, number, index))
+        return parts
+
+    def start(self):
+        pltpu.make_async_copy(self.source, self.target.at[self.ctx], self.local).start()
+        for copy in self.near_copies():
+            copy.start()
+
+    def hand_on(self):
+        for copy in self.near_copies():
+            copy.wait_recv()
+        for copy in self.far_copies():
+            copy.start()
+
+    def finish(self):
+        pltpu.make_async_copy(self.source, self.target.at[self.ctx], self.local).wait()
+        for copy in self.far_copies():
+            copy.wait()
+        for copy in self.near_copies():
+            copy.wait_send()
+
+
+def exchange_steps(
+    near,
+    n_ctx,
+    parts,
+    rows_ref,
+    stream_ref,
+    gain_ref,
+    result_ref,
+    gain_grad_ref,
+    all_ref,
+    spread,
+    rounded,
+    scratch,
+    ride=None,
+    ride_refs=None,
+    between=(),
+):
+    section, ctx, wt, n_wt = near.section, near.ctx, near.wt, near.n_wt
     peers = [(section, lax.rem(ctx + k, n_ctx), wt) for k in range(1, n_ctx)]
-    parts = refs.pop(0) if reduce else None
-    rows_ref = refs.pop(0)
-    stream_ref = refs.pop(0) if back else None
-    gain_ref = refs.pop(0) if (back or spread) else None
-    ride_ref = refs.pop(0) if ride else None
-    result_ref = refs.pop(0) if reduce else None
-    gain_grad_ref = refs.pop(0) if back else None
-    all_ref = refs.pop(0) if spread else None
-    rode_ref = refs.pop(0) if ride else None
-    token_ref = refs.pop(0)
-    token_ref[...] = jnp.zeros(token_ref.shape, F32)
-    if reduce:
-        sums = RowSum(near, CHUNKS, parts, refs[:9])
-        refs = refs[9:]
-        sum_ref = refs.pop(0) if rounded else result_ref
+    scratch = list(scratch)
+    sums = RowSum(near, CHUNKS, parts, scratch[:9])
+    scratch = scratch[9:]
+    sum_ref = scratch.pop(0) if rounded else result_ref
     if spread:
-        gathers = RowGather(near, CHUNKS, all_ref, refs[:4])
-        refs = refs[4:]
+        gathers = RowGather(near, CHUNKS, all_ref, scratch[:4])
+        scratch = scratch[4:]
+    chunk_rows = rows_ref.shape[0] // CHUNKS
+    sums.begin()
     if ride:
-        landed, ride_send, ride_recv, ride_local = refs
-    chunk_rows = rows_ref.shape[0] // CHUNKS
-    near.greet(peers if ride else ())
-    if reduce:
-        sums.begin()
-    if ride == "gather":
-        keep = pltpu.make_async_copy(ride_ref, rode_ref.at[ctx], ride_local)
-        keep.start()
-        riders = [
-            remote(ride_ref, rode_ref.at[ctx], ride_send.at[k], ride_recv.at[k], peers[k]) for k in range(n_ctx - 1)
-        ]
-    elif ride == "sum":
-        riders = [
-            remote(
-                ride_ref.at[lax.rem(ctx + 1 + k, n_ctx)], landed.at[k], ride_send.at[k], ride_recv.at[k], peers[k]
-            )
-            for k in range(n_ctx - 1)
-        ]
-    if ride:
-        for copy in riders:
-            copy.start()
+        ride_ref, rode_ref = ride_refs
+        if ride == "gather":
+            blocks = CtxGather(near, n_ctx, ride_ref, rode_ref, scratch)
+        else:
+            landed, ride_send, ride_recv = scratch
+            riders = [
+                remote(
+                    ride_ref.at[lax.rem(ctx + 1 + k, n_ctx)], landed.at[k], ride_send.at[k], ride_recv.at[k], peers[k]
+                )
+                for k in range(n_ctx - 1)
+            ]
+
+    def set_off():
+        if ride == "gather":
+            blocks.start()
+        elif ride:
+            for copy in riders:
+                copy.start()
+
+    between = list(between)
+    if not between:
+        set_off()
 
     def settle(chunk):
         at = rows_of(chunk, chunk_rows)
-        if reduce:
-            sums.collect(chunk, sum_ref)
-            total = sum_ref[at, :]
-            if back:
-                stream = stream_ref[at, :].astype(F32)
-                scale = norm_scale(stream)
-                weighted = gain_ref[...] * total
-                gain_part = jnp.sum(total * stream * scale, 0, keepdims=True)
-                gain_grad_ref[...] = gain_part if chunk == 0 else gain_grad_ref[...] + gain_part
-                total = scale * weighted - stream * (scale * scale * scale) * jnp.mean(
-                    weighted * stream, -1, keepdims=True
-                )
-            total = rows_ref[at, :].astype(F32) + total
-            if rounded:
-                total = total.astype(BF16)
-            result_ref[at, :] = total
-            total = total.astype(F32)
-        else:
-            total = rows_ref[at, :].astype(F32)
+        sums.collect(chunk, sum_ref)
+        total = sum_ref[at, :]
+        if stream_ref is not None:
+            stream = stream_ref[at, :].astype(F32)
+            scale = norm_scale(stream)
+            weighted = gain_ref[...] * total
+            gain_part = jnp.sum(total * stream * scale, 0, keepdims=True)
+            gain_grad_ref[...] = gain_part if chunk == 0 else gain_grad_ref[...] + gain_part
+            total = scale * weighted - stream * (scale * scale * scale) * jnp.mean(
+                weighted * stream, -1, keepdims=True
+            )
+        total = rows_ref[at, :].astype(F32) + total
+        if rounded:
+            total = total.astype(BF16)
+        result_ref[at, :] = total
+        total = total.astype(F32)
         if spread:
             if spread == "norm":
                 total = total * norm_scale(total) * gain_ref[...]
             all_ref[near.own, at, :] = total.astype(BF16)
             gathers.first(chunk)
 
-    stages = []
-    if reduce:
-        stages += [functools.partial(sums.step, step=step) for step in range(n_wt - 1)]
+    stages = [functools.partial(sums.step, step=step) for step in range(n_wt - 1)]
     stages.append(settle)
     if spread:
         stages += [functools.partial(gathers.hop, hop=hop) for hop in range(1, n_wt)]
@@ -344,13 +429,18 @@
         for chunk in reversed(range(CHUNKS)):
             if 0 <= slot - chunk < len(stages):
                 stages[slot - chunk](chunk)
+        if between:
+            between.pop(0)()
+            if not between:
+                set_off()
+
+        if ride == "gather" and slot == n_wt + 1:
+            blocks.hand_on()
 
     if spread:
         gathers.arrive()
     if ride == "gather":
-        keep.wait()
-        for copy in riders:
-            copy.wait()
+        blocks.finish()
     elif ride == "sum":
         total = ride_ref[ctx].astype(F32)
         for k, copy in enumerate(riders):
@@ -359,60 +449,90 @@
         rode_ref[...] = total
     if spread:
         gathers.end()
-    if reduce:
-        sums.end()
+    sums.end()
+
+
+def exchange_scratch(n_ctx, n_wt, shape, spread, rounded, ride=None, rider=None):
+    dma = pltpu.SemaphoreType.DMA
+    scratch = RowSum.scratch(n_wt, shape, CHUNKS)
+    scratch += [pltpu.VMEM(shape, F32)] if rounded else []
+    scratch += RowGather.scratch(n_wt, CHUNKS) if spread else []
+    if ride == "gather":
+        scratch += CtxGather.scratch(n_ctx)
+    elif ride:
+        scratch += [pltpu.VMEM((n_ctx - 1,) + tuple(rider[1:]), BF16), dma((n_ctx - 1,)), dma((n_ctx - 1,))]
+    return scratch
+
+
+def exchange_kernel(n_ctx, n_wt, back, spread, rounded, ride, ready, *refs):
+    refs = list(refs)
+    near = Near(n_wt)
+    peers = [(near.section, lax.rem(near.ctx + k, n_ctx), near.wt) for k in range(1, n_ctx)]
+    parts, rows_ref = refs.pop(0), refs.pop(0)
+    stream_ref = refs.pop(0) if back else None
+    gain_ref = refs.pop(0) if (back or spread) else None
+    ride_ref = refs.pop(0) if ride else None
+    result_ref = refs.pop(0)
+    gain_grad_ref = refs.pop(0) if back else None
+    all_ref = refs.pop(0) if spread else None
+    rode_ref = refs.pop(0) if ride else None
+    token_ref = refs.pop(0)
+    token_ref[...] = jnp.zeros(token_ref.shape, F32)
+    near.greet(peers if ride else ())
+    if ready:
+        ready()
+    exchange_steps(
+        near,
+        n_ctx,
+        parts,
+        rows_ref,
+        stream_ref,
+        gain_ref,
+        result_ref,
+        gain_grad_ref,
+        all_ref,
+        spread,
+        rounded,
+        refs,
+        ride,
+        (ride_ref, rode_ref),
+    )
 
 
 VMEM = pl.BlockSpec(memory_space=pltpu.VMEM)
 
 
-def exchange(number, parts, rows, stream=None, gain=None, spread=None, rounded=False, gather=None, add=None):
+def exchange(number, parts, rows, stream=None, gain=None, spread=None, rounded=False, gather=None, add=None, load=False):
     n_ctx, n_wt = lax.axis_size("ctx"), lax.axis_size("wt")
     shape = rows.shape
-    reduce, back = parts is not None, stream is not None
+    back = stream is not None
     ride = "gather" if gather is not None else "sum" if add is not None else None
-    rider = gather if gather is not None else add
-    operands = [
-        member
-        for member, wanted in (
-            (parts, reduce),
-            (rows, True),
-            (stream, back),
-            (gain, back or spread),
-            (rider, ride),
-        )
-        if wanted
-    ]
-    outs = []
-    scratch = []
-    dma = pltpu.SemaphoreType.DMA
-    if reduce:
-        outs.append(jax.ShapeDtypeStruct(shape, BF16 if rounded else F32))
-        scratch += RowSum.scratch(n_wt, shape, CHUNKS)
-        scratch += [pltpu.VMEM(shape, F32)] if rounded else []
+    rider = add if gather is None else gather
+    wanted = ((parts, True), (rows, True), (stream, back), (gain, back or spread), (rider, ride))
+    operands = [member for member, taken in wanted if taken]
+    outs = [jax.ShapeDtypeStruct(shape, BF16 if rounded else F32)]
     if back:
         outs.append(jax.ShapeDtypeStruct((1, shape[1]), F32))
     if spread:
         outs.append(jax.ShapeDtypeStruct((2 * n_wt,) + shape, BF16))
-        scratch += RowGather.scratch(n_wt, CHUNKS)
     if ride == "gather":
-        outs.append(jax.ShapeDtypeStruct((n_ctx,) + rider.shape, BF16))
-        scratch += [pltpu.VMEM((8, 128), BF16), dma((n_ctx - 1,)), dma((n_ctx - 1,)), dma]
+        outs.append(jax.ShapeDtypeStruct((n_ctx,) + gather.shape, BF16))
     elif ride == "sum":
-        outs.append(jax.ShapeDtypeStruct(rider.shape[1:], F32))
-        scratch += [pltpu.VMEM((n_ctx - 1,) + rider.shape[1:], BF16), dma((n_ctx - 1,)), dma((n_ctx - 1,)), dma]
+        outs.append(jax.ShapeDtypeStruct(add.shape[1:], F32))
     outs.append(jax.ShapeDtypeStruct((8, LANES), F32))
-    return pl.pallas_call(
-        functools.partial(exchange_kernel, n_ctx, n_wt, reduce, back, spread, rounded, ride),
+    kernel = functools.partial(exchange_kernel, n_ctx, n_wt, back, spread, rounded, ride)
+    call = dict(
         out_shape=outs,
-        in_specs=[VMEM] * len(operands),
         out_specs=[VMEM] * len(outs),
-        scratch_shapes=scratch,
+        scratch_shapes=exchange_scratch(n_ctx, n_wt, shape, spread, rounded, ride, rider.shape if ride else None),
         compiler_params=pltpu.CompilerParams(
-            collective_id=number, has_side_effects=True, vmem_limit_bytes=16 << 20
+            collective_id=number, has_side_effects=True, vmem_limit_bytes=(60 if load else 16) << 20
         ),
         cost_estimate=pl.CostEstimate(flops=0, bytes_accessed=110 << 20, transcendentals=0),
-    )(*operands)
+    )
+    if load:
+        return loaded(kernel, operands, [], **call)
+    return pl.pallas_call(functools.partial(kernel, None), in_specs=[VMEM] * len(operands), **call)(*operands)
 
 
 def finish_kernel(n_ctx, n_wt, *refs):
@@ -648,7 +768,6 @@
         scaled = jnp.where(low, part * (1.0 / HEAD_SIZE), 0.0).astype(BF16)
         q_ref[0, h] = scaled[:rows]
         q_ref[1, h] = scaled[rows:]
-    ride_on()
     top_ref[...] = jnp.full(top_ref.shape, MASKED, F32)
     sum_ref[...] = jnp.zeros(sum_ref.shape, F32)
     acc_ref[...] = jnp.zeros(acc_ref.shape, F32)
@@ -682,8 +801,9 @@
         blocks_of(lax.rem(ctx + n_ctx - k, n_ctx))
 
     arrived(1)
+    arrived(2)
     ride_on()
-    pl.loop(2, n_ctx)(arrived)
+    pl.loop(3, n_ctx)(arrived)
     while waiting:
         ride_on()
     low = lower_half((rows, LANES))
@@ -741,6 +861,7 @@
     n_ctx,
     n_wt,
     ride,
+    ready,
     a_ref,
     w_ref,
     cos_ref,
@@ -755,22 +876,31 @@
     *refs,
 ):
     refs = list(refs)
-    ride_refs = [refs.pop(0), refs.pop(0)] if ride else None
-    part_ref, raw_ref = refs.pop(0), refs.pop(0)
-    rode_ref = refs.pop(0) if ride else None
+    if ride:
+        rows_ref, stream_ref, gain_ref = [refs.pop(0) for _ in range(3)]
+        ride_refs = [refs.pop(0), refs.pop(0)]
+        raw_ref, result_ref, gain_grad_ref, all_ref, rode_ref = [refs.pop(0) for _ in range(5)]
+    else:
+        raw_ref, part_ref = refs.pop(0), refs.pop(0)
     do_ref, delta_ref, dq_ref, dkv_ref, own_ref, landed, send, recv = refs[:8]
+    refs = refs[8:]
     near = Near(n_wt)
     section, ctx, wt = near.section, near.ctx, near.wt
     peers = [(section, lax.rem(ctx + k, n_ctx), wt) for k in range(1, n_ctx)]
     waiting = []
     if ride:
-        sums = RowSum(near, 1, ride_refs[0], refs[8:17])
-        rode_sum = refs[17]
-        waiting = [functools.partial(sums.point, 0, number) for number in range(n_wt - 1)]
         near.greet(peers)
-        sums.begin()
     else:
         greet(peers)
+    if ready:
+        ready()
+    if ride:
+        part_ref = refs.pop(0)
+        sums = RowSum(near, 1, ride_refs[0], refs[:9])
+        rode_sum = refs[9]
+        refs = refs[10:]
+        waiting = [functools.partial(sums.point, 0, number) for number in range(n_wt - 1)]
+        sums.begin()
 
     def ride_on():
         if waiting:
@@ -842,45 +972,73 @@
     raw_ref[:, :LANES] = turned(first, cosine, -sine).astype(BF16)
     raw_ref[:, LANES : 2 * LANES] = turned(second, cosine, -sine).astype(BF16)
     raw_ref[:, 2 * LANES :] = jnp.where(low, over, 0.0).astype(BF16)
-    part_ref[...] = dot(raw_ref[...], w_ref[:, : 3 * LANES], ((1,), (1,))).astype(BF16)
+    partial = dot(raw_ref[...], w_ref[:, : 3 * LANES], ((1,), (1,))).astype(BF16)
+    part_ref[...] = partial.reshape(part_ref.shape)
     if ride:
         sums.collect(0, rode_sum)
         rode_ref[...] = (rode_sum[...] + ride_refs[1][...]).astype(BF16)
+
+    if ride:
+        exchange_steps(
+            near,
+            n_ctx,
+            part_ref,
+            rows_ref,
+            stream_ref,
+            gain_ref,
+            result_ref,
+            gain_grad_ref,
+            all_ref,
+            "plain",
+            True,
+            refs,
+        )
+    if ride:
         sums.end()
     for k in range(1, n_ctx):
         passing(k).wait_send()
 
 
-def attend_back(number, rows_a, weights, tables, kept, ride=()):
+def attend_back(number, rows_a, weights, tables, kept, then=()):
     n_ctx, n_wt = lax.axis_size("ctx"), lax.axis_size("wt")
     n_rows, width = rows_a.shape
-    rows = n_rows // 2
+    half = n_rows // 2
+    share = n_rows // (2 * n_wt)
     dma = pltpu.SemaphoreType.DMA
-    return pl.pallas_call(
-        functools.partial(attend_back_kernel, n_ctx, n_wt, bool(ride)),
-        out_shape=[
-            jax.ShapeDtypeStruct((n_rows, width), BF16),
-            jax.ShapeDtypeStruct((n_rows, 3 * LANES), BF16),
-        ]
-        + [jax.ShapeDtypeStruct(member.shape, BF16) for member in ride[1:]],
-        in_specs=[VMEM] * (11 + len(ride)),
-        out_specs=[VMEM] * (2 + len(ride) // 2),
-        scratch_shapes=[
-            pltpu.VMEM((2, HEADS, rows, LANES), BF16),
-            pltpu.VMEM((2, HEADS, 1, rows), F32),
-            pltpu.VMEM((2, HEADS, LANES, rows), F32),
-            pltpu.VMEM((n_ctx, n_rows, LANES), BF16),
-            pltpu.VMEM((n_rows, LANES), F32),
-            pltpu.VMEM((n_ctx - 1, n_rows, LANES), BF16),
-            dma((n_ctx,)),
-            dma((n_ctx,)),
-        ]
-        + (RowSum.scratch(n_wt, ride[1].shape, 1) + [pltpu.VMEM(ride[1].shape, F32)] if ride else []),
+    shape = (share, width)
+    blocks = jax.ShapeDtypeStruct((2 * n_wt,) + shape, BF16)
+    outs = [jax.ShapeDtypeStruct((n_rows, 3 * LANES), BF16)]
+    scratch = [
+        pltpu.VMEM((2, HEADS, half, LANES), BF16),
+        pltpu.VMEM((2, HEADS, 1, half), F32),
+        pltpu.VMEM((2, HEADS, LANES, half), F32),
+        pltpu.VMEM((n_ctx, n_rows, LANES), BF16),
+        pltpu.VMEM((n_rows, LANES), F32),
+        pltpu.VMEM((n_ctx - 1, n_rows, LANES), BF16),
+        dma((n_ctx,)),
+        dma((n_ctx,)),
+    ]
+    if then:
+        row = jax.ShapeDtypeStruct(shape, BF16)
+        outs += [row, jax.ShapeDtypeStruct((1, width), F32), blocks, row]
+        scratch += [pltpu.VMEM(blocks.shape, BF16)] + RowSum.scratch(n_wt, shape, 1) + [pltpu.VMEM(shape, F32)]
+        scratch += exchange_scratch(n_ctx, n_wt, shape, "plain", True)
+    else:
+        outs.append(blocks)
+    operands = [rows_a, weights, *tables, *kept, *then]
+    kernel = functools.partial(attend_back_kernel, n_ctx, n_wt, bool(then))
+    call = dict(
+        out_shape=outs,
+        out_specs=[VMEM] * len(outs),
+        scratch_shapes=scratch,
         compiler_params=pltpu.CompilerParams(
-            collective_id=number, has_side_effects=True, vmem_limit_bytes=24 << 20
+            collective_id=number, has_side_effects=True, vmem_limit_bytes=(60 if then else 24) << 20
         ),
-        cost_estimate=pl.CostEstimate(flops=0, bytes_accessed=100 << 20, transcendentals=0),
-    )(rows_a, weights, *tables, *kept, *ride)
+        cost_estimate=pl.CostEstimate(flops=0, bytes_accessed=(200 if then else 100) << 20, transcendentals=0),
+    )
+    if then:
+        return loaded(kernel, operands, [], **call)
+    return pl.pallas_call(functools.partial(kernel, None), in_specs=[VMEM] * len(operands), **call)(*operands)
 
 
 def expert_halves(inward, down, packed, half, per_core):
@@ -948,7 +1106,7 @@
     given = refs[:7]
     all_ref, rode_ref, pack, all_gains, all_router, all_routes = refs[7:13]
     tokens, query, pair, out, gains, router, routes = refs[13:20]
-    halves, first_pack, load, keep, send, recv, ride_send, ride_recv = refs[20:28]
+    halves, first_pack, load, send, recv = refs[20:25]
     near = Near(n_wt)
     loads = [
         pltpu.make_async_copy(source.at[near.section] if k == 0 else source, target, load.at[k])
@@ -958,6 +1116,7 @@
         copy.start()
     section, ctx, wt = near.section, near.ctx, near.wt
     peers = [(section, lax.rem(ctx + k, n_ctx), wt) for k in range(1, n_ctx)]
+    blocks = CtxGather(near, n_ctx, first_pack, rode_ref, refs[25:28])
     gathers = RowGather(near, CHUNKS, all_ref, refs[28:])
     near.greet(peers)
     for copy in loads:
@@ -1004,19 +1163,13 @@
         def _():
             remote(halves.at[layer], packs[1 - layer], send.at[3], recv.at[3], near.sibling).wait_recv()
 
-    own = pltpu.make_async_copy(first_pack, rode_ref.at[ctx], keep)
-    riders = [
-        remote(first_pack, rode_ref.at[ctx], ride_send.at[k], ride_recv.at[k], peers[k]) for k in range(n_ctx - 1)
-    ]
-    for copy in riders + [own]:
-        copy.start()
+    blocks.start()
     for hop in range(1, n_wt):
         for chunk in range(CHUNKS):
             gathers.hop(chunk, hop)
+    blocks.hand_on()
     gathers.arrive()
-    own.wait()
-    for copy in riders:
-        copy.wait()
+    blocks.finish()
     gathers.end()
     shared[0].wait_send()
     for copy in shared[1:]:
@@ -1047,12 +1200,10 @@
             pltpu.VMEM((2,) + pack, BF16),
             pltpu.VMEM(pack, BF16),
             dma((7,)),
-            dma,
             dma((4,)),
             dma((4,)),
-            dma((n_ctx - 1,)),
-            dma((n_ctx - 1,)),
         ]
+        + CtxGather.scratch(n_ctx)
         + RowGather.scratch(n_wt, CHUNKS),
         compiler_params=pltpu.CompilerParams(
             collective_id=number, has_side_effects=True, vmem_limit_bytes=16 << 20
@@ -1093,27 +1244,32 @@
     return expos / jnp.sum(expos, 1, keepdims=True)
 
 
-def experts_kernel(n_ctx, layer, forward, backward, depth, down_rows, ride, *refs):
+def experts_kernel(n_ctx, layer, forward, backward, depth, down_rows, ride, ready, *refs):
     refs = list(refs)
-    x_ref, packed_ref, router_ref, pick_ref = [refs.pop(0) for _ in range(4)]
+    x_ref, router_ref, pick_ref = [refs.pop(0) for _ in range(3)]
     if forward:
         hit_ref = refs.pop(0)
     else:
         gates_ref, gate_up_ref = refs.pop(0), refs.pop(0)
     d_ref = refs.pop(0) if backward else None
     ride_ref = refs.pop(0) if ride else None
+    packed_ref = refs.pop(0)
     part_ref = refs.pop(0) if forward else None
     if forward and not backward:
         gates_ref, gate_up_ref = refs.pop(0), refs.pop(0)
     if backward:
-        back_ref, grads_ref, router_grad_ref = [refs.pop(0) for _ in range(3)]
+        back_out, grads_ref, router_grad_ref = [refs.pop(0) for _ in range(3)]
     rode_ref = refs.pop(0) if ride else None
     inward, down, weighted, load = [refs.pop(0) for _ in range(4)]
     if forward and backward:
         gates_ref, gate_up_ref = refs.pop(0), refs.pop(0)
     if backward:
-        d_gate_up, x_turned, in_grad, down_grad, store = refs[:5]
-        refs = refs[5:]
+        d_gate_up, x_turned, in_grad, down_grad, store, back_ref, leave = refs[:7]
+        refs = refs[7:]
+        if forward:
+            part_out, part_ref = part_ref, refs.pop(0)
+            part_leave = pltpu.make_async_copy(part_ref, part_out, leave.at[1])
+        back_leave = pltpu.make_async_copy(back_ref, back_out, leave.at[0])
 
     pieces = expert_pieces(packed_ref, inward, down, depth, down_rows)
     loads = [pltpu.make_async_copy(source, target, load.at[k]) for k, (source, target) in enumerate(pieces)]
@@ -1133,6 +1289,8 @@
         ]
         for copy in riders:
             copy.start()
+    if ready:
+        ready()
     columns = [slice(t * TILE, (t + 1) * TILE) for t in range(2 * FF // TILE)]
     per_expert = FF // TILE
     width = x_ref.shape[1]
@@ -1166,6 +1324,8 @@
                 dot(weighted[:, :FF], down[0, :, at], ((1,), (0,)))
                 + dot(weighted[:, FF:], down[1, :, at], ((1,), (0,)))
             ).astype(BF16)
+        if backward:
+            part_leave.start()
     else:
         for copy in loads[:n_down]:
             copy.wait()
@@ -1202,6 +1362,7 @@
                 dot(d_gate_up[...], inward[at, :], ((1,), (1,)))
                 + dot(both, jnp.concatenate([table, table], 0), ((1,), (0,)))
             ).astype(BF16)
+        back_leave.start()
         x_turned[...] = jnp.transpose(x_ref[...])
         router_grad = dot(both, x_ref[...], ((0,), (0,)))
         named = router_grad_ref.shape[0]
@@ -1225,6 +1386,9 @@
             stores[n_down + c].start()
         for copy in stores:
             copy.wait()
+        back_leave.wait()
+        if forward:
+            part_leave.wait()
     if ride:
         total = ride_ref[ctx].astype(F32)
         for k, copy in enumerate(riders):
@@ -1240,11 +1404,10 @@
     forward, backward = hit is not None, d_rows is not None
     n_rows, width = x.shape
     any_place = pl.BlockSpec(memory_space=pl.ANY)
-    operands = [x, packed, router, pick]
+    operands = [x, router, pick]
     operands += [hit] if forward else list(kept)
     operands += [d_rows] if backward else []
     operands += [add] if add is not None else []
-    in_specs = [VMEM, any_place] + [VMEM] * (len(operands) - 2)
     rows_out = jax.ShapeDtypeStruct((n_rows, width), BF16)
     inner = [jax.ShapeDtypeStruct((n_rows, LANES), F32), jax.ShapeDtypeStruct((n_rows, 4 * FF), BF16)]
     n_pieces = 5 * packed.shape[0]
@@ -1258,13 +1421,13 @@
     out_specs = []
     if forward:
         outs += [rows_out]
-        out_specs += [VMEM]
+        out_specs += [any_place if backward else VMEM]
     if forward and not backward:
         outs += inner
         out_specs += [VMEM] * 2
     if backward:
         outs += [rows_out, jax.ShapeDtypeStruct(packed.shape, BF16), jax.ShapeDtypeStruct((n_experts, width), F32)]
-        out_specs += [VMEM, any_place, VMEM]
+        out_specs += [any_place, any_place, VMEM]
         if forward:
             scratch += [pltpu.VMEM(member.shape, member.dtype) for member in inner]
         scratch += [
@@ -1273,7 +1436,10 @@
             pltpu.VMEM((width, 4 * FF), BF16),
             pltpu.VMEM((2, FF, width), BF16),
             pltpu.SemaphoreType.DMA((n_pieces,)),
+            pltpu.VMEM((n_rows, width), BF16),
+            pltpu.SemaphoreType.DMA((2,)),
         ]
+        scratch += [pltpu.VMEM((n_rows, width), BF16)] if forward else []
     params = {}
     if add is not None:
         outs.append(jax.ShapeDtypeStruct(add.shape[1:], F32))
@@ -1285,15 +1451,19 @@
         ]
         params = dict(collective_id=number, has_side_effects=True)
     work = n_rows * 6 * width * FF * 2 * ((1 if forward else 0) + (2 if backward else 0))
-    return pl.pallas_call(
-        functools.partial(experts_kernel, n_ctx, layer, forward, backward, depth, down_rows, add is not None),
+    load = forward and backward
+    kernel = functools.partial(experts_kernel, n_ctx, layer, forward, backward, depth, down_rows, add is not None)
+    call = dict(
         out_shape=outs,
-        in_specs=in_specs,
         out_specs=out_specs,
         scratch_shapes=scratch,
-        compiler_params=pltpu.CompilerParams(vmem_limit_bytes=(44 if backward else 28) << 20, **params),
+        compiler_params=pltpu.CompilerParams(vmem_limit_bytes=(60 if load else 44 if backward else 28) << 20, **params),
         cost_estimate=pl.CostEstimate(flops=2 * work, bytes_accessed=40 << 20, transcendentals=0),
-    )(*operands)
+    )
+    if load:
+        return loaded(kernel, operands, [packed], **call)
+    in_specs = [VMEM] * len(operands) + [any_place]
+    return pl.pallas_call(functools.partial(kernel, None), in_specs=in_specs, **call)(*operands, packed)
 
 
 def shards(tokens, cotangent, blocks, routes, norm_gain, w_query, key_value_weight, w_attn_out, router, w_in, w_down):
@@ -1360,7 +1530,7 @@
     top = lax.dynamic_index_in_dim(cotangent, section, 0, False)
 
     attn_full[0] = full.reshape(-1, full.shape[2])
-    moe_full = [gather_experts(moe_pack[0]), None]
+    moe_full = [gather_experts(member) for member in moe_pack]
     saved = []
     outputs = []
     for layer in range(2):
@@ -1373,9 +1543,6 @@
         middle, normed_mid, token = exchange(
             4 + layer, blocked(partial), stream, gain=gain_pack[layer, 1:2], spread="norm"
         )
-        if layer == 0:
-            token, second = lax.optimization_barrier((token, moe_pack[1]))
-            moe_full[1] = gather_experts(second)
         token, moe_full[layer] = lax.optimization_barrier((token, moe_full[layer]))
         pick_now = pick + token
         rows_mid = full_rows(normed_mid)
@@ -1446,33 +1613,22 @@
             gain, moe_grads[1] = lax.optimization_barrier((gain, moe_grads[1]))
         moe_grads[layer] = lax.psum_scatter(packed_grad, "ctx", scatter_dimension=0, tiled=False)
         d_middle, gain_grad_mid, d_attn, token = exchange(
-            8 + layer, blocked(partial), upstream, kept["middle"], gain, spread="plain"
+            8 + layer, blocked(partial), upstream, kept["middle"], gain, spread="plain", load=layer == 1
         )
         rows_a = full_rows(d_attn)
         weights = attn_full[layer]
         if layer == 1:
-            partial, raw, last = attend_back(11, rows_a, weights, tables, kept["heads"], last_rows)
+            then = (d_middle, kept["stream"], gain_pack[1, 0:1], *last_rows)
+            raw, upstream, gain_grad_in, d_mixed, last = attend_back(11, rows_a, weights, tables, kept["heads"], then)
             outputs.append(last)
         else:
-            partial, raw = attend_back(10, rows_a, weights, tables, kept["heads"])
-        attn_parts = dot(kept["rows_in"], jnp.pad(raw, ((0, 0), (0, weights.shape[1] - raw.shape[1]))), ((0,), (0,)))
-        attn_parts = attn_parts + dot(
-            rows_a, jnp.pad(kept["attended"], ((0, 0), (weights.shape[1] - kept["attended"].shape[1], 0))), ((0,), (0,))
-        )
+            raw, partial = attend_back(10, rows_a, weights, tables, kept["heads"])
+        attn_parts = dot(kept["rows_in"], jnp.pad(raw, ((0, 0), (0, LANES))), ((0,), (0,)))
+        attn_parts = attn_parts + dot(rows_a, jnp.pad(kept["attended"], ((0, 0), (2 * LANES, 0))), ((0,), (0,)))
         attn_parts = attn_parts.astype(BF16).reshape(n_ctx, depth, -1)
-        if layer == 1:
-            upstream, gain_grad_in, d_mixed, token = exchange(
-                12,
-                blocked(partial),
-                d_middle,
-                kept["stream"],
-                gain_pack[1, 0:1],
-                spread="plain",
-                rounded=True,
-            )
-        else:
+        if layer == 0:
             upstream, gain_grad_in, attn_grads[0], token = exchange(
-                1, blocked(partial), d_middle, kept["stream"], gain_pack[0, 0:1], rounded=True, add=attn_parts
+                1, partial, d_middle, kept["stream"], gain_pack[0, 0:1], rounded=True, add=attn_parts
             )
         grads_in[layer] = upstream
         small[layer] = [router_grad, gain_grad_in, gain_grad_mid]

time: 560 us -> 541 us (0.966); the launches traced: 550 us -> 537 us
  local copies, waits for them, and re-layouts: 64.4 us -> 44.7 us
  waiting for transfers between devices: 5.21 us -> 11.7 us
    unnamed x213 -> x177, local copies, waits for them, and re-layouts: 59.5 us -> 40.1 us
    pallas_call x12 -> x11, Pallas kernels: 339 us -> 348 us  [the longest x5 176 us: exchange(): pl.pallas_call(functools.partial(kernel, None), in_specs=[VMEM] * len(ope...]
    all_gather x2, waiting for transfers between devices: 0.01 us -> 7.04 us  [gather_experts(): lax.all_gather(pack, 'ctx', axis=0, tiled=True)]
  transfers between devices with their start and end apart: 4 -> 4, of which waited for: 1 -> 3; matrix products, arithmetic and copies ran while one was open for 2% -> 2% of each run, Pallas kernels for 76% -> 77%
where the time goes in v6:
time: 541 us; the launch traced here: 537 us
  Pallas kernels  451 us (83%)
  local copies, waits for them, and re-layouts  44.7 us (8%)
  between operations  15.3 us (3%)
  waiting for transfers between devices  11.7 us (2%)
  other arithmetic  9.5 us (2%)
    pallas_call x5, Pallas kernels, exchange(): pl.pallas_call(functools.partial(kernel, None), in_specs=[VMEM] * len(ope...  176 us
    pallas_call x3, Pallas kernels, loaded(): return pl.pallas_call(body, **call)(*operands, *whole)  122 us
    pallas_call x2, Pallas kernels, attend(): pl.pallas_call(functools.partial(attend_kernel, n_ctx, n_wt, bool(riders)...  41.5 us
    unnamed x177, local copies, waits for them, and re-layouts  40.1 us
    pallas_call x1, Pallas kernels, begin(): pl.pallas_call(functools.partial(begin_kernel, n_ctx, n_wt), out_shape=[j...  37.6 us
    pallas_call x2, Pallas kernels, experts(): pl.pallas_call(functools.partial(kernel, None), in_specs=in_specs, **call)  29.6 us
    pallas_call x1, Pallas kernels, attend_back(): pl.pallas_call(functools.partial(kernel, None), in_specs=[VMEM] * len(ope...  20.4 us
    pallas_call x1, Pallas kernels, finish(): pl.pallas_call(functools.partial(finish_kernel, n_ctx, n_wt), out_shape=[...  12.8 us
  transfers between devices with their start and end apart: 4, of which 3 were waited for; matrix products, arithmetic and copies ran while one was open for 2% of the time, Pallas kernels for 77%

profile of v6, /device:TPU:0, one launch (start us, length us, event | category | flops | bytes accessed | tf_op | source)
XLA Modules:
  0.0 537.1 jit_solution(17551818934979643469)
XLA Ops:
  7.2 1.9 copy-done.11
  9.1 1.4 copy-done.18
  10.5 5.3 shard_map.181
  18.4 1.2 copy-done.37
  19.6 1.0 copy-done.38
  20.5 37.6 %shard_map.178 = (bf16[8,64,1536]{2,1,0:T(8,128)(2,1)S(1)}, bf16[4,384,512]{2,1,0:T(8,128)(2,1)S(1)}, bf16[384,512]{1,0:T(8,128)(2,1)S(1)}, f32[2,2,1536]{2,1,0:...) custom-call(bf16[2,64,1536]{2,1,0:T(8,128)(2,1)S(1)} %copy-done.22, ...), custom_call_target="tpu_custom_call" | custom-call | bytes 94371840 | tf_op jit(solution)/shard_map/pallas_call | solution.py:1185
  58.2 0.7 copy-done.35
  58.9 0.9 copy-done.69
  59.8 0.8 copy-done.72
  60.6 1.2 dynamic-slice_bitcast_fusion
  61.8 1.0 fusion.8
  62.9 21.5 %shard_map.179 = (bf16[512,1536]{1,0:T(8,128)(2,1)S(1)}, bf16[2,3,256,128]{3,2,1,0:T(8,128)(2,1)S(1)}, bf16[4,512,128]{2,1,0:T(8,128)(2,1)S(1)}, f32[2,3,256,128...) custom-call(bf16[512,1536]{1,0:T(8,128)(2,1)S(1)} %bitcast.84, ...), custom_call_target="tpu_custom_call" | custom-call | bytes 73400320 | tf_op jit(solution)/shard_map/pallas_call | solution.py:832
  84.4 0.7 copy-done.39
  85.1 1.1 copy-done.66
  86.2 0.7 slice_bitcast_fusion.1
  86.9 33.8 %shard_map.180 = (f32[64,1536]{1,0:T(8,128)S(1)}, bf16[8,64,1536]{2,1,0:T(8,128)(2,1)S(1)}, f32[8,128]{1,0:T(8,128)S(1)}) custom-call(bf16[8,64,1536]{2,1,0:T(8,128)(2,1)S(1)} %bitcast.97, bf16[64,1536]{1,0:T(8,128)(2,1)S(1)} %get-tuple-element.163.refs_1_.refs_2_, f32[1,1536]{1,0:T(1,128)S(1)} %get-tuple-element.123.refs_2_.refs_3_), custom_call_target="tpu_custom_call" | custom-call | bytes 115343360 | tf_op jit(solution)/shard_map/pallas_call | solution.py:535
  120.8 0.7 copy-done.19
  121.5 1.1 copy-done.63
  122.6 6.7 %all-gather.3.cloned.1.call-done = bf16[2304,2048]{1,0:T(8,128)(2,1)} async-done(((bf16[576,2048]{1,0:T(8,128)(2,1)}), bf16[2304,2048]{1,0:T(8,128)(2,1)}) %all-gather.3.cloned.1.call-update) | async-done | bytes 9437200 | tf_op jit(solution)/shard_map/all_gather | solution.py:1515
  129.5 3.7 copy-done.62
  133.1 1.4 copy-done.64
  134.5 1.1 copy-done.70
  135.7 1.0 copy-done.73
  136.7 8.1 %shard_map.182 = (bf16[512,1536]{1,0:T(8,128)(2,1)S(1)}, f32[512,128]{1,0:T(8,128)S(1)}, bf16[512,2048]{1,0:T(8,128)(2,1)S(1)}) custom-call(bf16[512,1536]{1,0:T(8,128)(2,1)S(1)} %bitcast.114, bf16[2,128,1536]{2,1,0:T(8,128)(2,1)S(1)} %copy-done.70, f32[8,128]{1,0:T(8,128)S(1)} %fusion.11.refs_2_, s32[2,2,256,8]{3,2,1,0:T(8,128)S(1)} %copy-done.73, ...), custom_call_target="tpu_custom_call" | custom-call | flops 9663676416 | bytes 41943040 | tf_op jit(solution)/shard_map/pallas_call | solution.py:1466
  144.9 38.8 %shard_map.183 = (bf16[64,1536]{1,0:T(8,128)(2,1)S(1)}, bf16[8,64,1536]{2,1,0:T(8,128)(2,1)S(1)}, bf16[4,384,512]{2,1,0:T(8,128)(2,1)S(1)}, f32[8,128]{1,0:T(8,128)}) custom-call(bf16[8,64,1536]{2,1,0:T(8,128)(2,1)S(1)} %bitcast.101, f32[64,1536]{1,0:T(8,128)S(1)} %copy-done.20, f32[1,1536]{1,0:T(1,128)S(1)} %get-tuple-element.157.refs_2_.refs_13_, ...), custom_call_target="tpu_custom_call" | custom-call | bytes 115343360 | tf_op jit(solution)/shard_map/pallas_call | solution.py:535
  183.8 20.0 %shard_map.184 = (bf16[512,1536]{1,0:T(8,128)(2,1)S(1)}, bf16[2,3,256,128]{3,2,1,0:T(8,128)(2,1)S(1)}, bf16[4,512,128]{2,1,0:T(8,128)(2,1)S(1)}, f32[2,3,256,128...) custom-call(bf16[512,1536]{1,0:T(8,128)(2,1)S(1)} %bitcast.86, ...), custom_call_target="tpu_custom_call" | custom-call | bytes 73400320 | tf_op jit(solution)/shard_map/pallas_call | solution.py:832
  203.9 0.9 copy-done.23
  204.8 0.8 copy-done.31
  205.6 0.7 copy-done.32
  206.3 0.7 copy-done.41
  207.0 36.0 %shard_map.185 = (f32[64,1536]{1,0:T(8,128)S(1)}, bf16[8,64,1536]{2,1,0:T(8,128)(2,1)S(1)}, f32[8,128]{1,0:T(8,128)S(1)}) custom-call(bf16[8,64,1536]{2,1,0:T(8,128)(2,1)S(1)} %bitcast.98, bf16[64,1536]{1,0:T(8,128)(2,1)S(1)} %get-tuple-element.100.refs_1_.refs_12_.refs_8_, f32[1,1536]{1,0:T(1,128)S(1)} %get-tuple-element.156.refs_2_.refs_3_), custom_call_target="tpu_custom_call" | custom-call | bytes 115343360 | tf_op jit(solution)/shard_map/pallas_call | solution.py:535
  243.1 0.7 copy-done.15
  243.8 1.1 copy-done.68
  245.9 26.1 %shard_map.186 = (bf16[512,1536]{1,0:T(8,128)(2,1)}, bf16[512,1536]{1,0:T(8,128)(2,1)}, bf16[4,576,2048]{2,1,0:T(8,128)(2,1)}, f32[16,1536]{1,0:T(8,128)}) custom-call(bf16[512,1536]{1,0:T(8,128)(2,1)} %bitcast.118, bf16[2,128,1536]{2,1,0:T(8,128)(2,1)} %copy-done.69, f32[8,128]{1,0:T(8,128)} %fusion.10.refs_2_, s32[2,2,256,8]{3,2,1,0:T(8,128)} %copy-done.72, ...), custom_call_target="tpu_custom_call" | custom-call | flops 28991029248 | bytes 41943040 | tf_op jit(solution)/shard_map/pallas_call | solution.py:74
  272.2 35.7 %shard_map.187 = (f32[64,1536]{1,0:T(8,128)}, f32[1,1536]{1,0:T(1,128)}, bf16[8,64,1536]{2,1,0:T(8,128)(2,1)}, f32[8,128]{1,0:T(8,128)}) custom-call(bf16[8,64,1536]{2,1,0:T(8,128)(2,1)} %bitcast.123, bf16[64,1536]{1,0:T(8,128)(2,1)} %copy-done.12, f32[64,1536]{1,0:T(8,128)} %copy-done.15, f32[1,1536]{1,0:T(1,128)} %copy-done.48), custom_call_target="tpu_custom_call" | custom-call | bytes 115343360 | tf_op jit(solution)/shard_map/pallas_call | solution.py:74
  307.9 60.2 %shard_map.188 = (bf16[512,384]{1,0:T(8,128)(2,1)}, bf16[64,1536]{1,0:T(8,128)(2,1)}, f32[1,1536]{1,0:T(1,128)}, bf16[8,64,1536]{2,1,0:T(8,128)(2,1)}, bf16[64,1536]{1,0:T(8,128)(2,1)}) custom-call(bf16[512,1536]{1,0:T(8,128)(2,1)} %bitcast.119, bf16[1536,512]{1,0:T(8,128)(2,1)} %bitcast.94, f32[512,128]{1,0:T(8,128)} %copy-done.6, f32[512,128]{1,0:T(8,128)} %copy-done.4, ...), custom_call_target="tpu_custom_call" | custom-call | bytes 209715200 | tf_op jit(solution)/shard_map/pallas_call | solution.py:74
  368.1 2.1 fusion.6
  370.3 1.0 fusion
  372.5 0.7 copy-done.75
  373.2 21.5 %shard_map.189 = (bf16[512,1536]{1,0:T(8,128)(2,1)S(1)}, bf16[4,576,2048]{2,1,0:T(8,128)(2,1)}, f32[16,1536]{1,0:T(8,128)S(1)}, f32[384,512]{1,0:T(8,128)S(1)}) custom-call(bf16[512,1536]{1,0:T(8,128)(2,1)S(1)} %bitcast.115, bf16[2,128,1536]{2,1,0:T(8,128)(2,1)S(1)} %copy-done.71, f32[8,128]{1,0:T(8,128)S(1)} %fusion.9.refs_2_, f32[512,128]{1,0:T(8,128)S(1)} %copy-done.77, ...), custom_call_target="tpu_custom_call" | custom-call | flops 19327352832 | bytes 41943040 | tf_op jit(solution)/shard_map/pallas_call | solution.py:1466
  394.6 1.1 copy-done.16
  395.8 0.9 copy-done.25
  397.4 0.8 copy-done.24
  398.2 1.4 copy-done.17
  399.6 1.0 copy-done.21
  400.6 34.1 %shard_map.190 = (f32[64,1536]{1,0:T(8,128)S(1)}, f32[1,1536]{1,0:T(1,128)S(1)}, bf16[8,64,1536]{2,1,0:T(8,128)(2,1)S(1)}, f32[8,128]{1,0:T(8,128)}) custom-call(bf16[8,64,1536]{2,1,0:T(8,128)(2,1)S(1)} %bitcast.96, bf16[64,1536]{1,0:T(8,128)(2,1)S(1)} %copy-done.24, f32[64,1536]{1,0:T(8,128)S(1)} %copy-done.21, f32[1,1536]{1,0:T(1,128)S(1)} %get-tuple-element.123.refs_2_.refs_3_), custom_call_target="tpu_custom_call" | custom-call | bytes 115343360 | tf_op jit(solution)/shard_map/pallas_call | solution.py:535
  434.8 1.6 copy-done.9
  436.5 1.1 copy-done.28
  437.6 1.0 copy-done.34
  438.6 0.7 copy-done.57
  439.3 20.4 %shard_map.191 = (bf16[512,384]{1,0:T(8,128)(2,1)S(1)}, bf16[8,64,1536]{2,1,0:T(8,128)(2,1)S(1)}) custom-call(bf16[512,1536]{1,0:T(8,128)(2,1)S(1)} %bitcast.90, bf16[1536,512]{1,0:T(8,128)(2,1)S(1)} %bitcast.89, f32[512,128]{1,0:T(8,128)S(1)} %copy-done.7, f32[512,128]{1,0:T(8,128)S(1)} %copy-done.5, s32[4,512,1]{2,1,0:T(8,128)S(1)} %copy-done.1, ...), custom_call_target="tpu_custom_call" | custom-call | bytes 104857600 | tf_op jit(solution)/shard_map/pallas_call | solution.py:1041
  459.7 1.0 fusion.3
  460.7 1.0 fusion.1
  461.9 33.6 %shard_map.192 = (bf16[64,1536]{1,0:T(8,128)(2,1)S(1)}, f32[1,1536]{1,0:T(1,128)S(1)}, f32[384,512]{1,0:T(8,128)S(1)}, f32[8,128]{1,0:T(8,128)}) custom-call(bf16[8,64,1536]{2,1,0:T(8,128)(2,1)S(1)} %get-tuple-element.129.refs_0_, f32[64,1536]{1,0:T(8,128)S(1)} %get-tuple-element.130.refs_1_, bf16[64,1536]{1,0:T(8,128)(2,1)S(1)} %get-tuple-element.163.refs_1_.refs_2_, ...), custom_call_target="tpu_custom_call" | custom-call | bytes 115343360 | tf_op jit(solution)/shard_map/pallas_call | solution.py:535
  495.5 12.8 %shard_map.193 = (f32[2,128]{1,0:T(2,128)S(1)}, f32[16,128]{1,0:T(8,128)S(1)}, f32[384,384]{1,0:T(8,128)S(1)}, f32[384,256]{1,0:T(8,128)S(1)}, f32[384,384]{1,0:...) custom-call(f32[16,1536]{1,0:T(8,128)S(1)} %copy-done.46, ...), custom_call_target="tpu_custom_call" | custom-call | bytes 41943040 | tf_op jit(solution)/shard_map/pallas_call | solution.py:615
  508.9 4.0 reduce-scatter.9.cloned.1.call-done
  512.8 5.0 shard_map.194
  517.9 5.5 %bitcast_convert_fusion = f32[1,4,384,1024]{3,2,1,0:T(8,128)} fusion(bf16[4,384,1024]{2,1,0:T(8,128)(2,1)} %get-tuple-element.151), kind=kLoop, calls=%fused_computation.2 | loop fusion | flops 1572864 | bytes 9437184 | tf_op jit(solution)/shard_map/broadcast_in_dim | solution.py:1650
  523.4 2.1 bitcast_convert_fusion.1
  525.4 0.9 broadcast_in_dim_reshape.3
  527.0 0.7 copy.48
  527.7 0.7 copy.49
  528.5 0.8 copy.50
  529.3 0.8 copy.51
  (172 shorter events, 6.7 us)
Async XLA Ops:
  7.2 122.2 %all-gather.3.cloned.1.call-start = ((), (), s32[]{:S(2)}) async-start(), calls=%async_computation.2 | async-start | bytes 11796480 | tf_op jit(solution)/shard_map/all_gather | solution.py:1515
  7.2 1.9 copy-start.11
  9.1 1.4 copy-start.18
  15.9 1.8 copy-start.81
  15.9 1.9 copy-start.80
  15.9 229.3 %all-gather.5.cloned.1.call-start = ((), (), s32[]{:S(2)}) async-start(), calls=%async_computation.3 | async-start | bytes 11796480 | tf_op jit(solution)/shard_map/all_gather | solution.py:1515
  16.0 2.4 copy-start.22
  16.0 2.4 copy-start.53
  16.0 2.4 copy-start.55
  16.7 380.7 %reduce-scatter.7.cloned.1.call-start = ((), (), s32[]{:S(2)}) async-start(), calls=%async_computation.4 | async-start | bytes 11796480
  17.0 166.8 %copy-start.49 = (s32[2,1,256]{2,1,0:T(1,128)}, s32[2,1,256]{2,1,0:T(1,128)S(1)}, u32[]{:S(2)}) copy-start(s32[2,1,256]{2,1,0:T(1,128)S(1)} %broadcast_in_dim.73.query_place.refs_5_) | copy-start | bytes 6148
  17.7 166.1 %copy-start.51 = (s32[2,1,256]{2,1,0:T(1,128)}, s32[2,1,256]{2,1,0:T(1,128)S(1)}, u32[]{:S(2)}) copy-start(s32[2,1,256]{2,1,0:T(1,128)S(1)} %broadcast_in_dim.74.query_start.refs_6_) | copy-start | bytes 6148
  17.9 43.9 %copy-start.82 = (f32[1,2,2,128]{3,1,2,0:T(2,128)S(1)}, f32[1,2,2,128]{3,1,2,0:T(2,128)}, u32[]{:S(2)}) copy-start(f32[1,2,2,128]{3,1,2,0:T(2,128)} %copy.39) | copy-start | bytes 6148
  18.3 165.5 %copy-start = (s32[4,512,1]{2,1,0:T(8,128)}, s32[4,512,1]{2,1,0:T(8,128)S(1)}, u32[]{:S(2)}) copy-start(s32[4,512,1]{2,1,0:T(8,128)S(1)} %copy.33.key_place.refs_4_) | copy-start | bytes 24580
  18.4 1.2 copy-start.37
  60.6 23.7 %copy-start.8 = (bf16[4,384,512]{2,1,0:T(8,128)(2,1)}, bf16[4,384,512]{2,1,0:T(8,128)(2,1)S(1)}, u32[]{:S(2)}) copy-start(bf16[4,384,512]{2,1,0:T(8,128)(2,1)S(1)} %get-tuple-element.82) | copy-start | bytes 4718596
  61.8 22.5 %copy-start.12 = (bf16[64,1536]{1,0:T(8,128)(2,1)}, bf16[64,1536]{1,0:T(8,128)(2,1)S(1)}, u32[]{:S(2)}) copy-start(bf16[64,1536]{1,0:T(8,128)(2,1)S(1)} %get-tuple-element.164.refs_0_.refs_1_) | copy-start | bytes 589828
  62.8 121.0 %copy-start.4 = (f32[512,128]{1,0:T(8,128)}, f32[512,128]{1,0:T(8,128)S(1)}, u32[]{:S(2)}) copy-start(f32[512,128]{1,0:T(8,128)S(1)} %get-tuple-element.159.sin_ref.refs_3_) | copy-start | bytes 786436
  62.9 121.0 %copy-start.6 = (f32[512,128]{1,0:T(8,128)}, f32[512,128]{1,0:T(8,128)S(1)}, u32[]{:S(2)}) copy-start(f32[512,128]{1,0:T(8,128)S(1)} %get-tuple-element.160.cos_ref.refs_2_) | copy-start | bytes 786436
  85.1 1.2 copy-start.66
  86.2 34.5 %copy-start.27 = (f32[2,3,256,128]{3,2,1,0:T(8,128)}, f32[2,3,256,128]{3,2,1,0:T(8,128)S(1)}, u32[]{:S(2)}) copy-start(f32[2,3,256,128]{3,2,1,0:T(8,128)S(1)} %get-tuple-element.127.out_ref) | copy-start | bytes 2359300
  86.2 34.5 %copy-start.29 = (bf16[4,512,128]{2,1,0:T(8,128)(2,1)}, bf16[4,512,128]{2,1,0:T(8,128)(2,1)S(1)}, u32[]{:S(2)}) copy-start(bf16[4,512,128]{2,1,0:T(8,128)(2,1)S(1)} %get-tuple-element.126.pairs_ref) | copy-start | bytes 1572868
  86.2 34.5 %copy-start.33 = (bf16[2,3,256,128]{3,2,1,0:T(8,128)(2,1)}, bf16[2,3,256,128]{3,2,1,0:T(8,128)(2,1)S(1)}, u32[]{:S(2)}) copy-start(bf16[2,3,256,128]{3,2,1,0:T(8,128)(2,1)S(1)} %get-tuple-element.125.q_ref) | copy-start | bytes 1179652
  86.2 34.5 %copy-start.56 = (f32[2,3,1,256]{3,2,1,0:T(1,128)}, f32[2,3,1,256]{3,2,1,0:T(1,128)S(1)}, u32[]{:S(2)}) copy-start(f32[2,3,1,256]{3,2,1,0:T(1,128)S(1)} %get-tuple-element.128.lse_ref) | copy-start | bytes 18436
  86.9 58.0 %copy-start.47 = (f32[1,1536]{1,0:T(1,128)}, f32[1,1536]{1,0:T(1,128)S(1)}, u32[]{:S(2)}) copy-start(f32[1,1536]{1,0:T(1,128)S(1)} %get-tuple-element.157.refs_2_.refs_13_) | copy-start | bytes 18436
  86.9 120.1 %copy-start.48 = (f32[1,1536]{1,0:T(1,128)}, f32[1,1536]{1,0:T(1,128)S(1)}, u32[]{:S(2)}) copy-start(f32[1,1536]{1,0:T(1,128)S(1)} %get-tuple-element.156.refs_2_.refs_3_) | copy-start | bytes 18436
  121.5 1.1 copy-start.63
  129.4 3.7 copy-start.62
  133.1 1.4 copy-start.64
  136.7 8.2 %copy-start.20 = (f32[64,1536]{1,0:T(8,128)S(1)}, f32[64,1536]{1,0:T(8,128)}, u32[]{:S(2)}) copy-start(f32[64,1536]{1,0:T(8,128)} %copy-done.19) | copy-start | bytes 1179652
  136.7 8.2 %copy-start.36 = (bf16[384,512]{1,0:T(8,128)(2,1)S(1)}, bf16[384,512]{1,0:T(8,128)(2,1)}, u32[]{:S(2)}) copy-start(bf16[384,512]{1,0:T(8,128)(2,1)} %copy-done.35) | copy-start | bytes 1179652
  144.9 59.0 %copy-start.74 = (bf16[512,2048]{1,0:T(8,128)(2,1)}, bf16[512,2048]{1,0:T(8,128)(2,1)S(1)}, u32[]{:S(2)}) copy-start(bf16[512,2048]{1,0:T(8,128)(2,1)S(1)} %get-tuple-element.93.refs_4_) | copy-start | bytes 6291460
  144.9 59.0 %copy-start.76 = (f32[512,128]{1,0:T(8,128)}, f32[512,128]{1,0:T(8,128)S(1)}, u32[]{:S(2)}) copy-start(f32[512,128]{1,0:T(8,128)S(1)} %get-tuple-element.92.refs_3_) | copy-start | bytes 786436
  183.7 20.1 %copy-start.2 = (bf16[8,64,1536]{2,1,0:T(8,128)(2,1)}, bf16[8,64,1536]{2,1,0:T(8,128)(2,1)S(1)}, u32[]{:S(2)}) copy-start(bf16[8,64,1536]{2,1,0:T(8,128)(2,1)S(1)} %get-tuple-element.97) | copy-start | bytes 4718596
  183.8 20.1 %copy-start.10 = (bf16[4,384,512]{2,1,0:T(8,128)(2,1)}, bf16[4,384,512]{2,1,0:T(8,128)(2,1)S(1)}, u32[]{:S(2)}) copy-start(bf16[4,384,512]{2,1,0:T(8,128)(2,1)S(1)} %get-tuple-element.98) | copy-start | bytes 4718596
  183.8 23.3 %copy-start.13 = (bf16[64,1536]{1,0:T(8,128)(2,1)}, bf16[64,1536]{1,0:T(8,128)(2,1)S(1)}, u32[]{:S(2)}) copy-start(bf16[64,1536]{1,0:T(8,128)(2,1)S(1)} %get-tuple-element.100.refs_1_.refs_12_.refs_8_) | copy-start | bytes 589828
  207.0 65.0 %copy-start.60 = (f32[2,3,1,256]{3,2,1,0:T(1,128)}, f32[2,3,1,256]{3,2,1,0:T(1,128)S(1)}, u32[]{:S(2)}) copy-start(f32[2,3,1,256]{3,2,1,0:T(1,128)S(1)} %get-tuple-element.113.refs_10_) | copy-start | bytes 18436
  272.0 240.8 %reduce-scatter.9.cloned.1.call-start = ((), (), s32[]{:S(2)}) async-start(), calls=%async_computation.5 | async-start | bytes 11796480
  307.9 60.2 %copy-start.3 = (bf16[8,64,1536]{2,1,0:T(8,128)(2,1)S(1)}, bf16[8,64,1536]{2,1,0:T(8,128)(2,1)}, u32[]{:S(2)}) copy-start(bf16[8,64,1536]{2,1,0:T(8,128)(2,1)} %copy-done.2) | copy-start | bytes 4718596
  368.1 2.2 copy-start.42
  368.1 2.2 copy-start.78
  370.3 1.5 copy-start.65
  370.3 2.0 copy-start.67
  370.3 2.2 copy-start.71
  370.3 2.8 copy-start.75
  370.3 2.8 copy-start.77
  394.6 1.1 copy-start.16
  397.3 37.5 %copy-start.50 = (s32[2,1,256]{2,1,0:T(1,128)S(1)}, s32[2,1,256]{2,1,0:T(1,128)}, u32[]{:S(2)}) copy-start(s32[2,1,256]{2,1,0:T(1,128)} %copy-done.49) | copy-start | bytes 6148
  397.3 37.5 %copy-start.52 = (s32[2,1,256]{2,1,0:T(1,128)S(1)}, s32[2,1,256]{2,1,0:T(1,128)}, u32[]{:S(2)}) copy-start(s32[2,1,256]{2,1,0:T(1,128)} %copy-done.51) | copy-start | bytes 6148
  397.3 37.5 %copy-start.1 = (s32[4,512,1]{2,1,0:T(8,128)S(1)}, s32[4,512,1]{2,1,0:T(8,128)}, u32[]{:S(2)}) copy-start(s32[4,512,1]{2,1,0:T(8,128)} %copy-done) | copy-start | bytes 24580
  397.3 37.5 %copy-start.5 = (f32[512,128]{1,0:T(8,128)S(1)}, f32[512,128]{1,0:T(8,128)}, u32[]{:S(2)}) copy-start(f32[512,128]{1,0:T(8,128)} %copy-done.4) | copy-start | bytes 786436
  397.3 37.5 %copy-start.7 = (f32[512,128]{1,0:T(8,128)S(1)}, f32[512,128]{1,0:T(8,128)}, u32[]{:S(2)}) copy-start(f32[512,128]{1,0:T(8,128)} %copy-done.6) | copy-start | bytes 786436
  398.2 1.4 copy-start.17
  400.6 34.2 %copy-start.30 = (bf16[4,512,128]{2,1,0:T(8,128)(2,1)S(1)}, bf16[4,512,128]{2,1,0:T(8,128)(2,1)}, u32[]{:S(2)}) copy-start(bf16[4,512,128]{2,1,0:T(8,128)(2,1)} %copy-done.29) | copy-start | bytes 1572868
  434.8 1.6 copy-start.9
  461.8 33.6 %copy-start.14 = (bf16[64,1536]{1,0:T(8,128)(2,1)S(1)}, bf16[64,1536]{1,0:T(8,128)(2,1)}, u32[]{:S(2)}) copy-start(bf16[64,1536]{1,0:T(8,128)(2,1)} %copy-done.13) | copy-start | bytes 589828
  461.8 33.6 %copy-start.26 = (f32[384,512]{1,0:T(8,128)S(1)}, f32[384,512]{1,0:T(8,128)}, u32[]{:S(2)}) copy-start(f32[384,512]{1,0:T(8,128)} %copy-done.25) | copy-start | bytes 2359300
  461.8 33.6 %copy-start.43 = (bf16[64,1536]{1,0:T(8,128)(2,1)S(1)}, bf16[64,1536]{1,0:T(8,128)(2,1)}, u32[]{:S(2)}) copy-start(bf16[64,1536]{1,0:T(8,128)(2,1)} %get-tuple-element.140.refs_9_) | copy-start | bytes 589828
  461.8 33.6 %copy-start.44 = (f32[16,1536]{1,0:T(8,128)S(1)}, f32[16,1536]{1,0:T(8,128)}, u32[]{:S(2)}) copy-start(f32[16,1536]{1,0:T(8,128)} %get-tuple-element.135.refs_3_) | copy-start | bytes 294916
  461.8 33.6 %copy-start.46 = (f32[16,1536]{1,0:T(8,128)S(1)}, f32[16,1536]{1,0:T(8,128)}, u32[]{:S(2)}) copy-start(f32[16,1536]{1,0:T(8,128)} %copy-done.45) | copy-start | bytes 294916
  461.8 33.6 %copy-start.58 = (f32[1,1536]{1,0:T(1,128)S(1)}, f32[1,1536]{1,0:T(1,128)}, u32[]{:S(2)}) copy-start(f32[1,1536]{1,0:T(1,128)} %get-tuple-element.137.refs_5_) | copy-start | bytes 18436
  461.9 33.6 %copy-start.59 = (f32[1,1536]{1,0:T(1,128)S(1)}, f32[1,1536]{1,0:T(1,128)}, u32[]{:S(2)}) copy-start(f32[1,1536]{1,0:T(1,128)} %get-tuple-element.136.refs_4_) | copy-start | bytes 18436
  508.3 4.5 copy-start.61
  517.9 5.5 %copy-start.79 = (bf16[4,128,1536]{2,1,0:T(8,128)(2,1)S(1)}, bf16[4,128,1536]{2,1,0:T(8,128)(2,1)}, u32[]{:S(2)}) copy-start(bf16[4,128,1536]{2,1,0:T(8,128)(2,1)} %get-tuple-element.152) | copy-start | bytes 4718596
  (24 other events, 21.2 us)
Sparse Core Ops, SparseCore 0:
  16.0 113.3 all-gather.2
  131.2 113.9 all-gather.4
  272.2 98.9 reduce-scatter.6
  397.4 115.3 reduce-scatter.8

commit v7 on v6

--- a/solution.py
+++ b/solution.py
@@ -342,6 +342,80 @@
         for copy in self.far_copies():
             copy.wait()
         for copy in self.near_copies():
+            copy.wait_send()
+
+
+class CtxSum:
+    def __init__(self, near, n_ctx, parts, scratch):
+        self.n_ctx, self.parts = n_ctx, parts
+        *self.buffers, self.send, self.recv = scratch
+        self.ctx = near.ctx
+        x, y = lax.rem(near.ctx, 2), near.ctx // 2
+        self.at_x, self.at_y, self.across = 2 * y + 1 - x, 2 * (1 - y) + x, 2 * (1 - y) + 1 - x
+        self.device = lambda index: (near.section, index, near.wt)
+        half = parts.shape[1] // 2
+        self.halves = (slice(0, half), slice(half, 2 * half))
+
+    @staticmethod
+    def scratch(n_ctx, shape):
+        dma = pltpu.SemaphoreType.DMA
+        rows, columns = shape[1:]
+        if n_ctx != 4:
+            return [pltpu.VMEM((n_ctx - 1, rows, columns), BF16), dma((n_ctx - 1,)), dma((n_ctx - 1,))]
+        return [
+            pltpu.VMEM((2, rows // 2, columns), BF16),
+            pltpu.VMEM((2, rows, columns), BF16),
+            pltpu.VMEM((2, rows, columns), BF16),
+            dma((4,)),
+            dma((4,)),
+        ]
+
+    def copy(self, source, target, number, index):
+        return remote(source, target, self.send.at[number], self.recv.at[number], self.device(index))
+
+    def direct(self):
+        blocks = [lax.rem(self.ctx + 1 + k, self.n_ctx) for k in range(self.n_ctx - 1)]
+        return [self.copy(self.parts.at[block], self.buffers[0].at[k], k, block) for k, block in enumerate(blocks)]
+
+    def far_copies(self):
+        return [
+            self.copy(self.parts.at[self.across, self.halves[k]], self.buffers[0].at[k], k, index)
+            for k, index in enumerate((self.at_x, self.at_y))
+        ]
+
+    def near_copies(self):
+        far, staged, landed = self.buffers
+        return [
+            self.copy(staged.at[k], landed.at[k], 2 + k, index) for k, index in enumerate((self.at_x, self.at_y))
+        ]
+
+    def start(self):
+        for copy in self.far_copies() if self.n_ctx == 4 else self.direct():
+            copy.start()
+
+    def hand_on(self):
+        if self.n_ctx != 4:
+            return
+        far, staged, landed = self.buffers
+        for k, block in ((1, self.at_y), (0, self.at_x)):
+            self.far_copies()[1 - k].wait_recv()
+            staged[k] = self.parts[block]
+            at = self.halves[1 - k]
+            staged[k, at, :] = (self.parts[block, at, :].astype(F32) + far[1 - k].astype(F32)).astype(BF16)
+            self.near_copies()[k].start()
+
+    def finish(self, result):
+        total = self.parts[self.ctx].astype(F32)
+        if self.n_ctx == 4:
+            for k, copy in enumerate(self.near_copies()):
+                copy.wait_recv()
+                total = total + self.buffers[2][k].astype(F32)
+        else:
+            for k, copy in enumerate(self.direct()):
+                copy.wait_recv()
+                total = total + self.buffers[0][k].astype(F32)
+        result[...] = total
+        for copy in self.far_copies() + self.near_copies() if self.n_ctx == 4 else self.direct():
             copy.wait_send()
 
 
@@ -360,10 +434,8 @@
     scratch,
     ride=None,
     ride_refs=None,
-    between=(),
 ):
-    section, ctx, wt, n_wt = near.section, near.ctx, near.wt, near.n_wt
-    peers = [(section, lax.rem(ctx + k, n_ctx), wt) for k in range(1, n_ctx)]
+    n_wt = near.n_wt
     scratch = list(scratch)
     sums = RowSum(near, CHUNKS, parts, scratch[:9])
     scratch = scratch[9:]
@@ -378,24 +450,8 @@
         if ride == "gather":
             blocks = CtxGather(near, n_ctx, ride_ref, rode_ref, scratch)
         else:
-            landed, ride_send, ride_recv = scratch
-            riders = [
-                remote(
-                    ride_ref.at[lax.rem(ctx + 1 + k, n_ctx)], landed.at[k], ride_send.at[k], ride_recv.at[k], peers[k]
-                )
-                for k in range(n_ctx - 1)
-            ]
-
-    def set_off():
-        if ride == "gather":
-            blocks.start()
-        elif ride:
-            for copy in riders:
-                copy.start()
-
-    between = list(between)
-    if not between:
-        set_off()
+            blocks = CtxSum(near, n_ctx, ride_ref, scratch)
+        blocks.start()
 
     def settle(chunk):
         at = rows_of(chunk, chunk_rows)
@@ -429,12 +485,7 @@
         for chunk in reversed(range(CHUNKS)):
             if 0 <= slot - chunk < len(stages):
                 stages[slot - chunk](chunk)
-        if between:
-            between.pop(0)()
-            if not between:
-                set_off()
-
-        if ride == "gather" and slot == n_wt + 1:
+        if ride and slot == (n_wt + 1 if spread else 1):
             blocks.hand_on()
 
     if spread:
@@ -442,11 +493,7 @@
     if ride == "gather":
         blocks.finish()
     elif ride == "sum":
-        total = ride_ref[ctx].astype(F32)
-        for k, copy in enumerate(riders):
-            copy.wait()
-            total = total + landed[k].astype(F32)
-        rode_ref[...] = total
+        blocks.finish(rode_ref)
     if spread:
         gathers.end()
     sums.end()
@@ -460,7 +507,7 @@
     if ride == "gather":
         scratch += CtxGather.scratch(n_ctx)
     elif ride:
-        scratch += [pltpu.VMEM((n_ctx - 1,) + tuple(rider[1:]), BF16), dma((n_ctx - 1,)), dma((n_ctx - 1,))]
+        scratch += CtxSum.scratch(n_ctx, rider)
     return scratch
 
 
@@ -1097,7 +1144,7 @@
         out_specs=[in_place] * 2,
         scratch_shapes=[pltpu.VMEM((2,) + shape, BF16), dma((12,)), dma, dma, dma],
         compiler_params=pltpu.CompilerParams(
-            collective_id=number, has_side_effects=True, vmem_limit_bytes=12 << 20
+            collective_id=number, has_side_effects=True, vmem_limit_bytes=60 << 20
         ),
     )(inward, down)
 
@@ -1277,18 +1324,10 @@
     for copy in (loads[n_down:] + loads[:n_down]) if forward else loads:
         copy.start()
     if ride:
-        landed, ride_send, ride_recv = refs
-        section, ctx, wt = place()
-        peers = [(section, lax.rem(ctx + k, n_ctx), wt) for k in range(1, n_ctx)]
-        greet(peers)
-        riders = [
-            remote(
-                ride_ref.at[lax.rem(ctx + 1 + k, n_ctx)], landed.at[k], ride_send.at[k], ride_recv.at[k], peers[k]
-            )
-            for k in range(n_ctx - 1)
-        ]
-        for copy in riders:
-            copy.start()
+        near = Near(1)
+        greet([(near.section, lax.rem(near.ctx + k, n_ctx), near.wt) for k in range(1, n_ctx)])
+        blocks = CtxSum(near, n_ctx, ride_ref, refs)
+        blocks.start()
     if ready:
         ready()
     columns = [slice(t * TILE, (t + 1) * TILE) for t in range(2 * FF // TILE)]
@@ -1346,6 +1385,8 @@
             d_hidden = d_weighted * weight
             d_gate_up[:, gate_at(t)] = (d_hidden * up * (sigmoid * (1.0 + gate * (1.0 - sigmoid)))).astype(BF16)
             d_gate_up[:, up_at(t)] = (d_hidden * activated).astype(BF16)
+        if ride:
+            blocks.hand_on()
         gates = gates_ref[...]
         terms = gates * (pick_ref[0:1, :] * d_weight[0] + pick_ref[1:2, :] * d_weight[1])
         d_logits = terms - gates * jnp.sum(terms, 1, keepdims=True)
@@ -1390,11 +1431,7 @@
         if forward:
             part_leave.wait()
     if ride:
-        total = ride_ref[ctx].astype(F32)
-        for k, copy in enumerate(riders):
-            copy.wait()
-            total = total + landed[k].astype(F32)
-        rode_ref[...] = total
+        blocks.finish(rode_ref)
 
 
 def experts(
@@ -1444,11 +1481,7 @@
     if add is not None:
         outs.append(jax.ShapeDtypeStruct(add.shape[1:], F32))
         out_specs.append(VMEM)
-        scratch += [
-            pltpu.VMEM((n_ctx - 1,) + add.shape[1:], BF16),
-            pltpu.SemaphoreType.DMA((n_ctx - 1,)),
-            pltpu.SemaphoreType.DMA((n_ctx - 1,)),
-        ]
+        scratch += CtxSum.scratch(n_ctx, add.shape)
         params = dict(collective_id=number, has_side_effects=True)
     work = n_rows * 6 * width * FF * 2 * ((1 if forward else 0) + (2 if backward else 0))
     load = forward and backward
@@ -1613,7 +1646,7 @@
             gain, moe_grads[1] = lax.optimization_barrier((gain, moe_grads[1]))
         moe_grads[layer] = lax.psum_scatter(packed_grad, "ctx", scatter_dimension=0, tiled=False)
         d_middle, gain_grad_mid, d_attn, token = exchange(
-            8 + layer, blocked(partial), upstream, kept["middle"], gain, spread="plain", load=layer == 1
+            8 + layer, blocked(partial), upstream, kept["middle"], gain, spread="plain", load=True
         )
         rows_a = full_rows(d_attn)
         weights = attn_full[layer]

time: 541 us -> 537 us (level)
  local copies, waits for them, and re-layouts: 44.7 us -> 36.8 us
  Pallas kernels: 451 us -> 457 us
    pallas_call x5 -> x4, Pallas kernels: 176 us -> 137 us  [exchange(): pl.pallas_call(functools.partial(kernel, None), in_specs=[VMEM] * len(ope...]
    pallas_call x3 -> x4, Pallas kernels: 122 us -> 160 us  [loaded(): return pl.pallas_call(body, **call)(*operands, *whole)]
    pallas_call x1, Pallas kernels: 12.8 us -> 20.7 us  [finish(): pl.pallas_call(functools.partial(finish_kernel, n_ctx, n_wt), out_shape=[...]
    unnamed x177 -> x165, local copies, waits for them, and re-layouts: 40.1 us -> 32.9 us
  transfers between devices with their start and end apart: 4 -> 4, of which waited for: 3 -> 2; matrix products, arithmetic and copies ran while one was open for 2% -> 2% of each run, Pallas kernels for 77% -> 79%
where the time goes in v7:
time: 537 us; the launch traced here: 534 us
  Pallas kernels  457 us (85%)
  local copies, waits for them, and re-layouts  36.8 us (7%)
  between operations  15.1 us (3%)
  waiting for transfers between devices  9.79 us (2%)
  other arithmetic  9.5 us (2%)
    pallas_call x4, Pallas kernels, loaded(): return pl.pallas_call(body, **call)(*operands, *whole)  160 us
    pallas_call x4, Pallas kernels, exchange(): pl.pallas_call(functools.partial(kernel, None), in_specs=[VMEM] * len(ope...  137 us
    pallas_call x2, Pallas kernels, attend(): pl.pallas_call(functools.partial(attend_kernel, n_ctx, n_wt, bool(riders)...  41.8 us
    pallas_call x1, Pallas kernels, begin(): pl.pallas_call(functools.partial(begin_kernel, n_ctx, n_wt), out_shape=[j...  37 us
    unnamed x165, local copies, waits for them, and re-layouts  32.9 us
    pallas_call x2, Pallas kernels, experts(): pl.pallas_call(functools.partial(kernel, None), in_specs=in_specs, **call)  28.1 us
    pallas_call x1, Pallas kernels, finish(): pl.pallas_call(functools.partial(finish_kernel, n_ctx, n_wt), out_shape=[...  20.7 us
    pallas_call x1, Pallas kernels, attend_back(): pl.pallas_call(functools.partial(kernel, None), in_specs=[VMEM] * len(ope...  20.5 us
  transfers between devices with their start and end apart: 4, of which 2 were waited for; matrix products, arithmetic and copies ran while one was open for 2% of the time, Pallas kernels for 79%

profile of v7, /device:TPU:0, one launch (start us, length us, event | category | flops | bytes accessed | tf_op | source)
XLA Modules:
  0.0 533.9 jit_solution(12942597966846312661)
XLA Ops:
  7.2 7.0 %shard_map.181 = (bf16[576,2048]{1,0:T(8,128)(2,1)}, bf16[576,2048]{1,0:T(8,128)(2,1)}) custom-call(bf16[4,384,1024]{2,1,0:T(8,128)(2,1)} %bitcast.119, bf16[4,128,1536]{2,1,0:T(8,128)(2,1)} %bitcast.123), custom_call_target="tpu_custom_call" | custom-call | tf_op jit(solution)/shard_map/pallas_call | solution.py:1140
  14.4 0.7 all-gather.5.cloned.1.call-update
  16.2 1.2 copy-done.35
  17.4 1.0 copy-done.36
  18.3 37.0 %shard_map.178 = (bf16[8,64,1536]{2,1,0:T(8,128)(2,1)S(1)}, bf16[4,384,512]{2,1,0:T(8,128)(2,1)S(1)}, bf16[384,512]{1,0:T(8,128)(2,1)S(1)}, f32[2,2,1536]{2,1,0:...) custom-call(bf16[2,64,1536]{2,1,0:T(8,128)(2,1)S(1)} %copy-done.19, ...), custom_call_target="tpu_custom_call" | custom-call | bytes 94371840 | tf_op jit(solution)/shard_map/pallas_call | solution.py:1232
  55.3 0.7 copy-done.32
  56.1 0.9 copy-done.64
  57.0 0.8 copy-done.67
  57.8 1.2 dynamic-slice_bitcast_fusion
  59.0 1.0 fusion.8
  60.0 21.7 %shard_map.179 = (bf16[512,1536]{1,0:T(8,128)(2,1)S(1)}, bf16[2,3,256,128]{3,2,1,0:T(8,128)(2,1)S(1)}, bf16[4,512,128]{2,1,0:T(8,128)(2,1)S(1)}, f32[2,3,256,128...) custom-call(bf16[512,1536]{1,0:T(8,128)(2,1)S(1)} %bitcast.84, ...), custom_call_target="tpu_custom_call" | custom-call | bytes 73400320 | tf_op jit(solution)/shard_map/pallas_call | solution.py:879
  81.8 0.7 copy-done.37
  82.5 1.2 copy-done.61
  83.7 33.8 %shard_map.180 = (f32[64,1536]{1,0:T(8,128)S(1)}, bf16[8,64,1536]{2,1,0:T(8,128)(2,1)S(1)}, f32[8,128]{1,0:T(8,128)S(1)}) custom-call(bf16[8,64,1536]{2,1,0:T(8,128)(2,1)S(1)} %bitcast.96, bf16[64,1536]{1,0:T(8,128)(2,1)S(1)} %get-tuple-element.163.refs_1_.refs_2_, f32[1,1536]{1,0:T(1,128)S(1)} %get-tuple-element.123.refs_2_.refs_3_), custom_call_target="tpu_custom_call" | custom-call | bytes 115343360 | tf_op jit(solution)/shard_map/pallas_call | solution.py:582
  117.5 0.7 copy-done.17
  118.3 1.1 copy-done.58
  119.4 8.6 %all-gather.3.cloned.1.call-done = bf16[2304,2048]{1,0:T(8,128)(2,1)} async-done(((bf16[576,2048]{1,0:T(8,128)(2,1)}), bf16[2304,2048]{1,0:T(8,128)(2,1)}) %all-gather.3.cloned.1.call-update) | async-done | bytes 9437200 | tf_op jit(solution)/shard_map/all_gather | solution.py:1548
  128.1 3.7 copy-done.57
  131.8 1.4 copy-done.59
  133.2 1.1 copy-done.65
  134.3 1.0 copy-done.68
  135.4 8.1 %shard_map.182 = (bf16[512,1536]{1,0:T(8,128)(2,1)S(1)}, f32[512,128]{1,0:T(8,128)S(1)}, bf16[512,2048]{1,0:T(8,128)(2,1)S(1)}) custom-call(bf16[512,1536]{1,0:T(8,128)(2,1)S(1)} %bitcast.112, bf16[2,128,1536]{2,1,0:T(8,128)(2,1)S(1)} %copy-done.65, f32[8,128]{1,0:T(8,128)S(1)} %fusion.11.refs_2_, s32[2,2,256,8]{3,2,1,0:T(8,128)S(1)} %copy-done.68, ...), custom_call_target="tpu_custom_call" | custom-call | flops 9663676416 | bytes 41943040 | tf_op jit(solution)/shard_map/pallas_call | solution.py:1499
  143.6 38.9 %shard_map.183 = (bf16[64,1536]{1,0:T(8,128)(2,1)S(1)}, bf16[8,64,1536]{2,1,0:T(8,128)(2,1)S(1)}, bf16[4,384,512]{2,1,0:T(8,128)(2,1)S(1)}, f32[8,128]{1,0:T(8,128)}) custom-call(bf16[8,64,1536]{2,1,0:T(8,128)(2,1)S(1)} %bitcast.99, f32[64,1536]{1,0:T(8,128)S(1)} %copy-done.18, f32[1,1536]{1,0:T(1,128)S(1)} %get-tuple-element.157.refs_2_.refs_13_, ...), custom_call_target="tpu_custom_call" | custom-call | bytes 115343360 | tf_op jit(solution)/shard_map/pallas_call | solution.py:582
  182.5 20.0 %shard_map.184 = (bf16[512,1536]{1,0:T(8,128)(2,1)S(1)}, bf16[2,3,256,128]{3,2,1,0:T(8,128)(2,1)S(1)}, bf16[4,512,128]{2,1,0:T(8,128)(2,1)S(1)}, f32[2,3,256,128...) custom-call(bf16[512,1536]{1,0:T(8,128)(2,1)S(1)} %bitcast.86, ...), custom_call_target="tpu_custom_call" | custom-call | bytes 73400320 | tf_op jit(solution)/shard_map/pallas_call | solution.py:879
  202.6 0.9 copy-done.20
  203.5 0.8 copy-done.28
  204.3 0.7 copy-done.29
  205.0 0.7 copy-done.39
  205.7 35.7 %shard_map.185 = (f32[64,1536]{1,0:T(8,128)S(1)}, bf16[8,64,1536]{2,1,0:T(8,128)(2,1)S(1)}, f32[8,128]{1,0:T(8,128)S(1)}) custom-call(bf16[8,64,1536]{2,1,0:T(8,128)(2,1)S(1)} %bitcast.97, bf16[64,1536]{1,0:T(8,128)(2,1)S(1)} %get-tuple-element.100.refs_1_.refs_12_.refs_8_, f32[1,1536]{1,0:T(1,128)S(1)} %get-tuple-element.156.refs_2_.refs_3_), custom_call_target="tpu_custom_call" | custom-call | bytes 115343360 | tf_op jit(solution)/shard_map/pallas_call | solution.py:582
  241.5 0.7 copy-done.15
  242.2 1.1 copy-done.63
  243.3 0.5 all-gather.5.cloned.1.call-done
  243.8 0.7 fusion.10.refs_2_
  244.5 26.1 %shard_map.186 = (bf16[512,1536]{1,0:T(8,128)(2,1)}, bf16[512,1536]{1,0:T(8,128)(2,1)}, bf16[4,576,2048]{2,1,0:T(8,128)(2,1)}, f32[16,1536]{1,0:T(8,128)}) custom-call(bf16[512,1536]{1,0:T(8,128)(2,1)} %bitcast.116, bf16[2,128,1536]{2,1,0:T(8,128)(2,1)} %copy-done.64, f32[8,128]{1,0:T(8,128)} %fusion.10.refs_2_, s32[2,2,256,8]{3,2,1,0:T(8,128)} %copy-done.67, ...), custom_call_target="tpu_custom_call" | custom-call | flops 28991029248 | bytes 41943040 | tf_op jit(solution)/shard_map/pallas_call | solution.py:74
  270.7 35.9 %shard_map.187 = (f32[64,1536]{1,0:T(8,128)}, f32[1,1536]{1,0:T(1,128)}, bf16[8,64,1536]{2,1,0:T(8,128)(2,1)}, f32[8,128]{1,0:T(8,128)}) custom-call(bf16[8,64,1536]{2,1,0:T(8,128)(2,1)} %bitcast.122, bf16[64,1536]{1,0:T(8,128)(2,1)} %copy-done.12, f32[64,1536]{1,0:T(8,128)} %copy-done.15, f32[1,1536]{1,0:T(1,128)} %copy-done.45), custom_call_target="tpu_custom_call" | custom-call | bytes 115343360 | tf_op jit(solution)/shard_map/pallas_call | solution.py:74
  306.6 60.1 %shard_map.188 = (bf16[512,384]{1,0:T(8,128)(2,1)}, bf16[64,1536]{1,0:T(8,128)(2,1)}, f32[1,1536]{1,0:T(1,128)}, bf16[8,64,1536]{2,1,0:T(8,128)(2,1)}, bf16[64,1536]{1,0:T(8,128)(2,1)}) custom-call(bf16[512,1536]{1,0:T(8,128)(2,1)} %bitcast.117, bf16[1536,512]{1,0:T(8,128)(2,1)} %bitcast.94, f32[512,128]{1,0:T(8,128)} %copy-done.6, f32[512,128]{1,0:T(8,128)} %copy-done.4, ...), custom_call_target="tpu_custom_call" | custom-call | bytes 209715200 | tf_op jit(solution)/shard_map/pallas_call | solution.py:74
  366.8 2.1 fusion.6
  369.0 1.0 fusion
  370.0 0.4 copy-done.60
  370.4 0.5 copy-done.62
  371.1 0.7 copy-done.70
  371.8 19.9 %shard_map.189 = (bf16[512,1536]{1,0:T(8,128)(2,1)S(1)}, bf16[4,576,2048]{2,1,0:T(8,128)(2,1)}, f32[16,1536]{1,0:T(8,128)S(1)}, f32[384,512]{1,0:T(8,128)S(1)}) custom-call(bf16[512,1536]{1,0:T(8,128)(2,1)S(1)} %bitcast.113, bf16[2,128,1536]{2,1,0:T(8,128)(2,1)S(1)} %copy-done.66, f32[8,128]{1,0:T(8,128)S(1)} %fusion.9.refs_2_, f32[512,128]{1,0:T(8,128)S(1)} %copy-done.72, ...), custom_call_target="tpu_custom_call" | custom-call | flops 19327352832 | bytes 41943040 | tf_op jit(solution)/shard_map/pallas_call | solution.py:1499
  391.7 1.1 copy-done.16
  392.9 0.9 copy-done.22
  393.9 37.9 %shard_map.190 = (f32[64,1536]{1,0:T(8,128)}, f32[1,1536]{1,0:T(1,128)}, bf16[8,64,1536]{2,1,0:T(8,128)(2,1)}, f32[8,128]{1,0:T(8,128)}) custom-call(bf16[8,64,1536]{2,1,0:T(8,128)(2,1)} %bitcast.95, bf16[64,1536]{1,0:T(8,128)(2,1)} %get-tuple-element.121.refs_1_.refs_11_, f32[64,1536]{1,0:T(8,128)} %copy-done.17, f32[1,1536]{1,0:T(1,128)} %copy-done.43), custom_call_target="tpu_custom_call" | custom-call | bytes 115343360 | tf_op jit(solution)/shard_map/pallas_call | solution.py:74
  431.9 1.4 copy-done.9
  433.3 1.5 copy-done.10
  434.8 1.1 copy-done.25
  435.9 1.0 copy-done.31
  436.9 20.5 %shard_map.191 = (bf16[512,384]{1,0:T(8,128)(2,1)S(1)}, bf16[8,64,1536]{2,1,0:T(8,128)(2,1)S(1)}) custom-call(bf16[512,1536]{1,0:T(8,128)(2,1)S(1)} %bitcast.90, bf16[1536,512]{1,0:T(8,128)(2,1)S(1)} %bitcast.89, f32[512,128]{1,0:T(8,128)S(1)} %copy-done.7, f32[512,128]{1,0:T(8,128)S(1)} %copy-done.5, s32[4,512,1]{2,1,0:T(8,128)S(1)} %copy-done.1, ...), custom_call_target="tpu_custom_call" | custom-call | bytes 104857600 | tf_op jit(solution)/shard_map/pallas_call | solution.py:1088
  457.5 1.0 fusion.3
  458.5 1.0 fusion.1
  459.6 28.8 %shard_map.192 = (bf16[64,1536]{1,0:T(8,128)(2,1)S(1)}, f32[1,1536]{1,0:T(1,128)S(1)}, f32[384,512]{1,0:T(8,128)S(1)}, f32[8,128]{1,0:T(8,128)}) custom-call(bf16[8,64,1536]{2,1,0:T(8,128)(2,1)S(1)} %get-tuple-element.129.refs_0_, f32[64,1536]{1,0:T(8,128)S(1)} %copy-done.34, bf16[64,1536]{1,0:T(8,128)(2,1)S(1)} %get-tuple-element.163.refs_1_.refs_2_, ...), custom_call_target="tpu_custom_call" | custom-call | bytes 115343360 | tf_op jit(solution)/shard_map/pallas_call | solution.py:582
  488.5 20.7 %shard_map.193 = (f32[2,128]{1,0:T(2,128)S(1)}, f32[16,128]{1,0:T(8,128)S(1)}, f32[384,384]{1,0:T(8,128)S(1)}, f32[384,256]{1,0:T(8,128)S(1)}, f32[384,384]{1,0:...) custom-call(f32[16,1536]{1,0:T(8,128)S(1)} %get-tuple-element.119.refs_0_, ...), custom_call_target="tpu_custom_call" | custom-call | bytes 41943040 | tf_op jit(solution)/shard_map/pallas_call | solution.py:662
  509.2 0.6 slice_bitcast_fusion.5
  509.8 5.0 shard_map.194
  514.9 5.5 %bitcast_convert_fusion = f32[1,4,384,1024]{3,2,1,0:T(8,128)} fusion(bf16[4,384,1024]{2,1,0:T(8,128)(2,1)} %get-tuple-element.151), kind=kLoop, calls=%fused_computation.2 | loop fusion | flops 1572864 | bytes 9437184 | tf_op jit(solution)/shard_map/broadcast_in_dim | solution.py:1683
  520.3 2.1 bitcast_convert_fusion.1
  522.4 0.9 broadcast_in_dim_reshape.3
  523.3 0.6 slice_bitcast_fusion
  523.9 0.7 copy.48
  524.7 0.7 copy.49
  525.4 0.8 copy.50
  526.2 0.8 copy.51
  (160 shorter events, 1.8 us)
Async XLA Ops:
  7.2 120.8 %all-gather.3.cloned.1.call-start = ((), (), s32[]{:S(2)}) async-start(), calls=%async_computation.2 | async-start | bytes 11796480 | tf_op jit(solution)/shard_map/all_gather | solution.py:1548
  14.3 1.2 copy-start.76
  14.3 1.3 copy-start.75
  14.3 229.5 %all-gather.5.cloned.1.call-start = ((), (), s32[]{:S(2)}) async-start(), calls=%async_computation.3 | async-start | bytes 11796480 | tf_op jit(solution)/shard_map/all_gather | solution.py:1548
  14.4 1.8 copy-start.19
  14.4 1.8 copy-start.50
  14.4 1.8 copy-start.51
  15.1 378.8 %reduce-scatter.7.cloned.1.call-start = ((), (), s32[]{:S(2)}) async-start(), calls=%async_computation.4 | async-start | bytes 11796480
  15.4 167.1 %copy-start.46 = (s32[2,1,256]{2,1,0:T(1,128)}, s32[2,1,256]{2,1,0:T(1,128)S(1)}, u32[]{:S(2)}) copy-start(s32[2,1,256]{2,1,0:T(1,128)S(1)} %broadcast_in_dim.73.query_place.refs_5_) | copy-start | bytes 6148
  15.5 167.0 %copy-start.48 = (s32[2,1,256]{2,1,0:T(1,128)}, s32[2,1,256]{2,1,0:T(1,128)S(1)}, u32[]{:S(2)}) copy-start(s32[2,1,256]{2,1,0:T(1,128)S(1)} %broadcast_in_dim.74.query_start.refs_6_) | copy-start | bytes 6148
  16.1 166.3 %copy-start = (s32[4,512,1]{2,1,0:T(8,128)}, s32[4,512,1]{2,1,0:T(8,128)S(1)}, u32[]{:S(2)}) copy-start(s32[4,512,1]{2,1,0:T(8,128)S(1)} %copy.33.key_place.refs_4_) | copy-start | bytes 24580
  16.2 1.2 copy-start.35
  57.7 24.0 %copy-start.8 = (bf16[4,384,512]{2,1,0:T(8,128)(2,1)}, bf16[4,384,512]{2,1,0:T(8,128)(2,1)S(1)}, u32[]{:S(2)}) copy-start(bf16[4,384,512]{2,1,0:T(8,128)(2,1)S(1)} %get-tuple-element.82) | copy-start | bytes 4718596
  59.0 22.8 %copy-start.12 = (bf16[64,1536]{1,0:T(8,128)(2,1)}, bf16[64,1536]{1,0:T(8,128)(2,1)S(1)}, u32[]{:S(2)}) copy-start(bf16[64,1536]{1,0:T(8,128)(2,1)S(1)} %get-tuple-element.164.refs_0_.refs_1_) | copy-start | bytes 589828
  60.0 122.5 %copy-start.4 = (f32[512,128]{1,0:T(8,128)}, f32[512,128]{1,0:T(8,128)S(1)}, u32[]{:S(2)}) copy-start(f32[512,128]{1,0:T(8,128)S(1)} %get-tuple-element.159.sin_ref.refs_3_) | copy-start | bytes 786436
  60.0 122.5 %copy-start.6 = (f32[512,128]{1,0:T(8,128)}, f32[512,128]{1,0:T(8,128)S(1)}, u32[]{:S(2)}) copy-start(f32[512,128]{1,0:T(8,128)S(1)} %get-tuple-element.160.cos_ref.refs_2_) | copy-start | bytes 786436
  82.5 1.2 copy-start.61
  83.6 33.9 %copy-start.24 = (f32[2,3,256,128]{3,2,1,0:T(8,128)}, f32[2,3,256,128]{3,2,1,0:T(8,128)S(1)}, u32[]{:S(2)}) copy-start(f32[2,3,256,128]{3,2,1,0:T(8,128)S(1)} %get-tuple-element.127.out_ref) | copy-start | bytes 2359300
  83.6 33.9 %copy-start.26 = (bf16[4,512,128]{2,1,0:T(8,128)(2,1)}, bf16[4,512,128]{2,1,0:T(8,128)(2,1)S(1)}, u32[]{:S(2)}) copy-start(bf16[4,512,128]{2,1,0:T(8,128)(2,1)S(1)} %get-tuple-element.126.pairs_ref) | copy-start | bytes 1572868
  83.6 33.9 %copy-start.30 = (bf16[2,3,256,128]{3,2,1,0:T(8,128)(2,1)}, bf16[2,3,256,128]{3,2,1,0:T(8,128)(2,1)S(1)}, u32[]{:S(2)}) copy-start(bf16[2,3,256,128]{3,2,1,0:T(8,128)(2,1)S(1)} %get-tuple-element.125.q_ref) | copy-start | bytes 1179652
  83.7 59.9 %copy-start.43 = (f32[1,1536]{1,0:T(1,128)}, f32[1,1536]{1,0:T(1,128)S(1)}, u32[]{:S(2)}) copy-start(f32[1,1536]{1,0:T(1,128)S(1)} %get-tuple-element.123.refs_2_.refs_3_) | copy-start | bytes 18436
  83.7 59.9 %copy-start.44 = (f32[1,1536]{1,0:T(1,128)}, f32[1,1536]{1,0:T(1,128)S(1)}, u32[]{:S(2)}) copy-start(f32[1,1536]{1,0:T(1,128)S(1)} %get-tuple-element.157.refs_2_.refs_13_) | copy-start | bytes 18436
  83.7 122.0 %copy-start.45 = (f32[1,1536]{1,0:T(1,128)}, f32[1,1536]{1,0:T(1,128)S(1)}, u32[]{:S(2)}) copy-start(f32[1,1536]{1,0:T(1,128)S(1)} %get-tuple-element.156.refs_2_.refs_3_) | copy-start | bytes 18436
  118.3 1.1 copy-start.58
  128.1 3.7 copy-start.57
  131.8 1.4 copy-start.59
  133.2 1.1 copy-start.65
  135.4 8.2 %copy-start.18 = (f32[64,1536]{1,0:T(8,128)S(1)}, f32[64,1536]{1,0:T(8,128)}, u32[]{:S(2)}) copy-start(f32[64,1536]{1,0:T(8,128)} %copy-done.17) | copy-start | bytes 1179652
  135.4 8.2 %copy-start.33 = (bf16[384,512]{1,0:T(8,128)(2,1)S(1)}, bf16[384,512]{1,0:T(8,128)(2,1)}, u32[]{:S(2)}) copy-start(bf16[384,512]{1,0:T(8,128)(2,1)} %copy-done.32) | copy-start | bytes 1179652
  143.5 59.0 %copy-start.69 = (bf16[512,2048]{1,0:T(8,128)(2,1)}, bf16[512,2048]{1,0:T(8,128)(2,1)S(1)}, u32[]{:S(2)}) copy-start(bf16[512,2048]{1,0:T(8,128)(2,1)S(1)} %get-tuple-element.93.refs_4_) | copy-start | bytes 6291460
  143.5 59.0 %copy-start.71 = (f32[512,128]{1,0:T(8,128)}, f32[512,128]{1,0:T(8,128)S(1)}, u32[]{:S(2)}) copy-start(f32[512,128]{1,0:T(8,128)S(1)} %get-tuple-element.92.refs_3_) | copy-start | bytes 786436
  182.4 20.1 %copy-start.2 = (bf16[8,64,1536]{2,1,0:T(8,128)(2,1)}, bf16[8,64,1536]{2,1,0:T(8,128)(2,1)S(1)}, u32[]{:S(2)}) copy-start(bf16[8,64,1536]{2,1,0:T(8,128)(2,1)S(1)} %get-tuple-element.97) | copy-start | bytes 4718596
  182.4 20.1 %copy-start.11 = (bf16[4,384,512]{2,1,0:T(8,128)(2,1)}, bf16[4,384,512]{2,1,0:T(8,128)(2,1)S(1)}, u32[]{:S(2)}) copy-start(bf16[4,384,512]{2,1,0:T(8,128)(2,1)S(1)} %get-tuple-element.98) | copy-start | bytes 4718596
  182.4 23.3 %copy-start.13 = (bf16[64,1536]{1,0:T(8,128)(2,1)}, bf16[64,1536]{1,0:T(8,128)(2,1)S(1)}, u32[]{:S(2)}) copy-start(bf16[64,1536]{1,0:T(8,128)(2,1)S(1)} %get-tuple-element.100.refs_1_.refs_12_.refs_8_) | copy-start | bytes 589828
  205.7 64.9 %copy-start.55 = (f32[2,3,1,256]{3,2,1,0:T(1,128)}, f32[2,3,1,256]{3,2,1,0:T(1,128)S(1)}, u32[]{:S(2)}) copy-start(f32[2,3,1,256]{3,2,1,0:T(1,128)S(1)} %get-tuple-element.113.refs_10_) | copy-start | bytes 18436
  242.2 1.1 copy-start.63
  270.6 239.2 %reduce-scatter.9.cloned.1.call-start = ((), (), s32[]{:S(2)}) async-start(), calls=%async_computation.5 | async-start | bytes 11796480
  306.6 60.1 %copy-start.3 = (bf16[8,64,1536]{2,1,0:T(8,128)(2,1)S(1)}, bf16[8,64,1536]{2,1,0:T(8,128)(2,1)}, u32[]{:S(2)}) copy-start(bf16[8,64,1536]{2,1,0:T(8,128)(2,1)} %copy-done.2) | copy-start | bytes 4718596
  366.7 2.2 copy-start.40
  366.7 2.2 copy-start.73
  368.9 1.5 copy-start.60
  368.9 2.0 copy-start.62
  368.9 2.2 copy-start.66
  368.9 2.9 copy-start.70
  369.0 2.8 copy-start.72
  391.7 1.1 copy-start.16
  393.8 38.0 %copy-start.1 = (s32[4,512,1]{2,1,0:T(8,128)S(1)}, s32[4,512,1]{2,1,0:T(8,128)}, u32[]{:S(2)}) copy-start(s32[4,512,1]{2,1,0:T(8,128)} %copy-done) | copy-start | bytes 24580
  393.8 38.0 %copy-start.5 = (f32[512,128]{1,0:T(8,128)S(1)}, f32[512,128]{1,0:T(8,128)}, u32[]{:S(2)}) copy-start(f32[512,128]{1,0:T(8,128)} %copy-done.4) | copy-start | bytes 786436
  393.8 38.0 %copy-start.7 = (f32[512,128]{1,0:T(8,128)S(1)}, f32[512,128]{1,0:T(8,128)}, u32[]{:S(2)}) copy-start(f32[512,128]{1,0:T(8,128)} %copy-done.6) | copy-start | bytes 786436
  393.8 38.0 %copy-start.47 = (s32[2,1,256]{2,1,0:T(1,128)S(1)}, s32[2,1,256]{2,1,0:T(1,128)}, u32[]{:S(2)}) copy-start(s32[2,1,256]{2,1,0:T(1,128)} %copy-done.46) | copy-start | bytes 6148
  393.8 38.0 %copy-start.49 = (s32[2,1,256]{2,1,0:T(1,128)S(1)}, s32[2,1,256]{2,1,0:T(1,128)}, u32[]{:S(2)}) copy-start(s32[2,1,256]{2,1,0:T(1,128)} %copy-done.48) | copy-start | bytes 6148
  393.9 38.0 %copy-start.27 = (bf16[4,512,128]{2,1,0:T(8,128)(2,1)S(1)}, bf16[4,512,128]{2,1,0:T(8,128)(2,1)}, u32[]{:S(2)}) copy-start(bf16[4,512,128]{2,1,0:T(8,128)(2,1)} %copy-done.26) | copy-start | bytes 1572868
  431.9 1.4 copy-start.9
  433.3 1.5 copy-start.10
  434.8 1.1 copy-start.25
  459.5 28.9 %copy-start.14 = (bf16[64,1536]{1,0:T(8,128)(2,1)S(1)}, bf16[64,1536]{1,0:T(8,128)(2,1)}, u32[]{:S(2)}) copy-start(bf16[64,1536]{1,0:T(8,128)(2,1)} %copy-done.13) | copy-start | bytes 589828
  459.5 28.9 %copy-start.21 = (bf16[64,1536]{1,0:T(8,128)(2,1)S(1)}, bf16[64,1536]{1,0:T(8,128)(2,1)}, u32[]{:S(2)}) copy-start(bf16[64,1536]{1,0:T(8,128)(2,1)} %get-tuple-element.121.refs_1_.refs_11_) | copy-start | bytes 589828
  459.6 28.9 %copy-start.23 = (f32[384,512]{1,0:T(8,128)S(1)}, f32[384,512]{1,0:T(8,128)}, u32[]{:S(2)}) copy-start(f32[384,512]{1,0:T(8,128)} %copy-done.22) | copy-start | bytes 2359300
  459.6 28.9 %copy-start.41 = (bf16[64,1536]{1,0:T(8,128)(2,1)S(1)}, bf16[64,1536]{1,0:T(8,128)(2,1)}, u32[]{:S(2)}) copy-start(bf16[64,1536]{1,0:T(8,128)(2,1)} %get-tuple-element.140.refs_9_) | copy-start | bytes 589828
  459.6 28.9 %copy-start.42 = (f32[16,1536]{1,0:T(8,128)S(1)}, f32[16,1536]{1,0:T(8,128)}, u32[]{:S(2)}) copy-start(f32[16,1536]{1,0:T(8,128)} %get-tuple-element.135.refs_3_) | copy-start | bytes 294916
  459.6 28.9 %copy-start.52 = (f32[1,1536]{1,0:T(1,128)S(1)}, f32[1,1536]{1,0:T(1,128)}, u32[]{:S(2)}) copy-start(f32[1,1536]{1,0:T(1,128)} %get-tuple-element.137.refs_5_) | copy-start | bytes 18436
  459.6 28.9 %copy-start.53 = (f32[1,1536]{1,0:T(1,128)S(1)}, f32[1,1536]{1,0:T(1,128)}, u32[]{:S(2)}) copy-start(f32[1,1536]{1,0:T(1,128)} %get-tuple-element.136.refs_4_) | copy-start | bytes 18436
  459.6 28.9 %copy-start.54 = (f32[1,1536]{1,0:T(1,128)S(1)}, f32[1,1536]{1,0:T(1,128)}, u32[]{:S(2)}) copy-start(f32[1,1536]{1,0:T(1,128)} %get-tuple-element.134.refs_2_) | copy-start | bytes 18436
  514.8 5.5 %copy-start.74 = (bf16[4,128,1536]{2,1,0:T(8,128)(2,1)S(1)}, bf16[4,128,1536]{2,1,0:T(8,128)(2,1)}, u32[]{:S(2)}) copy-start(bf16[4,128,1536]{2,1,0:T(8,128)(2,1)} %get-tuple-element.152) | copy-start | bytes 4718596
  (18 other events, 15.1 us)
Sparse Core Ops, SparseCore 0:
  14.4 113.5 all-gather.2
  129.9 113.9 all-gather.4
  270.7 99.1 reduce-scatter.6
  393.9 112.3 reduce-scatter.8

commit v8 on v7

--- a/solution.py
+++ b/solution.py
@@ -1079,13 +1079,11 @@
         out_specs=[VMEM] * len(outs),
         scratch_shapes=scratch,
         compiler_params=pltpu.CompilerParams(
-            collective_id=number, has_side_effects=True, vmem_limit_bytes=(60 if then else 24) << 20
+            collective_id=number, has_side_effects=True, vmem_limit_bytes=60 << 20
         ),
         cost_estimate=pl.CostEstimate(flops=0, bytes_accessed=(200 if then else 100) << 20, transcendentals=0),
     )
-    if then:
-        return loaded(kernel, operands, [], **call)
-    return pl.pallas_call(functools.partial(kernel, None), in_specs=[VMEM] * len(operands), **call)(*operands)
+    return loaded(kernel, operands, [], **call)
 
 
 def expert_halves(inward, down, packed, half, per_core):
@@ -1484,7 +1482,7 @@
         scratch += CtxSum.scratch(n_ctx, add.shape)
         params = dict(collective_id=number, has_side_effects=True)
     work = n_rows * 6 * width * FF * 2 * ((1 if forward else 0) + (2 if backward else 0))
-    load = forward and backward
+    load = forward
     kernel = functools.partial(experts_kernel, n_ctx, layer, forward, backward, depth, down_rows, add is not None)
     call = dict(
         out_shape=outs,

time: 537 us -> 535 us (level)
  local copies, waits for them, and re-layouts: 36.8 us -> 26.6 us
  Pallas kernels: 457 us -> 463 us
    pallas_call x4 -> x6, Pallas kernels: 160 us -> 197 us  [loaded(): return pl.pallas_call(body, **call)(*operands, *whole)]
    pallas_call x1 -> x0, Pallas kernels: 20.5 us -> none  [attend_back(): pl.pallas_call(functools.partial(kernel, None), in_specs=[VMEM] * len(ope...]
    unnamed x165 -> x137, local copies, waits for them, and re-layouts: 32.9 us -> 22.7 us
    pallas_call x2 -> x1, Pallas kernels: 28.1 us -> 20.1 us  [experts(): pl.pallas_call(functools.partial(kernel, None), in_specs=in_specs, **call)]
  transfers between devices with their start and end apart: 4 -> 4, of which waited for: 2 -> 2; matrix products, arithmetic and copies ran while one was open for 2% -> 2% of each run, Pallas kernels for 79% -> 80%
where the time goes in v8:
time: 535 us; the launch traced here: 532 us
  Pallas kernels  463 us (87%)
  local copies, waits for them, and re-layouts  26.6 us (5%)
  between operations  14.9 us (3%)
  waiting for transfers between devices  10.6 us (2%)
  other arithmetic  10.1 us (2%)
  matrix products  6.35 us (1%)
    pallas_call x6, Pallas kernels, loaded(): return pl.pallas_call(body, **call)(*operands, *whole)  197 us
    pallas_call x4, Pallas kernels, exchange(): pl.pallas_call(functools.partial(kernel, None), in_specs=[VMEM] * len(ope...  135 us
    pallas_call x2, Pallas kernels, attend(): pl.pallas_call(functools.partial(attend_kernel, n_ctx, n_wt, bool(riders)...  41.6 us
    pallas_call x1, Pallas kernels, begin(): pl.pallas_call(functools.partial(begin_kernel, n_ctx, n_wt), out_shape=[j...  37 us
    unnamed x137, local copies, waits for them, and re-layouts  22.7 us
    pallas_call x1, Pallas kernels, finish(): pl.pallas_call(functools.partial(finish_kernel, n_ctx, n_wt), out_shape=[...  20.5 us
    pallas_call x1, Pallas kernels, experts(): pl.pallas_call(functools.partial(kernel, None), in_specs=in_specs, **call)  20.1 us
  transfers between devices with their start and end apart: 4, of which 2 were waited for; matrix products, arithmetic and copies ran while one was open for 2% of the time, Pallas kernels for 80%

profile of v8, /device:TPU:0, one launch (start us, length us, event | category | flops | bytes accessed | tf_op | source)
XLA Modules:
  0.0 532.0 jit_solution(18310906615869311316)
XLA Ops:
  7.2 7.0 %shard_map.181 = (bf16[576,2048]{1,0:T(8,128)(2,1)}, bf16[576,2048]{1,0:T(8,128)(2,1)}) custom-call(bf16[4,384,1024]{2,1,0:T(8,128)(2,1)} %bitcast.117, bf16[4,128,1536]{2,1,0:T(8,128)(2,1)} %bitcast.121), custom_call_target="tpu_custom_call" | custom-call | tf_op jit(solution)/shard_map/pallas_call | solution.py:1138
  14.4 0.7 all-gather.5.cloned.1.call-update
  15.2 0.1 dynamic-slice.4
  15.3 0.1 subtract_select_fusion
  15.5 0.1 copy.32
  15.8 0.4 copy.33.key_place.refs_4_
  16.2 1.2 copy-done.27
  17.4 1.0 copy-done.28
  18.3 37.0 %shard_map.178 = (bf16[8,64,1536]{2,1,0:T(8,128)(2,1)S(1)}, bf16[4,384,512]{2,1,0:T(8,128)(2,1)S(1)}, bf16[384,512]{1,0:T(8,128)(2,1)S(1)}, f32[2,2,1536]{2,1,0:...) custom-call(bf16[2,64,1536]{2,1,0:T(8,128)(2,1)S(1)} %copy-done.16, ...), custom_call_target="tpu_custom_call" | custom-call | bytes 94371840 | tf_op jit(solution)/shard_map/pallas_call | solution.py:1230
  55.3 0.7 copy-done.24
  56.1 0.9 copy-done.53
  57.0 0.8 copy-done.55
  57.8 1.2 dynamic-slice_bitcast_fusion
  59.0 1.0 fusion.8
  60.0 21.7 %shard_map.179 = (bf16[512,1536]{1,0:T(8,128)(2,1)S(1)}, bf16[2,3,256,128]{3,2,1,0:T(8,128)(2,1)S(1)}, bf16[4,512,128]{2,1,0:T(8,128)(2,1)S(1)}, f32[2,3,256,128...) custom-call(bf16[512,1536]{1,0:T(8,128)(2,1)S(1)} %bitcast.84, ...), custom_call_target="tpu_custom_call" | custom-call | bytes 73400320 | tf_op jit(solution)/shard_map/pallas_call | solution.py:879
  81.8 0.7 copy-done.29
  82.4 1.2 copy-done.50
  83.7 33.8 %shard_map.180 = (f32[64,1536]{1,0:T(8,128)S(1)}, bf16[8,64,1536]{2,1,0:T(8,128)(2,1)S(1)}, f32[8,128]{1,0:T(8,128)S(1)}) custom-call(bf16[8,64,1536]{2,1,0:T(8,128)(2,1)S(1)} %bitcast.94, bf16[64,1536]{1,0:T(8,128)(2,1)S(1)} %get-tuple-element.163.refs_1_.refs_2_, f32[1,1536]{1,0:T(1,128)S(1)} %get-tuple-element.123.refs_2_.refs_3_), custom_call_target="tpu_custom_call" | custom-call | bytes 115343360 | tf_op jit(solution)/shard_map/pallas_call | solution.py:582
  117.5 0.7 copy-done.14
  118.3 1.1 copy-done.48
  119.4 8.6 %all-gather.3.cloned.1.call-done = bf16[2304,2048]{1,0:T(8,128)(2,1)} async-done(((bf16[576,2048]{1,0:T(8,128)(2,1)}), bf16[2304,2048]{1,0:T(8,128)(2,1)}) %all-gather.3.cloned.1.call-update) | async-done | bytes 9437200 | tf_op jit(solution)/shard_map/all_gather | solution.py:1546
  128.0 0.7 fusion.11.refs_2_
  128.6 13.0 %shard_map.182 = (bf16[512,1536]{1,0:T(8,128)(2,1)}, f32[512,128]{1,0:T(8,128)}, bf16[512,2048]{1,0:T(8,128)(2,1)}) custom-call(bf16[512,1536]{1,0:T(8,128)(2,1)} %bitcast.108, bf16[2,128,1536]{2,1,0:T(8,128)(2,1)} %copy-done.53, f32[8,128]{1,0:T(8,128)} %fusion.11.refs_2_, s32[2,2,256,8]{3,2,1,0:T(8,128)} %copy-done.55, bf16[4,576,2048]{2,1,0:T(8,128)(2,1)} %bitcast.127), custom_call_target="tpu_custom_call" | custom-call | flops 9663676416 | bytes 41943040 | tf_op jit(solution)/shard_map/pallas_call | solution.py:74
  141.7 1.5 copy-done.13
  143.2 1.0 copy-done.25
  144.2 38.9 %shard_map.183 = (bf16[64,1536]{1,0:T(8,128)(2,1)S(1)}, bf16[8,64,1536]{2,1,0:T(8,128)(2,1)S(1)}, bf16[4,384,512]{2,1,0:T(8,128)(2,1)S(1)}, f32[8,128]{1,0:T(8,128)}) custom-call(bf16[8,64,1536]{2,1,0:T(8,128)(2,1)S(1)} %bitcast.97, f32[64,1536]{1,0:T(8,128)S(1)} %copy-done.15, f32[1,1536]{1,0:T(1,128)S(1)} %get-tuple-element.157.refs_2_.refs_13_, ...), custom_call_target="tpu_custom_call" | custom-call | bytes 115343360 | tf_op jit(solution)/shard_map/pallas_call | solution.py:582
  183.2 19.9 %shard_map.184 = (bf16[512,1536]{1,0:T(8,128)(2,1)S(1)}, bf16[2,3,256,128]{3,2,1,0:T(8,128)(2,1)S(1)}, bf16[4,512,128]{2,1,0:T(8,128)(2,1)S(1)}, f32[2,3,256,128...) custom-call(bf16[512,1536]{1,0:T(8,128)(2,1)S(1)} %bitcast.86, ...), custom_call_target="tpu_custom_call" | custom-call | bytes 73400320 | tf_op jit(solution)/shard_map/pallas_call | solution.py:879
  203.2 0.9 copy-done.17
  204.1 0.8 copy-done.21
  204.8 0.7 copy-done.22
  205.6 0.7 copy-done.31
  206.3 33.8 %shard_map.185 = (f32[64,1536]{1,0:T(8,128)S(1)}, bf16[8,64,1536]{2,1,0:T(8,128)(2,1)S(1)}, f32[8,128]{1,0:T(8,128)S(1)}) custom-call(bf16[8,64,1536]{2,1,0:T(8,128)(2,1)S(1)} %bitcast.95, bf16[64,1536]{1,0:T(8,128)(2,1)S(1)} %get-tuple-element.100.refs_1_.refs_12_.refs_8_, f32[1,1536]{1,0:T(1,128)S(1)} %get-tuple-element.156.refs_2_.refs_3_), custom_call_target="tpu_custom_call" | custom-call | bytes 115343360 | tf_op jit(solution)/shard_map/pallas_call | solution.py:582
  240.1 0.7 copy-done.10
  240.8 1.1 copy-done.52
  241.9 1.4 all-gather.5.cloned.1.call-done
  243.3 0.6 fusion.10.refs_2_
  244.0 26.2 %shard_map.186 = (bf16[512,1536]{1,0:T(8,128)(2,1)}, bf16[512,1536]{1,0:T(8,128)(2,1)}, bf16[4,576,2048]{2,1,0:T(8,128)(2,1)}, f32[16,1536]{1,0:T(8,128)}) custom-call(bf16[512,1536]{1,0:T(8,128)(2,1)} %bitcast.112, bf16[2,128,1536]{2,1,0:T(8,128)(2,1)} %copy-done.53, f32[8,128]{1,0:T(8,128)} %fusion.10.refs_2_, s32[2,2,256,8]{3,2,1,0:T(8,128)} %copy-done.55, ...), custom_call_target="tpu_custom_call" | custom-call | flops 28991029248 | bytes 41943040 | tf_op jit(solution)/shard_map/pallas_call | solution.py:74
  270.3 36.9 %shard_map.187 = (f32[64,1536]{1,0:T(8,128)}, f32[1,1536]{1,0:T(1,128)}, bf16[8,64,1536]{2,1,0:T(8,128)(2,1)}, f32[8,128]{1,0:T(8,128)}) custom-call(bf16[8,64,1536]{2,1,0:T(8,128)(2,1)} %bitcast.120, bf16[64,1536]{1,0:T(8,128)(2,1)} %copy-done.7, f32[64,1536]{1,0:T(8,128)} %copy-done.10, f32[1,1536]{1,0:T(1,128)} %copy-done.37), custom_call_target="tpu_custom_call" | custom-call | bytes 115343360 | tf_op jit(solution)/shard_map/pallas_call | solution.py:74
  307.2 60.0 %shard_map.188 = (bf16[512,384]{1,0:T(8,128)(2,1)}, bf16[64,1536]{1,0:T(8,128)(2,1)}, f32[1,1536]{1,0:T(1,128)}, bf16[8,64,1536]{2,1,0:T(8,128)(2,1)}, bf16[64,1536]{1,0:T(8,128)(2,1)}) custom-call(bf16[512,1536]{1,0:T(8,128)(2,1)} %bitcast.115, bf16[1536,512]{1,0:T(8,128)(2,1)} %bitcast.92, f32[512,128]{1,0:T(8,128)} %copy-done.4, f32[512,128]{1,0:T(8,128)} %copy-done.3, ...), custom_call_target="tpu_custom_call" | custom-call | bytes 209715200 | tf_op jit(solution)/shard_map/pallas_call | solution.py:74
  367.3 2.1 fusion.6
  369.5 1.0 fusion
  370.6 0.4 copy-done.49
  370.9 0.5 copy-done.51
  371.5 0.2 copy-done.54
  371.7 0.7 copy-done.56
  372.4 20.1 %shard_map.189 = (bf16[512,1536]{1,0:T(8,128)(2,1)S(1)}, bf16[4,576,2048]{2,1,0:T(8,128)(2,1)}, f32[16,1536]{1,0:T(8,128)S(1)}, f32[384,512]{1,0:T(8,128)S(1)}) custom-call(bf16[512,1536]{1,0:T(8,128)(2,1)S(1)} %bitcast.109, bf16[2,128,1536]{2,1,0:T(8,128)(2,1)S(1)} %copy-done.54, f32[8,128]{1,0:T(8,128)S(1)} %fusion.9.refs_2_, f32[512,128]{1,0:T(8,128)S(1)} %copy-done.57, ...), custom_call_target="tpu_custom_call" | custom-call | flops 19327352832 | bytes 41943040 | tf_op jit(solution)/shard_map/pallas_call | solution.py:1497
  392.5 1.1 copy-done.11
  393.7 37.6 %shard_map.190 = (f32[64,1536]{1,0:T(8,128)}, f32[1,1536]{1,0:T(1,128)}, bf16[8,64,1536]{2,1,0:T(8,128)(2,1)}, f32[8,128]{1,0:T(8,128)}) custom-call(bf16[8,64,1536]{2,1,0:T(8,128)(2,1)} %bitcast.93, bf16[64,1536]{1,0:T(8,128)(2,1)} %get-tuple-element.121.refs_1_.refs_11_, f32[64,1536]{1,0:T(8,128)} %copy-done.14, f32[1,1536]{1,0:T(1,128)} %copy-done.35), custom_call_target="tpu_custom_call" | custom-call | bytes 115343360 | tf_op jit(solution)/shard_map/pallas_call | solution.py:74
  431.3 22.8 %shard_map.191 = (bf16[512,384]{1,0:T(8,128)(2,1)}, bf16[8,64,1536]{2,1,0:T(8,128)(2,1)}) custom-call(bf16[512,1536]{1,0:T(8,128)(2,1)} %bitcast.113, bf16[1536,512]{1,0:T(8,128)(2,1)} %bitcast.89, f32[512,128]{1,0:T(8,128)} %copy-done.4, f32[512,128]{1,0:T(8,128)} %copy-done.3, s32[4,512,1]{2,1,0:T(8,128)} %copy-done, s32[2,1,256]{2,1,0:T(1,128)} %copy-done.38, ...), custom_call_target="tpu_custom_call" | custom-call | bytes 104857600 | tf_op jit(solution)/shard_map/pallas_call | solution.py:74
  454.1 2.1 fusion.3
  456.3 1.0 fusion.1
  457.4 0.3 copy-done.12
  457.8 29.0 %shard_map.192 = (bf16[64,1536]{1,0:T(8,128)(2,1)S(1)}, f32[1,1536]{1,0:T(1,128)S(1)}, f32[384,512]{1,0:T(8,128)S(1)}, f32[8,128]{1,0:T(8,128)}) custom-call(bf16[8,64,1536]{2,1,0:T(8,128)(2,1)S(1)} %copy-done.12, f32[64,1536]{1,0:T(8,128)S(1)} %copy-done.26, bf16[64,1536]{1,0:T(8,128)(2,1)S(1)} %get-tuple-element.163.refs_1_.refs_2_, ...), custom_call_target="tpu_custom_call" | custom-call | bytes 115343360 | tf_op jit(solution)/shard_map/pallas_call | solution.py:582
  486.9 20.5 %shard_map.193 = (f32[2,128]{1,0:T(2,128)S(1)}, f32[16,128]{1,0:T(8,128)S(1)}, f32[384,384]{1,0:T(8,128)S(1)}, f32[384,256]{1,0:T(8,128)S(1)}, f32[384,384]{1,0:...) custom-call(f32[16,1536]{1,0:T(8,128)S(1)} %get-tuple-element.119.refs_0_, ...), custom_call_target="tpu_custom_call" | custom-call | bytes 41943040 | tf_op jit(solution)/shard_map/pallas_call | solution.py:662
  507.3 0.6 slice_bitcast_fusion.5
  507.9 5.0 shard_map.194
  513.0 5.5 %bitcast_convert_fusion = f32[1,4,384,1024]{3,2,1,0:T(8,128)} fusion(bf16[4,384,1024]{2,1,0:T(8,128)(2,1)} %get-tuple-element.151), kind=kLoop, calls=%fused_computation.2 | loop fusion | flops 1572864 | bytes 9437184 | tf_op jit(solution)/shard_map/broadcast_in_dim | solution.py:1681
  518.4 2.1 bitcast_convert_fusion.1
  520.5 0.9 broadcast_in_dim_reshape.3
  521.5 0.6 slice_bitcast_fusion
  522.1 0.7 copy.48
  522.8 0.7 copy.49
  523.6 0.8 copy.50
  524.4 0.8 copy.51
  (132 shorter events, 0.9 us)
Async XLA Ops:
  7.2 120.8 %all-gather.3.cloned.1.call-start = ((), (), s32[]{:S(2)}) async-start(), calls=%async_computation.2 | async-start | bytes 11796480 | tf_op jit(solution)/shard_map/all_gather | solution.py:1546
  14.3 0.8 copy-start.63
  14.3 1.2 copy-start.62
  14.3 1.3 copy-start.61
  14.3 229.0 %all-gather.5.cloned.1.call-start = ((), (), s32[]{:S(2)}) async-start(), calls=%async_computation.3 | async-start | bytes 11796480 | tf_op jit(solution)/shard_map/all_gather | solution.py:1546
  14.4 1.8 copy-start.16
  14.4 1.8 copy-start.40
  14.4 1.8 copy-start.41
  15.1 378.6 %reduce-scatter.7.cloned.1.call-start = ((), (), s32[]{:S(2)}) async-start(), calls=%async_computation.4 | async-start | bytes 11796480
  15.4 167.8 %copy-start.38 = (s32[2,1,256]{2,1,0:T(1,128)}, s32[2,1,256]{2,1,0:T(1,128)S(1)}, u32[]{:S(2)}) copy-start(s32[2,1,256]{2,1,0:T(1,128)S(1)} %broadcast_in_dim.73.query_place.refs_5_) | copy-start | bytes 6148
  15.5 167.7 %copy-start.39 = (s32[2,1,256]{2,1,0:T(1,128)}, s32[2,1,256]{2,1,0:T(1,128)S(1)}, u32[]{:S(2)}) copy-start(s32[2,1,256]{2,1,0:T(1,128)S(1)} %broadcast_in_dim.74.query_start.refs_6_) | copy-start | bytes 6148
  16.1 167.0 %copy-start = (s32[4,512,1]{2,1,0:T(8,128)}, s32[4,512,1]{2,1,0:T(8,128)S(1)}, u32[]{:S(2)}) copy-start(s32[4,512,1]{2,1,0:T(8,128)S(1)} %copy.33.key_place.refs_4_) | copy-start | bytes 24580
  16.2 1.2 copy-start.27
  17.4 1.0 copy-start.28
  55.3 0.7 copy-start.24
  56.1 0.9 copy-start.53
  57.0 0.8 copy-start.55
  57.8 24.0 %copy-start.5 = (bf16[4,384,512]{2,1,0:T(8,128)(2,1)}, bf16[4,384,512]{2,1,0:T(8,128)(2,1)S(1)}, u32[]{:S(2)}) copy-start(bf16[4,384,512]{2,1,0:T(8,128)(2,1)S(1)} %get-tuple-element.82) | copy-start | bytes 4718596
  59.0 22.8 %copy-start.7 = (bf16[64,1536]{1,0:T(8,128)(2,1)}, bf16[64,1536]{1,0:T(8,128)(2,1)S(1)}, u32[]{:S(2)}) copy-start(bf16[64,1536]{1,0:T(8,128)(2,1)S(1)} %get-tuple-element.164.refs_0_.refs_1_) | copy-start | bytes 589828
  60.0 123.2 %copy-start.3 = (f32[512,128]{1,0:T(8,128)}, f32[512,128]{1,0:T(8,128)S(1)}, u32[]{:S(2)}) copy-start(f32[512,128]{1,0:T(8,128)S(1)} %get-tuple-element.159.sin_ref.refs_3_) | copy-start | bytes 786436
  60.0 123.2 %copy-start.4 = (f32[512,128]{1,0:T(8,128)}, f32[512,128]{1,0:T(8,128)S(1)}, u32[]{:S(2)}) copy-start(f32[512,128]{1,0:T(8,128)S(1)} %get-tuple-element.160.cos_ref.refs_2_) | copy-start | bytes 786436
  82.4 1.2 copy-start.50
  83.6 33.9 %copy-start.19 = (f32[2,3,256,128]{3,2,1,0:T(8,128)}, f32[2,3,256,128]{3,2,1,0:T(8,128)S(1)}, u32[]{:S(2)}) copy-start(f32[2,3,256,128]{3,2,1,0:T(8,128)S(1)} %get-tuple-element.127.refs_9_) | copy-start | bytes 2359300
  83.6 33.9 %copy-start.20 = (bf16[4,512,128]{2,1,0:T(8,128)(2,1)}, bf16[4,512,128]{2,1,0:T(8,128)(2,1)S(1)}, u32[]{:S(2)}) copy-start(bf16[4,512,128]{2,1,0:T(8,128)(2,1)S(1)} %get-tuple-element.126.refs_8_) | copy-start | bytes 1572868
  83.6 33.9 %copy-start.23 = (bf16[2,3,256,128]{3,2,1,0:T(8,128)(2,1)}, bf16[2,3,256,128]{3,2,1,0:T(8,128)(2,1)S(1)}, u32[]{:S(2)}) copy-start(bf16[2,3,256,128]{3,2,1,0:T(8,128)(2,1)S(1)} %get-tuple-element.125.refs_7_) | copy-start | bytes 1179652
  83.6 33.9 %copy-start.42 = (f32[2,3,1,256]{3,2,1,0:T(1,128)}, f32[2,3,1,256]{3,2,1,0:T(1,128)S(1)}, u32[]{:S(2)}) copy-start(f32[2,3,1,256]{3,2,1,0:T(1,128)S(1)} %get-tuple-element.128.refs_10_) | copy-start | bytes 18436
  83.7 58.0 %copy-start.35 = (f32[1,1536]{1,0:T(1,128)}, f32[1,1536]{1,0:T(1,128)S(1)}, u32[]{:S(2)}) copy-start(f32[1,1536]{1,0:T(1,128)S(1)} %get-tuple-element.123.refs_2_.refs_3_) | copy-start | bytes 18436
  83.7 58.0 %copy-start.36 = (f32[1,1536]{1,0:T(1,128)}, f32[1,1536]{1,0:T(1,128)S(1)}, u32[]{:S(2)}) copy-start(f32[1,1536]{1,0:T(1,128)S(1)} %get-tuple-element.157.refs_2_.refs_13_) | copy-start | bytes 18436
  83.7 122.6 %copy-start.37 = (f32[1,1536]{1,0:T(1,128)}, f32[1,1536]{1,0:T(1,128)S(1)}, u32[]{:S(2)}) copy-start(f32[1,1536]{1,0:T(1,128)S(1)} %get-tuple-element.156.refs_2_.refs_3_) | copy-start | bytes 18436
  117.5 0.7 copy-start.14
  118.3 1.1 copy-start.48
  128.6 13.0 %copy-start.15 = (f32[64,1536]{1,0:T(8,128)S(1)}, f32[64,1536]{1,0:T(8,128)}, u32[]{:S(2)}) copy-start(f32[64,1536]{1,0:T(8,128)} %copy-done.14) | copy-start | bytes 1179652
  141.7 1.5 copy-start.13
  143.2 1.0 copy-start.25
  183.1 20.0 %copy-start.1 = (bf16[8,64,1536]{2,1,0:T(8,128)(2,1)}, bf16[8,64,1536]{2,1,0:T(8,128)(2,1)S(1)}, u32[]{:S(2)}) copy-start(bf16[8,64,1536]{2,1,0:T(8,128)(2,1)S(1)} %get-tuple-element.97) | copy-start | bytes 4718596
  183.1 20.0 %copy-start.6 = (bf16[4,384,512]{2,1,0:T(8,128)(2,1)}, bf16[4,384,512]{2,1,0:T(8,128)(2,1)S(1)}, u32[]{:S(2)}) copy-start(bf16[4,384,512]{2,1,0:T(8,128)(2,1)S(1)} %get-tuple-element.98) | copy-start | bytes 4718596
  183.2 23.2 %copy-start.8 = (bf16[64,1536]{1,0:T(8,128)(2,1)}, bf16[64,1536]{1,0:T(8,128)(2,1)S(1)}, u32[]{:S(2)}) copy-start(bf16[64,1536]{1,0:T(8,128)(2,1)S(1)} %get-tuple-element.100.refs_1_.refs_12_.refs_8_) | copy-start | bytes 589828
  203.2 0.9 copy-start.17
  204.1 0.8 copy-start.21
  206.3 63.9 %copy-start.46 = (f32[2,3,1,256]{3,2,1,0:T(1,128)}, f32[2,3,1,256]{3,2,1,0:T(1,128)S(1)}, u32[]{:S(2)}) copy-start(f32[2,3,1,256]{3,2,1,0:T(1,128)S(1)} %get-tuple-element.113.refs_10_) | copy-start | bytes 18436
  240.1 0.7 copy-start.10
  240.8 1.1 copy-start.52
  270.2 237.7 %reduce-scatter.9.cloned.1.call-start = ((), (), s32[]{:S(2)}) async-start(), calls=%async_computation.5 | async-start | bytes 11796480
  307.2 60.1 %copy-start.2 = (bf16[8,64,1536]{2,1,0:T(8,128)(2,1)S(1)}, bf16[8,64,1536]{2,1,0:T(8,128)(2,1)}, u32[]{:S(2)}) copy-start(bf16[8,64,1536]{2,1,0:T(8,128)(2,1)} %copy-done.1) | copy-start | bytes 4718596
  367.3 2.2 copy-start.32
  367.3 2.2 copy-start.59
  369.5 1.5 copy-start.49
  369.5 2.0 copy-start.51
  369.5 2.2 copy-start.54
  369.5 2.9 copy-start.56
  369.5 2.9 copy-start.57
  392.5 1.1 copy-start.11
  454.1 2.2 copy-start.30
  454.1 2.2 copy-start.58
  456.3 1.4 copy-start.12
  456.3 1.5 copy-start.26
  457.8 29.0 %copy-start.9 = (bf16[64,1536]{1,0:T(8,128)(2,1)S(1)}, bf16[64,1536]{1,0:T(8,128)(2,1)}, u32[]{:S(2)}) copy-start(bf16[64,1536]{1,0:T(8,128)(2,1)} %copy-done.8) | copy-start | bytes 589828
  457.8 29.0 %copy-start.18 = (bf16[64,1536]{1,0:T(8,128)(2,1)S(1)}, bf16[64,1536]{1,0:T(8,128)(2,1)}, u32[]{:S(2)}) copy-start(bf16[64,1536]{1,0:T(8,128)(2,1)} %get-tuple-element.121.refs_1_.refs_11_) | copy-start | bytes 589828
  457.8 29.0 %copy-start.33 = (bf16[64,1536]{1,0:T(8,128)(2,1)S(1)}, bf16[64,1536]{1,0:T(8,128)(2,1)}, u32[]{:S(2)}) copy-start(bf16[64,1536]{1,0:T(8,128)(2,1)} %get-tuple-element.140.refs_9_) | copy-start | bytes 589828
  457.8 29.0 %copy-start.34 = (f32[16,1536]{1,0:T(8,128)S(1)}, f32[16,1536]{1,0:T(8,128)}, u32[]{:S(2)}) copy-start(f32[16,1536]{1,0:T(8,128)} %get-tuple-element.135.refs_3_) | copy-start | bytes 294916
  457.8 29.0 %copy-start.43 = (f32[1,1536]{1,0:T(1,128)S(1)}, f32[1,1536]{1,0:T(1,128)}, u32[]{:S(2)}) copy-start(f32[1,1536]{1,0:T(1,128)} %get-tuple-element.137.refs_5_) | copy-start | bytes 18436
  457.8 29.0 %copy-start.44 = (f32[1,1536]{1,0:T(1,128)S(1)}, f32[1,1536]{1,0:T(1,128)}, u32[]{:S(2)}) copy-start(f32[1,1536]{1,0:T(1,128)} %get-tuple-element.136.refs_4_) | copy-start | bytes 18436
  457.8 29.0 %copy-start.45 = (f32[1,1536]{1,0:T(1,128)S(1)}, f32[1,1536]{1,0:T(1,128)}, u32[]{:S(2)}) copy-start(f32[1,1536]{1,0:T(1,128)} %get-tuple-element.134.refs_2_) | copy-start | bytes 18436
  513.0 5.5 %copy-start.60 = (bf16[4,128,1536]{2,1,0:T(8,128)(2,1)S(1)}, bf16[4,128,1536]{2,1,0:T(8,128)(2,1)}, u32[]{:S(2)}) copy-start(bf16[4,128,1536]{2,1,0:T(8,128)(2,1)} %get-tuple-element.152) | copy-start | bytes 4718596
  (4 other events, 2.7 us)
Sparse Core Ops, SparseCore 0:
  14.4 113.5 all-gather.2
  129.8 113.4 all-gather.4
  270.3 100.2 reduce-scatter.6
  393.8 111.4 reduce-scatter.8
